TPU v7x, 32 devices: a whole 2x2x4 slice. The times are simulated.
32 devices in a mesh: dp: 8 (over z, y), ctx: 4 (over x, core).
Axes of the slice: x: 2, y: 2, z: 4, core: 2. Of those that a mesh axis runs over, the one named last changes fastest.
Arguments:
- state_input: bfloat16 [8192, 4096], P(('dp', 'ctx')), may hold values from -6 to 6
- gate_values: bfloat16 [8192, 4096], P(('dp', 'ctx')), may hold values from -6 to 6
- input_matrix: bfloat16 [8192, 512], P(('dp', 'ctx')), may hold values from -1.2 to 1.2
- readout_matrix: bfloat16 [8192, 512], P(('dp', 'ctx')), may hold values from -1.1953125 to 1.1953125
- step_unbiased: float32 [8192, 64], P(('dp', 'ctx')), may hold values from -3 to 1280
- step_bias: float32 [64], replicated, may hold values from -1 to 0.5
- decay_rate_log: float32 [64], replicated
- skip_coefficients: float32 [64], replicated, may hold values from 3 to 10
- norm_gain: float32 [4096], replicated, may hold values from 0.1 to 8
- adapter_down: bfloat16 [64, 4096], replicated, may hold values from -0.09375 to 0.09375
- adapter_up: bfloat16 [64, 2048], replicated, may hold values from -0.75 to 0.75
- projection_weight: bfloat16 [2048, 4096], P(('dp', 'ctx')), may hold values from -0.09375 to 0.09375
- output_cotangent: bfloat16 [8192, 2048], P(('dp', 'ctx')), may hold values from -30 to 30
Outputs:
- input_gradient: bfloat16 [8192, 4096], P(('dp', 'ctx'))
- adapter_down_gradient: float32 [64, 4096], P(None, ('dp', 'ctx'))
- adapter_up_gradient: float32 [64, 2048], P(None, ('dp', 'ctx'))
All inputs are finite; a program needn't handle non-finite values.
Results may differ from a plain program's by a relative error of at most 0.009.
Values may be sent and summed in bfloat16 or wider, within the bound.
No kernel may reach another device: no remote copies, remote signals or barrier semaphores. Data moves between devices by JAX's collectives and lax.ppermute only.
A program may use at most 192 MiB of HBM per device.

v0:
```python
import jax
import jax.numpy as jnp
from jax import lax
from jax.sharding import PartitionSpec as P

H = 64
P_SIZE = 64
N = 128
G = 4
Q = 256
INNER_CHANNELS = 4096


EPS_NORM = 1e-05
CLIP_EPSILON = 1e-06
ADAPTER_SCALE = 2.0


def entering(value, axis, join, neutral):
    count, mine = (lax.axis_size(axis), lax.axis_index(axis))
    pieces = jax.tree.map(lambda part: lax.all_gather(part, axis), value)
    running = jax.tree.map(
        lambda part, zero: jnp.full_like(part, 0) + jnp.asarray(zero, part.dtype), value, neutral
    )

    def lap(position, running):
        longer = join(running, jax.tree.map(lambda part: part[position], pieces))
        return jax.tree.map(lambda new, old: jnp.where(position < mine, new, old), longer, running)

    return lax.fori_loop(0, count - 1, lap, running)


def carried_in(value, axis, join, neutral):
    count = lax.axis_size(axis)
    place = lax.axis_index(axis)
    ahead = count - 1 - place
    gathered = jax.tree.map(
        lambda a, kind: lax.all_gather(a.astype(kind), axis), value, (jnp.bfloat16, jnp.bfloat16)
    )
    state = jax.tree.map(lambda a, e: jnp.zeros_like(a) + jnp.asarray(e, a.dtype), value, neutral)

    def one(lap, state):
        source = count - 1 - lap
        return join(
            state,
            jax.tree.map(
                lambda a, own: lax.dynamic_index_in_dim(a, source, 0, False).astype(own.dtype),
                gathered,
                value,
            ),
        )

    return lax.fori_loop(0, ahead, one, state)


def combine(earlier, later):
    return (earlier[0] * later[0], earlier[1] * later[0][:, None, None] + later[1])


def spread_heads(grouped, lead):
    wide = jnp.broadcast_to(grouped[..., :, None, :], lead + (G, H // G, grouped.shape[-1]))
    return wide.reshape(lead + (H, grouped.shape[-1]))


def on_device(
    state_input,
    gate_values,
    input_matrix,
    readout_matrix,
    step_unbiased,
    step_bias,
    decay_rate_log,
    skip_coefficients,
    norm_gain,
    adapter_down,
    adapter_up,
    projection_weight,
    output_cotangent,
):
    row_count = state_input.shape[0]
    block_count = row_count // Q
    group_width = INNER_CHANNELS // G
    per_group = H // G
    step_size = jax.nn.softplus(step_unbiased + step_bias[None, :])
    cum_decay = jnp.cumsum(
        (-jnp.exp(decay_rate_log)[None, :] * step_size).reshape(block_count, Q, H), axis=1
    )
    block_total = cum_decay[:, -1, :]
    x_heads = state_input.reshape(row_count, H, P_SIZE)
    xdt_all = (
        (x_heads * step_size[:, :, None]).astype(jnp.bfloat16).reshape(block_count, Q, H, P_SIZE)
    )
    b_blocks = input_matrix.reshape(block_count, Q, G, N)
    c_blocks = readout_matrix.reshape(block_count, Q, G, N)
    inner_prod = jnp.einsum(
        "kign,kjgn->kgij", c_blocks, b_blocks, preferred_element_type=jnp.float32
    )
    inner_prod = jnp.broadcast_to(
        inner_prod[:, :, None], (block_count, G, per_group, Q, Q)
    ).reshape(block_count, H, Q, Q)
    cum_heads = jnp.swapaxes(cum_decay, 1, 2)
    gap_logs = cum_heads[:, :, :, None] - cum_heads[:, :, None, :]
    causal = (
        lax.broadcasted_iota(jnp.int32, (Q, Q), 0) >= lax.broadcasted_iota(jnp.int32, (Q, Q), 1)
    )[None, None]
    scores = (
        inner_prod * jnp.where(causal, jnp.exp(jnp.where(causal, gap_logs, 0.0)), 0.0)
    ).astype(jnp.bfloat16)
    intra_part = jnp.einsum("khij,kjhp->kihp", scores, xdt_all, preferred_element_type=jnp.float32)
    b_heads = spread_heads(b_blocks, (block_count, Q))
    b_weighted = (jnp.exp(block_total[:, None, :] - cum_decay)[..., None] * b_heads).astype(
        jnp.bfloat16
    )
    block_state = jnp.einsum(
        "kjhn,kjhp->khnp", b_weighted, xdt_all, preferred_element_type=jnp.float32
    )

    def step_forward(run_state, block_item):
        decay_log, fresh_state = block_item
        return (jnp.exp(decay_log)[:, None, None] * run_state + fresh_state, run_state)

    zero_state = jnp.zeros((H, N, P_SIZE), jnp.float32)
    device_state, local_in = lax.scan(step_forward, zero_state, (block_total, block_state))
    device_decay = jnp.exp(jnp.sum(block_total, axis=0))
    identity = (jnp.ones((H,), jnp.float32), zero_state)
    unused_decay, incoming = entering((device_decay, device_state), "ctx", combine, identity)
    before = jnp.cumsum(block_total, axis=0) - block_total
    state_in = local_in + jnp.exp(before)[:, :, None, None] * incoming[None]
    incoming_bf = state_in.astype(jnp.bfloat16).reshape(block_count, G, per_group, N, P_SIZE)
    inter_part = jnp.einsum(
        "kign,kgmnp->kigmp", c_blocks, incoming_bf, preferred_element_type=jnp.float32
    ).reshape(block_count, Q, H, P_SIZE)
    ssd_heads = (intra_part + jnp.exp(cum_decay)[..., None] * inter_part).reshape(
        row_count, H, P_SIZE
    ) + skip_coefficients[None, :, None] * x_heads
    silu_z = jax.nn.silu(gate_values.astype(jnp.float32))
    weight_groups = norm_gain.reshape(G, group_width)
    gated = (ssd_heads.reshape(row_count, INNER_CHANNELS) * silu_z).reshape(
        row_count, G, group_width
    )
    rstd = lax.rsqrt(jnp.mean(gated * gated, axis=-1, keepdims=True) + EPS_NORM)
    normalized = (
        (gated * rstd * weight_groups).reshape(row_count, INNER_CHANNELS).astype(jnp.bfloat16)
    )
    down_product = lax.dot_general(
        normalized, adapter_down, (((1,), (1,)), ((), ())), preferred_element_type=jnp.float32
    ).astype(jnp.bfloat16)
    upper_gradient = lax.dot_general(
        output_cotangent, adapter_up, (((1,), (1,)), ((), ())), preferred_element_type=jnp.float32
    ).astype(jnp.bfloat16)
    down_portion = ADAPTER_SCALE * lax.dot_general(
        upper_gradient, normalized, (((0,), (0,)), ((), ())), preferred_element_type=jnp.float32
    )
    up_portion = ADAPTER_SCALE * lax.dot_general(
        down_product, output_cotangent, (((0,), (0,)), ((), ())), preferred_element_type=jnp.float32
    )
    adapter_initial = ADAPTER_SCALE * jnp.dot(
        upper_gradient, adapter_down, preferred_element_type=jnp.float32
    )
    combined_weight = lax.all_gather(projection_weight, ("dp", "ctx"), axis=0, tiled=True)
    normed_gradient = adapter_initial + jnp.dot(
        output_cotangent, combined_weight, preferred_element_type=jnp.float32
    )
    weighted_grad = normed_gradient.reshape(row_count, G, group_width) * weight_groups
    d_gated = rstd * weighted_grad - gated * (rstd * rstd * rstd) * jnp.mean(
        gated * weighted_grad, axis=-1, keepdims=True
    )
    d_ssd = d_gated.reshape(row_count, INNER_CHANNELS) * silu_z
    d_ssd_bf = d_ssd.reshape(block_count, Q, H, P_SIZE).astype(jnp.bfloat16)
    intra_back = jnp.einsum("khij,kihp->kjhp", scores, d_ssd_bf, preferred_element_type=jnp.float32)
    c_heads = spread_heads(c_blocks, (block_count, Q))
    c_weighted = (jnp.exp(cum_decay)[..., None] * c_heads).astype(jnp.bfloat16)
    block_grad = jnp.einsum(
        "kihn,kihp->khnp", c_weighted, d_ssd_bf, preferred_element_type=jnp.float32
    )

    def step_backward(grad_state, block_item):
        decay_log, fresh_state = block_item
        return (jnp.exp(decay_log)[:, None, None] * grad_state + fresh_state, grad_state)

    device_grad, local_out = lax.scan(
        step_backward, zero_state, (block_total, block_grad), reverse=True
    )
    unused_back, outgoing = carried_in((device_decay, device_grad), "ctx", combine, identity)
    after_sum = jnp.flip(jnp.cumsum(jnp.flip(block_total, axis=0), axis=0), axis=0) - block_total
    grad_in = local_out + jnp.exp(after_sum)[:, :, None, None] * outgoing[None]
    outgoing_bf = grad_in.astype(jnp.bfloat16)
    cross_part = jnp.einsum(
        "kjhn,khnp->kjhp", b_weighted, outgoing_bf, preferred_element_type=jnp.float32
    )
    grad_heads = step_size[:, :, None] * (intra_back + cross_part).reshape(
        row_count, H, P_SIZE
    ) + skip_coefficients[None, :, None] * d_ssd.reshape(row_count, H, P_SIZE)
    input_gradient = grad_heads.reshape(row_count, INNER_CHANNELS).astype(jnp.bfloat16)
    down_total, up_total = lax.psum((down_portion, up_portion), ("dp", "ctx"))
    down_root_mean = jnp.sqrt(jnp.mean(down_total * down_total) + CLIP_EPSILON)
    up_root_mean = jnp.sqrt(jnp.mean(up_total * up_total) + CLIP_EPSILON)
    device_total = lax.axis_size(("dp", "ctx"))
    position = lax.axis_index(("dp", "ctx"))
    width_a = down_total.shape[1] // device_total
    width_b = up_total.shape[1] // device_total
    down_fraction = lax.dynamic_slice_in_dim(down_total, position * width_a, width_a, 1)
    up_fraction = lax.dynamic_slice_in_dim(up_total, position * width_b, width_b, 1)
    adapter_down_gradient = down_fraction / jnp.maximum(1.0, down_root_mean)
    adapter_up_gradient = up_fraction / jnp.maximum(1.0, up_root_mean)
    return (input_gradient, adapter_down_gradient, adapter_up_gradient)


def solution(mesh):
    placed = (
        P(("dp", "ctx"), None),
        P(("dp", "ctx"), None),
        P(("dp", "ctx"), None),
        P(("dp", "ctx"), None),
        P(("dp", "ctx"), None),
        P(),
        P(),
        P(),
        P(),
        P(),
        P(),
        P(("dp", "ctx"), None),
        P(("dp", "ctx"), None),
    )
    return jax.shard_map(
        on_device,
        mesh=mesh,
        in_specs=placed,
        out_specs=(P(("dp", "ctx"), None), P(None, ("dp", "ctx")), P(None, ("dp", "ctx"))),
        check_vma=False,
    )
```

profile of v0, /device:TPU:0, one launch (start us, length us, event | category | flops | bytes accessed | tf_op | source)
XLA Modules:
  0.0 479.0 jit_solution(8963864661822458579)
XLA Ops:
  8.0 1.0 multiply_bitcast_fusion
  11.9 1.0 reshape.323
  14.8 3.0 copy.121
  17.8 3.8 fusion.3
  21.6 2.1 copy-done.2
  23.7 2.2 convolution_add_fusion.1
  28.3 5.7 %fusion.1 = bf16[64,256,256]{2,1,0:T(8,128)(2,1)} fusion(f32[64,256]{1,0:T(8,128)S(1)} %bitcast_add_fusion.2, f32[4,256,256]{2,1,0:T(8,128)S(1)} %fusion.10, pred[256,256]{1,0:T(8,128)(4,1)S(1)} %iota_compare_fusion), kind=kLoop, calls=%fused_computation.8 | loop fusion | flops 20971520 | bytes 9568256 | tf_op jit(solution)/shard_map/convert_element_type | solution.py:108
  33.9 6.6 %all-gather = f32[4,1,64]{2,1,0:T(1,128)} all-gather(f32[1,1,64]{2,1,0:T(1,128)S(1)} %copy-done.22), channel_id=2, replica_groups=mesh['dp'=8,'ctx'=4] {'ctx'}, dimensions={0}, use_global_device_ids=true | all-gather | bytes 1280 | tf_op jit(solution)/shard_map/all_gather | solution.py:21
  40.5 1.1 convolution_convert_fusion
  41.6 45.5 %all-gather.10.cloned.1.call-done = f32[256,128,64]{1,2,0:T(8,128)} async-done(((f32[64,128,64]{1,2,0:T(8,128)}), f32[256,128,64]{1,2,0:T(8,128)}) %all-gather.10.cloned.1.call-update) | async-done | bytes 8388624 | tf_op jit(solution)/shard_map/all_gather | solution.py:21
  87.1 32.2 %while.19 = (s32[]{:T(128)}, f32[64,128,64]{2,1,0:T(8,128)}, s32[]{:T(128)}, f32[4,64]{1,0:T(4,128)}, f32[4,64,128,64]{2,3,1,0:T(8,128)}, /*index=5*/s32[]{:T(128)}, s32[]{:T(128)}) while((s32[]{:T(128)}, f32[64,128,64]{2,1,0:T(8,128)}, s32[]{:T(128)}, f32[4,64]{1,0:T(4,128)}, f32[4,64,128,64]{2,3,1,0:T(8,128)}, ...), condition=%wide.region_3.4_spmd.clone, body=%wide.region_2.3_spmd.clone.sunk | while | flops 2097156 | bytes 14680945 | solution.py:30
  87.1 1.7 constant_dynamic-slice_fusion.5
  88.8 2.7 copy.183
  92.2 4.7 fusion.43
  96.9 1.9 constant_dynamic-slice_fusion.5
  98.8 2.7 copy.183
  102.1 6.0 %fusion.43 = f32[64,128,64]{2,1,0:T(8,128)} fusion(f32[1,64,128,64]{3,2,1,0:T(8,128)} %copy.183, f32[64,128,64]{2,1,0:T(8,128)} %get-tuple-element.400, f32[64]{0:T(128)S(1)} %dynamic-slice_bitcast_fusion.2, pred[]{:T(512)S(6)} %compare.3, pred[]{:T(512)S(6)} %lt.51), kind=kLoop, calls=%fused_computation.4.clone.1 | loop fusion | flops 2097152 | bytes 6291714 | tf_op jit(solution)/shard_map/while/body/eval_jaxpr/jit(_where)/select_n | solution.py:28
  108.2 1.7 constant_dynamic-slice_fusion.5
  109.9 2.7 copy.183
  113.3 6.0 %fusion.43 = f32[64,128,64]{2,1,0:T(8,128)} fusion(f32[1,64,128,64]{3,2,1,0:T(8,128)} %copy.183, f32[64,128,64]{2,1,0:T(8,128)} %get-tuple-element.400, f32[64]{0:T(128)S(1)} %dynamic-slice_bitcast_fusion.2, pred[]{:T(512)S(6)} %compare.3, pred[]{:T(512)S(6)} %lt.51), kind=kLoop, calls=%fused_computation.4.clone.1 | loop fusion | flops 2097152 | bytes 6291714 | tf_op jit(solution)/shard_map/while/body/eval_jaxpr/jit(_where)/select_n | solution.py:28
  119.3 2.8 multiply_convert_fusion.2
  122.0 2.8 fusion.15
  124.8 8.3 %fusion.8 = f32[1,256,64,64]{1,3,2,0:T(8,128)} fusion(f32[4,16,64,256]{3,2,1,0:T(8,128)} %fusion.15, bf16[64,256,256]{2,1,0:T(8,128)(2,1)S(1)} %copy-done.1, f32[256,64]{0,1:T(8,128)S(1)} %copy.129, f32[256,64,64]{0,2,1:T(8,128)} %bitcast.133, f32[256,64]{0,1:T(8,128)S(1)} %get-tuple-element.320), kind=kOutput, calls=%fused_computation.22 | convolution fusion | flops 541065216 | bytes 21102592 | tf_op jit(solution)/shard_map/khij,kjhp->kihp/dot_general | solution.py:109
  133.1 5.8 %copy.135 = f32[256,4096]{1,0:T(8,128)} copy(f32[256,4096]{0,1:T(8,128)} %bitcast.141) | data formatting | bytes 8388608 | tf_op jit(solution)/shard_map/reshape | solution.py:133
  139.0 6.2 %add_multiply_fusion = f32[256,4096]{1,0:T(8,128)} fusion(f32[256,4096]{1,0:T(8,128)} %copy.135, f32[4096]{0:T(1024)S(1)} %mul.324, bf16[256,4096]{1,0:T(8,128)(2,1)} %param.18, bf16[256,4096]{1,0:T(8,128)(2,1)S(1)} %copy-done.8), kind=kLoop, calls=%fused_computation.29 | loop fusion | flops 9437184 | bytes 12599296 | tf_op jit(solution)/shard_map/mul | solution.py:138
  145.2 6.0 %reshape.335 = f32[256,4,1024]{2,1,0:T(4,128)} reshape(f32[256,4096]{1,0:T(8,128)} %add_multiply_fusion) | data formatting | bytes 8388608 | tf_op jit(solution)/shard_map/reshape | solution.py:138
  151.2 53.6 %all-gather.8.cloned.1.call-done = bf16[2048,4096]{1,0:T(8,128)(2,1)} async-done(((bf16[64,4096]{1,0:T(8,128)(2,1)}), bf16[2048,4096]{1,0:T(8,128)(2,1)}) %all-gather.8.cloned.1.call-update) | async-done | bytes 16777232 | tf_op jit(solution)/shard_map/all_gather | solution.py:160
  204.8 8.1 %fusion.19 = f32[256,4096]{1,0:T(8,128)S(1)} fusion(bf16[256,2048]{1,0:T(8,128)(2,1)S(1)} %copy-done, bf16[2048,4096]{1,0:T(8,128)(2,1)} %all-gather.8.cloned.1.call-done), kind=kOutput, calls=%fused_computation.71 | convolution fusion | flops 4294967296 | bytes 22020096 | tf_op jit(solution)/shard_map/dot_general | solution.py:161
  213.0 2.7 fusion.4
  215.7 6.0 %reshape.336 = f32[256,4,1024]{2,1,0:T(4,128)} reshape(f32[256,4096]{1,0:T(8,128)} %fusion.4) | data formatting | bytes 8388608 | tf_op jit(solution)/shard_map/reshape | solution.py:164
  221.7 5.0 %multiply_reduce_fusion.1 = (f32[256,4]{1,0:T(8,128)S(1)}, f32[256,4]{1,0:T(8,128)S(1)}) fusion(f32[256,4,1024]{2,1,0:T(4,128)} %reshape.335, f32[256,4,1024]{2,1,0:T(4,128)} %reshape.336, f32[4,1024]{1,0:T(4,128)S(1)} %copy-done.19), kind=kLoop, calls=%fused_computation.28 | loop fusion | flops 5240832 | bytes 8413184 | tf_op jit(solution)/shard_map/reduce_sum | solution.py:141
  227.4 5.7 %copy.163 = f32[32,8,4,1024]{3,1,2,0:T(8,128)} copy(f32[32,8,4,1024]{3,2,1,0:T(4,128)S(1)} %bitcast.142) | data formatting | bytes 8388608
  234.0 5.7 %copy.162 = f32[32,8,4,1024]{3,1,2,0:T(8,128)} copy(f32[32,8,4,1024]{3,2,1,0:T(4,128)S(1)} %bitcast.143) | data formatting | bytes 8388608
  240.5 4.1 copy.161
  244.7 6.4 %fusion.18 = (bf16[256,4096]{1,0:T(8,128)(2,1)}, f32[256,4096]{1,0:T(8,128)}, bf16[256,4096]{1,0:T(8,128)(2,1)S(1)}) fusion(bf16[256,4096]{1,0:T(8,128)(2,1)} %param.18, f32[256,4096]{1,0:T(8,128)S(1)} %bitcast.137, f32[256,4096]{1,0:T(8,128)S(1)} %copy-done.4, f32[256,4096]{1,0:T(8,128)} %bitcast.138, f32[256,4096]{1,0:T(8,128)S(1)} %bitcast.139, ...), kind=kLoop, calls=%fused_computation.70 | loop fusion | flops 15728640 | bytes 31473664 | tf_op jit(solution)/shard_map/convert_element_type | solution.py:169
  251.1 1.5 convolution_multiply_fusion.1
  252.6 3.1 convolution_multiply_fusion.2
  255.8 3.9 fusion.2
  259.7 3.3 copy.141
  263.0 4.2 add_convert_fusion.1
  267.2 2.3 mul.307
  269.5 5.7 %copy.146 = f32[256,4096]{1,0:T(8,128)} copy(f32[256,4096]{0,1:T(8,128)} %bitcast.145) | data formatting | bytes 8388608 | tf_op jit(solution)/shard_map/mul | solution.py:191
  275.2 5.0 %all-gather.3 = bf16[4,1,64]{2,1,0:T(2,128)(2,1)S(1)} all-gather(bf16[1,1,64]{2,1,0:T(2,128)(2,1)S(1)} %copy-done.21), channel_id=5, replica_groups=mesh['dp'=8,'ctx'=4] {'ctx'}, dimensions={0}, use_global_device_ids=true | all-gather | bytes 640 | tf_op jit(solution)/shard_map/all_gather | solution.py:38
  280.2 7.0 %fusion.20 = f32[64,64,256]{2,1,0:T(8,128)} fusion(bf16[256,64,64]{0,2,1:T(8,128)(2,1)S(1)} %bitcast.136, bf16[64,256,256]{2,1,0:T(8,128)(2,1)} %fusion.1), kind=kOutput, calls=%fused_computation.72 | convolution fusion | flops 536870912 | bytes 14680064 | tf_op jit(solution)/shard_map/khij,kihp->kjhp/dot_general | solution.py:170
  287.3 98.9 %all-reduce.3.cloned.1.call-done = (f32[64,4096]{1,0:T(8,128)}, f32[64,2048]{1,0:T(8,128)}) async-done(((f32[64,4096]{1,0:T(8,128)}, f32[64,2048]{1,0:T(8,128)}), (f32[64,4096]{1,0:T(8,128)}, f32[64,2048]{1,0:T(8,128)})) %all-reduce.3.cloned.1.call-update) | async-done | bytes 1572880 | tf_op jit(solution)/shard_map/psum | solution.py:195
  386.2 2.1 multiply_reduce_fusion.2
  388.9 1.8 multiply_reduce_fusion.3
  391.4 1.4 dynamic-slice_divide_fusion.1
  392.8 1.5 dynamic-slice_divide_fusion
  394.3 27.3 %all-gather.12.cloned.1.call-done = bf16[256,128,64]{1,2,0:T(8,128)(2,1)} async-done(((bf16[64,128,64]{1,2,0:T(8,128)(2,1)}), bf16[256,128,64]{1,2,0:T(8,128)(2,1)}) %all-gather.12.cloned.1.call-update) | async-done | bytes 4194320 | tf_op jit(solution)/shard_map/all_gather | solution.py:38
  421.6 2.5 broadcast_in_dim.45
  424.1 26.9 %while.18 = (s32[]{:T(128)}, f32[64,128,64]{2,1,0:T(8,128)}, s32[]{:T(128)}, bf16[4,64]{1,0:T(4,128)(2,1)S(1)}, bf16[4,64,128,64]{2,3,1,0:T(8,128)(2,1)}, /*index=5*/s32[]{:T(128)}, s32[]{:T(128)}, s32[]{:T(128)}, s32[]{:T(128)}) while((s32[]{:T(128)}, f32[64,128,64]{2,1,0:T(8,128)}, s32[]{:T(128)}, bf16[4,64]{1,0:T(4,128)(2,1)S(1)}, ...), condition=%wide.region_7.8_spmd, body=%wide.region_6.7_spmd.sunk | while | flops 1572934 | bytes 9437979 | solution.py:53
  424.1 2.3 constant_dynamic-slice_fusion.4
  426.3 2.0 copy.182
  428.4 4.6 convert_add_fusion.2
  433.0 2.3 constant_dynamic-slice_fusion.4
  435.3 2.0 copy.182
  437.3 4.6 convert_add_fusion.2
  442.0 2.3 constant_dynamic-slice_fusion.4
  444.3 2.0 copy.182
  446.3 4.6 convert_add_fusion.2
  451.0 8.4 %convolution_add_fusion = f32[64,64,256]{2,1,0:T(8,128)} fusion(f32[64,64,256]{2,1,0:T(8,128)} %fusion.20, bf16[256,64,128]{2,0,1:T(8,128)(2,1)} %copy-done.2, f32[64,128,64]{2,1,0:T(8,128)} %get-tuple-element.212, f32[64]{0:T(128)S(1)} %copy-done.20), kind=kOutput, calls=%fused_computation.33 | convolution fusion | flops 270532608 | bytes 14680320 | tf_op jit(solution)/shard_map/kjhn,khnp->kjhp/dot_general | solution.py:188
  459.4 5.6 %copy.147 = f32[256,4096]{1,0:T(8,128)} copy(f32[256,4096]{0,1:T(8,128)} %bitcast.140) | data formatting | bytes 8388608 | tf_op jit(solution)/shard_map/reshape | solution.py:191
  465.0 7.3 %add_convert_fusion = bf16[256,4096]{1,0:T(8,128)(2,1)} fusion(f32[256,4096]{1,0:T(8,128)} %get-tuple-element.316, f32[256,4096]{1,0:T(8,128)} %copy.146, f32[256,4096]{1,0:T(8,128)} %copy.147, f32[4096]{0:T(1024)S(1)} %mul.324), kind=kLoop, calls=%fused_computation.24 | loop fusion | flops 4194304 | bytes 14696448 | tf_op jit(solution)/shard_map/convert_element_type | solution.py:194
  (101 shorter events, 12.1 us)
Async XLA Ops:
  7.2 33.3 %copy-start = (bf16[256,2048]{1,0:T(8,128)(2,1)S(1)}, bf16[256,2048]{1,0:T(8,128)(2,1)}, u32[]{:S(2)}) copy-start(bf16[256,2048]{1,0:T(8,128)(2,1)} %param.29) | copy-start | bytes 3145732
  7.2 7.6 %copy-start.7 = (bf16[256,4096]{1,0:T(8,128)(2,1)S(1)}, bf16[256,4096]{1,0:T(8,128)(2,1)}, u32[]{:S(2)}) copy-start(bf16[256,4096]{1,0:T(8,128)(2,1)} %param.17) | copy-start | bytes 6291460
  7.2 79.9 %all-gather.10.cloned.1.call-start = ((), (), s32[]{:S(2)}) async-start(), calls=%async_computation.1 | async-start | bytes 10485760 | tf_op jit(solution)/shard_map/all_gather | solution.py:21
  10.7 0.6 copy-start.12
  11.9 9.7 %copy-start.23 = (f32[64]{0:T(128)}, f32[64]{0:T(128)S(1)}, u32[]{:S(2)}) copy-start(f32[64]{0:T(128)S(1)} %get-tuple-element.326) | copy-start | bytes 772
  17.8 5.9 %copy-start.3 = (f32[256,4096]{0,1:T(8,128)S(1)}, f32[256,4096]{0,1:T(8,128)}, u32[]{:S(2)}) copy-start(f32[256,4096]{0,1:T(8,128)} %copy.121) | copy-start | bytes 12582916
  21.6 2.1 copy-start.2
  23.7 3.1 copy-start.11
  23.7 3.3 copy-start.13
  23.7 3.4 copy-start.25
  23.7 3.6 copy-start.17
  25.9 2.0 copy-start.10
  26.0 178.9 %all-gather.8.cloned.1.call-start = ((), (), s32[]{:S(2)}) async-start(), calls=%async_computation | async-start | bytes 17301504 | tf_op jit(solution)/shard_map/all_gather | solution.py:160
  26.7 359.4 %all-reduce.3.cloned.1.call-start = ((), (), s32[]{:S(2)}) async-start(), calls=%async_computation.3 | async-start | bytes 3145728 | tf_op jit(solution)/shard_map/psum | solution.py:195
  28.3 5.7 %copy-start.22 = (f32[1,1,64]{2,1,0:T(1,128)S(1)}, f32[1,1,64]{2,1,0:T(1,128)}, u32[]{:S(2)}) copy-start(f32[1,1,64]{2,1,0:T(1,128)} %get-tuple-element.324) | copy-start | bytes 772
  28.3 12.2 %copy-start.16 = (bf16[64,2048]{1,0:T(8,128)(2,1)S(1)}, bf16[64,2048]{1,0:T(8,128)(2,1)}, u32[]{:S(2)}) copy-start(bf16[64,2048]{1,0:T(8,128)(2,1)} %param.27) | copy-start | bytes 786436
  119.3 5.6 %copy-start.1 = (bf16[64,256,256]{2,1,0:T(8,128)(2,1)S(1)}, bf16[64,256,256]{2,1,0:T(8,128)(2,1)}, u32[]{:S(2)}) copy-start(bf16[64,256,256]{2,1,0:T(8,128)(2,1)} %fusion.1) | copy-start | bytes 25165828
  133.1 5.9 %copy-start.8 = (bf16[256,4096]{1,0:T(8,128)(2,1)S(1)}, bf16[256,4096]{1,0:T(8,128)(2,1)}, u32[]{:S(2)}) copy-start(bf16[256,4096]{1,0:T(8,128)(2,1)} %param.17) | copy-start | bytes 6291460
  151.2 61.8 %copy-start.9 = (bf16[64,4096]{1,0:T(8,128)(2,1)S(1)}, bf16[64,4096]{1,0:T(8,128)(2,1)}, u32[]{:S(2)}) copy-start(bf16[64,4096]{1,0:T(8,128)(2,1)} %param.26) | copy-start | bytes 1572868
  151.2 61.8 %copy-start.14 = (bf16[256,64]{0,1:T(8,128)(2,1)S(1)}, bf16[256,64]{0,1:T(8,128)(2,1)}, u32[]{:S(2)}) copy-start(bf16[256,64]{0,1:T(8,128)(2,1)} %convolution_convert_fusion) | copy-start | bytes 98308
  215.7 6.0 %copy-start.19 = (f32[4,1024]{1,0:T(4,128)S(1)}, f32[4,1024]{1,0:T(4,128)}, u32[]{:S(2)}) copy-start(f32[4,1024]{1,0:T(4,128)} %mul.342) | copy-start | bytes 49156
  239.9 4.8 copy-start.6
  239.9 4.8 copy-start.18
  240.5 4.2 copy-start.4
  240.5 4.2 copy-start.5
  244.7 6.4 %copy-start.15 = (bf16[256,64]{0,1:T(8,128)(2,1)S(1)}, bf16[256,64]{0,1:T(8,128)(2,1)}, u32[]{:S(2)}) copy-start(bf16[256,64]{0,1:T(8,128)(2,1)} %convolution_convert_fusion) | copy-start | bytes 98308
  255.7 165.9 %all-gather.12.cloned.1.call-start = ((), (), s32[]{:S(2)}) async-start(), calls=%async_computation.2 | async-start | bytes 5242880 | tf_op jit(solution)/shard_map/all_gather | solution.py:38
  255.8 7.2 %copy-start.24 = (f32[64]{0:T(128)S(1)}, f32[64]{0:T(128)}, u32[]{:S(2)}) copy-start(f32[64]{0:T(128)} %copy-done.23) | copy-start | bytes 772
  269.5 5.7 %copy-start.21 = (bf16[1,1,64]{2,1,0:T(2,128)(2,1)S(1)}, bf16[1,1,64]{2,1,0:T(2,128)(2,1)}, u32[]{:S(2)}) copy-start(bf16[1,1,64]{2,1,0:T(2,128)(2,1)} %get-tuple-element.322) | copy-start | bytes 388
  424.1 26.9 %copy-start.20 = (f32[64]{0:T(128)S(1)}, f32[64]{0:T(128)}, u32[]{:S(2)}) copy-start(f32[64]{0:T(128)} %get-tuple-element.325) | copy-start | bytes 772
Sparse Core Ops, SparseCore 0:
  26.1 60.9 all-gather.9
  90.0 114.8 all-gather.7
  255.8 130.2 all-reduce.2
  388.1 33.3 all-gather.11
where the time goes:
time: 484 us; the launch traced here: 479 us
  waiting for transfers between devices  226 us (47%)
  local copies, waits for them, and re-layouts  91.9 us (19%)
  other arithmetic  83.8 us (17%)
  matrix products  49.6 us (10%)
  between operations  15.8 us (3%)
  blocking collectives  11.6 us (2%)
    psum x1, waiting for transfers between devices, on_device(): down_total, up_total = lax.psum((down_portion, up_portion), ('dp', 'ctx'))  98.9 us
    all_gather x1, waiting for transfers between devices, on_device(): lax.all_gather(projection_weight, ('dp', 'ctx'), axis=0, tiled=True)  53.6 us
    all_gather x1, waiting for transfers between devices, entering(): pieces = jax.tree.map(lambda part: lax.all_gather(part, axis), value)  45.5 us
    all_gather x1, waiting for transfers between devices, carried_in(): lax.all_gather(a.astype(kind), axis)  27.3 us
    unnamed x56, local copies, waits for them, and re-layouts  17.8 us
    select_n x3, other arithmetic, lap(): jnp.where(position < mine, new, old)  16.7 us
    add x3, other arithmetic, combine(): earlier[1] * later[0][:, None, None] + later[1]  13.9 us
    dynamic_slice x6, local copies, waits for them, and re-layouts, lap(): longer = join(running, jax.tree.map(lambda part: part[position], pieces))  13.5 us
  transfers between devices with their start and end apart: 4, of which 4 were waited for; matrix products, arithmetic and copies ran while one was open for 22% of the time, Pallas kernels for 0%

commit v1 on v0

v1 whole, which is shorter than its diff:
```python
import functools

import jax
import jax.numpy as jnp
from jax import lax
from jax.experimental import pallas as pl
from jax.experimental.pallas import tpu as pltpu
from jax.sharding import Mesh
from jax.sharding import PartitionSpec as P

P_SIZE = 64
N = 128
G = 4
Q = 256
EPS_NORM = 1e-05
CLIP_EPSILON = 1e-06
ADAPTER_SCALE = 2.0
WAVES = 2
VMEM_BYTES = 44 * 1024 * 1024

F32 = jnp.float32
BF16 = jnp.bfloat16
AXES = ("dp", "x", "core")


def dot(a, b, dims=((1,), (0,))):
    return lax.dot_general(a, b, (dims, ((), ())), preferred_element_type=F32)


def spread(values, pattern):
    high = values.astype(BF16)
    rest = values - high.astype(F32)
    mid = rest.astype(BF16)
    low = (rest - mid.astype(F32)).astype(BF16)
    return dot(high, pattern) + dot(mid, pattern) + dot(low, pattern)


def pair_rows(pair):
    lane = lax.broadcasted_iota(jnp.int32, pair.shape, 1)
    zero = jnp.zeros_like(pair)
    return jnp.concatenate(
        [jnp.where(lane < P_SIZE, pair, zero), jnp.where(lane >= P_SIZE, pair, zero)], axis=0
    )


def whole(shape):
    return pl.BlockSpec(shape, lambda *_: (0,) * len(shape))


def params(*semantics):
    return pltpu.CompilerParams(
        dimension_semantics=semantics or None, vmem_limit_bytes=VMEM_BYTES
    )


def local_kernel(
    first, heads, x_ref, b_ref, c_ref, step_ref, cum_ref, cum_t_ref, skip_ref, pattern_ref,
    scores_ref, ssd_ref, state_ref, total_ref, step_wide_ref, cum_wide_ref, weight_ref, decay_ref,
):
    block = pl.program_id(0)
    own = slice(first, first + heads)
    pattern = pattern_ref[...]
    step = step_ref[:, own]
    cum = cum_ref[:, own]
    last = cum[Q - 1 : Q, :]
    step_wide = spread(step, pattern)
    cum_wide = spread(jnp.exp(cum), pattern)
    weight = spread(step * jnp.exp(last - cum), pattern)
    step_wide_ref[...] = step_wide
    cum_wide_ref[...] = cum_wide
    weight_ref[...] = weight
    decay = cum_wide[Q - 1 : Q, :]
    decay_ref[...] = jnp.broadcast_to(decay, decay_ref.shape)
    x = x_ref[...].astype(F32)
    xdt = (x * step_wide).astype(BF16)
    state = dot(b_ref[...], (x * weight).astype(BF16), ((0,), (0,)))
    state_ref[...] = state

    @pl.when(block == 0)
    def _():
        total_ref[...] = state

    @pl.when(block > 0)
    def _():
        total_ref[...] = total_ref[...] * decay + state

    inner = dot(b_ref[...], c_ref[...], ((1,), (1,)))
    causal = lax.broadcasted_iota(jnp.int32, (Q, Q), 1) >= lax.broadcasted_iota(
        jnp.int32, (Q, Q), 0
    )
    masked = jnp.where(causal, inner, 0.0)
    for pair in range(heads // 2):
        parts = []
        for head in (2 * pair, 2 * pair + 1):
            gap = cum_t_ref[0, first + head : first + head + 1, :] - cum[:, head : head + 1]
            part = (masked * jnp.exp(jnp.where(causal, gap, 0.0))).astype(BF16)
            scores_ref[:, head * Q : (head + 1) * Q] = part
            parts.append(part)
        lanes = slice(pair * 2 * P_SIZE, (pair + 1) * 2 * P_SIZE)
        intra = dot(jnp.concatenate(parts, axis=0), pair_rows(xdt[:, lanes]), ((0,), (0,)))
        ssd_ref[:, lanes] = intra + skip_ref[:, lanes] * x_ref[:, lanes].astype(F32)


def local_part(group, heads, x, b, c, step, cum, cum_t, skip, pattern):
    rows = x.shape[0]
    blocks = rows // Q
    width = heads * P_SIZE
    row_block = pl.BlockSpec((Q, width), lambda i: (i, 0))
    return pl.pallas_call(
        functools.partial(local_kernel, group * heads, heads),
        grid=(blocks,),
        in_specs=[
            pl.BlockSpec((Q, width), lambda i: (i, group)),
            pl.BlockSpec((Q, N), lambda i: (i, group)),
            pl.BlockSpec((Q, N), lambda i: (i, group)),
            pl.BlockSpec((Q, step.shape[1]), lambda i: (i, 0)),
            pl.BlockSpec((Q, step.shape[1]), lambda i: (i, 0)),
            pl.BlockSpec((1,) + cum_t.shape[1:], lambda i: (i, 0, 0)),
            pl.BlockSpec((1, width), lambda i: (0, group)),
            whole(pattern.shape),
        ],
        out_specs=[
            pl.BlockSpec((Q, heads * Q), lambda i: (i, 0)),
            row_block,
            pl.BlockSpec((N, width), lambda i: (i, 0)),
            pl.BlockSpec((N, width), lambda i: (0, 0)),
            row_block,
            row_block,
            row_block,
            pl.BlockSpec((8, width), lambda i: (i, 0)),
        ],
        out_shape=[
            jax.ShapeDtypeStruct((rows, heads * Q), BF16),
            jax.ShapeDtypeStruct((rows, width), F32),
            jax.ShapeDtypeStruct((blocks * N, width), F32),
            jax.ShapeDtypeStruct((N, width), F32),
            jax.ShapeDtypeStruct((rows, width), F32),
            jax.ShapeDtypeStruct((rows, width), F32),
            jax.ShapeDtypeStruct((rows, width), F32),
            jax.ShapeDtypeStruct((blocks * 8, width), F32),
        ],
        compiler_params=params("arbitrary"),
        cost_estimate=pl.CostEstimate(
            flops=rows * width * Q * 4, bytes_accessed=rows * width * 24, transcendentals=0
        ),
        name="local_part",
    )(x, b, c, step, cum, cum_t, skip, pattern)


def norm_kernel(
    blocks, c_ref, incoming_ref, state_ref, decay_ref, cum_wide_ref, ssd_ref, z_ref, gain_ref,
    down_ref, up_ref, hat_ref, slope_ref, product_ref, sum_ref,
):
    gain = gain_ref[...]
    run = incoming_ref[...].astype(F32)
    total = None
    for block in range(blocks):
        rows = slice(block * Q, (block + 1) * Q)
        inter = dot(c_ref[rows, :], run.astype(BF16))
        ssd = ssd_ref[rows, :] + cum_wide_ref[rows, :] * inter
        z = z_ref[rows, :].astype(F32)
        silu = z / (1.0 + jnp.exp(-z))
        gated = ssd * silu
        rstd = lax.rsqrt(jnp.mean(gated * gated, axis=1, keepdims=True) + EPS_NORM)
        hat = gated * rstd
        normed = (hat * gain).astype(BF16)
        hat_ref[rows, :] = hat.astype(hat_ref.dtype)
        slope_ref[rows, :] = rstd * silu
        product_ref[rows, :] = dot(normed, down_ref[...], ((1,), (1,)))
        part = dot(up_ref[rows, :], normed, ((0,), (0,)))
        total = part if total is None else total + part
        if block + 1 < blocks:
            states = slice(block * N, (block + 1) * N)
            run = run * decay_ref[block * 8 : block * 8 + 1, :] + state_ref[states, :]
    sum_ref[...] = total


def norm_part(group, c, incoming, state, decay, cum_wide, ssd, z, gain, down, up_twice):
    rows, width = ssd.shape
    rank = down.shape[0]
    blocks = rows // Q
    return pl.pallas_call(
        functools.partial(norm_kernel, blocks),
        grid=(1,),
        in_specs=[
            pl.BlockSpec((rows, N), lambda i: (0, group)),
            whole(incoming.shape),
            whole(state.shape),
            whole(decay.shape),
            whole(cum_wide.shape),
            whole(ssd.shape),
            pl.BlockSpec((rows, width), lambda i: (0, group)),
            pl.BlockSpec((1, width), lambda i: (0, group)),
            pl.BlockSpec((rank, width), lambda i: (0, group)),
            whole(up_twice.shape),
        ],
        out_specs=[
            whole((rows, width)), whole((rows, width)), whole((rows, rank)), whole((rank, width)),
        ],
        out_shape=[
            jax.ShapeDtypeStruct((rows, width), F32),
            jax.ShapeDtypeStruct((rows, width), F32),
            jax.ShapeDtypeStruct((rows, rank), F32),
            jax.ShapeDtypeStruct((rank, width), F32),
        ],
        compiler_params=params("arbitrary"),
        cost_estimate=pl.CostEstimate(
            flops=rows * width * 512, bytes_accessed=rows * width * 20, transcendentals=0
        ),
        name="norm_part",
    )(c, incoming, state, decay, cum_wide, ssd, z, gain, down, up_twice)


def grad_kernel(
    blocks, segments, place_ref, cot_ref, up_ref, down_ref, gain_ref, hat_ref, slope_ref,
    cum_wide_ref, decay_ref, c_ref, *rest,
):
    count = len({segment[0] for segment in segments})
    pieces, rest = rest[:count], rest[count:]
    grad_ref, block_grad_ref, total_ref, weights, sems = rest
    copies = []
    for index, (piece, start, size, slot, offset, column) in enumerate(segments):
        target = pl.multiple_of(place_ref[slot] + offset, 16)
        copy = pltpu.make_async_copy(
            pieces[piece].at[pl.ds(start, size)],
            weights.at[pl.ds(target, size), pl.ds(column, pieces[piece].shape[1])],
            sems.at[index],
        )
        copy.start()
        copies.append(copy)
    for copy in copies:
        copy.wait()
    gain = gain_ref[...]
    later = None
    for block in reversed(range(blocks)):
        rows = slice(block * Q, (block + 1) * Q)
        product = dot(cot_ref[rows, :], weights[...]) + dot(up_ref[rows, :], down_ref[...])
        weighted = product * gain
        hat = hat_ref[rows, :]
        mean = jnp.mean(hat * weighted, axis=1, keepdims=True)
        grad = slope_ref[rows, :] * (weighted - hat * mean)
        grad_ref[rows, :] = grad
        fresh = dot(c_ref[rows, :], (cum_wide_ref[rows, :] * grad).astype(BF16), ((0,), (0,)))
        block_grad_ref[block * N : (block + 1) * N, :] = fresh
        later = (
            fresh
            if later is None
            else later * decay_ref[block * 8 : block * 8 + 1, :] + fresh
        )
    total_ref[...] = later.astype(BF16)


def grad_part(group, place, cot, up_twice, down, gain, hat, slope, cum_wide, decay, c, pieces, segments):
    rows, width = hat.shape
    rank = down.shape[0]
    blocks = rows // Q
    depth = cot.shape[1]
    return pl.pallas_call(
        functools.partial(grad_kernel, blocks, segments),
        grid=(1,),
        in_specs=[
            pl.BlockSpec(memory_space=pltpu.SMEM),
            whole(cot.shape),
            whole(up_twice.shape),
            pl.BlockSpec((rank, width), lambda i: (0, group)),
            pl.BlockSpec((1, width), lambda i: (0, group)),
            whole(hat.shape),
            whole(slope.shape),
            whole(cum_wide.shape),
            whole(decay.shape),
            pl.BlockSpec((rows, N), lambda i: (0, group)),
        ]
        + [pl.BlockSpec(memory_space=pl.ANY)] * len(pieces),
        out_specs=[whole((rows, width)), whole((blocks * N, width)), whole((N, width))],
        out_shape=[
            jax.ShapeDtypeStruct((rows, width), F32),
            jax.ShapeDtypeStruct((blocks * N, width), F32),
            jax.ShapeDtypeStruct((N, width), BF16),
        ],
        scratch_shapes=[
            pltpu.VMEM((depth, width), BF16),
            pltpu.SemaphoreType.DMA((len(segments),)),
        ],
        compiler_params=params("arbitrary"),
        cost_estimate=pl.CostEstimate(
            flops=2 * rows * width * depth, bytes_accessed=depth * width * 2 + rows * width * 20,
            transcendentals=0,
        ),
        name="grad_part",
    )(place, cot, up_twice, down, gain, hat, slope, cum_wide, decay, c, *pieces)


def back_kernel(heads, scores_ref, grad_ref, step_wide_ref, skip_ref, out_ref):
    for pair in range(heads // 2):
        lanes = slice(pair * 2 * P_SIZE, (pair + 1) * 2 * P_SIZE)
        grad = grad_ref[:, lanes]
        back = dot(
            scores_ref[:, 2 * pair * Q : 2 * (pair + 1) * Q], pair_rows(grad.astype(BF16))
        )
        out_ref[:, lanes] = step_wide_ref[:, lanes] * back + skip_ref[:, lanes] * grad


def back_part(group, heads, scores, grad, step_wide, skip):
    rows, width = grad.shape
    row_block = pl.BlockSpec((Q, width), lambda i: (i, 0))
    return pl.pallas_call(
        functools.partial(back_kernel, heads),
        grid=(rows // Q,),
        in_specs=[
            pl.BlockSpec((Q, heads * Q), lambda i: (i, 0)),
            row_block,
            row_block,
            pl.BlockSpec((1, width), lambda i: (0, group)),
        ],
        out_specs=row_block,
        out_shape=jax.ShapeDtypeStruct((rows, width), F32),
        compiler_params=params("arbitrary"),
        cost_estimate=pl.CostEstimate(
            flops=rows * width * Q * 2, bytes_accessed=rows * width * 20, transcendentals=0
        ),
        name="back_part",
    )(scores, grad, step_wide, skip)


def cross_kernel(blocks, b_ref, outgoing_ref, block_grad_ref, decay_ref, weight_ref, base_ref, out_ref):
    run = outgoing_ref[...].astype(F32)
    for block in reversed(range(blocks)):
        rows = slice(block * Q, (block + 1) * Q)
        cross = dot(b_ref[rows, :], run.astype(BF16))
        out_ref[rows, :] = (base_ref[rows, :] + weight_ref[rows, :] * cross).astype(out_ref.dtype)
        if block > 0:
            states = slice(block * N, (block + 1) * N)
            run = run * decay_ref[block * 8 : block * 8 + 1, :] + block_grad_ref[states, :]


def cross_part(group, b, outgoing, block_grad, decay, weight, base):
    rows, width = base.shape
    blocks = rows // Q
    return pl.pallas_call(
        functools.partial(cross_kernel, blocks),
        grid=(1,),
        in_specs=[
            pl.BlockSpec((rows, N), lambda i: (0, group)),
            whole(outgoing.shape),
            whole(block_grad.shape),
            whole(decay.shape),
            whole(weight.shape),
            whole(base.shape),
        ],
        out_specs=whole((rows, width)),
        out_shape=jax.ShapeDtypeStruct((rows, width), BF16),
        compiler_params=params("arbitrary"),
        cost_estimate=pl.CostEstimate(
            flops=rows * width * N * 2, bytes_accessed=rows * width * 12, transcendentals=0
        ),
        name="cross_part",
    )(b, outgoing, block_grad, decay, weight, base)


def ring_order(count):
    return list(range(0, count, 2)) + list(range(count - 1 - count % 2, 0, -2))


def rotations(count):
    return [[(i, (i + k) % count) for i in range(count)] for k in range(count)]


class Gather:
    def __init__(self):
        self.ring = lax.axis_size("dp")
        self.across = lax.axis_size("x")
        order = ring_order(self.ring)
        self.ahead = [(order[i], order[(i + 1) % self.ring]) for i in range(self.ring)]
        self.back = [(b, a) for a, b in self.ahead]
        self.turns = rotations(self.across)
        self.offsets = [0]
        for distance in range(1, (self.ring - 1) // 2 + 1):
            self.offsets += [-distance, distance]
        if self.ring % 2 == 0:
            self.offsets.append(self.ring // 2)
        seat = [0] * self.ring
        for position, member in enumerate(order):
            seat[member] = position
        table = jnp.asarray(order, jnp.int32)
        mine = jnp.asarray(seat, jnp.int32)[lax.axis_index("dp")]
        x = lax.axis_index("x")
        chips = []
        for offset in self.offsets:
            member = table[(mine + offset) % self.ring]
            chips += [member * self.across + (x - k) % self.across for k in range(self.across)]
        self.chips = jnp.stack(chips).astype(jnp.int32)

    def chain(self, own, spans):
        pieces = [(own, [(0 * self.across + s, o, r) for s, o, r in spans])]
        ahead = back = own
        for index in range(1, (self.ring - 1) // 2 + 1):
            ahead = lax.ppermute(ahead, "dp", self.ahead)
            back = lax.ppermute(back, "dp", self.back)
            for place, piece in ((2 * index - 1, ahead), (2 * index, back)):
                pieces.append((piece, [(place * self.across + s, o, r) for s, o, r in spans]))
        if self.ring % 2 == 0:
            half = own.shape[0] // 2
            place = len(self.offsets) - 1
            front, rear, seen = [], [], 0
            for s, o, r in spans:
                slot = place * self.across + s
                if seen + r <= half:
                    front.append((slot, o, r))
                elif seen >= half:
                    rear.append((slot, o, r))
                else:
                    front.append((slot, o, half - seen))
                    rear.append((slot, o + half - seen, r - half + seen))
                seen += r
            pieces.append((lax.ppermute(ahead[:half], "dp", self.ahead), front))
            pieces.append((lax.ppermute(back[half:], "dp", self.back), rear))
        return pieces

    def across_first(self, own):
        rows = own.shape[0]
        parts = [own] + [lax.ppermute(own, "x", turn) for turn in self.turns[1:]]
        spans = [(k, 0, rows) for k in range(self.across)]
        return self.chain(jnp.concatenate(parts, axis=0), spans)

    def across_last(self, own):
        pieces = self.chain(own, [(0, 0, own.shape[0])])
        batches = [pieces[:3], pieces[3:5], pieces[5:]]
        result = list(pieces)
        for batch in batches:
            if not batch:
                continue
            joined = jnp.concatenate([piece for piece, _ in batch], axis=0)
            spans = [span for _, listed in batch for span in listed]
            for k, turn in enumerate(self.turns[1:], 1):
                moved = lax.ppermute(joined, "x", turn)
                result.append((moved, [(slot + k, o, r) for slot, o, r in spans]))
        return result


def layout(parts):
    arrays, segments = [], []
    for pieces, column in parts:
        for array, spans in pieces:
            start = 0
            for slot, offset, rows in spans:
                segments.append((len(arrays), start, rows, slot, offset, column))
                start += rows
            arrays.append(array)
    return arrays, tuple(segments)


def summed_blocks(sum_a, sum_b):
    ring, across = lax.axis_size("dp"), lax.axis_size("x")
    rank = sum_a.shape[0]
    chips = ring * across
    wide_a, wide_b = sum_a.shape[1] // chips, sum_b.shape[1] // chips

    def by_block(value, width):
        return value.reshape(rank, chips, width).transpose(1, 0, 2)

    blocks = jnp.concatenate([by_block(sum_a, wide_a), by_block(sum_b, wide_b)], axis=2)
    blocks = blocks.reshape(ring, across, rank, wide_a + wide_b)
    x, place = lax.axis_index("x"), lax.axis_index("dp")

    def column(index):
        return lax.dynamic_index_in_dim(blocks, index, 1, False)

    total = column(x)
    for k, turn in enumerate(rotations(across)[1:], 1):
        sent = column((x + k) % across).astype(BF16)
        total = total + lax.ppermute(sent, "x", turn).astype(F32)
    distance = ring // 2
    while distance:
        upper = (place // distance) % 2
        kept = lax.dynamic_slice_in_dim(total, upper * distance, distance, 0)
        sent = lax.dynamic_slice_in_dim(total, (1 - upper) * distance, distance, 0)
        pairs = [(i, i ^ distance) for i in range(ring)]
        total = kept + lax.ppermute(sent.astype(BF16), "dp", pairs).astype(F32)
        distance //= 2
    return total[0, :, :wide_a], total[0, :, wide_a:]


def on_device(
    state_input, gate_values, input_matrix, readout_matrix, step_unbiased, step_bias,
    decay_rate_log, skip_coefficients, norm_gain, adapter_down, adapter_up, projection_weight,
    output_cotangent,
):
    ring, across = lax.axis_size("dp"), lax.axis_size("x")
    core = lax.axis_index("core")
    swap = [(0, 1), (1, 0)]
    near_rows = state_input.shape[0]
    groups = G // 2
    heads = step_bias.shape[0] // G
    width = heads * P_SIZE

    def half(value, which, axis=-1):
        size = value.shape[axis] // 2
        return lax.dynamic_slice_in_dim(value, which * size, size, axis)

    def in_order(near, far, axis=0):
        return jnp.concatenate(
            [jnp.where(core == 0, near, far), jnp.where(core == 0, far, near)], axis=axis
        )

    def both_cores(value):
        far = lax.ppermute(half(value, 1 - core), "core", swap)
        return in_order(half(value, core), far)

    gather = Gather()
    shard = both_cores(projection_weight)
    chip_rows = shard.shape[0]
    place = gather.chips * chip_rows
    plans = []
    if WAVES == 1:
        first = gather.across_first(shard[:, :width])
        second = gather.across_last(shard[:, width:])
        plans = [layout([(first, 0)]), layout([(second, 0)])]
    else:
        for group in range(groups):
            part = shard[:, group * width : (group + 1) * width]
            cut = width // 2
            plans.append(
                layout(
                    [(gather.across_first(part[:, :cut]), 0), (gather.across_last(part[:, cut:]), cut)]
                )
            )

    step_raw = both_cores(step_unbiased)
    rows = step_raw.shape[0]
    blocks = rows // Q
    x = both_cores(state_input)
    b = both_cores(input_matrix)
    c = both_cores(readout_matrix)
    z = both_cores(gate_values)
    cot = in_order(output_cotangent, lax.ppermute(output_cotangent, "core", swap))
    step = jax.nn.softplus(step_raw + half(step_bias, core)[None, :])
    log_decay = -jnp.exp(half(decay_rate_log, core))[None, :] * step
    cum_blocks = jnp.cumsum(log_decay.reshape(blocks, Q, -1), axis=1)
    cum = cum_blocks.reshape(rows, -1)
    cum_t = jnp.swapaxes(cum_blocks, 1, 2)
    skip = jnp.repeat(half(skip_coefficients, core), P_SIZE)[None, :]
    gain = half(norm_gain, core)[None, :]
    down = half(adapter_down, core)
    pattern = jnp.repeat(jnp.eye(heads, dtype=BF16), P_SIZE, axis=1)

    up_twice = (
        ADAPTER_SCALE * dot(cot, adapter_up, ((1,), (1,))).astype(BF16)
    ).astype(BF16)

    local = [
        local_part(group, heads, x, b, c, step, cum, cum_t, skip, pattern)
        for group in range(groups)
    ]
    forward = [(i, i + 1) for i in range(across - 1)]
    backward = [(i + 1, i) for i in range(across - 1)]

    def carried(fresh, decay, perm):
        chip_decay = None
        sent = fresh.astype(BF16)
        for lap in range(across - 1):
            arrived = lax.ppermute(sent, "x", perm)
            if lap + 2 < across:
                if chip_decay is None:
                    chip_decay = jnp.prod(decay.reshape(blocks, 8, -1)[:, :1], axis=0)
                sent = (arrived.astype(F32) * chip_decay + fresh.astype(F32)).astype(BF16)
        return arrived

    normed = []
    for group in range(groups):
        scores, ssd, state, total, step_wide, cum_wide, weight, decay = local[group]
        incoming = carried(total, decay, forward)
        normed.append(
            norm_part(group, c, incoming, state, decay, cum_wide, ssd, z, gain, down, up_twice)
        )

    product = functools.reduce(jnp.add, [part[2] for part in normed])
    arrived = lax.ppermute(half(product, 1 - core, 0), "core", swap)
    down_product = (half(product, core, 0) + arrived).astype(BF16)
    sum_a = jnp.concatenate([part[3] for part in normed], axis=1)
    part_b = ADAPTER_SCALE * dot(down_product, output_cotangent, ((0,), (0,)))
    far_b = lax.ppermute(half(part_b, 1 - core).astype(BF16), "core", swap)
    sum_b = half(part_b, core) + far_b.astype(F32)
    block_a, block_b = summed_blocks(sum_a, sum_b)
    squares = lax.psum(jnp.stack([jnp.sum(block_a * block_a), jnp.sum(block_b * block_b)]), AXES)
    devices = ring * across * 2
    entries = jnp.asarray([block_a.size * devices, block_b.size * devices], F32)
    scale = 1.0 / jnp.maximum(1.0, jnp.sqrt(squares / entries + CLIP_EPSILON))
    chips = ring * across
    homes = [
        ((chip * 2 + number), number * chips + chip) for chip in range(chips) for number in range(2)
    ]
    joined = jnp.concatenate([block_a * scale[0], block_b * scale[1]], axis=1)
    joined = lax.ppermute(joined, AXES, homes)
    gradient_a = joined[:, : block_a.shape[1]]
    gradient_b = joined[:, block_a.shape[1] :]

    near, far = [], []
    for group in range(groups):
        scores, ssd, state, total, step_wide, cum_wide, weight, decay = local[group]
        hat, slope = normed[group][:2]
        pieces, segments = plans[group]
        grad, block_grad, grad_total = grad_part(
            group, place, cot, up_twice, down, gain, hat, slope, cum_wide, decay, c, pieces, segments
        )
        outgoing = carried(grad_total, decay, backward)
        base = back_part(group, heads, scores, grad, step_wide, skip)
        result = cross_part(group, b, outgoing, block_grad, decay, weight, base)
        far.append(lax.ppermute(half(result, 1 - core, 0), "core", swap))
        near.append(half(result, core, 0))
    input_gradient = in_order(
        jnp.concatenate(near, axis=1), jnp.concatenate(far, axis=1), axis=1
    )
    return input_gradient, gradient_a, gradient_b


def solution(mesh):
    ring, ctx = mesh.shape["dp"], mesh.shape["ctx"]
    split = Mesh(mesh.devices.reshape(ring, ctx // 2, 2), AXES)
    rows = P(AXES, None)
    placed = (rows,) * 5 + (P(),) * 6 + (rows,) * 2
    return jax.shard_map(
        on_device,
        mesh=split,
        in_specs=placed,
        out_specs=(rows, P(None, AXES), P(None, AXES)),
        check_vma=False,
    )
```

time: 484 us -> 282 us (0.58)
  the two profiles are of different devices: /device:TPU:0 before, /device:TPU:2 now
where the time goes in v1:
time: 282 us; the launch traced here: 281 us
  starting transfers between devices  67.2 us (24%)
  waiting for transfers between devices  49.8 us (18%)
  Pallas kernels  48.8 us (17%)
  blocking collectives  41.3 us (15%)
  local copies, waits for them, and re-layouts  30.2 us (11%)
  other arithmetic  28.7 us (10%)
  between operations  13.7 us (5%)
    psum x1, blocking collectives, on_device(): lax.psum(jnp.stack([jnp.sum(block_a * block_a), jnp.sum(block_b * block_b...  41.3 us
    pallas_call x2, Pallas kernels, local_part(): pl.pallas_call(functools.partial(local_kernel, group * heads, heads), gri...  17.5 us
    pallas_call x2, Pallas kernels, grad_part(): pl.pallas_call(functools.partial(grad_kernel, blocks, segments), grid=(1,...  16.8 us
    ppermute x12, starting transfers between devices, chain(): ahead = lax.ppermute(ahead, 'dp', self.ahead)  14.9 us
    ppermute x1, waiting for transfers between devices, summed_blocks(): total = total + lax.ppermute(sent, 'x', turn).astype(F32)  13.5 us
    ppermute x12, starting transfers between devices, chain(): back = lax.ppermute(back, 'dp', self.back)  12.5 us
    ppermute x6, starting transfers between devices, across_last(): moved = lax.ppermute(joined, 'x', turn)  10.5 us
    dynamic_slice x13, local copies, waits for them, and re-layouts, half(): return lax.dynamic_slice_in_dim(value, which * size, size, axis)  10.3 us
  transfers between devices with their start and end apart: 60, of which 18 were waited for; matrix products, arithmetic and copies ran while one was open for 17% of the time, Pallas kernels for 17%

profile of v1, /device:TPU:2, one launch (start us, length us, event | category | flops | bytes accessed | tf_op | source)
XLA Modules:
  0.0 280.7 jit_solution(8498045648340855170)
XLA Ops:
  0.7 1.7 constant_dynamic-slice_fusion.9
  2.4 1.6 constant_dynamic-slice_fusion.11
  4.5 2.3 constant_dynamic-slice_fusion.6
  30.1 1.6 collective-permute-start.17
  32.8 1.4 collective-permute-start.30
  35.4 3.1 %collective-permute-done.8 = bf16[128,512]{1,0:T(8,128)(2,1)S(1)} collective-permute-done((bf16[128,512]{1,0:T(8,128)(2,1)S(1)}, bf16[128,512]{1,0:T(8,128)(2,1)S(1)}, u32[]{:S(2)}, u32[]{:S(2)}) %collective-permute-start.8) | collective-permute-done | bytes 131104 | tf_op jit(solution)/shard_map/ppermute | solution.py:421
  38.6 1.6 collective-permute-start.39
  40.8 1.6 collective-permute-start.19
  42.4 2.6 collective-permute-done.39.rest_10_
  44.9 1.5 collective-permute-start.20
  47.8 1.5 collective-permute-start.42
  50.2 1.6 collective-permute-start.21
  52.9 1.6 collective-permute-start.22
  56.3 1.5 collective-permute-start.44
  60.1 1.6 collective-permute-start.24
  64.4 1.6 collective-permute-start.10
  67.3 1.6 collective-permute-start.32
  68.9 3.3 %broadcast_select_fusion.3 = (bf16[256,2048]{1,0:T(8,128)(2,1)S(1)}, bf16[256,2048]{1,0:T(8,128)(2,1)}, bf16[256,2048]{1,0:T(8,128)(2,1)S(1)}, bf16[256,2048]{1,0:T(8,128)(2,1)S(1)}) fusion(bf16[256,2048]{1,0:T(8,128)(2,1)} %collective-permute-done.6, pred[]{:T(512)S(6)} %eq.52, bf16[256,4096]{1,0:T(8,128)(2,1)S(1)} %copy-done.82, s32[]{:T(128)S(6)} %select_n.301, ...), kind=kLoop, calls=%fused_computation.12 | loop fusion | flops 2097152 | bytes 8388613 | tf_op jit(solution)/shard_map/jit(_where)/select_n | solution.py:502
  72.3 1.5 pad_maximum_fusion.1.x_ref
  73.7 8.7 %local_part.2 = (bf16[512,4096]{1,0:T(8,128)(2,1)}, f32[512,1024]{1,0:T(8,128)S(1)}, f32[256,1024]{1,0:T(8,128)S(1)}, f32[128,1024]{1,0:T(8,128)S(1)}, f32[512,1...) custom-call(bf16[512,2048]{1,0:T(8,128)(2,1)} %pad_maximum_fusion.1.x_ref, ...), custom_call_target="tpu_custom_call" | custom-call | flops 536870912 | bytes 12582912 | tf_op jit(solution)/shard_map/local_part/pallas_call | solution.py:109
  82.4 1.4 copy-done.5
  83.8 1.3 copy-done.8
  85.2 1.5 collective-permute-start.5
  86.8 8.8 %local_part.3 = (bf16[512,4096]{1,0:T(8,128)(2,1)}, f32[512,1024]{1,0:T(8,128)S(1)}, f32[256,1024]{1,0:T(8,128)S(1)}, f32[128,1024]{1,0:T(8,128)S(1)}, f32[512,1...) custom-call(bf16[512,2048]{1,0:T(8,128)(2,1)} %pad_maximum_fusion.1.x_ref, ...), custom_call_target="tpu_custom_call" | custom-call | flops 536870912 | bytes 12582912 | tf_op jit(solution)/shard_map/local_part/pallas_call | solution.py:109
  95.6 1.3 copy-done.10
  97.0 1.3 collective-permute-start.29
  98.3 2.9 %pad_maximum_fusion.2.z_ref = bf16[512,2048]{1,0:T(8,128)(2,1)} fusion(bf16[256,2048]{1,0:T(8,128)(2,1)} %get-tuple-element.64, bf16[256,2048]{1,0:T(8,128)(2,1)S(1)} %get-tuple-element.63), kind=kLoop, calls=%fused_computation.3 | loop fusion | flops 4194304 | bytes 4194304 | tf_op jit(solution)/shard_map/concatenate | solution.py:501
  102.4 3.7 %norm_part.2 = (f32[512,1024]{1,0:T(8,128)S(1)}, f32[512,1024]{1,0:T(8,128)S(1)}, f32[512,64]{1,0:T(8,128)S(1)}, f32[64,1024]{1,0:T(8,128)S(1)}) custom-call(bf16[512,256]{1,0:T(8,128)(2,1)S(1)} %pad_maximum_fusion.11.c_ref, bf16[128,1024]{1,0:T(8,128)(2,1)S(1)} %collective-permute-done.5.incoming_ref, f32[256,1024]{1,0:T(8,128)S(1)} %get-tuple-element.34.state_ref, ...), custom_call_target="tpu_custom_call" | custom-call | flops 268435456 | bytes 10485760 | tf_op jit(solution)/shard_map/norm_part/pallas_call | solution.py:182
  106.1 1.3 copy-done.14
  107.5 1.3 copy-done.15
  108.8 1.4 collective-permute-start.11
  110.9 1.3 collective-permute-start.33
  112.9 3.6 %norm_part.3 = (f32[512,1024]{1,0:T(8,128)S(1)}, f32[512,1024]{1,0:T(8,128)S(1)}, f32[512,64]{1,0:T(8,128)S(1)}, f32[64,1024]{1,0:T(8,128)S(1)}) custom-call(bf16[512,256]{1,0:T(8,128)(2,1)S(1)} %pad_maximum_fusion.11.c_ref, bf16[128,1024]{1,0:T(8,128)(2,1)S(1)} %collective-permute-done.29.incoming_ref, f32[256,1024]{1,0:T(8,128)S(1)} %get-tuple-element.47.state_ref, ...), custom_call_target="tpu_custom_call" | custom-call | flops 268435456 | bytes 10485760 | tf_op jit(solution)/shard_map/norm_part/pallas_call | solution.py:182
  116.6 1.6 collective-permute-start.46
  118.3 4.9 %collective-permute-done.46.rest_17_ = bf16[64,512]{1,0:T(8,128)(2,1)S(1)} collective-permute-done((bf16[64,512]{1,0:T(8,128)(2,1)S(1)}, bf16[64,512]{1,0:T(8,128)(2,1)S(1)}, u32[]{:S(2)}, u32[]{:S(2)}) %collective-permute-start.46) | collective-permute-done | bytes 65568 | tf_op jit(solution)/shard_map/ppermute | solution.py:416
  124.0 1.6 collective-permute-start.13
  126.0 1.6 collective-permute-start.35
  128.5 1.5 pad_maximum_fusion.cot_ref
  130.0 3.1 %collective-permute-done.13.rest_5_ = bf16[256,512]{1,0:T(8,128)(2,1)S(1)} collective-permute-done((bf16[256,512]{1,0:T(8,128)(2,1)S(1)}, bf16[256,512]{1,0:T(8,128)(2,1)S(1)}, u32[]{:S(2)}, u32[]{:S(2)}) %collective-permute-start.13) | collective-permute-done | bytes 262176 | tf_op jit(solution)/shard_map/ppermute | solution.py:397
  133.1 2.4 collective-permute-start.25
  138.3 2.4 collective-permute-start.27
  141.4 1.6 collective-permute-start.15
  145.8 2.0 reshape.75
  147.8 1.4 copy.72
  151.4 2.0 collective-permute-start.48
  153.5 6.4 %collective-permute-done.27.rest_20_ = bf16[384,512]{1,0:T(8,128)(2,1)} collective-permute-done((bf16[384,512]{1,0:T(8,128)(2,1)}, bf16[384,512]{1,0:T(8,128)(2,1)}, u32[]{:S(2)}, u32[]{:S(2)}) %collective-permute-start.27) | collective-permute-done | bytes 393248 | tf_op jit(solution)/shard_map/ppermute | solution.py:435
  159.9 2.0 collective-permute-start.49
  161.9 1.6 collective-permute-start.37
  164.1 8.9 %grad_part.2 = (f32[512,1024]{1,0:T(8,128)S(1)}, f32[256,1024]{1,0:T(8,128)S(1)}, bf16[128,1024]{1,0:T(8,128)(2,1)S(1)}) custom-call(s32[16]{0:T(128)S(1)} %copy-done.79, bf16[512,2048]{1,0:T(8,128)(2,1)} %pad_maximum_fusion.cot_ref, bf16[512,64]{1,0:T(8,128)(2,1)S(1)} %fusion.up_ref, bf16[64,2048]{1,0:T(8,128)(2,1)S(1)} %constant_dynamic-slice_fusion.10.down_ref, ...), custom_call_target="tpu_custom_call" | custom-call | flops 2147483648 | bytes 14680064 | tf_op jit(solution)/shard_map/grad_part/pallas_call | solution.py:258
  172.9 13.5 %collective-permute-done.55 = bf16[8,64,192]{2,1,0:T(8,128)(2,1)S(1)} collective-permute-done((bf16[8,64,192]{2,1,0:T(8,128)(2,1)S(1)}, bf16[8,64,192]{2,1,0:T(8,128)(2,1)S(1)}, u32[]{:S(2)}, u32[]{:S(2)}) %collective-permute-start.55) | collective-permute-done | bytes 196640 | tf_op jit(solution)/shard_map/ppermute | solution.py:471
  187.0 3.7 %collective-permute-start.28 = (bf16[128,1024]{1,0:T(8,128)(2,1)S(1)}, bf16[128,1024]{1,0:T(8,128)(2,1)S(1)}, u32[]{:S(2)}, u32[]{:S(2)}) collective-permute-start(bf16[128,1024]{1,0:T(8,128)(2,1)S(1)} %get-tuple-element.40), channel_id=1, source_target_pairs={{2,0},{3,1},{6,4},{7,5},{10,8},{11,9},{14,12},{15,13},{18,16},{19,... | collective-permute-start | bytes 786440 | tf_op jit(solution)/shard_map/ppermute | solution.py:561
  190.7 2.7 collective-permute-start.56
  193.5 7.9 %grad_part.3 = (f32[512,1024]{1,0:T(8,128)S(1)}, f32[256,1024]{1,0:T(8,128)S(1)}, bf16[128,1024]{1,0:T(8,128)(2,1)S(1)}) custom-call(s32[16]{0:T(128)S(1)} %copy-done.80, bf16[512,2048]{1,0:T(8,128)(2,1)} %pad_maximum_fusion.cot_ref, bf16[512,64]{1,0:T(8,128)(2,1)S(1)} %fusion.up_ref, bf16[64,2048]{1,0:T(8,128)(2,1)S(1)} %constant_dynamic-slice_fusion.10.down_ref, ...), custom_call_target="tpu_custom_call" | custom-call | flops 2147483648 | bytes 14680064 | tf_op jit(solution)/shard_map/grad_part/pallas_call | solution.py:258
  202.4 2.9 %collective-permute-start.50 = (bf16[128,1024]{1,0:T(8,128)(2,1)S(1)}, bf16[128,1024]{1,0:T(8,128)(2,1)S(1)}, u32[]{:S(2)}, u32[]{:S(2)}) collective-permute-start(bf16[128,1024]{1,0:T(8,128)(2,1)S(1)} %get-tuple-element.53), channel_id=1, source_target_pairs={{2,0},{3,1},{6,4},{7,5},{10,8},{11,9},{14,12},{15,13},{18,16},{19,... | collective-permute-start | bytes 786440 | tf_op jit(solution)/shard_map/ppermute | solution.py:561
  205.3 3.2 %back_part.2.base_ref = f32[512,1024]{1,0:T(8,128)S(1)} custom-call(bf16[512,4096]{1,0:T(8,128)(2,1)} %get-tuple-element.43.scores_ref, f32[512,1024]{1,0:T(8,128)S(1)} %get-tuple-element.44.grad_ref, f32[512,1024]{1,0:T(8,128)S(1)} %copy-done.9, f32[1,2048]{1,0:T(1,128)S(1)} %broadcast_in_dim_reshape.3.skip_ref), custom_call_target="tpu_custom_call" | custom-call | flops 268435456 | bytes 10485760 | tf_op jit(solution)/shard_map/back_part/pallas_call | solution.py:306
  208.5 3.2 %back_part.3.base_ref = f32[512,1024]{1,0:T(8,128)S(1)} custom-call(bf16[512,4096]{1,0:T(8,128)(2,1)} %get-tuple-element.56.scores_ref, f32[512,1024]{1,0:T(8,128)S(1)} %get-tuple-element.57.grad_ref, f32[512,1024]{1,0:T(8,128)S(1)} %copy-done.11, f32[1,2048]{1,0:T(1,128)S(1)} %broadcast_in_dim_reshape.3.skip_ref), custom_call_target="tpu_custom_call" | custom-call | flops 268435456 | bytes 10485760 | tf_op jit(solution)/shard_map/back_part/pallas_call | solution.py:306
  213.8 3.7 %collective-permute-start.57 = (bf16[2,64,192]{2,1,0:T(8,128)(2,1)S(1)}, bf16[2,64,192]{2,1,0:T(8,128)(2,1)S(1)}, u32[]{:S(2)}, u32[]{:S(2)}) collective-permute-start(bf16[2,64,192]{2,1,0:T(8,128)(2,1)S(1)} %dynamic-slice_convert_fusion.3), channel_id=1, source_target_pairs={{0,8},{4,12},{8,0},{12,4},{16,24},{20,28},{24,16},{28,20},{1,9},{5... | collective-permute-start | bytes 147464 | tf_op jit(solution)/shard_map/ppermute | solution.py:478
  218.1 1.6 collective-permute-done.57
  219.9 3.8 %collective-permute-done.58 = bf16[1,64,192]{2,1,0:T(8,128)(2,1)S(1)} collective-permute-done((bf16[1,64,192]{2,1,0:T(8,128)(2,1)S(1)}, bf16[1,64,192]{2,1,0:T(8,128)(2,1)S(1)}, u32[]{:S(2)}, u32[]{:S(2)}) %collective-permute-start.58) | collective-permute-done | bytes 24608 | tf_op jit(solution)/shard_map/ppermute | solution.py:478
  225.0 1.4 pad_maximum_fusion.19
  226.4 41.3 %psum.7 = f32[2]{0:T(128)S(1)} all-reduce(f32[2]{0:T(128)S(1)} %pad_maximum_fusion.19), channel_id=1, replica_groups=mesh['dp'=8,'x'=2,'core'=2] {'dp','x','core'}, use_global_device_ids=true, to_apply=%region_4.5 | all-reduce | flops 2 | bytes 16 | tf_op jit(solution)/shard_map/psum | solution.py:584
  269.6 1.9 collective-permute-start.59
  271.5 5.8 %collective-permute-done.59 = f32[64,192]{1,0:T(8,128)S(1)} collective-permute-done((f32[64,192]{1,0:T(8,128)S(1)}, f32[64,192]{1,0:T(8,128)S(1)}, u32[]{:S(2)}, u32[]{:S(2)}) %collective-permute-start.59) | collective-permute-done | bytes 49184 | tf_op jit(solution)/shard_map/ppermute | solution.py:593
  279.2 1.5 pad_maximum_fusion.3
  (364 shorter events, 49.7 us)
Async XLA Ops:
  2.4 29.8 %collective-permute-start.2 = (bf16[256,256]{1,0:T(8,128)(2,1)}, bf16[256,256]{1,0:T(8,128)(2,1)S(1)}, u32[]{:S(2)}, u32[]{:S(2)}) collective-permute-start(bf16[256,256]{1,0:T(8,128)(2,1)} %constant_dynamic-slice_fusion.9), channel_id=1, source_target_pairs={{0,1},{1,0},{2,3},{3,2},{4,5},{5,4},{6,7},{7,6},{8,9},{9,8},{10,11... | collective-permute-start | bytes 393224 | tf_op jit(solution)/shard_map/ppermute | solution.py:506
  4.0 28.3 %collective-permute-start = (bf16[256,256]{1,0:T(8,128)(2,1)}, bf16[256,256]{1,0:T(8,128)(2,1)}, u32[]{:S(2)}, u32[]{:S(2)}) collective-permute-start(bf16[256,256]{1,0:T(8,128)(2,1)} %constant_dynamic-slice_fusion.11), channel_id=1, source_target_pairs={{0,1},{1,0},{2,3},{3,2},{4,5},{5,4},{6,7},{7,6},{8,9},{9,8},{10,11... | collective-permute-start | bytes 393224 | tf_op jit(solution)/shard_map/ppermute | solution.py:506
  6.8 59.9 %collective-permute-start.6 = (bf16[256,2048]{1,0:T(8,128)(2,1)}, bf16[256,2048]{1,0:T(8,128)(2,1)}, u32[]{:S(2)}, u32[]{:S(2)}) collective-permute-start(bf16[256,2048]{1,0:T(8,128)(2,1)} %constant_dynamic-slice_fusion.6), channel_id=1, source_target_pairs={{0,1},{1,0},{2,3},{3,2},{4,5},{5,4},{6,7},{7,6},{8,9},{9,8},{10,11... | collective-permute-start | bytes 3145736 | tf_op jit(solution)/shard_map/ppermute | solution.py:506
  7.5 19.0 %collective-permute-start.4 = (f32[256,32]{0,1:T(8,128)}, f32[256,32]{0,1:T(8,128)}, u32[]{:S(2)}, u32[]{:S(2)}) collective-permute-start(f32[256,32]{0,1:T(8,128)} %constant_dynamic-slice_fusion.7), channel_id=1, source_target_pairs={{0,1},{1,0},{2,3},{3,2},{4,5},{5,4},{6,7},{7,6},{8,9},{9,8},{10,11... | collective-permute-start | bytes 98312 | tf_op jit(solution)/shard_map/ppermute | solution.py:506
  8.7 21.3 %collective-permute-start.7 = (bf16[64,2048]{1,0:T(8,128)(2,1)}, bf16[64,2048]{1,0:T(8,128)(2,1)S(1)}, u32[]{:S(2)}, u32[]{:S(2)}) collective-permute-start(bf16[64,2048]{1,0:T(8,128)(2,1)} %constant_dynamic-slice_fusion.5), channel_id=1, source_target_pairs={{0,1},{1,0},{2,3},{3,2},{4,5},{5,4},{6,7},{7,6},{8,9},{9,8},{10,11... | collective-permute-start | bytes 786440 | tf_op jit(solution)/shard_map/ppermute | solution.py:506
  30.1 8.5 %collective-permute-start.17 = (bf16[128,512]{1,0:T(8,128)(2,1)S(1)}, bf16[128,512]{1,0:T(8,128)(2,1)S(1)}, u32[]{:S(2)}, u32[]{:S(2)}) collective-permute-start(bf16[128,512]{1,0:T(8,128)(2,1)S(1)} %get-tuple-element.79.rest_9_), channel_id=1, source_target_pairs={{0,8},{8,16},{16,24},{24,28},{28,20},{20,12},{12,4},{4,0},{1,9},{9... | collective-permute-start | bytes 393224 | tf_op jit(solution)/shard_map/ppermute | solution.py:397
  31.7 8.5 %collective-permute-start.18 = (bf16[128,512]{1,0:T(8,128)(2,1)S(1)}, bf16[128,512]{1,0:T(8,128)(2,1)S(1)}, u32[]{:S(2)}, u32[]{:S(2)}) collective-permute-start(bf16[128,512]{1,0:T(8,128)(2,1)S(1)} %get-tuple-element.79.rest_9_), channel_id=1, source_target_pairs={{8,0},{16,8},{24,16},{28,24},{20,28},{12,20},{4,12},{0,4},{9,1},{1... | collective-permute-start | bytes 393224 | tf_op jit(solution)/shard_map/ppermute | solution.py:398
  32.2 6.4 %collective-permute-start.8 = (bf16[128,512]{1,0:T(8,128)(2,1)S(1)}, bf16[128,512]{1,0:T(8,128)(2,1)S(1)}, u32[]{:S(2)}, u32[]{:S(2)}) collective-permute-start(bf16[128,512]{1,0:T(8,128)(2,1)S(1)} %get-tuple-element.78), channel_id=1, source_target_pairs={{0,2},{2,0},{1,3},{3,1},{4,6},{6,4},{5,7},{7,5},{8,10},{10,8},{9,1... | collective-permute-start | bytes 393224 | tf_op jit(solution)/shard_map/ppermute | solution.py:421
  32.8 7.9 %collective-permute-start.30 = (bf16[128,512]{1,0:T(8,128)(2,1)S(1)}, bf16[128,512]{1,0:T(8,128)(2,1)S(1)}, u32[]{:S(2)}, u32[]{:S(2)}) collective-permute-start(bf16[128,512]{1,0:T(8,128)(2,1)S(1)} %get-tuple-element.80), channel_id=1, source_target_pairs={{0,2},{2,0},{1,3},{3,1},{4,6},{6,4},{5,7},{7,5},{8,10},{10,8},{9,1... | collective-permute-start | bytes 393224 | tf_op jit(solution)/shard_map/ppermute | solution.py:421
  38.6 28.7 %collective-permute-start.3 = (bf16[256,2048]{1,0:T(8,128)(2,1)S(1)}, bf16[256,2048]{1,0:T(8,128)(2,1)S(1)}, u32[]{:S(2)}, u32[]{:S(2)}) collective-permute-start(bf16[256,2048]{1,0:T(8,128)(2,1)S(1)} %copy-done.87), channel_id=1, source_target_pairs={{0,1},{1,0},{2,3},{3,2},{4,5},{5,4},{6,7},{7,6},{8,9},{9,8},{10,11... | collective-permute-start | bytes 3145736 | tf_op jit(solution)/shard_map/ppermute | solution.py:506
  38.6 6.3 %collective-permute-start.39 = (bf16[128,512]{1,0:T(8,128)(2,1)S(1)}, bf16[128,512]{1,0:T(8,128)(2,1)S(1)}, u32[]{:S(2)}, u32[]{:S(2)}) collective-permute-start(bf16[128,512]{1,0:T(8,128)(2,1)S(1)} %get-tuple-element.77.rest_9_), channel_id=1, source_target_pairs={{0,8},{8,16},{16,24},{24,28},{28,20},{20,12},{12,4},{4,0},{1,9},{9... | collective-permute-start | bytes 393224 | tf_op jit(solution)/shard_map/ppermute | solution.py:397
  40.3 7.0 %collective-permute-start.40 = (bf16[128,512]{1,0:T(8,128)(2,1)S(1)}, bf16[128,512]{1,0:T(8,128)(2,1)S(1)}, u32[]{:S(2)}, u32[]{:S(2)}) collective-permute-start(bf16[128,512]{1,0:T(8,128)(2,1)S(1)} %get-tuple-element.77.rest_9_), channel_id=1, source_target_pairs={{8,0},{16,8},{24,16},{28,24},{20,28},{12,20},{4,12},{0,4},{9,1},{1... | collective-permute-start | bytes 393224 | tf_op jit(solution)/shard_map/ppermute | solution.py:398
  40.8 7.0 %collective-permute-start.19 = (bf16[128,512]{1,0:T(8,128)(2,1)S(1)}, bf16[128,512]{1,0:T(8,128)(2,1)S(1)}, u32[]{:S(2)}, u32[]{:S(2)}) collective-permute-start(bf16[128,512]{1,0:T(8,128)(2,1)S(1)} %collective-permute-done.17.rest_10_), channel_id=1, source_target_pairs={{0,8},{8,16},{16,24},{24,28},{28,20},{20,12},{12,4},{4,0},{1,9},{9... | collective-permute-start | bytes 393224 | tf_op jit(solution)/shard_map/ppermute | solution.py:397
  44.9 5.3 %collective-permute-start.20 = (bf16[128,512]{1,0:T(8,128)(2,1)S(1)}, bf16[128,512]{1,0:T(8,128)(2,1)S(1)}, u32[]{:S(2)}, u32[]{:S(2)}) collective-permute-start(bf16[128,512]{1,0:T(8,128)(2,1)S(1)} %collective-permute-done.18.rest_11_), channel_id=1, source_target_pairs={{8,0},{16,8},{24,16},{28,24},{20,28},{12,20},{4,12},{0,4},{9,1},{1... | collective-permute-start | bytes 393224 | tf_op jit(solution)/shard_map/ppermute | solution.py:398
  47.2 5.6 %collective-permute-start.41 = (bf16[128,512]{1,0:T(8,128)(2,1)S(1)}, bf16[128,512]{1,0:T(8,128)(2,1)S(1)}, u32[]{:S(2)}, u32[]{:S(2)}) collective-permute-start(bf16[128,512]{1,0:T(8,128)(2,1)S(1)} %collective-permute-done.39.rest_10_), channel_id=1, source_target_pairs={{0,8},{8,16},{16,24},{24,28},{28,20},{20,12},{12,4},{4,0},{1,9},{9... | collective-permute-start | bytes 393224 | tf_op jit(solution)/shard_map/ppermute | solution.py:397
  47.8 6.7 %collective-permute-start.42 = (bf16[128,512]{1,0:T(8,128)(2,1)S(1)}, bf16[128,512]{1,0:T(8,128)(2,1)S(1)}, u32[]{:S(2)}, u32[]{:S(2)}) collective-permute-start(bf16[128,512]{1,0:T(8,128)(2,1)S(1)} %collective-permute-done.40.rest_11_), channel_id=1, source_target_pairs={{8,0},{16,8},{24,16},{28,24},{20,28},{12,20},{4,12},{0,4},{9,1},{1... | collective-permute-start | bytes 393224 | tf_op jit(solution)/shard_map/ppermute | solution.py:398
  50.2 6.1 %collective-permute-start.21 = (bf16[128,512]{1,0:T(8,128)(2,1)S(1)}, bf16[128,512]{1,0:T(8,128)(2,1)S(1)}, u32[]{:S(2)}, u32[]{:S(2)}) collective-permute-start(bf16[128,512]{1,0:T(8,128)(2,1)S(1)} %collective-permute-done.19.rest_12_), channel_id=1, source_target_pairs={{0,8},{8,16},{16,24},{24,28},{28,20},{20,12},{12,4},{4,0},{1,9},{9... | collective-permute-start | bytes 393224 | tf_op jit(solution)/shard_map/ppermute | solution.py:397
  52.9 6.0 %collective-permute-start.22 = (bf16[128,512]{1,0:T(8,128)(2,1)S(1)}, bf16[128,512]{1,0:T(8,128)(2,1)S(1)}, u32[]{:S(2)}, u32[]{:S(2)}) collective-permute-start(bf16[128,512]{1,0:T(8,128)(2,1)S(1)} %collective-permute-done.20.rest_13_), channel_id=1, source_target_pairs={{8,0},{16,8},{24,16},{28,24},{20,28},{12,20},{4,12},{0,4},{9,1},{1... | collective-permute-start | bytes 393224 | tf_op jit(solution)/shard_map/ppermute | solution.py:398
  54.4 5.7 %collective-permute-start.43 = (bf16[128,512]{1,0:T(8,128)(2,1)S(1)}, bf16[128,512]{1,0:T(8,128)(2,1)S(1)}, u32[]{:S(2)}, u32[]{:S(2)}) collective-permute-start(bf16[128,512]{1,0:T(8,128)(2,1)S(1)} %collective-permute-done.41.rest_12_), channel_id=1, source_target_pairs={{0,8},{8,16},{16,24},{24,28},{28,20},{20,12},{12,4},{4,0},{1,9},{9... | collective-permute-start | bytes 393224 | tf_op jit(solution)/shard_map/ppermute | solution.py:397
  56.3 6.1 %collective-permute-start.44 = (bf16[128,512]{1,0:T(8,128)(2,1)S(1)}, bf16[128,512]{1,0:T(8,128)(2,1)S(1)}, u32[]{:S(2)}, u32[]{:S(2)}) collective-permute-start(bf16[128,512]{1,0:T(8,128)(2,1)S(1)} %collective-permute-done.42.rest_13_), channel_id=1, source_target_pairs={{8,0},{16,8},{24,16},{28,24},{20,28},{12,20},{4,12},{0,4},{9,1},{1... | collective-permute-start | bytes 393224 | tf_op jit(solution)/shard_map/ppermute | solution.py:398
  58.8 4.3 %collective-permute-start.23 = (bf16[64,512]{1,0:T(8,128)(2,1)S(1)}, bf16[64,512]{1,0:T(8,128)(2,1)S(1)}, u32[]{:S(2)}, u32[]{:S(2)}) collective-permute-start(bf16[64,512]{1,0:T(8,128)(2,1)S(1)} %slice.94), channel_id=1, source_target_pairs={{0,8},{8,16},{16,24},{24,28},{28,20},{20,12},{12,4},{4,0},{1,9},{9... | collective-permute-start | bytes 196616 | tf_op jit(solution)/shard_map/ppermute | solution.py:415
  60.1 4.3 %collective-permute-start.24 = (bf16[64,512]{1,0:T(8,128)(2,1)S(1)}, bf16[64,512]{1,0:T(8,128)(2,1)S(1)}, u32[]{:S(2)}, u32[]{:S(2)}) collective-permute-start(bf16[64,512]{1,0:T(8,128)(2,1)S(1)} %slice.95), channel_id=1, source_target_pairs={{8,0},{16,8},{24,16},{28,24},{20,28},{12,20},{4,12},{0,4},{9,1},{1... | collective-permute-start | bytes 196616 | tf_op jit(solution)/shard_map/ppermute | solution.py:416
  62.5 60.7 %copy-start.22 = (bf16[128,512]{1,0:T(8,128)(2,1)}, bf16[128,512]{1,0:T(8,128)(2,1)S(1)}, u32[]{:S(2)}) copy-start(bf16[128,512]{1,0:T(8,128)(2,1)S(1)} %collective-permute-done.44.rest_15_) | copy-start | bytes 393220
  62.5 22.7 %collective-permute-start.1 = (bf16[256,2048]{1,0:T(8,128)(2,1)S(1)}, bf16[256,2048]{1,0:T(8,128)(2,1)S(1)}, u32[]{:S(2)}, u32[]{:S(2)}) collective-permute-start(bf16[256,2048]{1,0:T(8,128)(2,1)S(1)} %copy-done.81), channel_id=1, source_target_pairs={{0,1},{1,0},{2,3},{3,2},{4,5},{5,4},{6,7},{7,6},{8,9},{9,8},{10,11... | collective-permute-start | bytes 3145736 | tf_op jit(solution)/shard_map/ppermute | solution.py:535
  63.1 33.9 %collective-permute-start.9 = (bf16[256,512]{1,0:T(8,128)(2,1)S(1)}, bf16[256,512]{1,0:T(8,128)(2,1)S(1)}, u32[]{:S(2)}, u32[]{:S(2)}) collective-permute-start(bf16[256,512]{1,0:T(8,128)(2,1)S(1)} %pad_maximum_fusion.12.rest_0_), channel_id=1, source_target_pairs={{0,8},{8,16},{16,24},{24,28},{28,20},{20,12},{12,4},{4,0},{1,9},{9... | collective-permute-start | bytes 786440 | tf_op jit(solution)/shard_map/ppermute | solution.py:397
  64.4 44.4 %collective-permute-start.10 = (bf16[256,512]{1,0:T(8,128)(2,1)S(1)}, bf16[256,512]{1,0:T(8,128)(2,1)S(1)}, u32[]{:S(2)}, u32[]{:S(2)}) collective-permute-start(bf16[256,512]{1,0:T(8,128)(2,1)S(1)} %pad_maximum_fusion.12.rest_0_), channel_id=1, source_target_pairs={{8,0},{16,8},{24,16},{28,24},{20,28},{12,20},{4,12},{0,4},{9,1},{1... | collective-permute-start | bytes 786440 | tf_op jit(solution)/shard_map/ppermute | solution.py:398
  66.8 43.4 %collective-permute-start.31 = (bf16[256,512]{1,0:T(8,128)(2,1)S(1)}, bf16[256,512]{1,0:T(8,128)(2,1)S(1)}, u32[]{:S(2)}, u32[]{:S(2)}) collective-permute-start(bf16[256,512]{1,0:T(8,128)(2,1)S(1)} %pad_maximum_fusion.14.rest_0_), channel_id=1, source_target_pairs={{0,8},{8,16},{16,24},{24,28},{28,20},{20,12},{12,4},{4,0},{1,9},{9... | collective-permute-start | bytes 786440 | tf_op jit(solution)/shard_map/ppermute | solution.py:397
  67.3 43.6 %collective-permute-start.32 = (bf16[256,512]{1,0:T(8,128)(2,1)S(1)}, bf16[256,512]{1,0:T(8,128)(2,1)S(1)}, u32[]{:S(2)}, u32[]{:S(2)}) collective-permute-start(bf16[256,512]{1,0:T(8,128)(2,1)S(1)} %pad_maximum_fusion.14.rest_0_), channel_id=1, source_target_pairs={{8,0},{16,8},{24,16},{28,24},{20,28},{12,20},{4,12},{0,4},{9,1},{1... | collective-permute-start | bytes 786440 | tf_op jit(solution)/shard_map/ppermute | solution.py:398
  85.2 16.1 %collective-permute-start.5 = (bf16[128,1024]{1,0:T(8,128)(2,1)S(1)}, bf16[128,1024]{1,0:T(8,128)(2,1)S(1)}, u32[]{:S(2)}, u32[]{:S(2)}) collective-permute-start(bf16[128,1024]{1,0:T(8,128)(2,1)S(1)} %convert_element_type.52), channel_id=1, source_target_pairs={{0,2},{1,3},{4,6},{5,7},{8,10},{9,11},{12,14},{13,15},{16,18},{17,... | collective-permute-start | bytes 786440 | tf_op jit(solution)/shard_map/ppermute | solution.py:561
  97.0 15.2 %collective-permute-start.29 = (bf16[128,1024]{1,0:T(8,128)(2,1)S(1)}, bf16[128,1024]{1,0:T(8,128)(2,1)S(1)}, u32[]{:S(2)}, u32[]{:S(2)}) collective-permute-start(bf16[128,1024]{1,0:T(8,128)(2,1)S(1)} %convert_element_type.53), channel_id=1, source_target_pairs={{0,2},{1,3},{4,6},{5,7},{8,10},{9,11},{12,14},{13,15},{16,18},{17,... | collective-permute-start | bytes 786440 | tf_op jit(solution)/shard_map/ppermute | solution.py:561
  101.3 15.4 %collective-permute-start.45 = (bf16[64,512]{1,0:T(8,128)(2,1)S(1)}, bf16[64,512]{1,0:T(8,128)(2,1)S(1)}, u32[]{:S(2)}, u32[]{:S(2)}) collective-permute-start(bf16[64,512]{1,0:T(8,128)(2,1)S(1)} %slice.100), channel_id=1, source_target_pairs={{0,8},{8,16},{16,24},{24,28},{28,20},{20,12},{12,4},{4,0},{1,9},{9... | collective-permute-start | bytes 196616 | tf_op jit(solution)/shard_map/ppermute | solution.py:415
  108.8 15.2 %collective-permute-start.11 = (bf16[256,512]{1,0:T(8,128)(2,1)S(1)}, bf16[256,512]{1,0:T(8,128)(2,1)S(1)}, u32[]{:S(2)}, u32[]{:S(2)}) collective-permute-start(bf16[256,512]{1,0:T(8,128)(2,1)S(1)} %collective-permute-done.9.rest_1_), channel_id=1, source_target_pairs={{0,8},{8,16},{16,24},{24,28},{28,20},{20,12},{12,4},{4,0},{1,9},{9... | collective-permute-start | bytes 786440 | tf_op jit(solution)/shard_map/ppermute | solution.py:397
  110.2 15.4 %collective-permute-start.12 = (bf16[256,512]{1,0:T(8,128)(2,1)S(1)}, bf16[256,512]{1,0:T(8,128)(2,1)S(1)}, u32[]{:S(2)}, u32[]{:S(2)}) collective-permute-start(bf16[256,512]{1,0:T(8,128)(2,1)S(1)} %collective-permute-done.10.rest_2_), channel_id=1, source_target_pairs={{8,0},{16,8},{24,16},{28,24},{20,28},{12,20},{4,12},{0,4},{9,1},{1... | collective-permute-start | bytes 786440 | tf_op jit(solution)/shard_map/ppermute | solution.py:398
  110.9 15.2 %collective-permute-start.33 = (bf16[256,512]{1,0:T(8,128)(2,1)S(1)}, bf16[256,512]{1,0:T(8,128)(2,1)S(1)}, u32[]{:S(2)}, u32[]{:S(2)}) collective-permute-start(bf16[256,512]{1,0:T(8,128)(2,1)S(1)} %collective-permute-done.31.rest_1_), channel_id=1, source_target_pairs={{0,8},{8,16},{16,24},{24,28},{28,20},{20,12},{12,4},{4,0},{1,9},{9... | collective-permute-start | bytes 786440 | tf_op jit(solution)/shard_map/ppermute | solution.py:397
  112.2 15.4 %collective-permute-start.34 = (bf16[256,512]{1,0:T(8,128)(2,1)S(1)}, bf16[256,512]{1,0:T(8,128)(2,1)S(1)}, u32[]{:S(2)}, u32[]{:S(2)}) collective-permute-start(bf16[256,512]{1,0:T(8,128)(2,1)S(1)} %collective-permute-done.32.rest_2_), channel_id=1, source_target_pairs={{8,0},{16,8},{24,16},{28,24},{20,28},{12,20},{4,12},{0,4},{9,1},{1... | collective-permute-start | bytes 786440 | tf_op jit(solution)/shard_map/ppermute | solution.py:398
  116.6 6.6 %collective-permute-start.46 = (bf16[64,512]{1,0:T(8,128)(2,1)S(1)}, bf16[64,512]{1,0:T(8,128)(2,1)S(1)}, u32[]{:S(2)}, u32[]{:S(2)}) collective-permute-start(bf16[64,512]{1,0:T(8,128)(2,1)S(1)} %slice.101), channel_id=1, source_target_pairs={{8,0},{16,8},{24,16},{28,24},{20,28},{12,20},{4,12},{0,4},{9,1},{1... | collective-permute-start | bytes 196616 | tf_op jit(solution)/shard_map/ppermute | solution.py:416
  123.2 4.9 %collective-permute-start.53 = (f32[256,64]{1,0:T(8,128)S(1)}, f32[256,64]{1,0:T(8,128)S(1)}, u32[]{:S(2)}, u32[]{:S(2)}) collective-permute-start(f32[256,64]{1,0:T(8,128)S(1)} %constant_dynamic-slice_fusion), channel_id=1, source_target_pairs={{0,1},{1,0},{2,3},{3,2},{4,5},{5,4},{6,7},{7,6},{8,9},{9,8},{10,11... | collective-permute-start | bytes 196616 | tf_op jit(solution)/shard_map/ppermute | solution.py:577
  124.0 9.1 %collective-permute-start.13 = (bf16[256,512]{1,0:T(8,128)(2,1)S(1)}, bf16[256,512]{1,0:T(8,128)(2,1)S(1)}, u32[]{:S(2)}, u32[]{:S(2)}) collective-permute-start(bf16[256,512]{1,0:T(8,128)(2,1)S(1)} %collective-permute-done.11.rest_3_), channel_id=1, source_target_pairs={{0,8},{8,16},{16,24},{24,28},{28,20},{20,12},{12,4},{4,0},{1,9},{9... | collective-permute-start | bytes 786440 | tf_op jit(solution)/shard_map/ppermute | solution.py:397
  125.6 10.6 %collective-permute-start.14 = (bf16[256,512]{1,0:T(8,128)(2,1)S(1)}, bf16[256,512]{1,0:T(8,128)(2,1)S(1)}, u32[]{:S(2)}, u32[]{:S(2)}) collective-permute-start(bf16[256,512]{1,0:T(8,128)(2,1)S(1)} %collective-permute-done.12.rest_4_), channel_id=1, source_target_pairs={{8,0},{16,8},{24,16},{28,24},{20,28},{12,20},{4,12},{0,4},{9,1},{1... | collective-permute-start | bytes 786440 | tf_op jit(solution)/shard_map/ppermute | solution.py:398
  126.0 12.3 %collective-permute-start.35 = (bf16[256,512]{1,0:T(8,128)(2,1)S(1)}, bf16[256,512]{1,0:T(8,128)(2,1)S(1)}, u32[]{:S(2)}, u32[]{:S(2)}) collective-permute-start(bf16[256,512]{1,0:T(8,128)(2,1)S(1)} %collective-permute-done.33.rest_3_), channel_id=1, source_target_pairs={{0,8},{8,16},{16,24},{24,28},{28,20},{20,12},{12,4},{4,0},{1,9},{9... | collective-permute-start | bytes 786440 | tf_op jit(solution)/shard_map/ppermute | solution.py:397
  127.6 13.8 %collective-permute-start.36 = (bf16[256,512]{1,0:T(8,128)(2,1)S(1)}, bf16[256,512]{1,0:T(8,128)(2,1)S(1)}, u32[]{:S(2)}, u32[]{:S(2)}) collective-permute-start(bf16[256,512]{1,0:T(8,128)(2,1)S(1)} %collective-permute-done.34.rest_4_), channel_id=1, source_target_pairs={{8,0},{16,8},{24,16},{28,24},{20,28},{12,20},{4,12},{0,4},{9,1},{1... | collective-permute-start | bytes 786440 | tf_op jit(solution)/shard_map/ppermute | solution.py:398
  128.4 16.1 %collective-permute-start.54 = (bf16[64,1024]{1,0:T(8,128)(2,1)S(1)}, bf16[64,1024]{1,0:T(8,128)(2,1)S(1)}, u32[]{:S(2)}, u32[]{:S(2)}) collective-permute-start(bf16[64,1024]{1,0:T(8,128)(2,1)S(1)} %dynamic-slice_convert_fusion.2), channel_id=1, source_target_pairs={{0,1},{1,0},{2,3},{3,2},{4,5},{5,4},{6,7},{7,6},{8,9},{9,8},{10,11... | collective-permute-start | bytes 393224 | tf_op jit(solution)/shard_map/ppermute | solution.py:581
  133.1 17.2 %collective-permute-start.25 = (bf16[384,512]{1,0:T(8,128)(2,1)}, bf16[384,512]{1,0:T(8,128)(2,1)S(1)}, u32[]{:S(2)}, u32[]{:S(2)}) collective-permute-start(bf16[384,512]{1,0:T(8,128)(2,1)} %pad_maximum_fusion.6), channel_id=1, source_target_pairs={{0,2},{2,0},{1,3},{3,1},{4,6},{6,4},{5,7},{7,5},{8,10},{10,8},{9,1... | collective-permute-start | bytes 1179656 | tf_op jit(solution)/shard_map/ppermute | solution.py:435
  136.1 15.3 %collective-permute-start.26 = (bf16[256,512]{1,0:T(8,128)(2,1)}, bf16[256,512]{1,0:T(8,128)(2,1)}, u32[]{:S(2)}, u32[]{:S(2)}) collective-permute-start(bf16[256,512]{1,0:T(8,128)(2,1)} %pad_maximum_fusion.13), channel_id=1, source_target_pairs={{0,2},{2,0},{1,3},{3,1},{4,6},{6,4},{5,7},{7,5},{8,10},{10,8},{9,1... | collective-permute-start | bytes 786440 | tf_op jit(solution)/shard_map/ppermute | solution.py:435
  138.3 21.5 %collective-permute-start.27 = (bf16[384,512]{1,0:T(8,128)(2,1)}, bf16[384,512]{1,0:T(8,128)(2,1)}, u32[]{:S(2)}, u32[]{:S(2)}) collective-permute-start(bf16[384,512]{1,0:T(8,128)(2,1)} %pad_maximum_fusion.7), channel_id=1, source_target_pairs={{0,2},{2,0},{1,3},{3,1},{4,6},{6,4},{5,7},{7,5},{8,10},{10,8},{9,1... | collective-permute-start | bytes 1179656 | tf_op jit(solution)/shard_map/ppermute | solution.py:435
  141.4 20.5 %collective-permute-start.15 = (bf16[128,512]{1,0:T(8,128)(2,1)}, bf16[128,512]{1,0:T(8,128)(2,1)}, u32[]{:S(2)}, u32[]{:S(2)}) collective-permute-start(bf16[128,512]{1,0:T(8,128)(2,1)} %slice.90), channel_id=1, source_target_pairs={{0,8},{8,16},{16,24},{24,28},{28,20},{20,12},{12,4},{4,0},{1,9},{9... | collective-permute-start | bytes 393224 | tf_op jit(solution)/shard_map/ppermute | solution.py:415
  144.5 19.0 %collective-permute-start.16 = (bf16[128,512]{1,0:T(8,128)(2,1)}, bf16[128,512]{1,0:T(8,128)(2,1)}, u32[]{:S(2)}, u32[]{:S(2)}) collective-permute-start(bf16[128,512]{1,0:T(8,128)(2,1)} %slice.91), channel_id=1, source_target_pairs={{8,0},{16,8},{24,16},{28,24},{20,28},{12,20},{4,12},{0,4},{9,1},{1... | collective-permute-start | bytes 393224 | tf_op jit(solution)/shard_map/ppermute | solution.py:416
  150.3 36.6 %collective-permute-start.47 = (bf16[384,512]{1,0:T(8,128)(2,1)S(1)}, bf16[384,512]{1,0:T(8,128)(2,1)S(1)}, u32[]{:S(2)}, u32[]{:S(2)}) collective-permute-start(bf16[384,512]{1,0:T(8,128)(2,1)S(1)} %copy-done.90), channel_id=1, source_target_pairs={{0,2},{2,0},{1,3},{3,1},{4,6},{6,4},{5,7},{7,5},{8,10},{10,8},{9,1... | collective-permute-start | bytes 1179656 | tf_op jit(solution)/shard_map/ppermute | solution.py:435
  151.4 39.2 %collective-permute-start.48 = (bf16[256,512]{1,0:T(8,128)(2,1)S(1)}, bf16[256,512]{1,0:T(8,128)(2,1)S(1)}, u32[]{:S(2)}, u32[]{:S(2)}) collective-permute-start(bf16[256,512]{1,0:T(8,128)(2,1)S(1)} %copy-done.92), channel_id=1, source_target_pairs={{0,2},{2,0},{1,3},{3,1},{4,6},{6,4},{5,7},{7,5},{8,10},{10,8},{9,1... | collective-permute-start | bytes 786440 | tf_op jit(solution)/shard_map/ppermute | solution.py:435
  159.9 33.5 %collective-permute-start.49 = (bf16[384,512]{1,0:T(8,128)(2,1)S(1)}, bf16[384,512]{1,0:T(8,128)(2,1)S(1)}, u32[]{:S(2)}, u32[]{:S(2)}) collective-permute-start(bf16[384,512]{1,0:T(8,128)(2,1)S(1)} %copy-done.91), channel_id=1, source_target_pairs={{0,2},{2,0},{1,3},{3,1},{4,6},{6,4},{5,7},{7,5},{8,10},{10,8},{9,1... | collective-permute-start | bytes 1179656 | tf_op jit(solution)/shard_map/ppermute | solution.py:435
  161.9 31.4 %collective-permute-start.37 = (bf16[128,512]{1,0:T(8,128)(2,1)S(1)}, bf16[128,512]{1,0:T(8,128)(2,1)S(1)}, u32[]{:S(2)}, u32[]{:S(2)}) collective-permute-start(bf16[128,512]{1,0:T(8,128)(2,1)S(1)} %copy-done.94), channel_id=1, source_target_pairs={{0,8},{8,16},{16,24},{24,28},{28,20},{20,12},{12,4},{4,0},{1,9},{9... | collective-permute-start | bytes 393224 | tf_op jit(solution)/shard_map/ppermute | solution.py:415
  163.5 23.0 %collective-permute-start.55 = (bf16[8,64,192]{2,1,0:T(8,128)(2,1)S(1)}, bf16[8,64,192]{2,1,0:T(8,128)(2,1)S(1)}, u32[]{:S(2)}, u32[]{:S(2)}) collective-permute-start(bf16[8,64,192]{2,1,0:T(8,128)(2,1)S(1)} %fusion.1), channel_id=1, source_target_pairs={{0,2},{2,0},{1,3},{3,1},{4,6},{6,4},{5,7},{7,5},{8,10},{10,8},{9,1... | collective-permute-start | bytes 589832 | tf_op jit(solution)/shard_map/ppermute | solution.py:471
  163.9 29.4 %copy-start.17 = (bf16[256,512]{1,0:T(8,128)(2,1)S(1)}, bf16[256,512]{1,0:T(8,128)(2,1)}, u32[]{:S(2)}) copy-start(bf16[256,512]{1,0:T(8,128)(2,1)} %copy-done.16) | copy-start | bytes 786436
  163.9 29.4 %copy-start.23 = (bf16[128,512]{1,0:T(8,128)(2,1)S(1)}, bf16[128,512]{1,0:T(8,128)(2,1)}, u32[]{:S(2)}) copy-start(bf16[128,512]{1,0:T(8,128)(2,1)} %copy-done.22) | copy-start | bytes 393220
  186.4 6.9 %collective-permute-start.38 = (bf16[128,512]{1,0:T(8,128)(2,1)S(1)}, bf16[128,512]{1,0:T(8,128)(2,1)S(1)}, u32[]{:S(2)}, u32[]{:S(2)}) collective-permute-start(bf16[128,512]{1,0:T(8,128)(2,1)S(1)} %copy-done.95), channel_id=1, source_target_pairs={{8,0},{16,8},{24,16},{28,24},{20,28},{12,20},{4,12},{0,4},{9,1},{1... | collective-permute-start | bytes 393224 | tf_op jit(solution)/shard_map/ppermute | solution.py:416
  187.0 24.8 %collective-permute-start.28 = (bf16[128,1024]{1,0:T(8,128)(2,1)S(1)}, bf16[128,1024]{1,0:T(8,128)(2,1)S(1)}, u32[]{:S(2)}, u32[]{:S(2)}) collective-permute-start(bf16[128,1024]{1,0:T(8,128)(2,1)S(1)} %get-tuple-element.40), channel_id=1, source_target_pairs={{2,0},{3,1},{6,4},{7,5},{10,8},{11,9},{14,12},{15,13},{18,16},{19,... | collective-permute-start | bytes 786440 | tf_op jit(solution)/shard_map/ppermute | solution.py:561
  190.7 21.6 %collective-permute-start.56 = (bf16[4,64,192]{2,1,0:T(8,128)(2,1)S(1)}, bf16[4,64,192]{2,1,0:T(8,128)(2,1)}, u32[]{:S(2)}, u32[]{:S(2)}) collective-permute-start(bf16[4,64,192]{2,1,0:T(8,128)(2,1)S(1)} %dynamic-slice_convert_fusion.1), channel_id=1, source_target_pairs={{0,16},{4,20},{8,24},{12,28},{16,0},{20,4},{24,8},{28,12},{1,17},{... | collective-permute-start | bytes 294920 | tf_op jit(solution)/shard_map/ppermute | solution.py:478
  202.4 15.2 %collective-permute-start.50 = (bf16[128,1024]{1,0:T(8,128)(2,1)S(1)}, bf16[128,1024]{1,0:T(8,128)(2,1)S(1)}, u32[]{:S(2)}, u32[]{:S(2)}) collective-permute-start(bf16[128,1024]{1,0:T(8,128)(2,1)S(1)} %get-tuple-element.53), channel_id=1, source_target_pairs={{2,0},{3,1},{6,4},{7,5},{10,8},{11,9},{14,12},{15,13},{18,16},{19,... | collective-permute-start | bytes 786440 | tf_op jit(solution)/shard_map/ppermute | solution.py:561
  213.8 5.9 %collective-permute-start.57 = (bf16[2,64,192]{2,1,0:T(8,128)(2,1)S(1)}, bf16[2,64,192]{2,1,0:T(8,128)(2,1)S(1)}, u32[]{:S(2)}, u32[]{:S(2)}) collective-permute-start(bf16[2,64,192]{2,1,0:T(8,128)(2,1)S(1)} %dynamic-slice_convert_fusion.3), channel_id=1, source_target_pairs={{0,8},{4,12},{8,0},{12,4},{16,24},{20,28},{24,16},{28,20},{1,9},{5... | collective-permute-start | bytes 147464 | tf_op jit(solution)/shard_map/ppermute | solution.py:478
  217.6 61.0 %collective-permute-start.51 = (bf16[256,1024]{1,0:T(8,128)(2,1)S(1)}, bf16[256,1024]{1,0:T(8,128)(2,1)S(1)}, u32[]{:S(2)}, u32[]{:S(2)}) collective-permute-start(bf16[256,1024]{1,0:T(8,128)(2,1)S(1)} %get-tuple-element.72), channel_id=1, source_target_pairs={{0,1},{1,0},{2,3},{3,2},{4,5},{5,4},{6,7},{7,6},{8,9},{9,8},{10,11... | collective-permute-start | bytes 1572872 | tf_op jit(solution)/shard_map/ppermute | solution.py:608
  218.1 49.5 %copy-start.100 = (f32[2]{0:T(128)S(1)}, f32[2]{0:T(128)}, u32[]{:S(2)}) copy-start(f32[2]{0:T(128)} %constant.206) | copy-start | bytes 28
  219.8 4.0 %collective-permute-start.58 = (bf16[1,64,192]{2,1,0:T(8,128)(2,1)S(1)}, bf16[1,64,192]{2,1,0:T(8,128)(2,1)S(1)}, u32[]{:S(2)}, u32[]{:S(2)}) collective-permute-start(bf16[1,64,192]{2,1,0:T(8,128)(2,1)S(1)} %dynamic-slice_convert_fusion.4), channel_id=1, source_target_pairs={{0,4},{4,0},{8,12},{12,8},{16,20},{20,16},{24,28},{28,24},{1,5},{5... | collective-permute-start | bytes 73736 | tf_op jit(solution)/shard_map/ppermute | solution.py:478
  226.3 52.3 %collective-permute-start.52 = (bf16[256,1024]{1,0:T(8,128)(2,1)S(1)}, bf16[256,1024]{1,0:T(8,128)(2,1)S(1)}, u32[]{:S(2)}, u32[]{:S(2)}) collective-permute-start(bf16[256,1024]{1,0:T(8,128)(2,1)S(1)} %get-tuple-element.74), channel_id=1, source_target_pairs={{0,1},{1,0},{2,3},{3,2},{4,5},{5,4},{6,7},{7,6},{8,9},{9,8},{10,11... | collective-permute-start | bytes 1572872 | tf_op jit(solution)/shard_map/ppermute | solution.py:608
  269.6 7.8 %collective-permute-start.59 = (f32[64,192]{1,0:T(8,128)S(1)}, f32[64,192]{1,0:T(8,128)S(1)}, u32[]{:S(2)}, u32[]{:S(2)}) collective-permute-start(f32[64,192]{1,0:T(8,128)S(1)} %pad_maximum_fusion.18), channel_id=1, source_target_pairs={{0,0},{1,16},{2,1},{3,17},{4,2},{5,18},{6,3},{7,19},{8,4},{9,20},{... | collective-permute-start | bytes 147464 | tf_op jit(solution)/shard_map/ppermute | solution.py:593
  (98 other events, 1383.0 us)

commit v2 on v1

v2 whole, which is shorter than its diff:
```python
import functools

import jax
import jax.numpy as jnp
import numpy as np
from jax import lax
from jax.experimental import pallas as pl
from jax.experimental.pallas import tpu as pltpu
from jax.sharding import Mesh
from jax.sharding import PartitionSpec as P

P_SIZE = 64
N = 128
G = 4
Q = 256
EPS_NORM = 1e-05
CLIP_EPSILON = 1e-06
ADAPTER_SCALE = 2.0
VMEM_BYTES = 24 * 1024 * 1024

F32 = jnp.float32
BF16 = jnp.bfloat16
AXES = ("dp", "x", "core")


def dot(a, b, dims=((1,), (0,))):
    return lax.dot_general(a, b, (dims, ((), ())), preferred_element_type=F32)


def spread(values, pattern):
    high = values.astype(BF16).astype(F32)
    rest = values - high
    mid = rest.astype(BF16).astype(F32)
    return dot(jnp.concatenate([high, mid, rest - mid], axis=1).astype(BF16), pattern)


def spread_pattern(heads):
    return np.tile(np.repeat(np.eye(heads), P_SIZE, axis=1), (3, 1)).astype(BF16)


def of_core(ref, rows, core, first, heads):
    half = ref.shape[1] // 2
    return jnp.where(
        core == 0, ref[rows, first : first + heads], ref[rows, half + first : half + first + heads]
    )


def pair_rows(pair):
    lane = lax.broadcasted_iota(jnp.int32, pair.shape, 1)
    zero = jnp.zeros_like(pair)
    return jnp.concatenate(
        [jnp.where(lane < P_SIZE, pair, zero), jnp.where(lane >= P_SIZE, pair, zero)], axis=0
    )


def whole(shape):
    return pl.BlockSpec(shape, lambda *_: (0,) * len(shape))


def cost(flops, slowdown):
    return pl.CostEstimate(flops=flops * slowdown, bytes_accessed=0, transcendentals=0)


def params(*semantics):
    return pltpu.CompilerParams(
        dimension_semantics=semantics or None, vmem_limit_bytes=VMEM_BYTES
    )


def step_kernel(blocks, core_ref, near_ref, far_ref, bias_ref, rate_ref, step_ref, cum_ref, cum_t_ref):
    lower = lax.broadcasted_iota(jnp.int32, (Q, Q), 0) >= lax.broadcasted_iota(
        jnp.int32, (Q, Q), 1
    )
    for block in range(blocks):
        rows = slice(block * Q, (block + 1) * Q)
        local = slice(block % (blocks // 2) * Q, (block % (blocks // 2) + 1) * Q)
        raw = jnp.where(
            core_ref[0] == block // (blocks // 2), near_ref[local, :], far_ref[local, :]
        )
        raw = raw + bias_ref[...]
        step = jnp.maximum(raw, 0.0) + jnp.log1p(jnp.exp(-jnp.abs(raw)))
        cum = lax.dot_general(
            lower.astype(F32),
            -jnp.exp(rate_ref[...]) * step,
            (((1,), (0,)), ((), ())),
            precision=lax.Precision.HIGHEST,
            preferred_element_type=F32,
        )
        step_ref[rows, :] = step
        cum_ref[rows, :] = cum
        cum_t_ref[block] = cum.T


def step_part(core, near, far, bias, rate):
    rows, heads = 2 * near.shape[0], near.shape[1]
    spec = pltpu.PrefetchScalarGridSpec(
        num_scalar_prefetch=1,
        grid=(1,),
        in_specs=[whole(near.shape), whole(far.shape), whole(bias.shape), whole(rate.shape)],
        out_specs=[whole((rows, heads)), whole((rows, heads)), whole((rows // Q, heads, Q))],
    )
    return pl.pallas_call(
        functools.partial(step_kernel, rows // Q),
        grid_spec=spec,
        out_shape=[
            jax.ShapeDtypeStruct((rows, heads), F32),
            jax.ShapeDtypeStruct((rows, heads), F32),
            jax.ShapeDtypeStruct((rows // Q, heads, Q), F32),
        ],
        compiler_params=params("arbitrary"),
        cost_estimate=cost(rows * heads * Q, 200),
        name="step_part",
    )(core, near, far, bias, rate)


def local_kernel(
    first, heads, core_ref, near_ref, far_ref, b_ref, c_ref, step_ref, cum_ref, cum_t_ref, skip_ref,
    pattern_ref, scores_ref, ssd_ref, state_ref, total_ref, x_ref,
):
    block = pl.program_id(0)
    core = core_ref[0]
    x_ref[...] = jnp.where(
        block // (pl.num_programs(0) // 2) == core, near_ref[...], far_ref[...]
    )
    pattern = pattern_ref[...]
    step = of_core(step_ref, slice(None), core, first, heads)
    cum = of_core(cum_ref, slice(None), core, first, heads)
    start = pl.multiple_of(core * (cum_t_ref.shape[1] // 2) + first, 8)
    cum_t = cum_t_ref[0, pl.ds(start, heads), :]
    last = cum[Q - 1 : Q, :]
    step_wide = spread(step, pattern)
    weight = spread(step * jnp.exp(last - cum), pattern)
    decay = spread(jnp.broadcast_to(jnp.exp(last), (8, heads)), pattern)[:1, :]
    x = x_ref[...].astype(F32)
    xdt = (x * step_wide).astype(BF16)
    state = dot(b_ref[...], (x * weight).astype(BF16), ((0,), (0,)))
    state_ref[...] = state

    @pl.when(block == 0)
    def _():
        total_ref[...] = state

    @pl.when(block > 0)
    def _():
        total_ref[...] = total_ref[...] * decay + state

    inner = dot(b_ref[...], c_ref[...], ((1,), (1,)))
    causal = lax.broadcasted_iota(jnp.int32, (Q, Q), 1) >= lax.broadcasted_iota(
        jnp.int32, (Q, Q), 0
    )
    masked = jnp.where(causal, inner, 0.0)
    for pair in range(heads // 2):
        parts = []
        for head in (2 * pair, 2 * pair + 1):
            gap = cum_t[head : head + 1, :] - cum[:, head : head + 1]
            part = (masked * jnp.exp(jnp.where(causal, gap, 0.0))).astype(BF16)
            scores_ref[:, head * Q : (head + 1) * Q] = part
            parts.append(part)
        lanes = slice(pair * 2 * P_SIZE, (pair + 1) * 2 * P_SIZE)
        intra = dot(jnp.concatenate(parts, axis=0), pair_rows(xdt[:, lanes]), ((0,), (0,)))
        ssd_ref[:, lanes] = intra + skip_ref[:, lanes] * x_ref[:, lanes].astype(F32)


def local_part(group, groups, heads, core, near, far, b, c, step, cum, cum_t, skip, pattern):
    rows = 2 * near.shape[0]
    blocks = rows // Q
    width = heads * P_SIZE
    row_block = pl.BlockSpec((Q, width), lambda i, s: (i, 0))
    spec = pltpu.PrefetchScalarGridSpec(
        num_scalar_prefetch=1,
        grid=(blocks,),
        in_specs=[
            pl.BlockSpec((Q, width), lambda i, s: (i % (blocks // 2), s[0] * groups + group)),
            pl.BlockSpec((Q, width), lambda i, s: (i % (blocks // 2), group)),
            pl.BlockSpec((Q, N), lambda i, s: (i, group)),
            pl.BlockSpec((Q, N), lambda i, s: (i, group)),
            pl.BlockSpec((Q, step.shape[1]), lambda i, s: (i, 0)),
            pl.BlockSpec((Q, step.shape[1]), lambda i, s: (i, 0)),
            pl.BlockSpec((1,) + cum_t.shape[1:], lambda i, s: (i, 0, 0)),
            pl.BlockSpec((1, width), lambda i, s: (0, s[0] * groups + group)),
            whole(pattern.shape),
        ],
        out_specs=[
            pl.BlockSpec((Q, heads * Q), lambda i, s: (i, 0)),
            row_block,
            pl.BlockSpec((N, width), lambda i, s: (i, 0)),
            pl.BlockSpec((N, width), lambda i, s: (0, 0)),
        ],
        scratch_shapes=[pltpu.VMEM((Q, width), BF16)],
    )
    return pl.pallas_call(
        functools.partial(local_kernel, group * heads, heads),
        grid_spec=spec,
        out_shape=[
            jax.ShapeDtypeStruct((rows, heads * Q), BF16),
            jax.ShapeDtypeStruct((rows, width), F32),
            jax.ShapeDtypeStruct((blocks * N, width), F32),
            jax.ShapeDtypeStruct((N, width), F32),
        ],
        compiler_params=params("arbitrary"),
        cost_estimate=cost(rows * width * Q * 4, 18),
        name="local_part",
    )(core, near, far, b, c, step, cum, cum_t, skip, pattern)


def norm_kernel(
    blocks, first, heads, core_ref, c_ref, incoming_ref, state_ref, cum_ref, pattern_ref, ssd_ref, near_ref,
    far_ref, gain_ref, down_ref, up_ref, hat_ref, slope_ref, product_ref, sum_ref,
):
    gain = gain_ref[...]
    run = incoming_ref[...].astype(F32)
    total = None
    for block in range(blocks):
        rows = slice(block * Q, (block + 1) * Q)
        inter = dot(c_ref[rows, :], run.astype(BF16))
        growth = spread(jnp.exp(of_core(cum_ref, rows, core_ref[0], first, heads)), pattern_ref[...])
        ssd = ssd_ref[rows, :] + growth * inter
        local = slice(block % (blocks // 2) * Q, (block % (blocks // 2) + 1) * Q)
        z = jnp.where(
            core_ref[0] == block // (blocks // 2), near_ref[local, :], far_ref[local, :]
        ).astype(F32)
        silu = z / (1.0 + jnp.exp(-z))
        gated = ssd * silu
        rstd = lax.rsqrt(jnp.mean(gated * gated, axis=1, keepdims=True) + EPS_NORM)
        hat = gated * rstd
        normed = (hat * gain).astype(BF16)
        hat_ref[rows, :] = hat.astype(hat_ref.dtype)
        slope_ref[rows, :] = rstd * silu
        product_ref[rows, :] = dot(normed, down_ref[...], ((1,), (1,)))
        part = dot(up_ref[rows, :], normed, ((0,), (0,)))
        total = part if total is None else total + part
        if block + 1 < blocks:
            states = slice(block * N, (block + 1) * N)
            run = run * growth[Q - 1 :, :] + state_ref[states, :]
    sum_ref[...] = total


def norm_part(
    group, groups, heads, core, c, incoming, state, cum, pattern, ssd, near, far, gain, down, up_twice
):
    rows, width = ssd.shape
    rank = down.shape[0]
    blocks = rows // Q
    spec = pltpu.PrefetchScalarGridSpec(
        num_scalar_prefetch=1,
        grid=(1,),
        in_specs=[
            pl.BlockSpec((rows, N), lambda i, s: (0, group)),
            whole(incoming.shape),
            whole(state.shape),
            whole(cum.shape),
            whole(pattern.shape),
            whole(ssd.shape),
            pl.BlockSpec((rows // 2, width), lambda i, s: (0, s[0] * groups + group)),
            pl.BlockSpec((rows // 2, width), lambda i, s: (0, group)),
            pl.BlockSpec((1, width), lambda i, s: (0, s[0] * groups + group)),
            pl.BlockSpec((rank, width), lambda i, s: (0, s[0] * groups + group)),
            whole(up_twice.shape),
        ],
        out_specs=[
            whole((rows, width)), whole((rows, width)), whole((rows, rank)), whole((rank, width)),
        ],
    )
    return pl.pallas_call(
        functools.partial(norm_kernel, blocks, group * heads, heads),
        grid_spec=spec,
        out_shape=[
            jax.ShapeDtypeStruct((rows, width), BF16),
            jax.ShapeDtypeStruct((rows, width), F32),
            jax.ShapeDtypeStruct((rows, rank), F32),
            jax.ShapeDtypeStruct((rank, width), F32),
        ],
        compiler_params=params("arbitrary"),
        cost_estimate=cost(rows * width * 512, 14),
        name="norm_part",
    )(core, c, incoming, state, cum, pattern, ssd, near, far, gain, down, up_twice)


def product_kernel(count, started, core_ref, near_ref, far_ref, *rest):
    pieces, out_ref = rest[started : started + count], rest[-1]
    weights = joined(pieces)
    half = near_ref.shape[0]
    for part in range(2):
        rows = slice(part * half, (part + 1) * half)
        cot = jnp.where(core_ref[0] == part, near_ref[...], far_ref[...])
        product = dot(cot, weights)
        out_ref[rows, :] = product + rest[0][rows, :] if started else product


def joined(pieces):
    return jnp.concatenate([piece[...] for piece in pieces], axis=0)


def product_part(core, near, far, earlier, pieces, width):
    rows = 2 * near.shape[0]
    held = [] if earlier is None else [earlier]
    spec = pltpu.PrefetchScalarGridSpec(
        num_scalar_prefetch=1,
        grid=(1,),
        in_specs=[whole(near.shape), whole(far.shape)]
        + [whole(array.shape) for array in held]
        + [whole(piece.shape) for piece in pieces],
        out_specs=whole((rows, width)),
    )
    return pl.pallas_call(
        functools.partial(product_kernel, len(pieces), len(held)),
        grid_spec=spec,
        out_shape=jax.ShapeDtypeStruct((rows, width), F32),
        compiler_params=params("arbitrary"),
        cost_estimate=cost(2 * rows * width * near.shape[1], 3),
        name="product_part",
    )(core, near, far, *held, *pieces)


def grad_kernel(
    blocks, first, heads, core_ref, near_ref, far_ref, earlier_ref, up_ref, down_ref, gain_ref, hat_ref,
    slope_ref, cum_ref, pattern_ref, c_ref, *rest,
):
    pieces, (grad_ref, block_grad_ref, total_ref) = rest[:-3], rest[-3:]
    weights = joined(pieces)
    gain = gain_ref[...]
    later = None
    for block in reversed(range(blocks)):
        rows = slice(block * Q, (block + 1) * Q)
        local = slice(block % (blocks // 2) * Q, (block % (blocks // 2) + 1) * Q)
        cot = jnp.where(
            core_ref[0] == block // (blocks // 2), near_ref[local, :], far_ref[local, :]
        )
        product = dot(cot, weights) + dot(up_ref[rows, :], down_ref[...]) + earlier_ref[rows, :]
        weighted = product * gain
        hat = hat_ref[rows, :].astype(F32)
        mean = jnp.mean(hat * weighted, axis=1, keepdims=True)
        grad = slope_ref[rows, :] * (weighted - hat * mean)
        grad_ref[rows, :] = grad
        growth = spread(jnp.exp(of_core(cum_ref, rows, core_ref[0], first, heads)), pattern_ref[...])
        fresh = dot(c_ref[rows, :], (growth * grad).astype(BF16), ((0,), (0,)))
        block_grad_ref[block * N : (block + 1) * N, :] = fresh
        later = (
            fresh
            if later is None
            else later * growth[Q - 1 :, :] + fresh
        )
    total_ref[...] = later.astype(BF16)


def grad_part(
    group, groups, heads, core, near, far, earlier, up_twice, down, gain, hat, slope, cum, pattern, c, pieces
):
    rows, width = hat.shape
    rank = down.shape[0]
    blocks = rows // Q
    spec = pltpu.PrefetchScalarGridSpec(
        num_scalar_prefetch=1,
        grid=(1,),
        in_specs=[
            whole(near.shape),
            whole(far.shape),
            whole(earlier.shape),
            whole(up_twice.shape),
            pl.BlockSpec((rank, width), lambda i, s: (0, s[0] * groups + group)),
            pl.BlockSpec((1, width), lambda i, s: (0, s[0] * groups + group)),
            whole(hat.shape),
            whole(slope.shape),
            whole(cum.shape),
            whole(pattern.shape),
            pl.BlockSpec((rows, N), lambda i, s: (0, group)),
        ]
        + [whole(piece.shape) for piece in pieces],
        out_specs=[whole((rows, width)), whole((blocks * N, width)), whole((N, width))],
    )
    return pl.pallas_call(
        functools.partial(grad_kernel, blocks, group * heads, heads),
        grid_spec=spec,
        out_shape=[
            jax.ShapeDtypeStruct((rows, width), F32),
            jax.ShapeDtypeStruct((blocks * N, width), F32),
            jax.ShapeDtypeStruct((N, width), BF16),
        ],
        compiler_params=params("arbitrary"),
        cost_estimate=cost(2 * rows * width * near.shape[1], 7),
        name="grad_part",
    )(
        core, near, far, earlier, up_twice, down, gain, hat, slope, cum, pattern, c,
        *pieces,
    )


def back_kernel(first, heads, core_ref, scores_ref, grad_ref, step_ref, pattern_ref, skip_ref, out_ref):
    step = of_core(step_ref, slice(None), core_ref[0], first, heads)
    out_ref[...] = spread(step, pattern_ref[...])
    for pair in range(heads // 2):
        lanes = slice(pair * 2 * P_SIZE, (pair + 1) * 2 * P_SIZE)
        grad = grad_ref[:, lanes]
        back = dot(
            scores_ref[:, 2 * pair * Q : 2 * (pair + 1) * Q], pair_rows(grad.astype(BF16))
        )
        out_ref[:, lanes] = out_ref[:, lanes] * back + skip_ref[:, lanes] * grad


def back_part(group, groups, heads, core, scores, grad, step, pattern, skip):
    rows, width = grad.shape
    row_block = pl.BlockSpec((Q, width), lambda i, s: (i, 0))
    spec = pltpu.PrefetchScalarGridSpec(
        num_scalar_prefetch=1,
        grid=(rows // Q,),
        in_specs=[
            pl.BlockSpec((Q, heads * Q), lambda i, s: (i, 0)),
            row_block,
            pl.BlockSpec((Q, step.shape[1]), lambda i, s: (i, 0)),
            whole(pattern.shape),
            pl.BlockSpec((1, width), lambda i, s: (0, s[0] * groups + group)),
        ],
        out_specs=row_block,
    )
    return pl.pallas_call(
        functools.partial(back_kernel, group * heads, heads),
        grid_spec=spec,
        out_shape=jax.ShapeDtypeStruct((rows, width), F32),
        compiler_params=params("arbitrary"),
        cost_estimate=cost(rows * width * Q * 2, 8),
        name="back_part",
    )(core, scores, grad, step, pattern, skip)


def cross_kernel(
    blocks, first, heads, core_ref, b_ref, outgoing_ref, block_grad_ref, step_ref, cum_ref, pattern_ref,
    base_ref, near_ref, far_ref,
):
    run = outgoing_ref[...].astype(F32)
    for block in reversed(range(blocks)):
        rows = slice(block * Q, (block + 1) * Q)
        local = slice(block % (blocks // 2) * Q, (block % (blocks // 2) + 1) * Q)
        cross = dot(b_ref[rows, :], run.astype(BF16))
        cum = of_core(cum_ref, rows, core_ref[0], first, heads)
        last = cum[Q - 1 :, :]
        step = of_core(step_ref, rows, core_ref[0], first, heads)
        weight = spread(step * jnp.exp(last - cum), pattern_ref[...])
        value = (base_ref[rows, :] + weight * cross).astype(near_ref.dtype)
        own = core_ref[0] == block // (blocks // 2)

        @pl.when(own)
        def _():
            near_ref[local, :] = value

        @pl.when(jnp.logical_not(own))
        def _():
            far_ref[local, :] = value

        if block > 0:
            states = slice(block * N, (block + 1) * N)
            decay = spread(jnp.broadcast_to(jnp.exp(last), (8, heads)), pattern_ref[...])[:1, :]
            run = run * decay + block_grad_ref[states, :]


def cross_part(group, heads, core, b, outgoing, block_grad, step, cum, pattern, base):
    rows, width = base.shape
    blocks = rows // Q
    spec = pltpu.PrefetchScalarGridSpec(
        num_scalar_prefetch=1,
        grid=(1,),
        in_specs=[
            pl.BlockSpec((rows, N), lambda i, s: (0, group)),
            whole(outgoing.shape),
            whole(block_grad.shape),
            whole(step.shape),
            whole(cum.shape),
            whole(pattern.shape),
            whole(base.shape),
        ],
        out_specs=[whole((rows // 2, width))] * 2,
    )
    return pl.pallas_call(
        functools.partial(cross_kernel, blocks, group * heads, heads),
        grid_spec=spec,
        out_shape=[jax.ShapeDtypeStruct((rows // 2, width), BF16)] * 2,
        compiler_params=params("arbitrary"),
        cost_estimate=cost(rows * width * N * 2, 6),
        name="cross_part",
    )(core, b, outgoing, block_grad, step, cum, pattern, base)


def ring_order(count):
    return list(range(0, count, 2)) + list(range(count - 1 - count % 2, 0, -2))


def rotations(count):
    return [[(i, (i + k) % count) for i in range(count)] for k in range(count)]


def chip_order():
    ring, across = lax.axis_size("dp"), lax.axis_size("x")
    offsets = [0]
    for distance in range(1, (ring - 1) // 2 + 1):
        offsets += [-distance, distance]
    if ring % 2 == 0:
        offsets.append(ring // 2)
    me, x = lax.axis_index("dp"), lax.axis_index("x")
    seat = jnp.where(me % 2 == 0, me // 2, ring - (me + 1) // 2)

    def member(place):
        return jnp.where(place < (ring + 1) // 2, 2 * place, 2 * (ring - place) - 1)

    return [
        [member((seat + offset + ring) % ring) * across + (x - k + across) % across for k in range(across)]
        for offset in offsets
    ]


def ring_perms():
    ring = lax.axis_size("dp")
    order = ring_order(ring)
    ahead = [(order[i], order[(i + 1) % ring]) for i in range(ring)]
    return ahead, [(b, a) for a, b in ahead]


class Gather:
    def __init__(self, shards):
        self.ring = lax.axis_size("dp")
        self.turns = rotations(lax.axis_size("x"))[1:]
        self.perms = ring_perms()
        self.shards = shards
        self.late = (shards[1], shards[1])
        self.early = None
        self.pieces = {}
        self.steps = self.ring // 2 + 2

    def onward(self, arrays, distance):
        if 2 * distance == self.ring:
            half = arrays[0].shape[0] // 2
            arrays = (arrays[0][:half], arrays[1][half:])
        return tuple(lax.ppermute(array, "dp", perm) for array, perm in zip(arrays, self.perms))

    def crossing(self, arrays):
        return [tuple(lax.ppermute(array, "x", turn) for turn in self.turns) for array in arrays]

    def step(self, index, beside):
        early = late = None
        if 2 * index <= self.ring:
            late = self.onward(self.late, index)
        if index == 1:
            crossed = self.crossing(self.shards)
        else:
            early = self.onward(self.early, index - 1)
            crossed = self.crossing(self.late)
        values = beside()
        early, late, crossed, values = lax.optimization_barrier((early, late, crossed, values))
        if index == 1:
            first = jnp.concatenate([self.shards[0], *crossed[0]], axis=0)
            self.early = (first, first)
            self.pieces[0] = [[first], [self.shards[1], *crossed[1]]]
        else:
            distance = index - 1
            if 2 * distance < self.ring:
                for side in range(2):
                    self.pieces[2 * distance - 1 + side] = [
                        [early[side]], [self.late[side], *crossed[side]]
                    ]
            else:
                halves = zip(*[(array, *met) for array, met in zip(self.late, crossed)])
                self.pieces[2 * distance - 1] = [
                    list(early), [array for pair in halves for array in pair]
                ]
            self.early = early
        self.late = late
        return values


def pack_kernel(ring, across, place_ref, first_ref, second_ref, own_ref, far_ref, mine_ref, *sent_refs):
    sums = (first_ref[...], second_ref[...])
    wide = sums[0].shape[1]
    other = own_ref[...] + far_ref[...].astype(F32)
    width_a = 2 * wide // (ring * across)
    width_b = other.shape[1] // (ring * across)
    for member in range(ring):
        blocks = []
        for x in range(across):
            chip = member * across + x
            start = chip * width_a % wide
            part = sums[chip * width_a // wide][:, start : start + width_a]
            blocks.append((part, other[:, chip * width_b : (chip + 1) * width_b]))
        for turn in range(across):
            target = (place_ref[1] + turn) % across
            chosen = blocks[0]
            for x in range(1, across):
                chosen = [jnp.where(target == x, new, old) for new, old in zip(blocks[x], chosen)]
            out = mine_ref if turn == 0 else sent_refs[turn - 1]
            out[member, :, :width_a] = chosen[0].astype(out.dtype)
            out[member, :, width_a:] = chosen[1].astype(out.dtype)


def split_kernel(ring, across, place_ref, mine_ref, *refs):
    arrived, (kept_ref, *sent_refs) = refs[: across - 1], refs[across - 1 :]
    for turn in range(ring):
        member = (place_ref[0] + turn) % ring
        total = mine_ref[member]
        for ref in arrived:
            total = total + ref[member].astype(F32)
        out = kept_ref if turn == 0 else sent_refs[turn - 1]
        out[...] = total.astype(out.dtype)


def total_kernel(width_a, kept_ref, *refs):
    arrived, (total_ref, square_ref) = refs[:-2], refs[-2:]
    total = kept_ref[...]
    for ref in arrived:
        total = total + ref[...].astype(F32)
    total_ref[...] = total
    squares = total * total
    lane = lax.broadcasted_iota(jnp.int32, squares.shape, 1)
    first = jnp.sum(jnp.where(lane < width_a, squares, 0.0))
    second = jnp.sum(jnp.where(lane >= width_a, squares, 0.0))
    column = lax.broadcasted_iota(jnp.int32, square_ref.shape, 1)
    square_ref[...] = jnp.where(column == 0, first, jnp.where(column == 1, second, 0.0))


def small_call(kernel, scalars, arrays, outs, name):
    spec = pltpu.PrefetchScalarGridSpec(
        num_scalar_prefetch=len(scalars),
        grid=(1,),
        in_specs=[whole(array.shape) for array in arrays],
        out_specs=[whole(out.shape) for out in outs],
    )
    return pl.pallas_call(
        kernel,
        grid_spec=spec,
        out_shape=outs,
        compiler_params=params("arbitrary"),
        cost_estimate=cost(10**9, 1),
        name=name,
    )(*scalars, *arrays)


class Sums:
    def __init__(self, sums_a, own_b, far_b):
        self.ring, self.across = lax.axis_size("dp"), lax.axis_size("x")
        self.place = jnp.stack([lax.axis_index("dp"), lax.axis_index("x")]).astype(jnp.int32)
        rank = own_b.shape[0]
        count = self.ring * self.across
        self.width_a = 2 * sums_a[0].shape[1] // count
        self.shape = (rank, self.width_a + own_b.shape[1] // count)
        wide = (self.ring,) + self.shape
        self.mine, *self.sent = small_call(
            functools.partial(pack_kernel, self.ring, self.across),
            [self.place],
            [*sums_a, own_b, far_b],
            [jax.ShapeDtypeStruct(wide, F32)]
            + [jax.ShapeDtypeStruct(wide, BF16)] * (self.across - 1),
            "pack_sums",
        )

    def over_x(self):
        turns = rotations(self.across)[1:]
        arrived = [lax.ppermute(value, "x", turn) for value, turn in zip(self.sent, turns)]
        self.mine, *self.sent = small_call(
            functools.partial(split_kernel, self.ring, self.across),
            [self.place],
            [self.mine, *arrived],
            [jax.ShapeDtypeStruct(self.shape, F32)]
            + [jax.ShapeDtypeStruct(self.shape, BF16)] * (self.ring - 1),
            "split_sums",
        )

    def over_dp(self):
        turns = rotations(self.ring)[1:]
        arrived = [lax.ppermute(value, "dp", turn) for value, turn in zip(self.sent, turns)]
        return small_call(
            functools.partial(total_kernel, self.width_a),
            [],
            [self.mine, *arrived],
            [jax.ShapeDtypeStruct(self.shape, F32), jax.ShapeDtypeStruct((8, 128), F32)],
            "total_sums",
        )


def everywhere(value):
    for axis in ("core", "x", "dp"):
        distance = 1
        while distance < lax.axis_size(axis):
            pairs = [(i, i ^ distance) for i in range(lax.axis_size(axis))]
            value = value + lax.ppermute(value, axis, pairs)
            distance *= 2
    return value


def on_device(
    state_input, gate_values, input_matrix, readout_matrix, step_unbiased, step_bias,
    decay_rate_log, skip_coefficients, norm_gain, adapter_down, adapter_up, projection_weight,
    output_cotangent,
):
    ring, across = lax.axis_size("dp"), lax.axis_size("x")
    core = lax.axis_index("core")
    swap = [(0, 1), (1, 0)]
    near_rows = state_input.shape[0]
    groups = G // 2
    heads = step_bias.shape[0] // G
    width = heads * P_SIZE

    def half(value, which, axis=-1):
        size = value.shape[axis] // 2
        return lax.dynamic_slice_in_dim(value, which * size, size, axis)

    def in_order(near, far, axis=0):
        return jnp.concatenate(
            [jnp.where(core == 0, near, far), jnp.where(core == 0, far, near)], axis=axis
        )

    def both_cores(value):
        far = lax.ppermute(half(value, 1 - core), "core", swap)
        return in_order(half(value, core), far)

    def swapped(value):
        return lax.ppermute(value, "core", swap)

    x_far = swapped(half(state_input, 1 - core))
    raw_far = swapped(step_unbiased)
    shard = both_cores(projection_weight)
    shards = [shard[:, group * width : (group + 1) * width] for group in range(groups)]
    (shards, state_input, gate_values, input_matrix, readout_matrix, step_unbiased, output_cotangent) = (
        lax.optimization_barrier(
            (shards, state_input, gate_values, input_matrix, readout_matrix, step_unbiased, output_cotangent)
        )
    )
    which = core.astype(jnp.int32)[None]
    chips = chip_order()
    chip_rows = shard.shape[0]
    slots = list(range(len(chips)))
    stages = [slots[:3], slots[3:5], slots[5:]] if len(slots) > 5 else [slots[:1], slots[1:]]
    rows = 2 * near_rows
    blocks = rows // Q
    gather = Gather(shards)
    forward = [(i, i + 1) for i in range(across - 1)]
    backward = [(i + 1, i) for i in range(across - 1)]

    def columns(stage):
        return jnp.concatenate(
            [
                lax.dynamic_slice_in_dim(output_cotangent, chip * chip_rows, chip_rows, 1)
                for offset in stage
                for chip in chips[offset]
            ],
            axis=1,
        )

    def staged(index, group):
        return [piece for slot in stages[index] for piece in gather.pieces[slot][group]]

    def carried(fresh, cum, group, perm):
        sent = fresh.astype(BF16)
        for lap in range(across - 1):
            arrived = lax.ppermute(sent, "x", perm)
            if lap + 2 < across:
                total = jnp.sum(cum.reshape(blocks, Q, -1)[:, Q - 1], axis=0)
                decay = jnp.exp(half(total, core)[group * heads : (group + 1) * heads])
                decay = jnp.repeat(decay, P_SIZE)[None, :]
                sent = (arrived.astype(F32) * decay + fresh.astype(F32)).astype(BF16)
        return arrived

    skip = jnp.repeat(skip_coefficients, P_SIZE)[None, :]
    gain = norm_gain[None, :]
    pattern = spread_pattern(heads)

    def inside(group, x_far, b, c, step, cum, cum_t):
        return local_part(
            group, groups, heads, which, state_input, x_far, b, c, step, cum, cum_t, skip, pattern
        )

    def prepare():
        step, cum, cum_t = step_part(
            which, step_unbiased, raw_far, step_bias[None, :], decay_rate_log[None, :]
        )
        b = both_cores(input_matrix)
        c = both_cores(readout_matrix)
        return step, cum, cum_t, b, c, inside(0, x_far, b, c, step, cum, cum_t)

    step, cum, cum_t, b, c, local_first = gather.step(1, prepare)

    def second():
        local_second = inside(1, x_far, b, c, step, cum, cum_t)
        up_near = (
            ADAPTER_SCALE * dot(output_cotangent, adapter_up, ((1,), (1,))).astype(BF16)
        ).astype(BF16)
        near = [columns(stage) for stage in stages]
        return (
            local_second,
            carried(local_first[3], cum, 0, forward),
            in_order(up_near, swapped(up_near)),
            [(part, swapped(part)) for part in near],
            swapped(half(gate_values, 1 - core)),
        )

    local_second, incoming_first, up_twice, cots, z_far = gather.step(2, second)
    local = [local_first, local_second]

    def norm(group, incoming):
        scores, ssd, state, total = local[group]
        return norm_part(
            group, groups, heads, which, c, incoming, state, cum, pattern, ssd, gate_values, z_far, gain,
            adapter_down, up_twice,
        )

    def products(index, earlier):
        return [
            product_part(which, *cots[index], earlier[group], staged(index, group), width)
            for group in range(groups)
        ]

    def third():
        incoming = carried(local[1][3], cum, 1, forward)
        return [norm(0, incoming_first), norm(1, incoming)]

    normed = gather.step(3, third) if gather.steps > 3 else third()
    nothing = [None] * groups

    def lora_down():
        product = functools.reduce(jnp.add, [part[2] for part in normed])
        arrived = swapped(half(product, 1 - core, 0))
        down_product = (half(product, core, 0) + arrived).astype(BF16)
        part_b = ADAPTER_SCALE * dot(down_product, output_cotangent, ((0,), (0,)))
        far_b = swapped(half(part_b, 1 - core).astype(BF16))
        return Sums([part[3] for part in normed], half(part_b, core), far_b)

    def fourth():
        return lora_down(), products(0, nothing)

    sums, earlier = fourth()
    sums.mine, sums.sent, earlier = (
        gather.step(4, lambda: (sums.mine, sums.sent, earlier))
        if gather.steps > 4
        else (sums.mine, sums.sent, earlier)
    )

    def fifth():
        sums.over_x()
        return sums.mine, sums.sent, products(1, earlier) if len(stages) > 2 else earlier

    sums.mine, sums.sent, earlier = gather.step(5, fifth) if gather.steps > 5 else fifth()
    for index in range(6, gather.steps):
        gather.step(index, lambda: ())
    total, squares = sums.over_dp()

    entries = jnp.asarray([sums.width_a, total.shape[1] - sums.width_a], F32)
    entries = entries * (total.shape[0] * ring * across * 2)
    squares = everywhere(squares[:1])[0, :2]
    scale = 1.0 / jnp.maximum(1.0, jnp.sqrt(squares / entries + CLIP_EPSILON))
    count = ring * across
    homes = [
        (chip * 2 + number, number * count + chip) for chip in range(count) for number in range(2)
    ]
    total = lax.ppermute(total, AXES, homes)
    gradient_a = total[:, : sums.width_a] * scale[0]
    gradient_b = total[:, sums.width_a :] * scale[1]

    near, far = [], []
    for group in range(groups):
        hat, slope = normed[group][:2]
        grad, block_grad, grad_total = grad_part(
            group, groups, heads, which, *cots[-1], earlier[group], up_twice, adapter_down, gain, hat, slope,
            cum, pattern, c, staged(len(stages) - 1, group),
        )
        outgoing = carried(grad_total, cum, group, backward)
        base = back_part(group, groups, heads, which, local[group][0], grad, step, pattern, skip)
        own, others = cross_part(
            group, heads, which, b, outgoing, block_grad, step, cum, pattern, base
        )
        far.append(swapped(others))
        near.append(own)
    input_gradient = in_order(
        jnp.concatenate(near, axis=1), jnp.concatenate(far, axis=1), axis=1
    )
    return input_gradient, gradient_a, gradient_b


def solution(mesh):
    ring, ctx = mesh.shape["dp"], mesh.shape["ctx"]
    split = Mesh(mesh.devices.reshape(ring, ctx // 2, 2), AXES)
    rows = P(AXES, None)
    placed = (rows,) * 5 + (P(),) * 6 + (rows,) * 2
    return jax.shard_map(
        on_device,
        mesh=split,
        in_specs=placed,
        out_specs=(rows, P(None, AXES), P(None, AXES)),
        check_vma=False,
    )
```

time: 282 us -> 167 us (0.59)
  the two profiles are of different devices: /device:TPU:2 before, /device:TPU:0 now
where the time goes in v2:
time: 167 us; the launch traced here: 165 us
  starting transfers between devices  68.8 us (41%)
  waiting for transfers between devices  43.4 us (26%)
  Pallas kernels  33.4 us (20%)
  local copies, waits for them, and re-layouts  10.2 us (6%)
  other arithmetic  6.4 us (4%)
    ppermute x16, waiting for transfers between devices, onward(): lax.ppermute(array, 'dp', perm)  25.9 us
    ppermute x16, starting transfers between devices, onward(): lax.ppermute(array, 'dp', perm)  17.7 us
    pallas_call x2, Pallas kernels, local_part(): pl.pallas_call(functools.partial(local_kernel, group * heads, heads), gri...  12.4 us
    ppermute x7, starting transfers between devices, over_dp(): lax.ppermute(value, 'dp', turn)  11.9 us
    ppermute x10, starting transfers between devices, crossing(): lax.ppermute(array, 'x', turn)  11 us
    ppermute x4, starting transfers between devices, carried(): arrived = lax.ppermute(sent, 'x', perm)  9.31 us
    ppermute x10, waiting for transfers between devices, crossing(): lax.ppermute(array, 'x', turn)  8.82 us
    ppermute x5, starting transfers between devices, everywhere(): value = value + lax.ppermute(value, axis, pairs)  8.09 us
  transfers between devices with their start and end apart: 58, of which 17 were waited for; matrix products, arithmetic and copies ran while one was open for 7% of the time, Pallas kernels for 20%

profile of v2, /device:TPU:0, one launch (start us, length us, event | category | flops | bytes accessed | tf_op | source)
XLA Modules:
  0.0 164.6 jit_solution(6639662493465798540)
XLA Ops:
  0.7 1.7 %constant_dynamic-slice_fusion.10 = bf16[64,2048]{1,0:T(8,128)(2,1)} fusion(bf16[64,4096]{1,0:T(8,128)(2,1)} %param.26, s32[]{:T(128)S(6)} %select_n.264), kind=kLoop, calls=%fused_computation.55 | loop fusion | bytes 524292 | tf_op jit(solution)/shard_map/dynamic_slice | solution.py:700
  2.9 1.6 copy.18
  4.5 2.3 %constant_dynamic-slice_fusion.7 = bf16[256,2048]{1,0:T(8,128)(2,1)} fusion(bf16[256,4096]{1,0:T(8,128)(2,1)} %near_ref.1, s32[]{:T(128)S(6)} %select_n.264), kind=kLoop, calls=%fused_computation.52 | loop fusion | bytes 2097156 | tf_op jit(solution)/shard_map/dynamic_slice | solution.py:700
  8.5 2.6 %collective-permute-start.1 = (bf16[128,1024]{1,0:T(8,128)(2,1)S(1)}, bf16[128,1024]{1,0:T(8,128)(2,1)S(1)}, u32[]{:S(2)}, u32[]{:S(2)}) collective-permute-start(bf16[128,1024]{1,0:T(8,128)(2,1)S(1)} %get-tuple-element.122.rest_0_), channel_id=1, source_target_pairs={{0,8},{8,16},{16,24},{24,28},{28,20},{20,12},{12,4},{4,0},{1,9},{9... | collective-permute-start | bytes 786440 | tf_op jit(solution)/shard_map/ppermute | solution.py:531
  12.9 1.1 copy-done.13
  16.5 2.0 %collective-permute-start.4 = (bf16[128,1024]{1,0:T(8,128)(2,1)S(1)}, bf16[128,1024]{1,0:T(8,128)(2,1)S(1)}, u32[]{:S(2)}, u32[]{:S(2)}) collective-permute-start(bf16[128,1024]{1,0:T(8,128)(2,1)S(1)} %get-tuple-element.122.rest_0_), channel_id=1, source_target_pairs={{0,2},{2,0},{1,3},{3,1},{4,6},{6,4},{5,7},{7,5},{8,10},{10,8},{9,1... | collective-permute-start | bytes 786440 | tf_op jit(solution)/shard_map/ppermute | solution.py:534
  18.6 1.0 broadcast_select_fusion.5
  20.4 6.2 %local_part.2 = (bf16[512,4096]{1,0:T(8,128)(2,1)S(1)}, f32[512,1024]{1,0:T(8,128)S(1)}, f32[256,1024]{1,0:T(8,128)S(1)}, f32[128,1024]{1,0:T(8,128)S(1)}) custom-call(s32[1]{0:T(128)} %bitcast.core_ref, bf16[256,4096]{1,0:T(8,128)(2,1)S(1)} %copy-done.3, bf16[256,2048]{1,0:T(8,128)(2,1)} %collective-permute-done.8.far_ref, ...), custom_call_target="tpu_custom_call" | custom-call | flops 9663676416 | tf_op jit(solution)/shard_map/local_part/pallas_call | solution.py:191
  27.1 3.5 %collective-permute-done.3 = bf16[128,1024]{1,0:T(8,128)(2,1)S(1)} collective-permute-done((bf16[128,1024]{1,0:T(8,128)(2,1)S(1)}, bf16[128,1024]{1,0:T(8,128)(2,1)S(1)}, u32[]{:S(2)}, u32[]{:S(2)}) %collective-permute-start.3) | collective-permute-done | bytes 262176 | tf_op jit(solution)/shard_map/ppermute | solution.py:534
  30.7 3.7 %collective-permute-start.15 = (bf16[128,1024]{1,0:T(8,128)(2,1)S(1)}, bf16[128,1024]{1,0:T(8,128)(2,1)S(1)}, u32[]{:S(2)}, u32[]{:S(2)}) collective-permute-start(bf16[128,1024]{1,0:T(8,128)(2,1)S(1)} %convert_element_type.15), channel_id=1, source_target_pairs={{0,2},{1,3},{4,6},{5,7},{8,10},{9,11},{12,14},{13,15},{16,18},{17,... | collective-permute-start | bytes 786440 | tf_op jit(solution)/shard_map/ppermute | solution.py:750
  34.4 1.6 collective-permute-start.11
  36.7 1.6 collective-permute-start.10
  38.2 1.0 collective-permute-done.15.incoming_ref
  39.2 1.6 collective-permute-start.9
  40.8 1.2 collective-permute-done.11.rest_1_
  42.0 1.3 collective-permute-start.13
  43.3 1.9 %collective-permute-done.12.rest_3_ = bf16[128,1024]{1,0:T(8,128)(2,1)S(1)} collective-permute-done((bf16[128,1024]{1,0:T(8,128)(2,1)S(1)}, bf16[128,1024]{1,0:T(8,128)(2,1)S(1)}, u32[]{:S(2)}, u32[]{:S(2)}) %collective-permute-start.12) | collective-permute-done | bytes 262176 | tf_op jit(solution)/shard_map/ppermute | solution.py:531
  45.3 6.2 %local_part.3 = (bf16[512,4096]{1,0:T(8,128)(2,1)S(1)}, f32[512,1024]{1,0:T(8,128)S(1)}, f32[256,1024]{1,0:T(8,128)S(1)}, f32[128,1024]{1,0:T(8,128)S(1)}) custom-call(s32[1]{0:T(128)} %bitcast.core_ref, bf16[256,4096]{1,0:T(8,128)(2,1)S(1)} %copy-done.3, bf16[256,2048]{1,0:T(8,128)(2,1)} %collective-permute-done.8.far_ref, ...), custom_call_target="tpu_custom_call" | custom-call | flops 9663676416 | tf_op jit(solution)/shard_map/local_part/pallas_call | solution.py:191
  51.5 1.9 %collective-permute-done.14.rest_5_ = bf16[128,1024]{1,0:T(8,128)(2,1)S(1)} collective-permute-done((bf16[128,1024]{1,0:T(8,128)(2,1)S(1)}, bf16[128,1024]{1,0:T(8,128)(2,1)S(1)}, u32[]{:S(2)}, u32[]{:S(2)}) %collective-permute-start.14) | collective-permute-done | bytes 262176 | tf_op jit(solution)/shard_map/ppermute | solution.py:534
  54.1 1.6 collective-permute-start.23
  55.7 1.1 collective-permute-start.25
  56.8 2.8 %collective-permute-start.27 = (bf16[128,1024]{1,0:T(8,128)(2,1)S(1)}, bf16[128,1024]{1,0:T(8,128)(2,1)S(1)}, u32[]{:S(2)}, u32[]{:S(2)}) collective-permute-start(bf16[128,1024]{1,0:T(8,128)(2,1)S(1)} %convert_element_type.17), channel_id=1, source_target_pairs={{0,2},{1,3},{4,6},{5,7},{8,10},{9,11},{12,14},{13,15},{16,18},{17,... | collective-permute-start | bytes 786440 | tf_op jit(solution)/shard_map/ppermute | solution.py:750
  59.7 1.6 collective-permute-start.21
  61.8 2.1 %norm_part.2 = (bf16[512,1024]{1,0:T(8,128)(2,1)S(1)}, f32[512,1024]{1,0:T(8,128)S(1)}, f32[512,64]{1,0:T(8,128)S(1)}, f32[64,1024]{1,0:T(8,128)S(1)}) custom-call(s32[1]{0:T(128)} %bitcast.core_ref, bf16[512,256]{1,0:T(8,128)(2,1)S(1)} %pad_maximum_fusion.3.c_ref, bf16[128,1024]{1,0:T(8,128)(2,1)S(1)} %collective-permute-done.15.incoming_ref, ...), custom_call_target="tpu_custom_call" | custom-call | flops 3758096384 | tf_op jit(solution)/shard_map/norm_part/pallas_call | solution.py:264
  63.8 2.3 %collective-permute-done.27.incoming_ref = bf16[128,1024]{1,0:T(8,128)(2,1)S(1)} collective-permute-done((bf16[128,1024]{1,0:T(8,128)(2,1)S(1)}, bf16[128,1024]{1,0:T(8,128)(2,1)S(1)}, u32[]{:S(2)}, u32[]{:S(2)}) %collective-permute-start.27) | collective-permute-done | bytes 262176 | tf_op jit(solution)/shard_map/ppermute | solution.py:750
  66.1 2.5 %collective-permute-start.26 = (bf16[128,1024]{1,0:T(8,128)(2,1)S(1)}, bf16[128,1024]{1,0:T(8,128)(2,1)S(1)}, u32[]{:S(2)}, u32[]{:S(2)}) collective-permute-start(bf16[128,1024]{1,0:T(8,128)(2,1)S(1)} %collective-permute-done.12.rest_3_), channel_id=1, source_target_pairs={{0,2},{2,0},{1,3},{3,1},{4,6},{6,4},{5,7},{7,5},{8,10},{10,8},{9,1... | collective-permute-start | bytes 786440 | tf_op jit(solution)/shard_map/ppermute | solution.py:534
  68.6 2.1 %norm_part.3 = (bf16[512,1024]{1,0:T(8,128)(2,1)S(1)}, f32[512,1024]{1,0:T(8,128)S(1)}, f32[512,64]{1,0:T(8,128)S(1)}, f32[64,1024]{1,0:T(8,128)S(1)}) custom-call(s32[1]{0:T(128)} %bitcast.core_ref, bf16[512,256]{1,0:T(8,128)(2,1)S(1)} %pad_maximum_fusion.3.c_ref, bf16[128,1024]{1,0:T(8,128)(2,1)S(1)} %collective-permute-done.27.incoming_ref, ...), custom_call_target="tpu_custom_call" | custom-call | flops 3758096384 | tf_op jit(solution)/shard_map/norm_part/pallas_call | solution.py:264
  70.7 6.6 %collective-permute-done.24.rest_2_ = bf16[128,1024]{1,0:T(8,128)(2,1)S(1)} collective-permute-done((bf16[128,1024]{1,0:T(8,128)(2,1)S(1)}, bf16[128,1024]{1,0:T(8,128)(2,1)S(1)}, u32[]{:S(2)}, u32[]{:S(2)}) %collective-permute-start.24) | collective-permute-done | bytes 262176 | tf_op jit(solution)/shard_map/ppermute | solution.py:531
  78.6 1.6 collective-permute-start.28
  80.7 1.5 collective-permute-start.30
  82.2 2.0 %collective-permute-start.33 = (bf16[128,1024]{1,0:T(8,128)(2,1)S(1)}, bf16[128,1024]{1,0:T(8,128)(2,1)S(1)}, u32[]{:S(2)}, u32[]{:S(2)}) collective-permute-start(bf16[128,1024]{1,0:T(8,128)(2,1)S(1)} %collective-permute-done.24.rest_2_), channel_id=1, source_target_pairs={{0,2},{2,0},{1,3},{3,1},{4,6},{6,4},{5,7},{7,5},{8,10},{10,8},{9,1... | collective-permute-start | bytes 786440 | tf_op jit(solution)/shard_map/ppermute | solution.py:534
  84.5 11.3 %collective-permute-done.30.rest_4_ = bf16[64,1024]{1,0:T(8,128)(2,1)S(1)} collective-permute-done((bf16[64,1024]{1,0:T(8,128)(2,1)S(1)}, bf16[64,1024]{1,0:T(8,128)(2,1)S(1)}, u32[]{:S(2)}, u32[]{:S(2)}) %collective-permute-start.30) | collective-permute-done | bytes 131104 | tf_op jit(solution)/shard_map/ppermute | solution.py:531
  95.8 1.0 product_part.5.rest_0_
  97.6 1.0 pack_sums.1
  98.6 4.1 %collective-permute-done.31.rest_5_ = bf16[64,1024]{1,0:T(8,128)(2,1)S(1)} collective-permute-done((bf16[64,1024]{1,0:T(8,128)(2,1)S(1)}, bf16[64,1024]{1,0:T(8,128)(2,1)S(1)}, u32[]{:S(2)}, u32[]{:S(2)}) %collective-permute-start.31) | collective-permute-done | bytes 131104 | tf_op jit(solution)/shard_map/ppermute | solution.py:531
  102.8 1.7 %collective-permute-start.40 = (bf16[8,64,192]{2,1,0:T(8,128)(2,1)S(1)}, bf16[8,64,192]{2,1,0:T(8,128)(2,1)S(1)}, u32[]{:S(2)}, u32[]{:S(2)}) collective-permute-start(bf16[8,64,192]{2,1,0:T(8,128)(2,1)S(1)} %get-tuple-element.192), channel_id=1, source_target_pairs={{0,2},{2,0},{1,3},{3,1},{4,6},{6,4},{5,7},{7,5},{8,10},{10,8},{9,1... | collective-permute-start | bytes 589832 | tf_op jit(solution)/shard_map/ppermute | solution.py:653
  104.5 1.6 collective-permute-start.36
  107.0 1.7 %collective-permute-start.39 = (bf16[64,1024]{1,0:T(8,128)(2,1)S(1)}, bf16[64,1024]{1,0:T(8,128)(2,1)S(1)}, u32[]{:S(2)}, u32[]{:S(2)}) collective-permute-start(bf16[64,1024]{1,0:T(8,128)(2,1)S(1)} %collective-permute-done.31.rest_5_), channel_id=1, source_target_pairs={{0,2},{2,0},{1,3},{3,1},{4,6},{6,4},{5,7},{7,5},{8,10},{10,8},{9,1... | collective-permute-start | bytes 393224 | tf_op jit(solution)/shard_map/ppermute | solution.py:534
  110.2 1.9 %collective-permute-done.40.refs_0_ = bf16[8,64,192]{2,1,0:T(8,128)(2,1)S(1)} collective-permute-done((bf16[8,64,192]{2,1,0:T(8,128)(2,1)S(1)}, bf16[8,64,192]{2,1,0:T(8,128)(2,1)S(1)}, u32[]{:S(2)}, u32[]{:S(2)}) %collective-permute-start.40) | collective-permute-done | bytes 196640 | tf_op jit(solution)/shard_map/ppermute | solution.py:653
  112.7 2.0 %collective-permute-done.38.rest_6_ = bf16[64,1024]{1,0:T(8,128)(2,1)S(1)} collective-permute-done((bf16[64,1024]{1,0:T(8,128)(2,1)S(1)}, bf16[64,1024]{1,0:T(8,128)(2,1)S(1)}, u32[]{:S(2)}, u32[]{:S(2)}) %collective-permute-start.38) | collective-permute-done | bytes 131104 | tf_op jit(solution)/shard_map/ppermute | solution.py:534
  114.7 1.4 collective-permute-done.39.rest_7_
  116.5 1.1 collective-permute-start.46
  117.7 2.6 %collective-permute-start.47 = (bf16[64,192]{1,0:T(8,128)(2,1)S(1)}, bf16[64,192]{1,0:T(8,128)(2,1)S(1)}, u32[]{:S(2)}, u32[]{:S(2)}) collective-permute-start(bf16[64,192]{1,0:T(8,128)(2,1)S(1)} %get-tuple-element.234), channel_id=1, source_target_pairs={{0,12},{4,16},{8,20},{12,24},{16,28},{20,0},{24,4},{28,8},{1,13},{... | collective-permute-start | bytes 73736 | tf_op jit(solution)/shard_map/ppermute | solution.py:665
  120.3 2.6 %collective-permute-start.48 = (bf16[64,192]{1,0:T(8,128)(2,1)S(1)}, bf16[64,192]{1,0:T(8,128)(2,1)S(1)}, u32[]{:S(2)}, u32[]{:S(2)}) collective-permute-start(bf16[64,192]{1,0:T(8,128)(2,1)S(1)} %get-tuple-element.235), channel_id=1, source_target_pairs={{0,16},{4,20},{8,24},{12,28},{16,0},{20,4},{24,8},{28,12},{1,17},{... | collective-permute-start | bytes 73736 | tf_op jit(solution)/shard_map/ppermute | solution.py:665
  123.1 2.1 %collective-permute-start.50 = (bf16[64,192]{1,0:T(8,128)(2,1)S(1)}, bf16[64,192]{1,0:T(8,128)(2,1)S(1)}, u32[]{:S(2)}, u32[]{:S(2)}) collective-permute-start(bf16[64,192]{1,0:T(8,128)(2,1)S(1)} %get-tuple-element.237), channel_id=1, source_target_pairs={{0,24},{4,28},{8,0},{12,4},{16,8},{20,12},{24,16},{28,20},{1,25},{... | collective-permute-start | bytes 73736 | tf_op jit(solution)/shard_map/ppermute | solution.py:665
  125.3 2.8 %collective-permute-start.51 = (bf16[64,192]{1,0:T(8,128)(2,1)S(1)}, bf16[64,192]{1,0:T(8,128)(2,1)S(1)}, u32[]{:S(2)}, u32[]{:S(2)}) collective-permute-start(bf16[64,192]{1,0:T(8,128)(2,1)S(1)} %get-tuple-element.238), channel_id=1, source_target_pairs={{0,28},{4,0},{8,4},{12,8},{16,12},{20,16},{24,20},{28,24},{1,29},{... | collective-permute-start | bytes 73736 | tf_op jit(solution)/shard_map/ppermute | solution.py:665
  128.1 1.6 collective-permute-done.51.refs_6_
  129.9 1.1 collective-permute-done.53
  131.0 1.7 %collective-permute-start.54 = (f32[1,128]{1,0:T(1,128)S(1)}, f32[1,128]{1,0:T(1,128)S(1)}, u32[]{:S(2)}, u32[]{:S(2)}) collective-permute-start(f32[1,128]{1,0:T(1,128)S(1)} %slice_add_fusion), channel_id=1, source_target_pairs={{0,2},{2,0},{1,3},{3,1},{4,6},{6,4},{5,7},{7,5},{8,10},{10,8},{9,1... | collective-permute-start | bytes 1544 | tf_op jit(solution)/shard_map/ppermute | solution.py:680
  132.7 2.2 %grad_part.3 = (f32[512,1024]{1,0:T(8,128)S(1)}, f32[256,1024]{1,0:T(8,128)S(1)}, bf16[128,1024]{1,0:T(8,128)(2,1)S(1)}) custom-call(s32[1]{0:T(128)} %bitcast.core_ref, bf16[256,768]{1,0:T(8,128)(2,1)S(1)} %get-tuple-element.150.near_ref, bf16[256,768]{1,0:T(8,128)(2,1)S(1)} %collective-permute-done.19.far_ref, f32[512,1024]{1,0:T(8,128)S(1)} %product_part.7.earlier_ref, ...), custom_call_target="tpu_custom_call" | custom-call | flops 5637144576 | tf_op jit(solution)/shard_map/grad_part/pallas_call | solution.py:371
  134.9 1.3 collective-permute-start.42
  136.2 1.4 collective-permute-start.55
  137.6 2.2 %grad_part.2 = (f32[512,1024]{1,0:T(8,128)S(1)}, f32[256,1024]{1,0:T(8,128)S(1)}, bf16[128,1024]{1,0:T(8,128)(2,1)S(1)}) custom-call(s32[1]{0:T(128)} %bitcast.core_ref, bf16[256,768]{1,0:T(8,128)(2,1)S(1)} %get-tuple-element.150.near_ref, bf16[256,768]{1,0:T(8,128)(2,1)S(1)} %collective-permute-done.19.far_ref, f32[512,1024]{1,0:T(8,128)S(1)} %product_part.6.earlier_ref, ...), custom_call_target="tpu_custom_call" | custom-call | flops 5637144576 | tf_op jit(solution)/shard_map/grad_part/pallas_call | solution.py:371
  139.8 1.5 collective-permute-start.41
  141.3 1.7 %collective-permute-start.56 = (f32[1,128]{1,0:T(1,128)S(1)}, f32[1,128]{1,0:T(1,128)S(1)}, u32[]{:S(2)}, u32[]{:S(2)}) collective-permute-start(f32[1,128]{1,0:T(1,128)S(1)} %add.360), channel_id=1, source_target_pairs={{0,8},{4,12},{8,0},{12,4},{16,24},{20,28},{24,16},{28,20},{1,9},{5... | collective-permute-start | bytes 1544 | tf_op jit(solution)/shard_map/ppermute | solution.py:680
  143.0 2.1 %back_part.3.base_ref = f32[512,1024]{1,0:T(8,128)S(1)} custom-call(s32[1]{0:T(128)} %bitcast.core_ref, bf16[512,4096]{1,0:T(8,128)(2,1)S(1)} %get-tuple-element.226.scores_ref, f32[512,1024]{1,0:T(8,128)S(1)} %get-tuple-element.227.grad_ref, f32[512,64]{1,0:T(8,128)S(1)} %get-tuple-element.140.step_ref, bf16[48,1024]{1,0:T(8,128)(2,1)S(1)} %copy-done.2, ...), custom_call_target="tpu_custom_call" | custom-call | flops 2147483648 | tf_op jit(solution)/shard_map/back_part/pallas_call | solution.py:415
  145.1 3.2 %collective-permute-start.57 = (f32[1,128]{1,0:T(1,128)S(1)}, f32[1,128]{1,0:T(1,128)S(1)}, u32[]{:S(2)}, u32[]{:S(2)}) collective-permute-start(f32[1,128]{1,0:T(1,128)S(1)} %add.361), channel_id=1, source_target_pairs={{0,16},{4,20},{8,24},{12,28},{16,0},{20,4},{24,8},{28,12},{1,17},{... | collective-permute-start | bytes 1544 | tf_op jit(solution)/shard_map/ppermute | solution.py:680
  148.3 2.0 %back_part.2.base_ref = f32[512,1024]{1,0:T(8,128)S(1)} custom-call(s32[1]{0:T(128)} %bitcast.core_ref, bf16[512,4096]{1,0:T(8,128)(2,1)S(1)} %get-tuple-element.214.scores_ref, f32[512,1024]{1,0:T(8,128)S(1)} %get-tuple-element.215.grad_ref, f32[512,64]{1,0:T(8,128)S(1)} %get-tuple-element.140.step_ref, bf16[48,1024]{1,0:T(8,128)(2,1)S(1)} %copy-done.2, ...), custom_call_target="tpu_custom_call" | custom-call | flops 2147483648 | tf_op jit(solution)/shard_map/back_part/pallas_call | solution.py:415
  151.7 1.3 slice_multiply_fusion
  153.0 1.3 cross_part.2
  154.2 5.4 %collective-permute-start.43 = (bf16[256,1024]{1,0:T(8,128)(2,1)S(1)}, bf16[256,1024]{1,0:T(8,128)(2,1)S(1)}, u32[]{:S(2)}, u32[]{:S(2)}) collective-permute-start(bf16[256,1024]{1,0:T(8,128)(2,1)S(1)} %get-tuple-element.229), channel_id=1, source_target_pairs={{0,1},{1,0},{2,3},{3,2},{4,5},{5,4},{6,7},{7,6},{8,9},{9,8},{10,11... | collective-permute-start | bytes 1572872 | tf_op jit(solution)/shard_map/ppermute | solution.py:712
  159.6 1.3 cross_part.3
  161.0 1.3 slice_multiply_fusion.1
  163.1 1.5 pad_maximum_fusion
  (172 shorter events, 18.3 us)
Async XLA Ops:
  0.6 15.1 %copy-start = (bf16[64,2048]{1,0:T(8,128)(2,1)S(1)}, bf16[64,2048]{1,0:T(8,128)(2,1)}, u32[]{:S(2)}) copy-start(bf16[64,2048]{1,0:T(8,128)(2,1)} %param.25) | copy-start | bytes 786436
  2.4 5.2 %collective-permute-start = (bf16[64,2048]{1,0:T(8,128)(2,1)}, bf16[64,2048]{1,0:T(8,128)(2,1)S(1)}, u32[]{:S(2)}, u32[]{:S(2)}) collective-permute-start(bf16[64,2048]{1,0:T(8,128)(2,1)} %constant_dynamic-slice_fusion.10), channel_id=1, source_target_pairs={{0,1},{1,0},{2,3},{3,2},{4,5},{5,4},{6,7},{7,6},{8,9},{9,8},{10,11... | collective-permute-start | bytes 786440 | tf_op jit(solution)/shard_map/ppermute | solution.py:708
  4.5 9.9 %collective-permute-start.5 = (f32[256,64]{1,0:T(8,128)}, f32[256,64]{1,0:T(8,128)S(1)}, u32[]{:S(2)}, u32[]{:S(2)}) collective-permute-start(f32[256,64]{1,0:T(8,128)} %copy.18), channel_id=1, source_target_pairs={{0,1},{1,0},{2,3},{3,2},{4,5},{5,4},{6,7},{7,6},{8,9},{9,8},{10,11... | collective-permute-start | bytes 196616 | tf_op jit(solution)/shard_map/ppermute | solution.py:712
  6.8 13.5 %collective-permute-start.8 = (bf16[256,2048]{1,0:T(8,128)(2,1)}, bf16[256,2048]{1,0:T(8,128)(2,1)}, u32[]{:S(2)}, u32[]{:S(2)}) collective-permute-start(bf16[256,2048]{1,0:T(8,128)(2,1)} %constant_dynamic-slice_fusion.7), channel_id=1, source_target_pairs={{0,1},{1,0},{2,3},{3,2},{4,5},{5,4},{6,7},{7,6},{8,9},{9,8},{10,11... | collective-permute-start | bytes 3145736 | tf_op jit(solution)/shard_map/ppermute | solution.py:712
  8.5 11.2 %collective-permute-start.1 = (bf16[128,1024]{1,0:T(8,128)(2,1)S(1)}, bf16[128,1024]{1,0:T(8,128)(2,1)S(1)}, u32[]{:S(2)}, u32[]{:S(2)}) collective-permute-start(bf16[128,1024]{1,0:T(8,128)(2,1)S(1)} %get-tuple-element.122.rest_0_), channel_id=1, source_target_pairs={{0,8},{8,16},{16,24},{24,28},{28,20},{20,12},{12,4},{4,0},{1,9},{9... | collective-permute-start | bytes 786440 | tf_op jit(solution)/shard_map/ppermute | solution.py:531
  11.1 8.7 %collective-permute-start.2 = (bf16[128,1024]{1,0:T(8,128)(2,1)S(1)}, bf16[128,1024]{1,0:T(8,128)(2,1)S(1)}, u32[]{:S(2)}, u32[]{:S(2)}) collective-permute-start(bf16[128,1024]{1,0:T(8,128)(2,1)S(1)} %get-tuple-element.122.rest_0_), channel_id=1, source_target_pairs={{8,0},{16,8},{24,16},{28,24},{20,28},{12,20},{4,12},{0,4},{9,1},{1... | collective-permute-start | bytes 786440 | tf_op jit(solution)/shard_map/ppermute | solution.py:531
  11.8 4.7 %collective-permute-start.6 = (bf16[256,256]{1,0:T(8,128)(2,1)}, bf16[256,256]{1,0:T(8,128)(2,1)}, u32[]{:S(2)}, u32[]{:S(2)}) collective-permute-start(bf16[256,256]{1,0:T(8,128)(2,1)} %constant_dynamic-slice_fusion.9), channel_id=1, source_target_pairs={{0,1},{1,0},{2,3},{3,2},{4,5},{5,4},{6,7},{7,6},{8,9},{9,8},{10,11... | collective-permute-start | bytes 393224 | tf_op jit(solution)/shard_map/ppermute | solution.py:708
  14.3 4.2 %collective-permute-start.7 = (bf16[256,256]{1,0:T(8,128)(2,1)S(1)}, bf16[256,256]{1,0:T(8,128)(2,1)S(1)}, u32[]{:S(2)}, u32[]{:S(2)}) collective-permute-start(bf16[256,256]{1,0:T(8,128)(2,1)S(1)} %copy-done.21), channel_id=1, source_target_pairs={{0,1},{1,0},{2,3},{3,2},{4,5},{5,4},{6,7},{7,6},{8,9},{9,8},{10,11... | collective-permute-start | bytes 393224 | tf_op jit(solution)/shard_map/ppermute | solution.py:708
  16.5 10.1 %collective-permute-start.4 = (bf16[128,1024]{1,0:T(8,128)(2,1)S(1)}, bf16[128,1024]{1,0:T(8,128)(2,1)S(1)}, u32[]{:S(2)}, u32[]{:S(2)}) collective-permute-start(bf16[128,1024]{1,0:T(8,128)(2,1)S(1)} %get-tuple-element.122.rest_0_), channel_id=1, source_target_pairs={{0,2},{2,0},{1,3},{3,1},{4,6},{6,4},{5,7},{7,5},{8,10},{10,8},{9,1... | collective-permute-start | bytes 786440 | tf_op jit(solution)/shard_map/ppermute | solution.py:534
  18.5 12.1 %collective-permute-start.3 = (bf16[128,1024]{1,0:T(8,128)(2,1)S(1)}, bf16[128,1024]{1,0:T(8,128)(2,1)S(1)}, u32[]{:S(2)}, u32[]{:S(2)}) collective-permute-start(bf16[128,1024]{1,0:T(8,128)(2,1)S(1)} %copy-done.14), channel_id=1, source_target_pairs={{0,2},{2,0},{1,3},{3,1},{4,6},{6,4},{5,7},{7,5},{8,10},{10,8},{9,1... | collective-permute-start | bytes 786440 | tf_op jit(solution)/shard_map/ppermute | solution.py:534
  19.7 16.3 %collective-permute-start.18 = (bf16[256,512]{1,0:T(8,128)(2,1)S(1)}, bf16[256,512]{1,0:T(8,128)(2,1)S(1)}, u32[]{:S(2)}, u32[]{:S(2)}) collective-permute-start(bf16[256,512]{1,0:T(8,128)(2,1)S(1)} %pad_maximum_fusion.4.near_ref), channel_id=1, source_target_pairs={{0,1},{1,0},{2,3},{3,2},{4,5},{5,4},{6,7},{7,6},{8,9},{9,8},{10,11... | collective-permute-start | bytes 786440 | tf_op jit(solution)/shard_map/ppermute | solution.py:712
  19.8 16.7 %collective-permute-start.17 = (bf16[256,768]{1,0:T(8,128)(2,1)S(1)}, bf16[256,768]{1,0:T(8,128)(2,1)S(1)}, u32[]{:S(2)}, u32[]{:S(2)}) collective-permute-start(bf16[256,768]{1,0:T(8,128)(2,1)S(1)} %get-tuple-element.182.near_ref), channel_id=1, source_target_pairs={{0,1},{1,0},{2,3},{3,2},{4,5},{5,4},{6,7},{7,6},{8,9},{9,8},{10,11... | collective-permute-start | bytes 1179656 | tf_op jit(solution)/shard_map/ppermute | solution.py:712
  20.3 14.1 %collective-permute-start.16 = (bf16[256,64]{1,0:T(8,128)(2,1)S(1)}, bf16[256,64]{1,0:T(8,128)(2,1)S(1)}, u32[]{:S(2)}, u32[]{:S(2)}) collective-permute-start(bf16[256,64]{1,0:T(8,128)(2,1)S(1)} %fusion), channel_id=1, source_target_pairs={{0,1},{1,0},{2,3},{3,2},{4,5},{5,4},{6,7},{7,6},{8,9},{9,8},{10,11... | collective-permute-start | bytes 98312 | tf_op jit(solution)/shard_map/ppermute | solution.py:712
  26.6 10.0 %collective-permute-start.19 = (bf16[256,768]{1,0:T(8,128)(2,1)S(1)}, bf16[256,768]{1,0:T(8,128)(2,1)S(1)}, u32[]{:S(2)}, u32[]{:S(2)}) collective-permute-start(bf16[256,768]{1,0:T(8,128)(2,1)S(1)} %get-tuple-element.150.near_ref), channel_id=1, source_target_pairs={{0,1},{1,0},{2,3},{3,2},{4,5},{5,4},{6,7},{7,6},{8,9},{9,8},{10,11... | collective-permute-start | bytes 1179656 | tf_op jit(solution)/shard_map/ppermute | solution.py:712
  30.7 8.5 %collective-permute-start.15 = (bf16[128,1024]{1,0:T(8,128)(2,1)S(1)}, bf16[128,1024]{1,0:T(8,128)(2,1)S(1)}, u32[]{:S(2)}, u32[]{:S(2)}) collective-permute-start(bf16[128,1024]{1,0:T(8,128)(2,1)S(1)} %convert_element_type.15), channel_id=1, source_target_pairs={{0,2},{1,3},{4,6},{5,7},{8,10},{9,11},{12,14},{13,15},{16,18},{17,... | collective-permute-start | bytes 786440 | tf_op jit(solution)/shard_map/ppermute | solution.py:750
  34.4 7.6 %collective-permute-start.11 = (bf16[128,1024]{1,0:T(8,128)(2,1)S(1)}, bf16[128,1024]{1,0:T(8,128)(2,1)S(1)}, u32[]{:S(2)}, u32[]{:S(2)}) collective-permute-start(bf16[128,1024]{1,0:T(8,128)(2,1)S(1)} %collective-permute-done.1.rest_2_), channel_id=1, source_target_pairs={{0,8},{8,16},{16,24},{24,28},{28,20},{20,12},{12,4},{4,0},{1,9},{9... | collective-permute-start | bytes 786440 | tf_op jit(solution)/shard_map/ppermute | solution.py:531
  36.0 9.2 %collective-permute-start.12 = (bf16[128,1024]{1,0:T(8,128)(2,1)S(1)}, bf16[128,1024]{1,0:T(8,128)(2,1)S(1)}, u32[]{:S(2)}, u32[]{:S(2)}) collective-permute-start(bf16[128,1024]{1,0:T(8,128)(2,1)S(1)} %collective-permute-done.2.rest_4_), channel_id=1, source_target_pairs={{8,0},{16,8},{24,16},{28,24},{20,28},{12,20},{4,12},{0,4},{9,1},{1... | collective-permute-start | bytes 786440 | tf_op jit(solution)/shard_map/ppermute | solution.py:531
  36.5 16.9 %collective-permute-start.20 = (bf16[256,2048]{1,0:T(8,128)(2,1)S(1)}, bf16[256,2048]{1,0:T(8,128)(2,1)S(1)}, u32[]{:S(2)}, u32[]{:S(2)}) collective-permute-start(bf16[256,2048]{1,0:T(8,128)(2,1)S(1)} %constant_dynamic-slice_fusion.2), channel_id=1, source_target_pairs={{0,1},{1,0},{2,3},{3,2},{4,5},{5,4},{6,7},{7,6},{8,9},{9,8},{10,11... | collective-permute-start | bytes 3145736 | tf_op jit(solution)/shard_map/ppermute | solution.py:712
  36.6 25.1 %copy-start.5 = (bf16[64,4096]{1,0:T(8,128)(2,1)S(1)}, bf16[64,4096]{1,0:T(8,128)(2,1)}, u32[]{:S(2)}) copy-start(bf16[64,4096]{1,0:T(8,128)(2,1)} %down_ref.7) | copy-start | bytes 1572868
  36.6 25.1 %copy-start.6 = (f32[4096]{0:T(1024)S(1)}, f32[4096]{0:T(1024)}, u32[]{:S(2)}) copy-start(f32[4096]{0:T(1024)} %param.23) | copy-start | bytes 49156
  36.7 17.4 %collective-permute-start.10 = (bf16[256,1024]{1,0:T(8,128)(2,1)S(1)}, bf16[256,1024]{1,0:T(8,128)(2,1)S(1)}, u32[]{:S(2)}, u32[]{:S(2)}) collective-permute-start(bf16[256,1024]{1,0:T(8,128)(2,1)S(1)} %constant_dynamic-update-slice_fusion.rest_0_), channel_id=1, source_target_pairs={{8,0},{16,8},{24,16},{28,24},{20,28},{12,20},{4,12},{0,4},{9,1},{1... | collective-permute-start | bytes 1572872 | tf_op jit(solution)/shard_map/ppermute | solution.py:531
  39.2 14.8 %collective-permute-start.9 = (bf16[256,1024]{1,0:T(8,128)(2,1)S(1)}, bf16[256,1024]{1,0:T(8,128)(2,1)S(1)}, u32[]{:S(2)}, u32[]{:S(2)}) collective-permute-start(bf16[256,1024]{1,0:T(8,128)(2,1)S(1)} %constant_dynamic-update-slice_fusion.rest_0_), channel_id=1, source_target_pairs={{0,8},{8,16},{16,24},{24,28},{28,20},{20,12},{12,4},{4,0},{1,9},{9... | collective-permute-start | bytes 1572872 | tf_op jit(solution)/shard_map/ppermute | solution.py:531
  42.0 9.5 %collective-permute-start.13 = (bf16[128,1024]{1,0:T(8,128)(2,1)S(1)}, bf16[128,1024]{1,0:T(8,128)(2,1)S(1)}, u32[]{:S(2)}, u32[]{:S(2)}) collective-permute-start(bf16[128,1024]{1,0:T(8,128)(2,1)S(1)} %collective-permute-done.1.rest_2_), channel_id=1, source_target_pairs={{0,2},{2,0},{1,3},{3,1},{4,6},{6,4},{5,7},{7,5},{8,10},{10,8},{9,1... | collective-permute-start | bytes 786440 | tf_op jit(solution)/shard_map/ppermute | solution.py:534
  45.3 8.1 %collective-permute-start.14 = (bf16[128,1024]{1,0:T(8,128)(2,1)S(1)}, bf16[128,1024]{1,0:T(8,128)(2,1)S(1)}, u32[]{:S(2)}, u32[]{:S(2)}) collective-permute-start(bf16[128,1024]{1,0:T(8,128)(2,1)S(1)} %collective-permute-done.2.rest_4_), channel_id=1, source_target_pairs={{0,2},{2,0},{1,3},{3,1},{4,6},{6,4},{5,7},{7,5},{8,10},{10,8},{9,1... | collective-permute-start | bytes 786440 | tf_op jit(solution)/shard_map/ppermute | solution.py:534
  54.1 12.0 %collective-permute-start.23 = (bf16[128,1024]{1,0:T(8,128)(2,1)S(1)}, bf16[128,1024]{1,0:T(8,128)(2,1)S(1)}, u32[]{:S(2)}, u32[]{:S(2)}) collective-permute-start(bf16[128,1024]{1,0:T(8,128)(2,1)S(1)} %collective-permute-done.11.rest_1_), channel_id=1, source_target_pairs={{0,8},{8,16},{16,24},{24,28},{28,20},{20,12},{12,4},{4,0},{1,9},{9... | collective-permute-start | bytes 786440 | tf_op jit(solution)/shard_map/ppermute | solution.py:531
  55.7 21.7 %collective-permute-start.25 = (bf16[128,1024]{1,0:T(8,128)(2,1)S(1)}, bf16[128,1024]{1,0:T(8,128)(2,1)S(1)}, u32[]{:S(2)}, u32[]{:S(2)}) collective-permute-start(bf16[128,1024]{1,0:T(8,128)(2,1)S(1)} %collective-permute-done.11.rest_1_), channel_id=1, source_target_pairs={{0,2},{2,0},{1,3},{3,1},{4,6},{6,4},{5,7},{7,5},{8,10},{10,8},{9,1... | collective-permute-start | bytes 786440 | tf_op jit(solution)/shard_map/ppermute | solution.py:534
  56.8 9.3 %collective-permute-start.27 = (bf16[128,1024]{1,0:T(8,128)(2,1)S(1)}, bf16[128,1024]{1,0:T(8,128)(2,1)S(1)}, u32[]{:S(2)}, u32[]{:S(2)}) collective-permute-start(bf16[128,1024]{1,0:T(8,128)(2,1)S(1)} %convert_element_type.17), channel_id=1, source_target_pairs={{0,2},{1,3},{4,6},{5,7},{8,10},{9,11},{12,14},{13,15},{16,18},{17,... | collective-permute-start | bytes 786440 | tf_op jit(solution)/shard_map/ppermute | solution.py:750
  59.7 17.7 %collective-permute-start.21 = (bf16[256,1024]{1,0:T(8,128)(2,1)S(1)}, bf16[256,1024]{1,0:T(8,128)(2,1)S(1)}, u32[]{:S(2)}, u32[]{:S(2)}) collective-permute-start(bf16[256,1024]{1,0:T(8,128)(2,1)S(1)} %collective-permute-done.9.rest_1_), channel_id=1, source_target_pairs={{0,8},{8,16},{16,24},{24,28},{28,20},{20,12},{12,4},{4,0},{1,9},{9... | collective-permute-start | bytes 1572872 | tf_op jit(solution)/shard_map/ppermute | solution.py:531
  61.3 16.0 %collective-permute-start.22 = (bf16[256,1024]{1,0:T(8,128)(2,1)S(1)}, bf16[256,1024]{1,0:T(8,128)(2,1)S(1)}, u32[]{:S(2)}, u32[]{:S(2)}) collective-permute-start(bf16[256,1024]{1,0:T(8,128)(2,1)S(1)} %collective-permute-done.10.rest_2_), channel_id=1, source_target_pairs={{8,0},{16,8},{24,16},{28,24},{20,28},{12,20},{4,12},{0,4},{9,1},{1... | collective-permute-start | bytes 1572872 | tf_op jit(solution)/shard_map/ppermute | solution.py:531
  66.1 11.2 %collective-permute-start.24 = (bf16[128,1024]{1,0:T(8,128)(2,1)S(1)}, bf16[128,1024]{1,0:T(8,128)(2,1)S(1)}, u32[]{:S(2)}, u32[]{:S(2)}) collective-permute-start(bf16[128,1024]{1,0:T(8,128)(2,1)S(1)} %collective-permute-done.12.rest_3_), channel_id=1, source_target_pairs={{8,0},{16,8},{24,16},{28,24},{20,28},{12,20},{4,12},{0,4},{9,1},{1... | collective-permute-start | bytes 786440 | tf_op jit(solution)/shard_map/ppermute | solution.py:531
  66.1 11.2 %collective-permute-start.26 = (bf16[128,1024]{1,0:T(8,128)(2,1)S(1)}, bf16[128,1024]{1,0:T(8,128)(2,1)S(1)}, u32[]{:S(2)}, u32[]{:S(2)}) collective-permute-start(bf16[128,1024]{1,0:T(8,128)(2,1)S(1)} %collective-permute-done.12.rest_3_), channel_id=1, source_target_pairs={{0,2},{2,0},{1,3},{3,1},{4,6},{6,4},{5,7},{7,5},{8,10},{10,8},{9,1... | collective-permute-start | bytes 786440 | tf_op jit(solution)/shard_map/ppermute | solution.py:534
  70.7 7.8 %copy-start.9 = (f32[512,1024]{1,0:T(8,128)}, f32[512,1024]{1,0:T(8,128)S(1)}, u32[]{:S(2)}) copy-start(f32[512,1024]{1,0:T(8,128)S(1)} %get-tuple-element.219.slope_ref) | copy-start | bytes 6291460
  77.4 4.8 %collective-permute-start.34 = (f32[256,64]{1,0:T(8,128)S(1)}, f32[256,64]{1,0:T(8,128)S(1)}, u32[]{:S(2)}, u32[]{:S(2)}) collective-permute-start(f32[256,64]{1,0:T(8,128)S(1)} %constant_dynamic-slice_fusion.1), channel_id=1, source_target_pairs={{0,1},{1,0},{2,3},{3,2},{4,5},{5,4},{6,7},{7,6},{8,9},{9,8},{10,11... | collective-permute-start | bytes 196616 | tf_op jit(solution)/shard_map/ppermute | solution.py:712
  78.5 24.2 %collective-permute-start.32 = (bf16[128,1024]{1,0:T(8,128)(2,1)S(1)}, bf16[128,1024]{1,0:T(8,128)(2,1)S(1)}, u32[]{:S(2)}, u32[]{:S(2)}) collective-permute-start(bf16[128,1024]{1,0:T(8,128)(2,1)S(1)} %collective-permute-done.23.rest_0_), channel_id=1, source_target_pairs={{0,2},{2,0},{1,3},{3,1},{4,6},{6,4},{5,7},{7,5},{8,10},{10,8},{9,1... | collective-permute-start | bytes 786440 | tf_op jit(solution)/shard_map/ppermute | solution.py:534
  78.6 24.2 %collective-permute-start.28 = (bf16[256,1024]{1,0:T(8,128)(2,1)S(1)}, bf16[256,1024]{1,0:T(8,128)(2,1)S(1)}, u32[]{:S(2)}, u32[]{:S(2)}) collective-permute-start(bf16[256,1024]{1,0:T(8,128)(2,1)S(1)} %collective-permute-done.21.rest_1_), channel_id=1, source_target_pairs={{0,8},{8,16},{16,24},{24,28},{28,20},{20,12},{12,4},{4,0},{1,9},{9... | collective-permute-start | bytes 1572872 | tf_op jit(solution)/shard_map/ppermute | solution.py:531
  80.2 22.6 %collective-permute-start.29 = (bf16[256,1024]{1,0:T(8,128)(2,1)S(1)}, bf16[256,1024]{1,0:T(8,128)(2,1)S(1)}, u32[]{:S(2)}, u32[]{:S(2)}) collective-permute-start(bf16[256,1024]{1,0:T(8,128)(2,1)S(1)} %collective-permute-done.22.rest_2_), channel_id=1, source_target_pairs={{8,0},{16,8},{24,16},{28,24},{20,28},{12,20},{4,12},{0,4},{9,1},{1... | collective-permute-start | bytes 1572872 | tf_op jit(solution)/shard_map/ppermute | solution.py:531
  80.7 15.1 %collective-permute-start.30 = (bf16[64,1024]{1,0:T(8,128)(2,1)S(1)}, bf16[64,1024]{1,0:T(8,128)(2,1)S(1)}, u32[]{:S(2)}, u32[]{:S(2)}) collective-permute-start(bf16[64,1024]{1,0:T(8,128)(2,1)S(1)} %slice.38), channel_id=1, source_target_pairs={{0,8},{8,16},{16,24},{24,28},{28,20},{20,12},{12,4},{4,0},{1,9},{9... | collective-permute-start | bytes 393224 | tf_op jit(solution)/shard_map/ppermute | solution.py:531
  82.2 20.6 %collective-permute-start.33 = (bf16[128,1024]{1,0:T(8,128)(2,1)S(1)}, bf16[128,1024]{1,0:T(8,128)(2,1)S(1)}, u32[]{:S(2)}, u32[]{:S(2)}) collective-permute-start(bf16[128,1024]{1,0:T(8,128)(2,1)S(1)} %collective-permute-done.24.rest_2_), channel_id=1, source_target_pairs={{0,2},{2,0},{1,3},{3,1},{4,6},{6,4},{5,7},{7,5},{8,10},{10,8},{9,1... | collective-permute-start | bytes 786440 | tf_op jit(solution)/shard_map/ppermute | solution.py:534
  95.8 1.3 collective-permute-start.35
  97.1 5.6 %collective-permute-start.31 = (bf16[64,1024]{1,0:T(8,128)(2,1)S(1)}, bf16[64,1024]{1,0:T(8,128)(2,1)S(1)}, u32[]{:S(2)}, u32[]{:S(2)}) collective-permute-start(bf16[64,1024]{1,0:T(8,128)(2,1)S(1)} %slice.39), channel_id=1, source_target_pairs={{8,0},{16,8},{24,16},{28,24},{20,28},{12,20},{4,12},{0,4},{9,1},{1... | collective-permute-start | bytes 393224 | tf_op jit(solution)/shard_map/ppermute | solution.py:531
  102.8 9.3 %collective-permute-start.40 = (bf16[8,64,192]{2,1,0:T(8,128)(2,1)S(1)}, bf16[8,64,192]{2,1,0:T(8,128)(2,1)S(1)}, u32[]{:S(2)}, u32[]{:S(2)}) collective-permute-start(bf16[8,64,192]{2,1,0:T(8,128)(2,1)S(1)} %get-tuple-element.192), channel_id=1, source_target_pairs={{0,2},{2,0},{1,3},{3,1},{4,6},{6,4},{5,7},{7,5},{8,10},{10,8},{9,1... | collective-permute-start | bytes 589832 | tf_op jit(solution)/shard_map/ppermute | solution.py:653
  104.5 11.5 %collective-permute-start.36 = (bf16[128,1024]{1,0:T(8,128)(2,1)S(1)}, bf16[128,1024]{1,0:T(8,128)(2,1)S(1)}, u32[]{:S(2)}, u32[]{:S(2)}) collective-permute-start(bf16[128,1024]{1,0:T(8,128)(2,1)S(1)} %slice.40), channel_id=1, source_target_pairs={{0,8},{8,16},{16,24},{24,28},{28,20},{20,12},{12,4},{4,0},{1,9},{9... | collective-permute-start | bytes 786440 | tf_op jit(solution)/shard_map/ppermute | solution.py:531
  106.1 9.9 %collective-permute-start.37 = (bf16[128,1024]{1,0:T(8,128)(2,1)S(1)}, bf16[128,1024]{1,0:T(8,128)(2,1)S(1)}, u32[]{:S(2)}, u32[]{:S(2)}) collective-permute-start(bf16[128,1024]{1,0:T(8,128)(2,1)S(1)} %slice.41), channel_id=1, source_target_pairs={{8,0},{16,8},{24,16},{28,24},{20,28},{12,20},{4,12},{0,4},{9,1},{1... | collective-permute-start | bytes 786440 | tf_op jit(solution)/shard_map/ppermute | solution.py:531
  106.7 8.0 %collective-permute-start.38 = (bf16[64,1024]{1,0:T(8,128)(2,1)S(1)}, bf16[64,1024]{1,0:T(8,128)(2,1)S(1)}, u32[]{:S(2)}, u32[]{:S(2)}) collective-permute-start(bf16[64,1024]{1,0:T(8,128)(2,1)S(1)} %collective-permute-done.30.rest_4_), channel_id=1, source_target_pairs={{0,2},{2,0},{1,3},{3,1},{4,6},{6,4},{5,7},{7,5},{8,10},{10,8},{9,1... | collective-permute-start | bytes 393224 | tf_op jit(solution)/shard_map/ppermute | solution.py:534
  107.0 9.0 %collective-permute-start.39 = (bf16[64,1024]{1,0:T(8,128)(2,1)S(1)}, bf16[64,1024]{1,0:T(8,128)(2,1)S(1)}, u32[]{:S(2)}, u32[]{:S(2)}) collective-permute-start(bf16[64,1024]{1,0:T(8,128)(2,1)S(1)} %collective-permute-done.31.rest_5_), channel_id=1, source_target_pairs={{0,2},{2,0},{1,3},{3,1},{4,6},{6,4},{5,7},{7,5},{8,10},{10,8},{9,1... | collective-permute-start | bytes 393224 | tf_op jit(solution)/shard_map/ppermute | solution.py:534
  112.7 20.0 %copy-start.10 = (f32[512,1024]{1,0:T(8,128)S(1)}, f32[512,1024]{1,0:T(8,128)}, u32[]{:S(2)}) copy-start(f32[512,1024]{1,0:T(8,128)} %copy-done.9) | copy-start | bytes 6291460
  112.7 20.0 %copy-start.12 = (bf16[512,1024]{1,0:T(8,128)(2,1)S(1)}, bf16[512,1024]{1,0:T(8,128)(2,1)}, u32[]{:S(2)}) copy-start(bf16[512,1024]{1,0:T(8,128)(2,1)} %copy-done.11) | copy-start | bytes 3145732
  116.1 7.0 %collective-permute-start.45 = (bf16[64,192]{1,0:T(8,128)(2,1)S(1)}, bf16[64,192]{1,0:T(8,128)(2,1)S(1)}, u32[]{:S(2)}, u32[]{:S(2)}) collective-permute-start(bf16[64,192]{1,0:T(8,128)(2,1)S(1)} %get-tuple-element.232), channel_id=1, source_target_pairs={{0,4},{4,8},{8,12},{12,16},{16,20},{20,24},{24,28},{28,0},{1,5},{5... | collective-permute-start | bytes 73736 | tf_op jit(solution)/shard_map/ppermute | solution.py:665
  116.5 8.7 %collective-permute-start.46 = (bf16[64,192]{1,0:T(8,128)(2,1)S(1)}, bf16[64,192]{1,0:T(8,128)(2,1)S(1)}, u32[]{:S(2)}, u32[]{:S(2)}) collective-permute-start(bf16[64,192]{1,0:T(8,128)(2,1)S(1)} %get-tuple-element.233), channel_id=1, source_target_pairs={{0,8},{4,12},{8,16},{12,20},{16,24},{20,28},{24,0},{28,4},{1,9},{5... | collective-permute-start | bytes 73736 | tf_op jit(solution)/shard_map/ppermute | solution.py:665
  117.7 10.4 %collective-permute-start.47 = (bf16[64,192]{1,0:T(8,128)(2,1)S(1)}, bf16[64,192]{1,0:T(8,128)(2,1)S(1)}, u32[]{:S(2)}, u32[]{:S(2)}) collective-permute-start(bf16[64,192]{1,0:T(8,128)(2,1)S(1)} %get-tuple-element.234), channel_id=1, source_target_pairs={{0,12},{4,16},{8,20},{12,24},{16,28},{20,0},{24,4},{28,8},{1,13},{... | collective-permute-start | bytes 73736 | tf_op jit(solution)/shard_map/ppermute | solution.py:665
  120.3 7.7 %collective-permute-start.48 = (bf16[64,192]{1,0:T(8,128)(2,1)S(1)}, bf16[64,192]{1,0:T(8,128)(2,1)S(1)}, u32[]{:S(2)}, u32[]{:S(2)}) collective-permute-start(bf16[64,192]{1,0:T(8,128)(2,1)S(1)} %get-tuple-element.235), channel_id=1, source_target_pairs={{0,16},{4,20},{8,24},{12,28},{16,0},{20,4},{24,8},{28,12},{1,17},{... | collective-permute-start | bytes 73736 | tf_op jit(solution)/shard_map/ppermute | solution.py:665
  122.9 5.2 %collective-permute-start.49 = (bf16[64,192]{1,0:T(8,128)(2,1)S(1)}, bf16[64,192]{1,0:T(8,128)(2,1)S(1)}, u32[]{:S(2)}, u32[]{:S(2)}) collective-permute-start(bf16[64,192]{1,0:T(8,128)(2,1)S(1)} %get-tuple-element.236), channel_id=1, source_target_pairs={{0,20},{4,24},{8,28},{12,0},{16,4},{20,8},{24,12},{28,16},{1,21},{... | collective-permute-start | bytes 73736 | tf_op jit(solution)/shard_map/ppermute | solution.py:665
  123.1 4.9 %collective-permute-start.50 = (bf16[64,192]{1,0:T(8,128)(2,1)S(1)}, bf16[64,192]{1,0:T(8,128)(2,1)S(1)}, u32[]{:S(2)}, u32[]{:S(2)}) collective-permute-start(bf16[64,192]{1,0:T(8,128)(2,1)S(1)} %get-tuple-element.237), channel_id=1, source_target_pairs={{0,24},{4,28},{8,0},{12,4},{16,8},{20,12},{24,16},{28,20},{1,25},{... | collective-permute-start | bytes 73736 | tf_op jit(solution)/shard_map/ppermute | solution.py:665
  125.3 4.4 %collective-permute-start.51 = (bf16[64,192]{1,0:T(8,128)(2,1)S(1)}, bf16[64,192]{1,0:T(8,128)(2,1)S(1)}, u32[]{:S(2)}, u32[]{:S(2)}) collective-permute-start(bf16[64,192]{1,0:T(8,128)(2,1)S(1)} %get-tuple-element.238), channel_id=1, source_target_pairs={{0,28},{4,0},{8,4},{12,8},{16,12},{20,16},{24,20},{28,24},{1,29},{... | collective-permute-start | bytes 73736 | tf_op jit(solution)/shard_map/ppermute | solution.py:665
  129.8 1.2 collective-permute-start.53
  131.0 5.2 %collective-permute-start.54 = (f32[1,128]{1,0:T(1,128)S(1)}, f32[1,128]{1,0:T(1,128)S(1)}, u32[]{:S(2)}, u32[]{:S(2)}) collective-permute-start(f32[1,128]{1,0:T(1,128)S(1)} %slice_add_fusion), channel_id=1, source_target_pairs={{0,2},{2,0},{1,3},{3,1},{4,6},{6,4},{5,7},{7,5},{8,10},{10,8},{9,1... | collective-permute-start | bytes 1544 | tf_op jit(solution)/shard_map/ppermute | solution.py:680
  134.9 24.7 %collective-permute-start.42 = (bf16[128,1024]{1,0:T(8,128)(2,1)S(1)}, bf16[128,1024]{1,0:T(8,128)(2,1)S(1)}, u32[]{:S(2)}, u32[]{:S(2)}) collective-permute-start(bf16[128,1024]{1,0:T(8,128)(2,1)S(1)} %get-tuple-element.224), channel_id=1, source_target_pairs={{2,0},{3,1},{6,4},{7,5},{10,8},{11,9},{14,12},{15,13},{18,16},{19,... | collective-permute-start | bytes 786440 | tf_op jit(solution)/shard_map/ppermute | solution.py:750
  136.2 5.1 %collective-permute-start.55 = (f32[1,128]{1,0:T(1,128)S(1)}, f32[1,128]{1,0:T(1,128)S(1)}, u32[]{:S(2)}, u32[]{:S(2)}) collective-permute-start(f32[1,128]{1,0:T(1,128)S(1)} %add.359), channel_id=1, source_target_pairs={{0,4},{4,0},{8,12},{12,8},{16,20},{20,16},{24,28},{28,24},{1,5},{5... | collective-permute-start | bytes 1544 | tf_op jit(solution)/shard_map/ppermute | solution.py:680
  139.8 13.2 %collective-permute-start.41 = (bf16[128,1024]{1,0:T(8,128)(2,1)S(1)}, bf16[128,1024]{1,0:T(8,128)(2,1)S(1)}, u32[]{:S(2)}, u32[]{:S(2)}) collective-permute-start(bf16[128,1024]{1,0:T(8,128)(2,1)S(1)} %get-tuple-element.212), channel_id=1, source_target_pairs={{2,0},{3,1},{6,4},{7,5},{10,8},{11,9},{14,12},{15,13},{18,16},{19,... | collective-permute-start | bytes 786440 | tf_op jit(solution)/shard_map/ppermute | solution.py:750
  141.3 3.8 %collective-permute-start.56 = (f32[1,128]{1,0:T(1,128)S(1)}, f32[1,128]{1,0:T(1,128)S(1)}, u32[]{:S(2)}, u32[]{:S(2)}) collective-permute-start(f32[1,128]{1,0:T(1,128)S(1)} %add.360), channel_id=1, source_target_pairs={{0,8},{4,12},{8,0},{12,4},{16,24},{20,28},{24,16},{28,20},{1,9},{5... | collective-permute-start | bytes 1544 | tf_op jit(solution)/shard_map/ppermute | solution.py:680
  145.1 5.9 %collective-permute-start.57 = (f32[1,128]{1,0:T(1,128)S(1)}, f32[1,128]{1,0:T(1,128)S(1)}, u32[]{:S(2)}, u32[]{:S(2)}) collective-permute-start(f32[1,128]{1,0:T(1,128)S(1)} %add.361), channel_id=1, source_target_pairs={{0,16},{4,20},{8,24},{12,28},{16,0},{20,4},{24,8},{28,12},{1,17},{... | collective-permute-start | bytes 1544 | tf_op jit(solution)/shard_map/ppermute | solution.py:680
  150.4 1.3 collective-permute-start.52
  154.2 8.1 %collective-permute-start.43 = (bf16[256,1024]{1,0:T(8,128)(2,1)S(1)}, bf16[256,1024]{1,0:T(8,128)(2,1)S(1)}, u32[]{:S(2)}, u32[]{:S(2)}) collective-permute-start(bf16[256,1024]{1,0:T(8,128)(2,1)S(1)} %get-tuple-element.229), channel_id=1, source_target_pairs={{0,1},{1,0},{2,3},{3,2},{4,5},{5,4},{6,7},{7,6},{8,9},{9,8},{10,11... | collective-permute-start | bytes 1572872 | tf_op jit(solution)/shard_map/ppermute | solution.py:712
  160.9 2.0 %collective-permute-start.44 = (bf16[256,1024]{1,0:T(8,128)(2,1)S(1)}, bf16[256,1024]{1,0:T(8,128)(2,1)S(1)}, u32[]{:S(2)}, u32[]{:S(2)}) collective-permute-start(bf16[256,1024]{1,0:T(8,128)(2,1)S(1)} %get-tuple-element.230), channel_id=1, source_target_pairs={{0,1},{1,0},{2,3},{3,2},{4,5},{5,4},{6,7},{7,6},{8,9},{9,8},{10,11... | collective-permute-start | bytes 1572872 | tf_op jit(solution)/shard_map/ppermute | solution.py:712
  (18 other events, 77.2 us)

commit v3 on v2

--- a/solution.py
+++ b/solution.py
@@ -16,7 +16,7 @@
 EPS_NORM = 1e-05
 CLIP_EPSILON = 1e-06
 ADAPTER_SCALE = 2.0
-VMEM_BYTES = 24 * 1024 * 1024
+VMEM_BYTES = 18 * 1024 * 1024
 
 F32 = jnp.float32
 BF16 = jnp.bfloat16
@@ -158,7 +158,9 @@
             parts.append(part)
         lanes = slice(pair * 2 * P_SIZE, (pair + 1) * 2 * P_SIZE)
         intra = dot(jnp.concatenate(parts, axis=0), pair_rows(xdt[:, lanes]), ((0,), (0,)))
-        ssd_ref[:, lanes] = intra + skip_ref[:, lanes] * x_ref[:, lanes].astype(F32)
+        ssd_ref[:, lanes] = (
+            intra + skip_ref[:, lanes] * x_ref[:, lanes].astype(F32)
+        ).astype(ssd_ref.dtype)
 
 
 def local_part(group, groups, heads, core, near, far, b, c, step, cum, cum_t, skip, pattern):
@@ -192,8 +194,8 @@
         functools.partial(local_kernel, group * heads, heads),
         grid_spec=spec,
         out_shape=[
-            jax.ShapeDtypeStruct((rows, heads * Q), BF16),
-            jax.ShapeDtypeStruct((rows, width), F32),
+            pltpu.HBM((rows, heads * Q), BF16),
+            jax.ShapeDtypeStruct((rows, width), BF16),
             jax.ShapeDtypeStruct((blocks * N, width), F32),
             jax.ShapeDtypeStruct((N, width), F32),
         ],
@@ -214,7 +216,7 @@
         rows = slice(block * Q, (block + 1) * Q)
         inter = dot(c_ref[rows, :], run.astype(BF16))
         growth = spread(jnp.exp(of_core(cum_ref, rows, core_ref[0], first, heads)), pattern_ref[...])
-        ssd = ssd_ref[rows, :] + growth * inter
+        ssd = ssd_ref[rows, :].astype(F32) + growth * inter
         local = slice(block % (blocks // 2) * Q, (block % (blocks // 2) + 1) * Q)
         z = jnp.where(
             core_ref[0] == block // (blocks // 2), near_ref[local, :], far_ref[local, :]
@@ -225,7 +227,7 @@
         hat = gated * rstd
         normed = (hat * gain).astype(BF16)
         hat_ref[rows, :] = hat.astype(hat_ref.dtype)
-        slope_ref[rows, :] = rstd * silu
+        slope_ref[rows, :] = (rstd * silu).astype(slope_ref.dtype)
         product_ref[rows, :] = dot(normed, down_ref[...], ((1,), (1,)))
         part = dot(up_ref[rows, :], normed, ((0,), (0,)))
         total = part if total is None else total + part
@@ -246,7 +248,7 @@
         grid=(1,),
         in_specs=[
             pl.BlockSpec((rows, N), lambda i, s: (0, group)),
-            whole(incoming.shape),
+            pl.BlockSpec((N, width), lambda i, s: (group, 0)),
             whole(state.shape),
             whole(cum.shape),
             whole(pattern.shape),
@@ -266,7 +268,7 @@
         grid_spec=spec,
         out_shape=[
             jax.ShapeDtypeStruct((rows, width), BF16),
-            jax.ShapeDtypeStruct((rows, width), F32),
+            jax.ShapeDtypeStruct((rows, width), BF16),
             jax.ShapeDtypeStruct((rows, rank), F32),
             jax.ShapeDtypeStruct((rank, width), F32),
         ],
@@ -276,62 +278,67 @@
     )(core, c, incoming, state, cum, pattern, ssd, near, far, gain, down, up_twice)
 
 
-def product_kernel(count, started, core_ref, near_ref, far_ref, *rest):
-    pieces, out_ref = rest[started : started + count], rest[-1]
-    weights = joined(pieces)
+def product_kernel(first, spans, started, core_ref, near_ref, far_ref, *rest):
+    pieces, out_ref = rest[started:-1], rest[-1]
+    weights = joined(pieces, spans)
+    depth = slice(first, first + weights.shape[0])
     half = near_ref.shape[0]
     for part in range(2):
         rows = slice(part * half, (part + 1) * half)
-        cot = jnp.where(core_ref[0] == part, near_ref[...], far_ref[...])
+        cot = jnp.where(core_ref[0] == part, near_ref[:, depth], far_ref[:, depth])
         product = dot(cot, weights)
         out_ref[rows, :] = product + rest[0][rows, :] if started else product
 
 
-def joined(pieces):
-    return jnp.concatenate([piece[...] for piece in pieces], axis=0)
-
-
-def product_part(core, near, far, earlier, pieces, width):
+def joined(pieces, spans):
+    return jnp.concatenate(
+        [piece[start : start + rows, :] for piece, (start, rows) in zip(pieces, spans)], axis=0
+    )
+
+
+def product_part(core, near, far, cut, first, earlier, pieces, width):
     rows = 2 * near.shape[0]
     held = [] if earlier is None else [earlier]
+    columns = pl.BlockSpec((near.shape[0], cut), lambda i, s: (0, near.shape[1] // cut - 1))
     spec = pltpu.PrefetchScalarGridSpec(
         num_scalar_prefetch=1,
         grid=(1,),
-        in_specs=[whole(near.shape), whole(far.shape)]
+        in_specs=[columns, columns]
         + [whole(array.shape) for array in held]
-        + [whole(piece.shape) for piece in pieces],
+        + [whole(piece[0].shape) for piece in pieces],
         out_specs=whole((rows, width)),
     )
     return pl.pallas_call(
-        functools.partial(product_kernel, len(pieces), len(held)),
+        functools.partial(product_kernel, first, tuple(piece[1:] for piece in pieces), len(held)),
         grid_spec=spec,
         out_shape=jax.ShapeDtypeStruct((rows, width), F32),
         compiler_params=params("arbitrary"),
-        cost_estimate=cost(2 * rows * width * near.shape[1], 3),
+        cost_estimate=cost(2 * rows * width * Q, 4),
         name="product_part",
-    )(core, near, far, *held, *pieces)
+    )(core, near, far, *held, *[piece[0] for piece in pieces])
 
 
 def grad_kernel(
-    blocks, first, heads, core_ref, near_ref, far_ref, earlier_ref, up_ref, down_ref, gain_ref, hat_ref,
+    blocks, first, heads, start, spans, core_ref, near_ref, far_ref, earlier_ref, up_ref, down_ref, gain_ref, hat_ref,
     slope_ref, cum_ref, pattern_ref, c_ref, *rest,
 ):
     pieces, (grad_ref, block_grad_ref, total_ref) = rest[:-3], rest[-3:]
-    weights = joined(pieces)
+    weights = joined(pieces, spans)
+    depth = slice(start, start + weights.shape[0])
     gain = gain_ref[...]
     later = None
     for block in reversed(range(blocks)):
         rows = slice(block * Q, (block + 1) * Q)
         local = slice(block % (blocks // 2) * Q, (block % (blocks // 2) + 1) * Q)
         cot = jnp.where(
-            core_ref[0] == block // (blocks // 2), near_ref[local, :], far_ref[local, :]
+            core_ref[0] == block // (blocks // 2), near_ref[local, depth], far_ref[local, depth]
         )
         product = dot(cot, weights) + dot(up_ref[rows, :], down_ref[...]) + earlier_ref[rows, :]
         weighted = product * gain
         hat = hat_ref[rows, :].astype(F32)
         mean = jnp.mean(hat * weighted, axis=1, keepdims=True)
-        grad = slope_ref[rows, :] * (weighted - hat * mean)
-        grad_ref[rows, :] = grad
+        grad = slope_ref[rows, :].astype(F32) * (weighted - hat * mean)
+        grad_ref[rows, :] = grad.astype(grad_ref.dtype)
         growth = spread(jnp.exp(of_core(cum_ref, rows, core_ref[0], first, heads)), pattern_ref[...])
         fresh = dot(c_ref[rows, :], (growth * grad).astype(BF16), ((0,), (0,)))
         block_grad_ref[block * N : (block + 1) * N, :] = fresh
@@ -344,17 +351,18 @@
 
 
 def grad_part(
-    group, groups, heads, core, near, far, earlier, up_twice, down, gain, hat, slope, cum, pattern, c, pieces
+    group, groups, heads, core, near, far, cut, start, earlier, up_twice, down, gain, hat, slope, cum, pattern, c, pieces
 ):
     rows, width = hat.shape
     rank = down.shape[0]
     blocks = rows // Q
+    columns = pl.BlockSpec((near.shape[0], cut), lambda i, s: (0, near.shape[1] // cut - 1))
     spec = pltpu.PrefetchScalarGridSpec(
         num_scalar_prefetch=1,
         grid=(1,),
         in_specs=[
-            whole(near.shape),
-            whole(far.shape),
+            columns,
+            columns,
             whole(earlier.shape),
             whole(up_twice.shape),
             pl.BlockSpec((rank, width), lambda i, s: (0, s[0] * groups + group)),
@@ -365,23 +373,25 @@
             whole(pattern.shape),
             pl.BlockSpec((rows, N), lambda i, s: (0, group)),
         ]
-        + [whole(piece.shape) for piece in pieces],
+        + [whole(piece[0].shape) for piece in pieces],
         out_specs=[whole((rows, width)), whole((blocks * N, width)), whole((N, width))],
     )
     return pl.pallas_call(
-        functools.partial(grad_kernel, blocks, group * heads, heads),
+        functools.partial(
+            grad_kernel, blocks, group * heads, heads, start, tuple(piece[1:] for piece in pieces)
+        ),
         grid_spec=spec,
         out_shape=[
-            jax.ShapeDtypeStruct((rows, width), F32),
+            jax.ShapeDtypeStruct((rows, width), BF16),
             jax.ShapeDtypeStruct((blocks * N, width), F32),
             jax.ShapeDtypeStruct((N, width), BF16),
         ],
         compiler_params=params("arbitrary"),
-        cost_estimate=cost(2 * rows * width * near.shape[1], 7),
+        cost_estimate=cost(2 * rows * width * Q, 8),
         name="grad_part",
     )(
         core, near, far, earlier, up_twice, down, gain, hat, slope, cum, pattern, c,
-        *pieces,
+        *[piece[0] for piece in pieces],
     )
 
 
@@ -392,9 +402,9 @@
         lanes = slice(pair * 2 * P_SIZE, (pair + 1) * 2 * P_SIZE)
         grad = grad_ref[:, lanes]
         back = dot(
-            scores_ref[:, 2 * pair * Q : 2 * (pair + 1) * Q], pair_rows(grad.astype(BF16))
-        )
-        out_ref[:, lanes] = out_ref[:, lanes] * back + skip_ref[:, lanes] * grad
+            scores_ref[:, 2 * pair * Q : 2 * (pair + 1) * Q], pair_rows(grad)
+        )
+        out_ref[:, lanes] = out_ref[:, lanes] * back + skip_ref[:, lanes] * grad.astype(F32)
 
 
 def back_part(group, groups, heads, core, scores, grad, step, pattern, skip):
@@ -513,56 +523,135 @@
     return ahead, [(b, a) for a, b in ahead]
 
 
+def cut_kernel(plans, count, *refs):
+    arrays, outs = refs[:count], refs[count:]
+    for out, plan in zip(outs, plans):
+        row = 0
+        for index, start, rows, column in plan:
+            out[row : row + rows, :] = arrays[index][
+                start : start + rows, column : column + out.shape[1]
+            ]
+            row += rows
+
+
+def cut(arrays, plans, width):
+    return small_call(
+        functools.partial(cut_kernel, plans, len(arrays)),
+        [],
+        arrays,
+        [
+            jax.ShapeDtypeStruct((sum(part[2] for part in plan), width), arrays[0].dtype)
+            for plan in plans
+        ],
+        "cut_rows",
+    )
+
+
 class Gather:
-    def __init__(self, shards):
+    def __init__(self, shard):
         self.ring = lax.axis_size("dp")
-        self.turns = rotations(lax.axis_size("x"))[1:]
+        self.across = lax.axis_size("x")
+        self.turns = rotations(self.across)[1:]
         self.perms = ring_perms()
-        self.shards = shards
-        self.late = (shards[1], shards[1])
-        self.early = None
+        self.shard = shard
+        self.size = shard.shape[0]
+        self.width = shard.shape[1] // 2
+        late = shard[:, self.width :]
+        self.late = [(late, 0, self.size)] * 2
+        self.moving = [late, late]
+        self.crossing = shard
         self.pieces = {}
         self.steps = self.ring // 2 + 2
 
-    def onward(self, arrays, distance):
-        if 2 * distance == self.ring:
-            half = arrays[0].shape[0] // 2
-            arrays = (arrays[0][:half], arrays[1][half:])
-        return tuple(lax.ppermute(array, "dp", perm) for array, perm in zip(arrays, self.perms))
-
-    def crossing(self, arrays):
-        return [tuple(lax.ppermute(array, "x", turn) for turn in self.turns) for array in arrays]
+    def sizes(self, index):
+        early = 0 if index == 1 else self.across * self.size
+        late = self.size
+        if 2 * index == self.ring:
+            late //= 2
+        elif 2 * index > self.ring:
+            early, late = early // 2, 0
+        return early, late
 
     def step(self, index, beside):
-        early = late = None
-        if 2 * index <= self.ring:
-            late = self.onward(self.late, index)
+        ring, size, width = self.ring, self.size, self.width
+        early_size, late_size = self.sizes(index)
+        got = tuple(lax.ppermute(array, "dp", perm) for array, perm in zip(self.moving, self.perms))
+        crossed = tuple(lax.ppermute(self.crossing, "x", turn) for turn in self.turns)
+        values = beside()
+        got, crossed, values = lax.optimization_barrier((got, crossed, values))
+        late = [(got[0], early_size, late_size), (got[1], 0, late_size)]
+        early = [(got[0], 0, early_size), (got[1], late_size, early_size)]
+        after_early, after_late = self.sizes(index + 1)
+        more = index + 1 < self.steps
         if index == 1:
-            crossed = self.crossing(self.shards)
-        else:
-            early = self.onward(self.early, index - 1)
-            crossed = self.crossing(self.late)
-        values = beside()
-        early, late, crossed, values = lax.optimization_barrier((early, late, crossed, values))
-        if index == 1:
-            first = jnp.concatenate([self.shards[0], *crossed[0]], axis=0)
-            self.early = (first, first)
-            self.pieces[0] = [[first], [self.shards[1], *crossed[1]]]
+            first = [(0, 0, size, 0)] + [(1 + k, 0, size, 0) for k in range(len(crossed))]
+            base = 1 + len(crossed)
+            self.first, *rest = cut(
+                [self.shard, *crossed, *got],
+                [
+                    first,
+                    first + [(base, 0, after_late, 0)],
+                    [(base + 1, size - after_late, after_late, 0)] + first,
+                    [(base, 0, size, 0), (base + 1, 0, size, 0)],
+                ],
+                width,
+            )
+            self.moving, self.crossing = rest[:2], rest[2]
+            met = [array[:, width:] for array in crossed]
+            self.pieces[0] = [
+                [(self.first, 0, self.first.shape[0])],
+                [self.late[0]] + [(array, 0, size) for array in met],
+            ]
         else:
             distance = index - 1
-            if 2 * distance < self.ring:
+            if 2 * distance < ring:
                 for side in range(2):
                     self.pieces[2 * distance - 1 + side] = [
-                        [early[side]], [self.late[side], *crossed[side]]
+                        [early[side]],
+                        [self.late[side]] + [(array, side * size, size) for array in crossed],
                     ]
             else:
-                halves = zip(*[(array, *met) for array, met in zip(self.late, crossed)])
                 self.pieces[2 * distance - 1] = [
-                    list(early), [array for pair in halves for array in pair]
+                    early, self.late + [(array, 0, size) for array in crossed]
                 ]
-            self.early = early
+            if more:
+                plans = [[(0, early_size, late_size, 0), (1, 0, late_size, 0)]]
+                whole_array = (after_early, after_late) == (early_size, late_size)
+                if not whole_array:
+                    plans += [
+                        [(0, 0, after_early, 0), (0, early_size, after_late, 0)],
+                        [
+                            (1, late_size - after_late, after_late, 0),
+                            (1, late_size + early_size - after_early, after_early, 0),
+                        ],
+                    ]
+                plans = [[part for part in plan if part[2]] for plan in plans]
+                self.crossing, *moving = cut(list(got), plans, width)
+                self.moving = moving or list(got)
         self.late = late
         return values
+
+
+def down_kernel(core_ref, product_ref, arrived_ref, cot_ref, own_ref, sent_ref):
+    down = (product_ref[...] + arrived_ref[...]).astype(BF16)
+    half = own_ref.shape[1]
+    parts = [
+        ADAPTER_SCALE * dot(down, cot_ref[:, part * half : (part + 1) * half], ((0,), (0,)))
+        for part in range(2)
+    ]
+    own_ref[...] = jnp.where(core_ref[0] == 0, parts[0], parts[1])
+    sent_ref[...] = jnp.where(core_ref[0] == 0, parts[1], parts[0]).astype(sent_ref.dtype)
+
+
+def down_part(core, product, arrived, cot):
+    shape = (product.shape[1], cot.shape[1] // 2)
+    return small_call(
+        down_kernel,
+        [core],
+        [product, arrived, cot],
+        [jax.ShapeDtypeStruct(shape, F32), jax.ShapeDtypeStruct(shape, BF16)],
+        "down_part",
+    )
 
 
 def pack_kernel(ring, across, place_ref, first_ref, second_ref, own_ref, far_ref, mine_ref, *sent_refs):
@@ -588,29 +677,32 @@
             out[member, :, width_a:] = chosen[1].astype(out.dtype)
 
 
-def split_kernel(ring, across, place_ref, mine_ref, *refs):
-    arrived, (kept_ref, *sent_refs) = refs[: across - 1], refs[across - 1 :]
-    for turn in range(ring):
-        member = (place_ref[0] + turn) % ring
-        total = mine_ref[member]
+def halve_kernel(bit_ref, mine_ref, *refs):
+    arrived, (kept_ref, sent_ref) = refs[:-2], refs[-2:]
+    half = kept_ref.shape[0]
+    for out, start in ((kept_ref, bit_ref[0] * half), (sent_ref, (1 - bit_ref[0]) * half)):
+        total = mine_ref[pl.ds(start, half)]
         for ref in arrived:
-            total = total + ref[member].astype(F32)
-        out = kept_ref if turn == 0 else sent_refs[turn - 1]
+            total = total + ref[pl.ds(start, half)].astype(F32)
         out[...] = total.astype(out.dtype)
 
 
-def total_kernel(width_a, kept_ref, *refs):
-    arrived, (total_ref, square_ref) = refs[:-2], refs[-2:]
-    total = kept_ref[...]
-    for ref in arrived:
-        total = total + ref[...].astype(F32)
+def add_kernel(mine_ref, arrived_ref, total_ref, sent_ref):
+    total = mine_ref[...] + arrived_ref[...].astype(F32)
     total_ref[...] = total
+    sent_ref[...] = total.astype(sent_ref.dtype)
+
+
+def total_kernel(width_a, place_ref, mine_ref, arrived_ref, total_ref, square_ref):
+    total = mine_ref[...] + arrived_ref[...].astype(F32)
     squares = total * total
-    lane = lax.broadcasted_iota(jnp.int32, squares.shape, 1)
+    lane = lax.broadcasted_iota(jnp.int32, squares.shape, 2)
     first = jnp.sum(jnp.where(lane < width_a, squares, 0.0))
     second = jnp.sum(jnp.where(lane >= width_a, squares, 0.0))
     column = lax.broadcasted_iota(jnp.int32, square_ref.shape, 1)
     square_ref[...] = jnp.where(column == 0, first, jnp.where(column == 1, second, 0.0))
+    own = place_ref[0] % mine_ref.shape[0]
+    total_ref[...] = mine_ref[own] + arrived_ref[own].astype(F32)
 
 
 def small_call(kernel, scalars, arrays, outs, name):
@@ -630,55 +722,65 @@
     )(*scalars, *arrays)
 
 
-class Sums:
-    def __init__(self, sums_a, own_b, far_b):
-        self.ring, self.across = lax.axis_size("dp"), lax.axis_size("x")
-        self.place = jnp.stack([lax.axis_index("dp"), lax.axis_index("x")]).astype(jnp.int32)
-        rank = own_b.shape[0]
-        count = self.ring * self.across
-        self.width_a = 2 * sums_a[0].shape[1] // count
-        self.shape = (rank, self.width_a + own_b.shape[1] // count)
-        wide = (self.ring,) + self.shape
-        self.mine, *self.sent = small_call(
-            functools.partial(pack_kernel, self.ring, self.across),
-            [self.place],
-            [*sums_a, own_b, far_b],
-            [jax.ShapeDtypeStruct(wide, F32)]
-            + [jax.ShapeDtypeStruct(wide, BF16)] * (self.across - 1),
-            "pack_sums",
-        )
-
-    def over_x(self):
-        turns = rotations(self.across)[1:]
-        arrived = [lax.ppermute(value, "x", turn) for value, turn in zip(self.sent, turns)]
-        self.mine, *self.sent = small_call(
-            functools.partial(split_kernel, self.ring, self.across),
-            [self.place],
-            [self.mine, *arrived],
-            [jax.ShapeDtypeStruct(self.shape, F32)]
-            + [jax.ShapeDtypeStruct(self.shape, BF16)] * (self.ring - 1),
-            "split_sums",
-        )
-
-    def over_dp(self):
-        turns = rotations(self.ring)[1:]
-        arrived = [lax.ppermute(value, "dp", turn) for value, turn in zip(self.sent, turns)]
-        return small_call(
-            functools.partial(total_kernel, self.width_a),
-            [],
-            [self.mine, *arrived],
-            [jax.ShapeDtypeStruct(self.shape, F32), jax.ShapeDtypeStruct((8, 128), F32)],
-            "total_sums",
-        )
-
-
-def everywhere(value):
-    for axis in ("core", "x", "dp"):
-        distance = 1
-        while distance < lax.axis_size(axis):
-            pairs = [(i, i ^ distance) for i in range(lax.axis_size(axis))]
-            value = value + lax.ppermute(value, axis, pairs)
-            distance *= 2
+def packed(sums_a, own_b, far_b):
+    ring, across = lax.axis_size("dp"), lax.axis_size("x")
+    place = jnp.stack([lax.axis_index("dp"), lax.axis_index("x")]).astype(jnp.int32)
+    count = ring * across
+    shape = (ring, own_b.shape[0], (2 * sums_a[0].shape[1] + own_b.shape[1]) // count)
+    mine, *sent = small_call(
+        functools.partial(pack_kernel, ring, across),
+        [place],
+        [*sums_a, own_b, far_b],
+        [jax.ShapeDtypeStruct(shape, F32)] + [jax.ShapeDtypeStruct(shape, BF16)] * (across - 1),
+        "pack_sums",
+    )
+    return mine, sent
+
+
+def halved(mine, arrived, distance):
+    shape = (distance,) + mine.shape[1:]
+    return small_call(
+        halve_kernel,
+        [((lax.axis_index("dp") // distance) % 2).astype(jnp.int32)[None]],
+        [mine, *arrived],
+        [jax.ShapeDtypeStruct(shape, F32), jax.ShapeDtypeStruct(shape, BF16)],
+        "halve_sums",
+    )
+
+
+def over_x(sent):
+    return [lax.ppermute(value, "x", turn) for value, turn in zip(sent, rotations(lax.axis_size("x"))[1:])]
+
+
+def far_in_dp(value, distance):
+    return lax.ppermute(value, "dp", [(i, i ^ distance) for i in range(lax.axis_size("dp"))])
+
+
+def added(mine, arrived):
+    return small_call(
+        add_kernel,
+        [],
+        [mine, arrived],
+        [jax.ShapeDtypeStruct(mine.shape, F32), jax.ShapeDtypeStruct(mine.shape, BF16)],
+        "add_sums",
+    )
+
+
+def totals(mine, arrived, width_a):
+    return small_call(
+        functools.partial(total_kernel, width_a),
+        [lax.axis_index("dp").astype(jnp.int32)[None]],
+        [mine, arrived],
+        [jax.ShapeDtypeStruct(mine.shape[1:], F32), jax.ShapeDtypeStruct((8, 128), F32)],
+        "total_sums",
+    )
+
+
+def everywhere(value, distance):
+    value = value + far_in_dp(value, distance)
+    for axis in ("core", "x"):
+        turns = rotations(lax.axis_size(axis))[1:]
+        value = functools.reduce(jnp.add, [lax.ppermute(value, axis, turn) for turn in turns], value)
     return value
 
 
@@ -704,55 +806,51 @@
             [jnp.where(core == 0, near, far), jnp.where(core == 0, far, near)], axis=axis
         )
 
-    def both_cores(value):
-        far = lax.ppermute(half(value, 1 - core), "core", swap)
-        return in_order(half(value, core), far)
-
     def swapped(value):
         return lax.ppermute(value, "core", swap)
 
-    x_far = swapped(half(state_input, 1 - core))
+    sent_weight = half(projection_weight, 1 - core)
+    sent_weight, state_input, step_unbiased, input_matrix, readout_matrix = lax.optimization_barrier(
+        (sent_weight, state_input, step_unbiased, input_matrix, readout_matrix)
+    )
+    shard = in_order(half(projection_weight, core), swapped(sent_weight))
     raw_far = swapped(step_unbiased)
-    shard = both_cores(projection_weight)
-    shards = [shard[:, group * width : (group + 1) * width] for group in range(groups)]
-    (shards, state_input, gate_values, input_matrix, readout_matrix, step_unbiased, output_cotangent) = (
-        lax.optimization_barrier(
-            (shards, state_input, gate_values, input_matrix, readout_matrix, step_unbiased, output_cotangent)
-        )
+    x_far = swapped(
+        jnp.concatenate(
+            [half(value, 1 - core) for value in (state_input, input_matrix, readout_matrix)], axis=1
+        )
+    )
+    shard, gate_values, output_cotangent = lax.optimization_barrier(
+        (shard, gate_values, output_cotangent)
     )
     which = core.astype(jnp.int32)[None]
     chips = chip_order()
     chip_rows = shard.shape[0]
     slots = list(range(len(chips)))
-    stages = [slots[:3], slots[3:5], slots[5:]] if len(slots) > 5 else [slots[:1], slots[1:]]
+    stages = [slots[:3], slots[3:5], slots[5:7], slots[7:]] if len(slots) > 7 else [slots[:1], slots[1:]]
     rows = 2 * near_rows
     blocks = rows // Q
-    gather = Gather(shards)
+    gather = Gather(shard)
     forward = [(i, i + 1) for i in range(across - 1)]
     backward = [(i + 1, i) for i in range(across - 1)]
 
-    def columns(stage):
-        return jnp.concatenate(
-            [
-                lax.dynamic_slice_in_dim(output_cotangent, chip * chip_rows, chip_rows, 1)
-                for offset in stage
-                for chip in chips[offset]
-            ],
-            axis=1,
-        )
-
     def staged(index, group):
         return [piece for slot in stages[index] for piece in gather.pieces[slot][group]]
 
-    def carried(fresh, cum, group, perm):
-        sent = fresh.astype(BF16)
+    def depth(index):
+        return sum(len(stage) for stage in stages[:index]) * across * chip_rows
+
+    def carried(fresh, cum, perm, group=None):
+        sent = fresh
         for lap in range(across - 1):
             arrived = lax.ppermute(sent, "x", perm)
             if lap + 2 < across:
                 total = jnp.sum(cum.reshape(blocks, Q, -1)[:, Q - 1], axis=0)
-                decay = jnp.exp(half(total, core)[group * heads : (group + 1) * heads])
-                decay = jnp.repeat(decay, P_SIZE)[None, :]
-                sent = (arrived.astype(F32) * decay + fresh.astype(F32)).astype(BF16)
+                decay = jnp.repeat(jnp.exp(half(total, core)).reshape(groups, 1, heads), P_SIZE, axis=2)
+                if group is not None:
+                    decay = decay[group : group + 1]
+                parts = [value.astype(F32).reshape(-1, N, width) for value in (arrived, fresh)]
+                sent = (parts[0] * decay + parts[1]).astype(BF16).reshape(fresh.shape)
         return arrived
 
     skip = jnp.repeat(skip_coefficients, P_SIZE)[None, :]
@@ -768,102 +866,118 @@
         step, cum, cum_t = step_part(
             which, step_unbiased, raw_far, step_bias[None, :], decay_rate_log[None, :]
         )
-        b = both_cores(input_matrix)
-        c = both_cores(readout_matrix)
-        return step, cum, cum_t, b, c, inside(0, x_far, b, c, step, cum, cum_t)
-
-    step, cum, cum_t, b, c, local_first = gather.step(1, prepare)
+        cut = groups * width
+        b = in_order(half(input_matrix, core), x_far[:, cut : cut + groups * N])
+        c = in_order(half(readout_matrix, core), x_far[:, cut + groups * N :])
+        local = [inside(group, x_far, b, c, step, cum, cum_t) for group in range(groups)]
+        return step, cum, cum_t, b, c, local
+
+    step, cum, cum_t, b, c, local = gather.step(1, prepare)
 
     def second():
-        local_second = inside(1, x_far, b, c, step, cum, cum_t)
+        fresh = jnp.concatenate([part[3].astype(BF16) for part in local], axis=0)
+        incoming = carried(fresh, cum, forward)
         up_near = (
             ADAPTER_SCALE * dot(output_cotangent, adapter_up, ((1,), (1,))).astype(BF16)
         ).astype(BF16)
-        near = [columns(stage) for stage in stages]
-        return (
-            local_second,
-            carried(local_first[3], cum, 0, forward),
-            in_order(up_near, swapped(up_near)),
-            [(part, swapped(part)) for part in near],
-            swapped(half(gate_values, 1 - core)),
-        )
-
-    local_second, incoming_first, up_twice, cots, z_far = gather.step(2, second)
-    local = [local_first, local_second]
-
-    def norm(group, incoming):
-        scores, ssd, state, total = local[group]
-        return norm_part(
-            group, groups, heads, which, c, incoming, state, cum, pattern, ssd, gate_values, z_far, gain,
-            adapter_down, up_twice,
-        )
-
-    def products(index, earlier):
-        return [
-            product_part(which, *cots[index], earlier[group], staged(index, group), width)
-            for group in range(groups)
+        parts = [
+            lax.dynamic_slice_in_dim(output_cotangent, chip * chip_rows, chip_rows, 1)
+            for offset in chips
+            for chip in offset
         ]
+        near = jnp.concatenate([half(gate_values, 1 - core)] + parts, axis=1)
+        up_twice = in_order(up_near, swapped(up_near))
+        far = swapped(near)
+        normed = []
+        for group in range(groups):
+            scores, ssd, state, total = local[group]
+            normed.append(
+                norm_part(
+                    group, groups, heads, which, c, incoming, state, cum, pattern, ssd, gate_values,
+                    far, gain, adapter_down, up_twice,
+                )
+            )
+        product = functools.reduce(jnp.add, [part[2] for part in normed])
+        far_product = swapped(half(product, 1 - core, 0))
+        return up_twice, near, far, normed, half(product, core, 0), far_product
+
+    up_twice, cot_near, cot_far, normed, product, far_product = gather.step(2, second)
+    cot_width = output_cotangent.shape[1]
+
+    def during(index, beside):
+        return gather.step(index, beside) if gather.steps > index else beside()
+
+    distances = [ring >> k for k in range(1, ring.bit_length())]
 
     def third():
-        incoming = carried(local[1][3], cum, 1, forward)
-        return [norm(0, incoming_first), norm(1, incoming)]
-
-    normed = gather.step(3, third) if gather.steps > 3 else third()
-    nothing = [None] * groups
-
-    def lora_down():
-        product = functools.reduce(jnp.add, [part[2] for part in normed])
-        arrived = swapped(half(product, 1 - core, 0))
-        down_product = (half(product, core, 0) + arrived).astype(BF16)
-        part_b = ADAPTER_SCALE * dot(down_product, output_cotangent, ((0,), (0,)))
-        far_b = swapped(half(part_b, 1 - core).astype(BF16))
-        return Sums([part[3] for part in normed], half(part_b, core), far_b)
+        own_b, sent_b = down_part(which, product, far_product, output_cotangent)
+        mine, sent = packed([part[3] for part in normed], own_b, swapped(sent_b))
+        return halved(mine, over_x(sent), distances[0])
+
+    mine, sent = during(3, third)
+
+    def products(indices, earlier):
+        for index in indices:
+            earlier = [
+                product_part(
+                    which, cot_near, cot_far, cot_width, depth(index), earlier[group], staged(index, group), width
+                )
+                for group in range(groups)
+            ]
+        return earlier
+
+    def doubled(value, rounded, hops):
+        for distance in hops:
+            value, rounded = added(value, far_in_dp(rounded, distance))
+        return value, rounded
 
     def fourth():
-        return lora_down(), products(0, nothing)
-
-    sums, earlier = fourth()
-    sums.mine, sums.sent, earlier = (
-        gather.step(4, lambda: (sums.mine, sums.sent, earlier))
-        if gather.steps > 4
-        else (sums.mine, sums.sent, earlier)
-    )
+        held = list(range(len(stages) - 1))[:2]
+        return doubled(mine, sent, distances[:-2]), products(held, [None] * groups)
+
+    (mine, sent), earlier = during(4, fourth)
+    width_a = 2 * width // (ring * across)
 
     def fifth():
-        sums.over_x()
-        return sums.mine, sums.sent, products(1, earlier) if len(stages) > 2 else earlier
-
-    sums.mine, sums.sent, earlier = gather.step(5, fifth) if gather.steps > 5 else fifth()
+        held = list(range(len(stages) - 1))[2:]
+        return doubled(mine, sent, distances[:-1][-1:]), products(held, earlier)
+
+    (mine, sent), earlier = during(5, fifth)
     for index in range(6, gather.steps):
         gather.step(index, lambda: ())
-    total, squares = sums.over_dp()
-
-    entries = jnp.asarray([sums.width_a, total.shape[1] - sums.width_a], F32)
+    total, squares = totals(mine, far_in_dp(sent, distances[-1]), width_a)
+
+    grads = [
+        grad_part(
+            group, groups, heads, which, cot_near, cot_far, cot_width, depth(len(stages) - 1), earlier[group],
+            up_twice, adapter_down, gain, *normed[group][:2], cum, pattern, c, staged(len(stages) - 1, group),
+        )
+        for group in range(groups)
+    ]
+    outgoing = [carried(part[2], cum, backward, group) for group, part in enumerate(grads)]
+    bases = [
+        back_part(group, groups, heads, which, local[group][0], grads[group][0], step, pattern, skip)
+        for group in range(groups)
+    ]
+    near, far = [], []
+    for group in range(groups):
+        own, others = cross_part(
+            group, heads, which, b, outgoing[group], grads[group][1], step, cum, pattern, bases[group]
+        )
+        far.append(swapped(others))
+        near.append(own)
+    entries = jnp.asarray([width_a, total.shape[1] - width_a], F32)
     entries = entries * (total.shape[0] * ring * across * 2)
-    squares = everywhere(squares[:1])[0, :2]
-    scale = 1.0 / jnp.maximum(1.0, jnp.sqrt(squares / entries + CLIP_EPSILON))
     count = ring * across
     homes = [
         (chip * 2 + number, number * count + chip) for chip in range(count) for number in range(2)
     ]
+    total, near[-1] = lax.optimization_barrier((total, near[-1]))
     total = lax.ppermute(total, AXES, homes)
-    gradient_a = total[:, : sums.width_a] * scale[0]
-    gradient_b = total[:, sums.width_a :] * scale[1]
-
-    near, far = [], []
-    for group in range(groups):
-        hat, slope = normed[group][:2]
-        grad, block_grad, grad_total = grad_part(
-            group, groups, heads, which, *cots[-1], earlier[group], up_twice, adapter_down, gain, hat, slope,
-            cum, pattern, c, staged(len(stages) - 1, group),
-        )
-        outgoing = carried(grad_total, cum, group, backward)
-        base = back_part(group, groups, heads, which, local[group][0], grad, step, pattern, skip)
-        own, others = cross_part(
-            group, heads, which, b, outgoing, block_grad, step, cum, pattern, base
-        )
-        far.append(swapped(others))
-        near.append(own)
+    squares = everywhere(squares, distances[0])[0, :2]
+    scale = 1.0 / jnp.maximum(1.0, jnp.sqrt(squares / entries + CLIP_EPSILON))
+    gradient_a = total[:, :width_a] * scale[0]
+    gradient_b = total[:, width_a:] * scale[1]
     input_gradient = in_order(
         jnp.concatenate(near, axis=1), jnp.concatenate(far, axis=1), axis=1
     )

time: 167 us -> 145 us (0.87)
  starting transfers between devices: 68.8 us -> 36.8 us
  Pallas kernels: 33.4 us -> 48 us
  waiting for transfers between devices: 43.4 us -> 38.8 us
    ppermute x41 -> x21, starting transfers between devices: 49.8 us -> 26.8 us  [the longest x10 11 us: step(): lax.ppermute(array, 'dp', perm)]
    ppermute x41 -> x21, waiting for transfers between devices: 37.4 us -> 16.7 us  [the longest x4 9.44 us: far_in_dp(): lax.ppermute(value, 'dp', [(i, i ^ distance) for i in range(lax.axis_size...]
    ppermute x1, waiting for transfers between devices: 1.92 us -> 12.5 us  [over_x(): lax.ppermute(value, 'x', turn)]
    pallas_call x4 -> x6, Pallas kernels: 3.39 us -> 10.4 us  [product_part(): pl.pallas_call(functools.partial(product_kernel, first, tuple((piece[1:]...]
    pallas_call x3 -> x10, Pallas kernels: 1.76 us -> 7.11 us  [small_call(): pl.pallas_call(kernel, grid_spec=spec, out_shape=outs, compiler_params=pa...]
    ppermute x4 -> x3, starting transfers between devices: 9.31 us -> 4.8 us  [carried(): arrived = lax.ppermute(sent, 'x', perm)]
    ppermute x4 -> x3, waiting for transfers between devices: 3.31 us -> 7.33 us  [carried(): arrived = lax.ppermute(sent, 'x', perm)]
    dynamic_slice x7 -> x4, local copies, waits for them, and re-layouts: 5.52 us -> 2.39 us  [half(): return lax.dynamic_slice_in_dim(value, which * size, size, axis)]
  transfers between devices with their start and end apart: 58 -> 35, of which waited for: 17 -> 10; matrix products, arithmetic and copies ran while one was open for 7% -> 6% of each run, Pallas kernels for 20% -> 32%
where the time goes in v3:
time: 145 us; the launch traced here: 143 us
  Pallas kernels  48 us (33%)
  waiting for transfers between devices  38.8 us (27%)
  starting transfers between devices  36.8 us (25%)
  local copies, waits for them, and re-layouts  9.97 us (7%)
  other arithmetic  6.89 us (5%)
  between operations  1.92 us (1%)
    pallas_call x2, Pallas kernels, local_part(): pl.pallas_call(functools.partial(local_kernel, group * heads, heads), gri...  14.9 us
    ppermute x1, waiting for transfers between devices, over_x(): lax.ppermute(value, 'x', turn)  12.5 us
    ppermute x10, starting transfers between devices, step(): lax.ppermute(array, 'dp', perm)  11 us
    pallas_call x6, Pallas kernels, product_part(): pl.pallas_call(functools.partial(product_kernel, first, tuple((piece[1:]...  10.4 us
    ppermute x4, waiting for transfers between devices, far_in_dp(): lax.ppermute(value, 'dp', [(i, i ^ distance) for i in range(lax.axis_size...  9.44 us
    ppermute x3, waiting for transfers between devices, carried(): arrived = lax.ppermute(sent, 'x', perm)  7.33 us
    ppermute x5, starting transfers between devices, step(): lax.ppermute(self.crossing, 'x', turn)  7.11 us
    pallas_call x10, Pallas kernels, small_call(): pl.pallas_call(kernel, grid_spec=spec, out_shape=outs, compiler_params=pa...  7.11 us
  transfers between devices with their start and end apart: 35, of which 10 were waited for; matrix products, arithmetic and copies ran while one was open for 6% of the time, Pallas kernels for 32%

profile of v3, /device:TPU:0, one launch (start us, length us, event | category | flops | bytes accessed | tf_op | source)
XLA Modules:
  0.0 142.7 jit_solution(6204170049874555967)
XLA Ops:
  0.7 1.0 constant_dynamic-slice_fusion.5
  1.7 0.9 copy.19.near_ref
  2.7 0.5 collective-permute-start.4
  3.3 1.3 constant_dynamic-slice_fusion.4
  4.6 1.2 pad_maximum_fusion.1
  6.5 0.8 step_part.1
  7.8 2.6 %collective-permute-start.2 = (bf16[128,1024]{1,0:T(8,128)(2,1)S(1)}, bf16[128,1024]{1,0:T(8,128)(2,1)S(1)}, u32[]{:S(2)}, u32[]{:S(2)}) collective-permute-start(bf16[128,1024]{1,0:T(8,128)(2,1)S(1)} %slice.27.rest_0_), channel_id=1, source_target_pairs={{8,0},{16,8},{24,16},{28,24},{20,28},{12,20},{4,12},{0,4},{9,1},{1... | collective-permute-start | bytes 786440 | tf_op jit(solution)/shard_map/ppermute | solution.py:578
  10.6 1.9 %collective-permute-start.3 = (bf16[128,2048]{1,0:T(8,128)(2,1)S(1)}, bf16[128,2048]{1,0:T(8,128)(2,1)S(1)}, u32[]{:S(2)}, u32[]{:S(2)}) collective-permute-start(bf16[128,2048]{1,0:T(8,128)(2,1)S(1)} %pad_maximum_fusion.2.refs_0_), channel_id=1, source_target_pairs={{0,2},{2,0},{1,3},{3,1},{4,6},{6,4},{5,7},{7,5},{8,10},{10,8},{9,1... | collective-permute-start | bytes 1572872 | tf_op jit(solution)/shard_map/ppermute | solution.py:579
  13.4 1.1 broadcast_select_fusion.5
  14.5 7.4 %local_part.3 = (bf16[512,4096]{1,0:T(8,128)(2,1)}, bf16[512,1024]{1,0:T(8,128)(2,1)S(1)}, f32[256,1024]{1,0:T(8,128)S(1)}, f32[128,1024]{1,0:T(8,128)S(1)}) custom-call(s32[1]{0:T(128)} %bitcast.core_ref, bf16[256,4096]{1,0:T(8,128)(2,1)S(1)} %copy-done.28, bf16[256,2560]{1,0:T(8,128)(2,1)} %collective-permute-done.5.far_ref, ...), custom_call_target="tpu_custom_call" | custom-call | flops 9663676416 | tf_op jit(solution)/shard_map/local_part/pallas_call | solution.py:193
  22.0 7.5 %local_part.2 = (bf16[512,4096]{1,0:T(8,128)(2,1)}, bf16[512,1024]{1,0:T(8,128)(2,1)S(1)}, f32[256,1024]{1,0:T(8,128)S(1)}, f32[128,1024]{1,0:T(8,128)S(1)}) custom-call(s32[1]{0:T(128)} %bitcast.core_ref, bf16[256,4096]{1,0:T(8,128)(2,1)S(1)} %copy-done.28, bf16[256,2560]{1,0:T(8,128)(2,1)} %collective-permute-done.5.far_ref, ...), custom_call_target="tpu_custom_call" | custom-call | flops 9663676416 | tf_op jit(solution)/shard_map/local_part/pallas_call | solution.py:193
  29.6 2.1 %collective-permute-start.11 = (bf16[256,1024]{1,0:T(8,128)(2,1)S(1)}, bf16[256,1024]{1,0:T(8,128)(2,1)S(1)}, u32[]{:S(2)}, u32[]{:S(2)}) collective-permute-start(bf16[256,1024]{1,0:T(8,128)(2,1)S(1)} %pad_maximum_fusion.3), channel_id=1, source_target_pairs={{0,2},{1,3},{4,6},{5,7},{8,10},{9,11},{12,14},{13,15},{16,18},{17,... | collective-permute-start | bytes 1572872 | tf_op jit(solution)/shard_map/ppermute | solution.py:846
  32.5 1.1 collective-permute-done.9
  33.8 0.8 copy-done.26
  34.6 2.0 %collective-permute-start.6 = (bf16[384,1024]{1,0:T(8,128)(2,1)S(1)}, bf16[384,1024]{1,0:T(8,128)(2,1)S(1)}, u32[]{:S(2)}, u32[]{:S(2)}) collective-permute-start(bf16[384,1024]{1,0:T(8,128)(2,1)S(1)} %get-tuple-element.133), channel_id=1, source_target_pairs={{0,8},{8,16},{16,24},{24,28},{28,20},{20,12},{12,4},{4,0},{1,9},{9... | collective-permute-start | bytes 2359304 | tf_op jit(solution)/shard_map/ppermute | solution.py:578
  36.6 7.3 %collective-permute-done.11.incoming_ref = bf16[256,1024]{1,0:T(8,128)(2,1)S(1)} collective-permute-done((bf16[256,1024]{1,0:T(8,128)(2,1)S(1)}, bf16[256,1024]{1,0:T(8,128)(2,1)S(1)}, u32[]{:S(2)}, u32[]{:S(2)}) %collective-permute-start.11) | collective-permute-done | bytes 524320 | tf_op jit(solution)/shard_map/ppermute | solution.py:846
  43.9 2.2 %norm_part.3 = (bf16[512,1024]{1,0:T(8,128)(2,1)S(1)}, bf16[512,1024]{1,0:T(8,128)(2,1)S(1)}, f32[512,64]{1,0:T(8,128)S(1)}, f32[64,1024]{1,0:T(8,128)S(1)}) custom-call(s32[1]{0:T(128)} %bitcast.core_ref, bf16[512,256]{1,0:T(8,128)(2,1)S(1)} %pad_maximum_fusion.5.c_ref, bf16[256,1024]{1,0:T(8,128)(2,1)S(1)} %collective-permute-done.11.incoming_ref, ...), custom_call_target="tpu_custom_call" | custom-call | flops 3758096384 | tf_op jit(solution)/shard_map/norm_part/pallas_call | solution.py:266
  46.1 1.0 copy-done.22
  47.1 1.0 copy-done.24
  48.1 2.2 %norm_part.2 = (bf16[512,1024]{1,0:T(8,128)(2,1)S(1)}, bf16[512,1024]{1,0:T(8,128)(2,1)S(1)}, f32[512,64]{1,0:T(8,128)S(1)}, f32[64,1024]{1,0:T(8,128)S(1)}) custom-call(s32[1]{0:T(128)} %bitcast.core_ref, bf16[512,256]{1,0:T(8,128)(2,1)S(1)} %pad_maximum_fusion.5.c_ref, bf16[256,1024]{1,0:T(8,128)(2,1)S(1)} %collective-permute-done.11.incoming_ref, ...), custom_call_target="tpu_custom_call" | custom-call | flops 3758096384 | tf_op jit(solution)/shard_map/norm_part/pallas_call | solution.py:266
  50.4 4.3 %collective-permute-done.8.rest_3_.rest_5_ = bf16[256,1024]{1,0:T(8,128)(2,1)S(1)} collective-permute-done((bf16[256,1024]{1,0:T(8,128)(2,1)S(1)}, bf16[256,1024]{1,0:T(8,128)(2,1)S(1)}, u32[]{:S(2)}, u32[]{:S(2)}) %collective-permute-start.8) | collective-permute-done | bytes 524320 | tf_op jit(solution)/shard_map/ppermute | solution.py:579
  54.7 1.3 collective-permute-done.7.refs_1_.rest_2_.rest_3_
  56.0 1.6 %collective-permute-start.13 = (bf16[384,1024]{1,0:T(8,128)(2,1)S(1)}, bf16[384,1024]{1,0:T(8,128)(2,1)}, u32[]{:S(2)}, u32[]{:S(2)}) collective-permute-start(bf16[384,1024]{1,0:T(8,128)(2,1)S(1)} %collective-permute-done.6.refs_0_.rest_1_), channel_id=1, source_target_pairs={{0,8},{8,16},{16,24},{24,28},{28,20},{20,12},{12,4},{4,0},{1,9},{9... | collective-permute-start | bytes 2359304 | tf_op jit(solution)/shard_map/ppermute | solution.py:578
  57.6 0.4 collective-permute-start.14
  58.0 2.0 %cut_rows.5 = bf16[256,1024]{1,0:T(8,128)(2,1)} custom-call(bf16[384,1024]{1,0:T(8,128)(2,1)S(1)} %collective-permute-done.6.refs_0_.rest_1_, bf16[384,1024]{1,0:T(8,128)(2,1)} %collective-permute-done.7.refs_1_.rest_2_.rest_3_), custom_call_target="tpu_custom_call" | custom-call | flops 1000000000 | tf_op jit(solution)/shard_map/cut_rows/pallas_call | solution.py:715
  60.0 1.7 %collective-permute-start.15 = (bf16[256,1024]{1,0:T(8,128)(2,1)}, bf16[256,1024]{1,0:T(8,128)(2,1)}, u32[]{:S(2)}, u32[]{:S(2)}) collective-permute-start(bf16[256,1024]{1,0:T(8,128)(2,1)} %cut_rows.5), channel_id=1, source_target_pairs={{0,2},{2,0},{1,3},{3,1},{4,6},{6,4},{5,7},{7,5},{8,10},{10,8},{9,1... | collective-permute-start | bytes 1572872 | tf_op jit(solution)/shard_map/ppermute | solution.py:579
  62.2 1.3 collective-permute-done.16.far_ref
  63.5 1.7 %pack_sums.1 = (f32[8,64,192]{2,1,0:T(8,128)S(1)}, bf16[8,64,192]{2,1,0:T(8,128)(2,1)}) custom-call(s32[2]{0:T(128)S(1)} %pad_add_fusion.place_ref, f32[64,1024]{1,0:T(8,128)S(1)} %get-tuple-element.158.first_ref, f32[64,1024]{1,0:T(8,128)S(1)} %get-tuple-element.159.second_ref, f32[64,1024]{1,0:T(8,128)S(1)} %get-tuple-element.162.own_ref, ...), custom_call_target="tpu_custom_call" | custom-call | flops 1000000000 | tf_op jit(solution)/shard_map/pack_sums/pallas_call | solution.py:715
  65.2 0.8 copy-done.41
  66.3 12.5 %collective-permute-done.17.refs_0_ = bf16[8,64,192]{2,1,0:T(8,128)(2,1)} collective-permute-done((bf16[8,64,192]{2,1,0:T(8,128)(2,1)}, bf16[8,64,192]{2,1,0:T(8,128)(2,1)}, u32[]{:S(2)}, u32[]{:S(2)}) %collective-permute-start.17) | collective-permute-done | bytes 196640 | tf_op jit(solution)/shard_map/ppermute | solution.py:752
  78.8 1.0 copy-done.42
  79.8 1.0 halve_sums.1
  80.9 1.6 %cut_rows.6 = (bf16[256,1024]{1,0:T(8,128)(2,1)S(1)}, bf16[320,1024]{1,0:T(8,128)(2,1)S(1)}, bf16[320,1024]{1,0:T(8,128)(2,1)S(1)}) custom-call(bf16[384,1024]{1,0:T(8,128)(2,1)} %collective-permute-done.13.refs_0_.rest_1_, bf16[384,1024]{1,0:T(8,128)(2,1)} %collective-permute-done.14.refs_1_.rest_2_.rest_3_), custom_call_target="tpu_custom_call" | custom-call | flops 1000000000 | tf_op jit(solution)/shard_map/cut_rows/pallas_call | solution.py:715
  82.5 1.8 %collective-permute-start.18 = (bf16[320,1024]{1,0:T(8,128)(2,1)S(1)}, bf16[320,1024]{1,0:T(8,128)(2,1)S(1)}, u32[]{:S(2)}, u32[]{:S(2)}) collective-permute-start(bf16[320,1024]{1,0:T(8,128)(2,1)S(1)} %get-tuple-element.170), channel_id=1, source_target_pairs={{0,8},{8,16},{16,24},{24,28},{28,20},{20,12},{12,4},{4,0},{1,9},{9... | collective-permute-start | bytes 1966088 | tf_op jit(solution)/shard_map/ppermute | solution.py:578
  84.6 1.7 %collective-permute-start.20 = (bf16[256,1024]{1,0:T(8,128)(2,1)S(1)}, bf16[256,1024]{1,0:T(8,128)(2,1)S(1)}, u32[]{:S(2)}, u32[]{:S(2)}) collective-permute-start(bf16[256,1024]{1,0:T(8,128)(2,1)S(1)} %get-tuple-element.172), channel_id=1, source_target_pairs={{0,2},{2,0},{1,3},{3,1},{4,6},{6,4},{5,7},{7,5},{8,10},{10,8},{9,1... | collective-permute-start | bytes 1572872 | tf_op jit(solution)/shard_map/ppermute | solution.py:579
  86.4 2.3 %product_part.6.rest_0_ = f32[512,1024]{1,0:T(8,128)S(1)} custom-call(s32[1]{0:T(128)} %bitcast.core_ref, bf16[256,4096]{1,0:T(8,128)(2,1)S(1)} %dynamic-slice_dynamic-update-slice_fusion.1.near_ref, bf16[256,4096]{1,0:T(8,128)(2,1)S(1)} %copy-done.3, bf16[256,1024]{1,0:T(8,128)(2,1)S(1)} %copy-done.27, ...), custom_call_target="tpu_custom_call" | custom-call | flops 1073741824 | tf_op jit(solution)/shard_map/product_part/pallas_call | solution.py:311
  88.7 1.0 product_part.8.rest_0_
  89.7 2.8 %collective-permute-start.21 = (bf16[4,64,192]{2,1,0:T(8,128)(2,1)S(1)}, bf16[4,64,192]{2,1,0:T(8,128)(2,1)S(1)}, u32[]{:S(2)}, u32[]{:S(2)}) collective-permute-start(bf16[4,64,192]{2,1,0:T(8,128)(2,1)S(1)} %get-tuple-element.174), channel_id=1, source_target_pairs={{0,16},{4,20},{8,24},{12,28},{16,0},{20,4},{24,8},{28,12},{1,17},{... | collective-permute-start | bytes 294920 | tf_op jit(solution)/shard_map/ppermute | solution.py:756
  92.5 2.1 %product_part.7.rest_0_ = f32[512,1024]{1,0:T(8,128)S(1)} custom-call(s32[1]{0:T(128)} %bitcast.core_ref, bf16[256,4096]{1,0:T(8,128)(2,1)S(1)} %dynamic-slice_dynamic-update-slice_fusion.1.near_ref, bf16[256,4096]{1,0:T(8,128)(2,1)S(1)} %copy-done.3, f32[512,1024]{1,0:T(8,128)S(1)} %product_part.6.rest_0_, ...), custom_call_target="tpu_custom_call" | custom-call | flops 1073741824 | tf_op jit(solution)/shard_map/product_part/pallas_call | solution.py:311
  94.7 2.2 %product_part.9.rest_0_ = f32[512,1024]{1,0:T(8,128)S(1)} custom-call(s32[1]{0:T(128)} %bitcast.core_ref, bf16[256,4096]{1,0:T(8,128)(2,1)S(1)} %dynamic-slice_dynamic-update-slice_fusion.1.near_ref, bf16[256,4096]{1,0:T(8,128)(2,1)S(1)} %copy-done.3, f32[512,1024]{1,0:T(8,128)S(1)} %product_part.8.rest_0_, ...), custom_call_target="tpu_custom_call" | custom-call | flops 1073741824 | tf_op jit(solution)/shard_map/product_part/pallas_call | solution.py:311
  96.9 9.0 %collective-permute-done.21.arrived_ref = bf16[4,64,192]{2,1,0:T(8,128)(2,1)S(1)} collective-permute-done((bf16[4,64,192]{2,1,0:T(8,128)(2,1)S(1)}, bf16[4,64,192]{2,1,0:T(8,128)(2,1)S(1)}, u32[]{:S(2)}, u32[]{:S(2)}) %collective-permute-start.21) | collective-permute-done | bytes 98336 | tf_op jit(solution)/shard_map/ppermute | solution.py:756
  106.1 2.1 %collective-permute-start.22 = (bf16[128,1024]{1,0:T(8,128)(2,1)S(1)}, bf16[128,1024]{1,0:T(8,128)(2,1)S(1)}, u32[]{:S(2)}, u32[]{:S(2)}) collective-permute-start(bf16[128,1024]{1,0:T(8,128)(2,1)S(1)} %get-tuple-element.182), channel_id=1, source_target_pairs={{0,8},{8,16},{16,24},{24,28},{28,20},{20,12},{12,4},{4,0},{1,9},{9... | collective-permute-start | bytes 786440 | tf_op jit(solution)/shard_map/ppermute | solution.py:578
  108.2 1.7 %collective-permute-start.24 = (bf16[128,1024]{1,0:T(8,128)(2,1)S(1)}, bf16[128,1024]{1,0:T(8,128)(2,1)S(1)}, u32[]{:S(2)}, u32[]{:S(2)}) collective-permute-start(bf16[128,1024]{1,0:T(8,128)(2,1)S(1)} %get-tuple-element.184), channel_id=1, source_target_pairs={{0,2},{2,0},{1,3},{3,1},{4,6},{6,4},{5,7},{7,5},{8,10},{10,8},{9,1... | collective-permute-start | bytes 786440 | tf_op jit(solution)/shard_map/ppermute | solution.py:579
  109.9 0.7 product_part.10.earlier_ref
  110.6 2.2 %product_part.11.earlier_ref = f32[512,1024]{1,0:T(8,128)S(1)} custom-call(s32[1]{0:T(128)} %bitcast.core_ref, bf16[256,4096]{1,0:T(8,128)(2,1)S(1)} %dynamic-slice_dynamic-update-slice_fusion.1.near_ref, bf16[256,4096]{1,0:T(8,128)(2,1)S(1)} %copy-done.3, f32[512,1024]{1,0:T(8,128)S(1)} %product_part.9.rest_0_, ...), custom_call_target="tpu_custom_call" | custom-call | flops 1073741824 | tf_op jit(solution)/shard_map/product_part/pallas_call | solution.py:311
  113.3 1.2 collective-permute-done.23.rest_1_
  114.5 1.2 collective-permute-start.27
  115.8 1.8 %grad_part.2 = (bf16[512,1024]{1,0:T(8,128)(2,1)S(1)}, f32[256,1024]{1,0:T(8,128)S(1)}, bf16[128,1024]{1,0:T(8,128)(2,1)S(1)}) custom-call(s32[1]{0:T(128)} %bitcast.core_ref, bf16[256,4096]{1,0:T(8,128)(2,1)S(1)} %dynamic-slice_dynamic-update-slice_fusion.1.near_ref, bf16[256,4096]{1,0:T(8,128)(2,1)S(1)} %copy-done.3, ...), custom_call_target="tpu_custom_call" | custom-call | flops 2147483648 | tf_op jit(solution)/shard_map/grad_part/pallas_call | solution.py:379
  117.6 1.4 collective-permute-start.26
  119.0 0.5 collective-permute-done.27.arrived_ref
  119.7 1.8 %collective-permute-start.32 = (f32[8,128]{1,0:T(8,128)S(1)}, f32[8,128]{1,0:T(8,128)S(1)}, u32[]{:S(2)}, u32[]{:S(2)}) collective-permute-start(f32[8,128]{1,0:T(8,128)S(1)} %get-tuple-element.220), channel_id=1, source_target_pairs={{0,16},{4,20},{8,24},{12,28},{16,0},{20,4},{24,8},{28,12},{1,17},{... | collective-permute-start | bytes 12296 | tf_op jit(solution)/shard_map/ppermute | solution.py:756
  121.5 1.8 %grad_part.3 = (bf16[512,1024]{1,0:T(8,128)(2,1)S(1)}, f32[256,1024]{1,0:T(8,128)S(1)}, bf16[128,1024]{1,0:T(8,128)(2,1)S(1)}) custom-call(s32[1]{0:T(128)} %bitcast.core_ref, bf16[256,4096]{1,0:T(8,128)(2,1)S(1)} %dynamic-slice_dynamic-update-slice_fusion.1.near_ref, bf16[256,4096]{1,0:T(8,128)(2,1)S(1)} %copy-done.3, ...), custom_call_target="tpu_custom_call" | custom-call | flops 2147483648 | tf_op jit(solution)/shard_map/grad_part/pallas_call | solution.py:379
  123.3 1.3 collective-permute-start.28
  124.7 2.1 %back_part.3.base_ref = f32[512,1024]{1,0:T(8,128)S(1)} custom-call(s32[1]{0:T(128)} %bitcast.core_ref, bf16[512,4096]{1,0:T(8,128)(2,1)S(1)} %copy-done.40, bf16[512,1024]{1,0:T(8,128)(2,1)S(1)} %get-tuple-element.214.grad_ref, f32[512,64]{1,0:T(8,128)S(1)} %copy-done.18, bf16[48,1024]{1,0:T(8,128)(2,1)S(1)} %copy-done.12, ...), custom_call_target="tpu_custom_call" | custom-call | flops 2147483648 | tf_op jit(solution)/shard_map/back_part/pallas_call | solution.py:425
  126.9 2.7 %collective-permute-start.34 = (f32[8,128]{1,0:T(8,128)S(1)}, f32[8,128]{1,0:T(8,128)S(1)}, u32[]{:S(2)}, u32[]{:S(2)}) collective-permute-start(f32[8,128]{1,0:T(8,128)S(1)} %add.346), channel_id=1, source_target_pairs={{0,2},{2,0},{1,3},{3,1},{4,6},{6,4},{5,7},{7,5},{8,10},{10,8},{9,1... | collective-permute-start | bytes 12296 | tf_op jit(solution)/shard_map/ppermute | solution.py:783
  129.6 2.1 %back_part.2.base_ref = f32[512,1024]{1,0:T(8,128)S(1)} custom-call(s32[1]{0:T(128)} %bitcast.core_ref, bf16[512,4096]{1,0:T(8,128)(2,1)S(1)} %copy-done.39, bf16[512,1024]{1,0:T(8,128)(2,1)S(1)} %get-tuple-element.202.grad_ref, f32[512,64]{1,0:T(8,128)S(1)} %copy-done.18, bf16[48,1024]{1,0:T(8,128)(2,1)S(1)} %copy-done.12, ...), custom_call_target="tpu_custom_call" | custom-call | flops 2147483648 | tf_op jit(solution)/shard_map/back_part/pallas_call | solution.py:425
  131.7 0.6 fusion.1
  132.3 1.3 cross_part.3
  133.6 0.7 collective-permute-start.31
  134.3 1.3 cross_part.2
  135.7 2.6 %collective-permute-start.30 = (bf16[256,1024]{1,0:T(8,128)(2,1)S(1)}, bf16[256,1024]{1,0:T(8,128)(2,1)S(1)}, u32[]{:S(2)}, u32[]{:S(2)}) collective-permute-start(bf16[256,1024]{1,0:T(8,128)(2,1)S(1)} %get-tuple-element.218), channel_id=1, source_target_pairs={{0,1},{1,0},{2,3},{3,2},{4,5},{5,4},{6,7},{7,6},{8,9},{9,8},{10,11... | collective-permute-start | bytes 1572872 | tf_op jit(solution)/shard_map/ppermute | solution.py:810
  138.4 1.3 slice_multiply_fusion
  139.7 1.3 slice_multiply_fusion.1
  141.2 1.5 %pad_maximum_fusion = bf16[256,4096]{1,0:T(8,128)(2,1)} fusion(bf16[256,2048]{1,0:T(8,128)(2,1)S(1)} %get-tuple-element.222, bf16[256,2048]{1,0:T(8,128)(2,1)S(1)} %get-tuple-element.221), kind=kLoop, calls=%fused_computation | loop fusion | flops 4194304 | bytes 4194304 | tf_op jit(solution)/shard_map/concatenate | solution.py:805
  (186 shorter events, 5.9 us)
Async XLA Ops:
  0.6 31.1 %copy-start = (bf16[64,2048]{1,0:T(8,128)(2,1)S(1)}, bf16[64,2048]{1,0:T(8,128)(2,1)}, u32[]{:S(2)}) copy-start(bf16[64,2048]{1,0:T(8,128)(2,1)} %param.25) | copy-start | bytes 786436
  0.6 3.9 %copy-start.44 = (bf16[256,512]{1,0:T(8,128)(2,1)S(1)}, bf16[256,512]{1,0:T(8,128)(2,1)}, u32[]{:S(2)}) copy-start(bf16[256,512]{1,0:T(8,128)(2,1)} %param.18) | copy-start | bytes 786436
  0.7 3.9 %copy-start.46 = (bf16[256,512]{1,0:T(8,128)(2,1)S(1)}, bf16[256,512]{1,0:T(8,128)(2,1)}, u32[]{:S(2)}) copy-start(bf16[256,512]{1,0:T(8,128)(2,1)} %param.17) | copy-start | bytes 786436
  2.7 3.8 %collective-permute-start.4 = (f32[256,64]{1,0:T(8,128)S(1)}, f32[256,64]{1,0:T(8,128)S(1)}, u32[]{:S(2)}, u32[]{:S(2)}) collective-permute-start(f32[256,64]{1,0:T(8,128)S(1)} %copy.19.near_ref), channel_id=1, source_target_pairs={{0,1},{1,0},{2,3},{3,2},{4,5},{5,4},{6,7},{7,6},{8,9},{9,8},{10,11... | collective-permute-start | bytes 196616 | tf_op jit(solution)/shard_map/ppermute | solution.py:810
  3.2 4.2 %collective-permute-start = (bf16[64,2048]{1,0:T(8,128)(2,1)S(1)}, bf16[64,2048]{1,0:T(8,128)(2,1)S(1)}, u32[]{:S(2)}, u32[]{:S(2)}) collective-permute-start(bf16[64,2048]{1,0:T(8,128)(2,1)S(1)} %constant_dynamic-slice_fusion.5), channel_id=1, source_target_pairs={{0,1},{1,0},{2,3},{3,2},{4,5},{5,4},{6,7},{7,6},{8,9},{9,8},{10,11... | collective-permute-start | bytes 786440 | tf_op jit(solution)/shard_map/ppermute | solution.py:810
  5.8 7.5 %collective-permute-start.5 = (bf16[256,2560]{1,0:T(8,128)(2,1)}, bf16[256,2560]{1,0:T(8,128)(2,1)}, u32[]{:S(2)}, u32[]{:S(2)}) collective-permute-start(bf16[256,2560]{1,0:T(8,128)(2,1)} %pad_maximum_fusion.1), channel_id=1, source_target_pairs={{0,1},{1,0},{2,3},{3,2},{4,5},{5,4},{6,7},{7,6},{8,9},{9,8},{10,11... | collective-permute-start | bytes 3932168 | tf_op jit(solution)/shard_map/ppermute | solution.py:810
  7.3 14.6 %copy-start.17 = (f32[512,64]{1,0:T(8,128)}, f32[512,64]{1,0:T(8,128)S(1)}, u32[]{:S(2)}) copy-start(f32[512,64]{1,0:T(8,128)S(1)} %get-tuple-element.200.step_ref) | copy-start | bytes 393220
  7.3 5.1 %copy-start.29 = (bf16[256,4096]{1,0:T(8,128)(2,1)S(1)}, bf16[256,4096]{1,0:T(8,128)(2,1)}, u32[]{:S(2)}) copy-start(bf16[256,4096]{1,0:T(8,128)(2,1)} %near_ref.3) | copy-start | bytes 6291460
  7.7 4.9 %copy-start.19 = (bf16[256,2048]{1,0:T(8,128)(2,1)S(1)}, bf16[256,2048]{1,0:T(8,128)(2,1)}, u32[]{:S(2)}) copy-start(bf16[256,2048]{1,0:T(8,128)(2,1)} %cot_ref) | copy-start | bytes 3145732
  7.8 5.5 %copy-start.20 = (bf16[128,1024]{1,0:T(8,128)(2,1)}, bf16[128,1024]{1,0:T(8,128)(2,1)S(1)}, u32[]{:S(2)}) copy-start(bf16[128,1024]{1,0:T(8,128)(2,1)S(1)} %slice.27.rest_0_) | copy-start | bytes 786436
  7.8 5.6 %copy-start.45 = (bf16[256,512]{1,0:T(8,128)(2,1)S(1)}, bf16[256,512]{1,0:T(8,128)(2,1)}, u32[]{:S(2)}) copy-start(bf16[256,512]{1,0:T(8,128)(2,1)} %param.18) | copy-start | bytes 786436
  7.8 5.6 %copy-start.47 = (bf16[256,512]{1,0:T(8,128)(2,1)S(1)}, bf16[256,512]{1,0:T(8,128)(2,1)}, u32[]{:S(2)}) copy-start(bf16[256,512]{1,0:T(8,128)(2,1)} %param.17) | copy-start | bytes 786436
  7.8 21.7 %collective-permute-start.2 = (bf16[128,1024]{1,0:T(8,128)(2,1)S(1)}, bf16[128,1024]{1,0:T(8,128)(2,1)S(1)}, u32[]{:S(2)}, u32[]{:S(2)}) collective-permute-start(bf16[128,1024]{1,0:T(8,128)(2,1)S(1)} %slice.27.rest_0_), channel_id=1, source_target_pairs={{8,0},{16,8},{24,16},{28,24},{20,28},{12,20},{4,12},{0,4},{9,1},{1... | collective-permute-start | bytes 786440 | tf_op jit(solution)/shard_map/ppermute | solution.py:578
  10.4 19.0 %collective-permute-start.1 = (bf16[128,1024]{1,0:T(8,128)(2,1)S(1)}, bf16[128,1024]{1,0:T(8,128)(2,1)S(1)}, u32[]{:S(2)}, u32[]{:S(2)}) collective-permute-start(bf16[128,1024]{1,0:T(8,128)(2,1)S(1)} %slice.27.rest_0_), channel_id=1, source_target_pairs={{0,8},{8,16},{16,24},{24,28},{28,20},{20,12},{12,4},{4,0},{1,9},{9... | collective-permute-start | bytes 786440 | tf_op jit(solution)/shard_map/ppermute | solution.py:578
  10.6 18.9 %collective-permute-start.3 = (bf16[128,2048]{1,0:T(8,128)(2,1)S(1)}, bf16[128,2048]{1,0:T(8,128)(2,1)S(1)}, u32[]{:S(2)}, u32[]{:S(2)}) collective-permute-start(bf16[128,2048]{1,0:T(8,128)(2,1)S(1)} %pad_maximum_fusion.2.refs_0_), channel_id=1, source_target_pairs={{0,2},{2,0},{1,3},{3,1},{4,6},{6,4},{5,7},{7,5},{8,10},{10,8},{9,1... | collective-permute-start | bytes 1572872 | tf_op jit(solution)/shard_map/ppermute | solution.py:579
  13.2 30.7 %collective-permute-start.10 = (bf16[256,4096]{1,0:T(8,128)(2,1)S(1)}, bf16[256,4096]{1,0:T(8,128)(2,1)S(1)}, u32[]{:S(2)}, u32[]{:S(2)}) collective-permute-start(bf16[256,4096]{1,0:T(8,128)(2,1)S(1)} %dynamic-slice_dynamic-update-slice_fusion.1.near_ref), channel_id=1, source_target_pairs={{0,1},{1,0},{2,3},{3,2},{4,5},{5,4},{6,7},{7,6},{8,9},{9,8},{10,11... | collective-permute-start | bytes 6291464 | tf_op jit(solution)/shard_map/ppermute | solution.py:810
  14.5 31.7 %copy-start.6 = (bf16[512,256]{1,0:T(8,128)(2,1)}, bf16[512,256]{1,0:T(8,128)(2,1)S(1)}, u32[]{:S(2)}) copy-start(bf16[512,256]{1,0:T(8,128)(2,1)S(1)} %pad_maximum_fusion.5.c_ref) | copy-start | bytes 786436
  14.5 7.5 %copy-start.4 = (bf16[512,256]{1,0:T(8,128)(2,1)}, bf16[512,256]{1,0:T(8,128)(2,1)S(1)}, u32[]{:S(2)}) copy-start(bf16[512,256]{1,0:T(8,128)(2,1)S(1)} %pad_maximum_fusion.4.b_ref) | copy-start | bytes 786436
  29.5 4.1 %copy-start.30 = (bf16[128,1024]{1,0:T(8,128)(2,1)}, bf16[128,1024]{1,0:T(8,128)(2,1)S(1)}, u32[]{:S(2)}) copy-start(bf16[128,1024]{1,0:T(8,128)(2,1)S(1)} %collective-permute-done.2.refs_3_.rest_4_) | copy-start | bytes 786436
  29.5 4.1 %copy-start.32 = (bf16[128,1024]{1,0:T(8,128)(2,1)}, bf16[128,1024]{1,0:T(8,128)(2,1)S(1)}, u32[]{:S(2)}) copy-start(bf16[128,1024]{1,0:T(8,128)(2,1)S(1)} %collective-permute-done.1.refs_2_.rest_2_) | copy-start | bytes 786436
  29.5 4.1 %copy-start.34 = (bf16[128,2048]{1,0:T(8,128)(2,1)}, bf16[128,2048]{1,0:T(8,128)(2,1)S(1)}, u32[]{:S(2)}) copy-start(bf16[128,2048]{1,0:T(8,128)(2,1)S(1)} %collective-permute-done.3.refs_1_) | copy-start | bytes 1572868
  29.6 14.3 %collective-permute-start.11 = (bf16[256,1024]{1,0:T(8,128)(2,1)S(1)}, bf16[256,1024]{1,0:T(8,128)(2,1)S(1)}, u32[]{:S(2)}, u32[]{:S(2)}) collective-permute-start(bf16[256,1024]{1,0:T(8,128)(2,1)S(1)} %pad_maximum_fusion.3), channel_id=1, source_target_pairs={{0,2},{1,3},{4,6},{5,7},{8,10},{9,11},{12,14},{13,15},{16,18},{17,... | collective-permute-start | bytes 1572872 | tf_op jit(solution)/shard_map/ppermute | solution.py:846
  32.2 11.8 %copy-start.8 = (bf16[64,4096]{1,0:T(8,128)(2,1)S(1)}, bf16[64,4096]{1,0:T(8,128)(2,1)}, u32[]{:S(2)}) copy-start(bf16[64,4096]{1,0:T(8,128)(2,1)} %down_ref.7) | copy-start | bytes 1572868
  32.2 11.7 %copy-start.36 = (f32[4096]{0:T(1024)S(1)}, f32[4096]{0:T(1024)}, u32[]{:S(2)}) copy-start(f32[4096]{0:T(1024)} %param.23) | copy-start | bytes 49156
  32.2 1.3 collective-permute-start.9
  34.6 20.2 %collective-permute-start.8 = (bf16[256,1024]{1,0:T(8,128)(2,1)S(1)}, bf16[256,1024]{1,0:T(8,128)(2,1)S(1)}, u32[]{:S(2)}, u32[]{:S(2)}) collective-permute-start(bf16[256,1024]{1,0:T(8,128)(2,1)S(1)} %get-tuple-element.135), channel_id=1, source_target_pairs={{0,2},{2,0},{1,3},{3,1},{4,6},{6,4},{5,7},{7,5},{8,10},{10,8},{9,1... | collective-permute-start | bytes 1572872 | tf_op jit(solution)/shard_map/ppermute | solution.py:579
  34.6 20.2 %collective-permute-start.6 = (bf16[384,1024]{1,0:T(8,128)(2,1)S(1)}, bf16[384,1024]{1,0:T(8,128)(2,1)S(1)}, u32[]{:S(2)}, u32[]{:S(2)}) collective-permute-start(bf16[384,1024]{1,0:T(8,128)(2,1)S(1)} %get-tuple-element.133), channel_id=1, source_target_pairs={{0,8},{8,16},{16,24},{24,28},{28,20},{20,12},{12,4},{4,0},{1,9},{9... | collective-permute-start | bytes 2359304 | tf_op jit(solution)/shard_map/ppermute | solution.py:578
  36.5 19.5 %collective-permute-start.7 = (bf16[384,1024]{1,0:T(8,128)(2,1)S(1)}, bf16[384,1024]{1,0:T(8,128)(2,1)}, u32[]{:S(2)}, u32[]{:S(2)}) collective-permute-start(bf16[384,1024]{1,0:T(8,128)(2,1)S(1)} %get-tuple-element.134), channel_id=1, source_target_pairs={{8,0},{16,8},{24,16},{28,24},{20,28},{12,20},{4,12},{0,4},{9,1},{1... | collective-permute-start | bytes 2359304 | tf_op jit(solution)/shard_map/ppermute | solution.py:578
  50.3 9.7 %copy-start.13 = (bf16[512,1024]{1,0:T(8,128)(2,1)}, bf16[512,1024]{1,0:T(8,128)(2,1)S(1)}, u32[]{:S(2)}) copy-start(bf16[512,1024]{1,0:T(8,128)(2,1)S(1)} %get-tuple-element.194.hat_ref) | copy-start | bytes 3145732
  50.3 9.7 %copy-start.15 = (bf16[512,1024]{1,0:T(8,128)(2,1)}, bf16[512,1024]{1,0:T(8,128)(2,1)S(1)}, u32[]{:S(2)}) copy-start(bf16[512,1024]{1,0:T(8,128)(2,1)S(1)} %get-tuple-element.195.slope_ref) | copy-start | bytes 3145732
  50.4 5.6 %collective-permute-start.12 = (f32[256,64]{1,0:T(8,128)S(1)}, f32[256,64]{1,0:T(8,128)S(1)}, u32[]{:S(2)}, u32[]{:S(2)}) collective-permute-start(f32[256,64]{1,0:T(8,128)S(1)} %get-tuple-element.231), channel_id=1, source_target_pairs={{0,1},{1,0},{2,3},{3,2},{4,5},{5,4},{6,7},{7,6},{8,9},{9,8},{10,11... | collective-permute-start | bytes 196616 | tf_op jit(solution)/shard_map/ppermute | solution.py:810
  54.7 7.4 %copy-start.10 = (bf16[256,1024]{1,0:T(8,128)(2,1)}, bf16[256,1024]{1,0:T(8,128)(2,1)S(1)}, u32[]{:S(2)}) copy-start(bf16[256,1024]{1,0:T(8,128)(2,1)S(1)} %collective-permute-done.8.rest_3_.rest_5_) | copy-start | bytes 1572868
  56.0 24.8 %collective-permute-start.13 = (bf16[384,1024]{1,0:T(8,128)(2,1)S(1)}, bf16[384,1024]{1,0:T(8,128)(2,1)}, u32[]{:S(2)}, u32[]{:S(2)}) collective-permute-start(bf16[384,1024]{1,0:T(8,128)(2,1)S(1)} %collective-permute-done.6.refs_0_.rest_1_), channel_id=1, source_target_pairs={{0,8},{8,16},{16,24},{24,28},{28,20},{20,12},{12,4},{4,0},{1,9},{9... | collective-permute-start | bytes 2359304 | tf_op jit(solution)/shard_map/ppermute | solution.py:578
  57.6 23.3 %collective-permute-start.14 = (bf16[384,1024]{1,0:T(8,128)(2,1)}, bf16[384,1024]{1,0:T(8,128)(2,1)}, u32[]{:S(2)}, u32[]{:S(2)}) collective-permute-start(bf16[384,1024]{1,0:T(8,128)(2,1)} %collective-permute-done.7.refs_1_.rest_2_.rest_3_), channel_id=1, source_target_pairs={{8,0},{16,8},{24,16},{28,24},{20,28},{12,20},{4,12},{0,4},{9,1},{1... | collective-permute-start | bytes 2359304 | tf_op jit(solution)/shard_map/ppermute | solution.py:578
  60.0 20.8 %collective-permute-start.15 = (bf16[256,1024]{1,0:T(8,128)(2,1)}, bf16[256,1024]{1,0:T(8,128)(2,1)}, u32[]{:S(2)}, u32[]{:S(2)}) collective-permute-start(bf16[256,1024]{1,0:T(8,128)(2,1)} %cut_rows.5), channel_id=1, source_target_pairs={{0,2},{2,0},{1,3},{3,1},{4,6},{6,4},{5,7},{7,5},{8,10},{10,8},{9,1... | collective-permute-start | bytes 1572872 | tf_op jit(solution)/shard_map/ppermute | solution.py:579
  62.1 1.4 collective-permute-start.16
  66.0 12.7 %collective-permute-start.17 = (bf16[8,64,192]{2,1,0:T(8,128)(2,1)}, bf16[8,64,192]{2,1,0:T(8,128)(2,1)}, u32[]{:S(2)}, u32[]{:S(2)}) collective-permute-start(bf16[8,64,192]{2,1,0:T(8,128)(2,1)} %get-tuple-element.165), channel_id=1, source_target_pairs={{0,2},{2,0},{1,3},{3,1},{4,6},{6,4},{5,7},{7,5},{8,10},{10,8},{9,1... | collective-permute-start | bytes 589832 | tf_op jit(solution)/shard_map/ppermute | solution.py:752
  80.8 5.5 %copy-start.35 = (bf16[128,2048]{1,0:T(8,128)(2,1)S(1)}, bf16[128,2048]{1,0:T(8,128)(2,1)}, u32[]{:S(2)}) copy-start(bf16[128,2048]{1,0:T(8,128)(2,1)} %copy-done.34) | copy-start | bytes 1572868
  80.9 5.5 %copy-start.3 = (bf16[256,4096]{1,0:T(8,128)(2,1)S(1)}, bf16[256,4096]{1,0:T(8,128)(2,1)}, u32[]{:S(2)}) copy-start(bf16[256,4096]{1,0:T(8,128)(2,1)} %copy-done.2) | copy-start | bytes 6291460
  80.9 5.5 %copy-start.27 = (bf16[256,1024]{1,0:T(8,128)(2,1)S(1)}, bf16[256,1024]{1,0:T(8,128)(2,1)}, u32[]{:S(2)}) copy-start(bf16[256,1024]{1,0:T(8,128)(2,1)} %copy-done.26) | copy-start | bytes 1572868
  82.5 23.4 %collective-permute-start.18 = (bf16[320,1024]{1,0:T(8,128)(2,1)S(1)}, bf16[320,1024]{1,0:T(8,128)(2,1)S(1)}, u32[]{:S(2)}, u32[]{:S(2)}) collective-permute-start(bf16[320,1024]{1,0:T(8,128)(2,1)S(1)} %get-tuple-element.170), channel_id=1, source_target_pairs={{0,8},{8,16},{16,24},{24,28},{28,20},{20,12},{12,4},{4,0},{1,9},{9... | collective-permute-start | bytes 1966088 | tf_op jit(solution)/shard_map/ppermute | solution.py:578
  84.3 21.6 %collective-permute-start.19 = (bf16[320,1024]{1,0:T(8,128)(2,1)S(1)}, bf16[320,1024]{1,0:T(8,128)(2,1)S(1)}, u32[]{:S(2)}, u32[]{:S(2)}) collective-permute-start(bf16[320,1024]{1,0:T(8,128)(2,1)S(1)} %get-tuple-element.171), channel_id=1, source_target_pairs={{8,0},{16,8},{24,16},{28,24},{20,28},{12,20},{4,12},{0,4},{9,1},{1... | collective-permute-start | bytes 1966088 | tf_op jit(solution)/shard_map/ppermute | solution.py:578
  84.6 21.3 %collective-permute-start.20 = (bf16[256,1024]{1,0:T(8,128)(2,1)S(1)}, bf16[256,1024]{1,0:T(8,128)(2,1)S(1)}, u32[]{:S(2)}, u32[]{:S(2)}) collective-permute-start(bf16[256,1024]{1,0:T(8,128)(2,1)S(1)} %get-tuple-element.172), channel_id=1, source_target_pairs={{0,2},{2,0},{1,3},{3,1},{4,6},{6,4},{5,7},{7,5},{8,10},{10,8},{9,1... | collective-permute-start | bytes 1572872 | tf_op jit(solution)/shard_map/ppermute | solution.py:579
  89.7 16.1 %collective-permute-start.21 = (bf16[4,64,192]{2,1,0:T(8,128)(2,1)S(1)}, bf16[4,64,192]{2,1,0:T(8,128)(2,1)S(1)}, u32[]{:S(2)}, u32[]{:S(2)}) collective-permute-start(bf16[4,64,192]{2,1,0:T(8,128)(2,1)S(1)} %get-tuple-element.174), channel_id=1, source_target_pairs={{0,16},{4,20},{8,24},{12,28},{16,0},{20,4},{24,8},{28,12},{1,17},{... | collective-permute-start | bytes 294920 | tf_op jit(solution)/shard_map/ppermute | solution.py:756
  105.9 6.9 %collective-permute-start.25 = (bf16[4,64,192]{2,1,0:T(8,128)(2,1)S(1)}, bf16[4,64,192]{2,1,0:T(8,128)(2,1)S(1)}, u32[]{:S(2)}, u32[]{:S(2)}) collective-permute-start(bf16[4,64,192]{2,1,0:T(8,128)(2,1)S(1)} %get-tuple-element.186), channel_id=1, source_target_pairs={{0,8},{4,12},{8,0},{12,4},{16,24},{20,28},{24,16},{28,20},{1,9},{5... | collective-permute-start | bytes 294920 | tf_op jit(solution)/shard_map/ppermute | solution.py:756
  106.1 7.2 %collective-permute-start.22 = (bf16[128,1024]{1,0:T(8,128)(2,1)S(1)}, bf16[128,1024]{1,0:T(8,128)(2,1)S(1)}, u32[]{:S(2)}, u32[]{:S(2)}) collective-permute-start(bf16[128,1024]{1,0:T(8,128)(2,1)S(1)} %get-tuple-element.182), channel_id=1, source_target_pairs={{0,8},{8,16},{16,24},{24,28},{28,20},{20,12},{12,4},{4,0},{1,9},{9... | collective-permute-start | bytes 786440 | tf_op jit(solution)/shard_map/ppermute | solution.py:578
  108.1 6.4 %collective-permute-start.23 = (bf16[128,1024]{1,0:T(8,128)(2,1)S(1)}, bf16[128,1024]{1,0:T(8,128)(2,1)S(1)}, u32[]{:S(2)}, u32[]{:S(2)}) collective-permute-start(bf16[128,1024]{1,0:T(8,128)(2,1)S(1)} %get-tuple-element.183), channel_id=1, source_target_pairs={{8,0},{16,8},{24,16},{28,24},{20,28},{12,20},{4,12},{0,4},{9,1},{1... | collective-permute-start | bytes 786440 | tf_op jit(solution)/shard_map/ppermute | solution.py:578
  108.2 6.4 %collective-permute-start.24 = (bf16[128,1024]{1,0:T(8,128)(2,1)S(1)}, bf16[128,1024]{1,0:T(8,128)(2,1)S(1)}, u32[]{:S(2)}, u32[]{:S(2)}) collective-permute-start(bf16[128,1024]{1,0:T(8,128)(2,1)S(1)} %get-tuple-element.184), channel_id=1, source_target_pairs={{0,2},{2,0},{1,3},{3,1},{4,6},{6,4},{5,7},{7,5},{8,10},{10,8},{9,1... | collective-permute-start | bytes 786440 | tf_op jit(solution)/shard_map/ppermute | solution.py:579
  112.8 3.0 %copy-start.7 = (bf16[512,256]{1,0:T(8,128)(2,1)S(1)}, bf16[512,256]{1,0:T(8,128)(2,1)}, u32[]{:S(2)}) copy-start(bf16[512,256]{1,0:T(8,128)(2,1)} %copy-done.6) | copy-start | bytes 786436
  112.8 3.0 %copy-start.9 = (bf16[64,4096]{1,0:T(8,128)(2,1)S(1)}, bf16[64,4096]{1,0:T(8,128)(2,1)}, u32[]{:S(2)}) copy-start(bf16[64,4096]{1,0:T(8,128)(2,1)} %down_ref.7) | copy-start | bytes 1572868
  114.5 5.0 %collective-permute-start.27 = (bf16[4,64,192]{2,1,0:T(8,128)(2,1)S(1)}, bf16[4,64,192]{2,1,0:T(8,128)(2,1)S(1)}, u32[]{:S(2)}, u32[]{:S(2)}) collective-permute-start(bf16[4,64,192]{2,1,0:T(8,128)(2,1)S(1)} %get-tuple-element.205), channel_id=1, source_target_pairs={{0,4},{4,0},{8,12},{12,8},{16,20},{20,16},{24,28},{28,24},{1,5},{5... | collective-permute-start | bytes 294920 | tf_op jit(solution)/shard_map/ppermute | solution.py:756
  117.6 3.9 %copy-start.23 = (bf16[512,1024]{1,0:T(8,128)(2,1)S(1)}, bf16[512,1024]{1,0:T(8,128)(2,1)}, u32[]{:S(2)}) copy-start(bf16[512,1024]{1,0:T(8,128)(2,1)} %copy-done.22) | copy-start | bytes 3145732
  117.6 3.9 %copy-start.25 = (bf16[512,1024]{1,0:T(8,128)(2,1)S(1)}, bf16[512,1024]{1,0:T(8,128)(2,1)}, u32[]{:S(2)}) copy-start(bf16[512,1024]{1,0:T(8,128)(2,1)} %copy-done.24) | copy-start | bytes 3145732
  117.6 16.7 %collective-permute-start.26 = (bf16[128,1024]{1,0:T(8,128)(2,1)S(1)}, bf16[128,1024]{1,0:T(8,128)(2,1)S(1)}, u32[]{:S(2)}, u32[]{:S(2)}) collective-permute-start(bf16[128,1024]{1,0:T(8,128)(2,1)S(1)} %get-tuple-element.198), channel_id=1, source_target_pairs={{2,0},{3,1},{6,4},{7,5},{10,8},{11,9},{14,12},{15,13},{18,16},{19,... | collective-permute-start | bytes 786440 | tf_op jit(solution)/shard_map/ppermute | solution.py:846
  119.7 5.0 %copy-start.18 = (f32[512,64]{1,0:T(8,128)S(1)}, f32[512,64]{1,0:T(8,128)}, u32[]{:S(2)}) copy-start(f32[512,64]{1,0:T(8,128)} %copy-done.17) | copy-start | bytes 393220
  119.7 5.0 %copy-start.40 = (bf16[512,4096]{1,0:T(8,128)(2,1)S(1)}, bf16[512,4096]{1,0:T(8,128)(2,1)}, u32[]{:S(2)}) copy-start(bf16[512,4096]{1,0:T(8,128)(2,1)} %get-tuple-element.213.scores_ref) | copy-start | bytes 12582916
  119.7 4.9 %collective-permute-start.32 = (f32[8,128]{1,0:T(8,128)S(1)}, f32[8,128]{1,0:T(8,128)S(1)}, u32[]{:S(2)}, u32[]{:S(2)}) collective-permute-start(f32[8,128]{1,0:T(8,128)S(1)} %get-tuple-element.220), channel_id=1, source_target_pairs={{0,16},{4,20},{8,24},{12,28},{16,0},{20,4},{24,8},{28,12},{1,17},{... | collective-permute-start | bytes 12296 | tf_op jit(solution)/shard_map/ppermute | solution.py:756
  123.3 9.0 %collective-permute-start.28 = (bf16[128,1024]{1,0:T(8,128)(2,1)S(1)}, bf16[128,1024]{1,0:T(8,128)(2,1)S(1)}, u32[]{:S(2)}, u32[]{:S(2)}) collective-permute-start(bf16[128,1024]{1,0:T(8,128)(2,1)S(1)} %get-tuple-element.211), channel_id=1, source_target_pairs={{2,0},{3,1},{6,4},{7,5},{10,8},{11,9},{14,12},{15,13},{18,16},{19,... | collective-permute-start | bytes 786440 | tf_op jit(solution)/shard_map/ppermute | solution.py:846
  124.6 2.2 %collective-permute-start.33 = (f32[8,128]{1,0:T(8,128)S(1)}, f32[8,128]{1,0:T(8,128)S(1)}, u32[]{:S(2)}, u32[]{:S(2)}) collective-permute-start(f32[8,128]{1,0:T(8,128)S(1)} %add.345), channel_id=1, source_target_pairs={{0,1},{1,0},{2,3},{3,2},{4,5},{5,4},{6,7},{7,6},{8,9},{9,8},{10,11... | collective-permute-start | bytes 12296 | tf_op jit(solution)/shard_map/ppermute | solution.py:783
  124.7 4.9 %copy-start.39 = (bf16[512,4096]{1,0:T(8,128)(2,1)S(1)}, bf16[512,4096]{1,0:T(8,128)(2,1)}, u32[]{:S(2)}) copy-start(bf16[512,4096]{1,0:T(8,128)(2,1)} %get-tuple-element.201.scores_ref) | copy-start | bytes 12582916
  126.9 4.8 %collective-permute-start.34 = (f32[8,128]{1,0:T(8,128)S(1)}, f32[8,128]{1,0:T(8,128)S(1)}, u32[]{:S(2)}, u32[]{:S(2)}) collective-permute-start(f32[8,128]{1,0:T(8,128)S(1)} %add.346), channel_id=1, source_target_pairs={{0,2},{2,0},{1,3},{3,1},{4,6},{6,4},{5,7},{7,5},{8,10},{10,8},{9,1... | collective-permute-start | bytes 12296 | tf_op jit(solution)/shard_map/ppermute | solution.py:783
  133.6 4.8 %collective-permute-start.31 = (f32[64,192]{1,0:T(8,128)S(1)}, f32[64,192]{1,0:T(8,128)S(1)}, u32[]{:S(2)}, u32[]{:S(2)}) collective-permute-start(f32[64,192]{1,0:T(8,128)S(1)} %get-tuple-element.219), channel_id=1, source_target_pairs={{0,0},{1,16},{2,1},{3,17},{4,2},{5,18},{6,3},{7,19},{8,4},{9,20},{... | collective-permute-start | bytes 147464 | tf_op jit(solution)/shard_map/ppermute | solution.py:976
  135.7 5.3 %collective-permute-start.30 = (bf16[256,1024]{1,0:T(8,128)(2,1)S(1)}, bf16[256,1024]{1,0:T(8,128)(2,1)S(1)}, u32[]{:S(2)}, u32[]{:S(2)}) collective-permute-start(bf16[256,1024]{1,0:T(8,128)(2,1)S(1)} %get-tuple-element.218), channel_id=1, source_target_pairs={{0,1},{1,0},{2,3},{3,2},{4,5},{5,4},{6,7},{7,6},{8,9},{9,8},{10,11... | collective-permute-start | bytes 1572872 | tf_op jit(solution)/shard_map/ppermute | solution.py:810
  138.3 2.7 %collective-permute-start.29 = (bf16[256,1024]{1,0:T(8,128)(2,1)S(1)}, bf16[256,1024]{1,0:T(8,128)(2,1)S(1)}, u32[]{:S(2)}, u32[]{:S(2)}) collective-permute-start(bf16[256,1024]{1,0:T(8,128)(2,1)S(1)} %get-tuple-element.217), channel_id=1, source_target_pairs={{0,1},{1,0},{2,3},{3,2},{4,5},{5,4},{6,7},{7,6},{8,9},{9,8},{10,11... | collective-permute-start | bytes 1572872 | tf_op jit(solution)/shard_map/ppermute | solution.py:810
  (21 other events, 38.9 us)

commit v4 on v3

--- a/solution.py
+++ b/solution.py
@@ -51,6 +51,13 @@
     return jnp.concatenate(
         [jnp.where(lane < P_SIZE, pair, zero), jnp.where(lane >= P_SIZE, pair, zero)], axis=0
     )
+
+
+def of_quarter(ref, rows, quarter, heads):
+    value = ref[rows, :heads]
+    for index in range(1, ref.shape[1] // heads):
+        value = jnp.where(quarter == index, ref[rows, index * heads : (index + 1) * heads], value)
+    return value
 
 
 def whole(shape):
@@ -114,18 +121,19 @@
 
 
 def local_kernel(
-    first, heads, core_ref, near_ref, far_ref, b_ref, c_ref, step_ref, cum_ref, cum_t_ref, skip_ref,
-    pattern_ref, scores_ref, ssd_ref, state_ref, total_ref, x_ref,
+    heads, core_ref, near_ref, far_ref, b_ref, c_ref, step_ref, cum_ref, cum_t_ref, skip_ref,
+    pattern_ref, top_ref, low_ref, ssd_ref, state_ref, sent_ref, x_ref, total_ref,
 ):
-    block = pl.program_id(0)
+    block = pl.program_id(1)
     core = core_ref[0]
+    quarter = core * pl.num_programs(0) + pl.program_id(0)
     x_ref[...] = jnp.where(
-        block // (pl.num_programs(0) // 2) == core, near_ref[...], far_ref[...]
+        block // (pl.num_programs(1) // 2) == core, near_ref[...], far_ref[...]
     )
     pattern = pattern_ref[...]
-    step = of_core(step_ref, slice(None), core, first, heads)
-    cum = of_core(cum_ref, slice(None), core, first, heads)
-    start = pl.multiple_of(core * (cum_t_ref.shape[1] // 2) + first, 8)
+    step = of_quarter(step_ref, slice(None), quarter, heads)
+    cum = of_quarter(cum_ref, slice(None), quarter, heads)
+    start = pl.multiple_of(quarter * heads, 8)
     cum_t = cum_t_ref[0, pl.ds(start, heads), :]
     last = cum[Q - 1 : Q, :]
     step_wide = spread(step, pattern)
@@ -144,78 +152,99 @@
     def _():
         total_ref[...] = total_ref[...] * decay + state
 
+    sent_ref[...] = total_ref[...].astype(sent_ref.dtype)
+
+    half = Q // 2
     inner = dot(b_ref[...], c_ref[...], ((1,), (1,)))
-    causal = lax.broadcasted_iota(jnp.int32, (Q, Q), 1) >= lax.broadcasted_iota(
-        jnp.int32, (Q, Q), 0
-    )
-    masked = jnp.where(causal, inner, 0.0)
+    causal = lax.broadcasted_iota(jnp.int32, (half, half), 1) >= lax.broadcasted_iota(
+        jnp.int32, (half, half), 0
+    )
+    corner = jnp.where(causal, inner[:half, :half], 0.0)
+    right = inner[:half, half:]
+    end = jnp.where(causal, inner[half:, half:], 0.0)
     for pair in range(heads // 2):
-        parts = []
+        corners, rights = [], []
         for head in (2 * pair, 2 * pair + 1):
-            gap = cum_t[head : head + 1, :] - cum[:, head : head + 1]
-            part = (masked * jnp.exp(jnp.where(causal, gap, 0.0))).astype(BF16)
-            scores_ref[:, head * Q : (head + 1) * Q] = part
-            parts.append(part)
+            across, down = cum_t[head : head + 1, :], cum[:, head : head + 1]
+            gap = across[:, :half] - down[:half, :]
+            first = (corner * jnp.exp(jnp.where(causal, gap, 0.0))).astype(BF16)
+            second = (right * jnp.exp(across[:, half:] - down[:half, :])).astype(BF16)
+            gap = across[:, half:] - down[half:, :]
+            third = (end * jnp.exp(jnp.where(causal, gap, 0.0))).astype(BF16)
+            top_ref[:, head * Q : head * Q + half] = first
+            top_ref[:, head * Q + half : (head + 1) * Q] = second
+            low_ref[:, head * half : (head + 1) * half] = third
+            corners.append(first)
+            rights += [second, third]
         lanes = slice(pair * 2 * P_SIZE, (pair + 1) * 2 * P_SIZE)
-        intra = dot(jnp.concatenate(parts, axis=0), pair_rows(xdt[:, lanes]), ((0,), (0,)))
-        ssd_ref[:, lanes] = (
-            intra + skip_ref[:, lanes] * x_ref[:, lanes].astype(F32)
-        ).astype(ssd_ref.dtype)
-
-
-def local_part(group, groups, heads, core, near, far, b, c, step, cum, cum_t, skip, pattern):
+        values = xdt[:, lanes]
+        intra = (
+            dot(jnp.concatenate(corners, axis=0), pair_rows(values[:half, :]), ((0,), (0,))),
+            dot(jnp.concatenate(rights, axis=0), pair_rows(values), ((0,), (0,))),
+        )
+        for part, rows in zip(intra, (slice(0, half), slice(half, Q))):
+            ssd_ref[rows, lanes] = (
+                part + skip_ref[:, lanes] * x_ref[rows, lanes].astype(F32)
+            ).astype(ssd_ref.dtype)
+
+
+def local_part(groups, heads, core, near, far, b, c, step, cum, cum_t, skip, pattern):
     rows = 2 * near.shape[0]
     blocks = rows // Q
     width = heads * P_SIZE
-    row_block = pl.BlockSpec((Q, width), lambda i, s: (i, 0))
+    row_block = pl.BlockSpec((Q, width), lambda g, i, s: (g * blocks + i, 0))
     spec = pltpu.PrefetchScalarGridSpec(
         num_scalar_prefetch=1,
-        grid=(blocks,),
+        grid=(groups, blocks),
         in_specs=[
-            pl.BlockSpec((Q, width), lambda i, s: (i % (blocks // 2), s[0] * groups + group)),
-            pl.BlockSpec((Q, width), lambda i, s: (i % (blocks // 2), group)),
-            pl.BlockSpec((Q, N), lambda i, s: (i, group)),
-            pl.BlockSpec((Q, N), lambda i, s: (i, group)),
-            pl.BlockSpec((Q, step.shape[1]), lambda i, s: (i, 0)),
-            pl.BlockSpec((Q, step.shape[1]), lambda i, s: (i, 0)),
-            pl.BlockSpec((1,) + cum_t.shape[1:], lambda i, s: (i, 0, 0)),
-            pl.BlockSpec((1, width), lambda i, s: (0, s[0] * groups + group)),
+            pl.BlockSpec((Q, width), lambda g, i, s: (i % (blocks // 2), s[0] * groups + g)),
+            pl.BlockSpec((Q, width), lambda g, i, s: (i % (blocks // 2), g)),
+            pl.BlockSpec((Q, N), lambda g, i, s: (i, g)),
+            pl.BlockSpec((Q, N), lambda g, i, s: (i, g)),
+            pl.BlockSpec((Q, step.shape[1]), lambda g, i, s: (i, 0)),
+            pl.BlockSpec((Q, step.shape[1]), lambda g, i, s: (i, 0)),
+            pl.BlockSpec((1,) + cum_t.shape[1:], lambda g, i, s: (i, 0, 0)),
+            pl.BlockSpec((1, width), lambda g, i, s: (0, s[0] * groups + g)),
             whole(pattern.shape),
         ],
         out_specs=[
-            pl.BlockSpec((Q, heads * Q), lambda i, s: (i, 0)),
+            pl.BlockSpec((Q // 2, heads * Q), lambda g, i, s: (g * blocks + i, 0)),
+            pl.BlockSpec((Q // 2, heads * Q // 2), lambda g, i, s: (g * blocks + i, 0)),
             row_block,
-            pl.BlockSpec((N, width), lambda i, s: (i, 0)),
-            pl.BlockSpec((N, width), lambda i, s: (0, 0)),
+            pl.BlockSpec((N, width), lambda g, i, s: (g * blocks + i, 0)),
+            pl.BlockSpec((N, width), lambda g, i, s: (g, 0)),
         ],
-        scratch_shapes=[pltpu.VMEM((Q, width), BF16)],
+        scratch_shapes=[pltpu.VMEM((Q, width), BF16), pltpu.VMEM((N, width), F32)],
     )
     return pl.pallas_call(
-        functools.partial(local_kernel, group * heads, heads),
+        functools.partial(local_kernel, heads),
         grid_spec=spec,
         out_shape=[
-            pltpu.HBM((rows, heads * Q), BF16),
-            jax.ShapeDtypeStruct((rows, width), BF16),
-            jax.ShapeDtypeStruct((blocks * N, width), F32),
-            jax.ShapeDtypeStruct((N, width), F32),
+            pltpu.HBM((groups * rows // 2, heads * Q), BF16),
+            pltpu.HBM((groups * rows // 2, heads * Q // 2), BF16),
+            jax.ShapeDtypeStruct((groups * rows, width), BF16),
+            jax.ShapeDtypeStruct((groups * blocks * N, width), F32),
+            jax.ShapeDtypeStruct((groups * N, width), BF16),
         ],
-        compiler_params=params("arbitrary"),
-        cost_estimate=cost(rows * width * Q * 4, 18),
+        compiler_params=params("arbitrary", "arbitrary"),
+        cost_estimate=cost(groups * rows * width * Q * 4, 16),
         name="local_part",
     )(core, near, far, b, c, step, cum, cum_t, skip, pattern)
 
 
 def norm_kernel(
-    blocks, first, heads, core_ref, c_ref, incoming_ref, state_ref, cum_ref, pattern_ref, ssd_ref, near_ref,
+    blocks, heads, core_ref, c_ref, incoming_ref, state_ref, cum_ref, pattern_ref, ssd_ref, near_ref,
     far_ref, gain_ref, down_ref, up_ref, hat_ref, slope_ref, product_ref, sum_ref,
 ):
     gain = gain_ref[...]
+    group = pl.program_id(0)
+    quarter = core_ref[0] * pl.num_programs(0) + group
     run = incoming_ref[...].astype(F32)
     total = None
     for block in range(blocks):
         rows = slice(block * Q, (block + 1) * Q)
         inter = dot(c_ref[rows, :], run.astype(BF16))
-        growth = spread(jnp.exp(of_core(cum_ref, rows, core_ref[0], first, heads)), pattern_ref[...])
+        growth = spread(jnp.exp(of_quarter(cum_ref, rows, quarter, heads)), pattern_ref[...])
         ssd = ssd_ref[rows, :].astype(F32) + growth * inter
         local = slice(block % (blocks // 2) * Q, (block % (blocks // 2) + 1) * Q)
         z = jnp.where(
@@ -228,7 +257,8 @@
         normed = (hat * gain).astype(BF16)
         hat_ref[rows, :] = hat.astype(hat_ref.dtype)
         slope_ref[rows, :] = (rstd * silu).astype(slope_ref.dtype)
-        product_ref[rows, :] = dot(normed, down_ref[...], ((1,), (1,)))
+        product = dot(normed, down_ref[...], ((1,), (1,)))
+        product_ref[rows, :] = jnp.where(group == 0, product, product_ref[rows, :] + product)
         part = dot(up_ref[rows, :], normed, ((0,), (0,)))
         total = part if total is None else total + part
         if block + 1 < blocks:
@@ -237,43 +267,45 @@
     sum_ref[...] = total
 
 
-def norm_part(
-    group, groups, heads, core, c, incoming, state, cum, pattern, ssd, near, far, gain, down, up_twice
-):
-    rows, width = ssd.shape
+def norm_part(groups, heads, core, c, incoming, state, cum, pattern, ssd, near, far, gain, down, up_twice):
+    rows, width = 2 * near.shape[0], heads * P_SIZE
     rank = down.shape[0]
     blocks = rows // Q
+    group_rows = pl.BlockSpec((rows, width), lambda g, s: (g, 0))
     spec = pltpu.PrefetchScalarGridSpec(
         num_scalar_prefetch=1,
-        grid=(1,),
+        grid=(groups,),
         in_specs=[
-            pl.BlockSpec((rows, N), lambda i, s: (0, group)),
-            pl.BlockSpec((N, width), lambda i, s: (group, 0)),
-            whole(state.shape),
+            pl.BlockSpec((rows, N), lambda g, s: (0, g)),
+            pl.BlockSpec((N, width), lambda g, s: (g, 0)),
+            pl.BlockSpec((blocks * N, width), lambda g, s: (g, 0)),
             whole(cum.shape),
             whole(pattern.shape),
-            whole(ssd.shape),
-            pl.BlockSpec((rows // 2, width), lambda i, s: (0, s[0] * groups + group)),
-            pl.BlockSpec((rows // 2, width), lambda i, s: (0, group)),
-            pl.BlockSpec((1, width), lambda i, s: (0, s[0] * groups + group)),
-            pl.BlockSpec((rank, width), lambda i, s: (0, s[0] * groups + group)),
+            group_rows,
+            pl.BlockSpec((rows // 2, width), lambda g, s: (0, s[0] * groups + g)),
+            pl.BlockSpec((rows // 2, width), lambda g, s: (0, g)),
+            pl.BlockSpec((1, width), lambda g, s: (0, s[0] * groups + g)),
+            pl.BlockSpec((rank, width), lambda g, s: (0, s[0] * groups + g)),
             whole(up_twice.shape),
         ],
         out_specs=[
-            whole((rows, width)), whole((rows, width)), whole((rows, rank)), whole((rank, width)),
+            group_rows,
+            group_rows,
+            whole((rows, rank)),
+            pl.BlockSpec((rank, width), lambda g, s: (0, g)),
         ],
     )
     return pl.pallas_call(
-        functools.partial(norm_kernel, blocks, group * heads, heads),
+        functools.partial(norm_kernel, blocks, heads),
         grid_spec=spec,
         out_shape=[
-            jax.ShapeDtypeStruct((rows, width), BF16),
-            jax.ShapeDtypeStruct((rows, width), BF16),
+            jax.ShapeDtypeStruct((groups * rows, width), BF16),
+            jax.ShapeDtypeStruct((groups * rows, width), BF16),
             jax.ShapeDtypeStruct((rows, rank), F32),
-            jax.ShapeDtypeStruct((rank, width), F32),
+            jax.ShapeDtypeStruct((rank, groups * width), F32),
         ],
         compiler_params=params("arbitrary"),
-        cost_estimate=cost(rows * width * 512, 14),
+        cost_estimate=cost(groups * rows * width * 512, 12),
         name="norm_part",
     )(core, c, incoming, state, cum, pattern, ssd, near, far, gain, down, up_twice)
 
@@ -312,6 +344,7 @@
         functools.partial(product_kernel, first, tuple(piece[1:] for piece in pieces), len(held)),
         grid_spec=spec,
         out_shape=jax.ShapeDtypeStruct((rows, width), F32),
+        input_output_aliases={3: 0} if held else {},
         compiler_params=params("arbitrary"),
         cost_estimate=cost(2 * rows * width * Q, 4),
         name="product_part",
@@ -353,7 +386,7 @@
 def grad_part(
     group, groups, heads, core, near, far, cut, start, earlier, up_twice, down, gain, hat, slope, cum, pattern, c, pieces
 ):
-    rows, width = hat.shape
+    rows, width = earlier.shape
     rank = down.shape[0]
     blocks = rows // Q
     columns = pl.BlockSpec((near.shape[0], cut), lambda i, s: (0, near.shape[1] // cut - 1))
@@ -367,8 +400,8 @@
             whole(up_twice.shape),
             pl.BlockSpec((rank, width), lambda i, s: (0, s[0] * groups + group)),
             pl.BlockSpec((1, width), lambda i, s: (0, s[0] * groups + group)),
-            whole(hat.shape),
-            whole(slope.shape),
+            pl.BlockSpec((rows, width), lambda i, s: (group, 0)),
+            pl.BlockSpec((rows, width), lambda i, s: (group, 0)),
             whole(cum.shape),
             whole(pattern.shape),
             pl.BlockSpec((rows, N), lambda i, s: (0, group)),
@@ -395,26 +428,34 @@
     )
 
 
-def back_kernel(first, heads, core_ref, scores_ref, grad_ref, step_ref, pattern_ref, skip_ref, out_ref):
+def back_kernel(
+    first, heads, core_ref, top_ref, low_ref, grad_ref, step_ref, pattern_ref, skip_ref, out_ref
+):
+    half = Q // 2
     step = of_core(step_ref, slice(None), core_ref[0], first, heads)
     out_ref[...] = spread(step, pattern_ref[...])
     for pair in range(heads // 2):
         lanes = slice(pair * 2 * P_SIZE, (pair + 1) * 2 * P_SIZE)
         grad = grad_ref[:, lanes]
-        back = dot(
-            scores_ref[:, 2 * pair * Q : 2 * (pair + 1) * Q], pair_rows(grad)
-        )
-        out_ref[:, lanes] = out_ref[:, lanes] * back + skip_ref[:, lanes] * grad.astype(F32)
-
-
-def back_part(group, groups, heads, core, scores, grad, step, pattern, skip):
+        back = (
+            dot(top_ref[:, 2 * pair * Q : 2 * (pair + 1) * Q], pair_rows(grad)),
+            dot(low_ref[:, 2 * pair * half : 2 * (pair + 1) * half], pair_rows(grad[half:, :])),
+        )
+        for part, rows in zip(back, (slice(0, half), slice(half, Q))):
+            out_ref[rows, lanes] = out_ref[rows, lanes] * part + skip_ref[:, lanes] * grad_ref[
+                rows, lanes
+            ].astype(F32)
+
+
+def back_part(group, groups, heads, core, top, low, grad, step, pattern, skip):
     rows, width = grad.shape
     row_block = pl.BlockSpec((Q, width), lambda i, s: (i, 0))
     spec = pltpu.PrefetchScalarGridSpec(
         num_scalar_prefetch=1,
         grid=(rows // Q,),
         in_specs=[
-            pl.BlockSpec((Q, heads * Q), lambda i, s: (i, 0)),
+            pl.BlockSpec((Q // 2, heads * Q), lambda i, s: (group * (rows // Q) + i, 0)),
+            pl.BlockSpec((Q // 2, heads * Q // 2), lambda i, s: (group * (rows // Q) + i, 0)),
             row_block,
             pl.BlockSpec((Q, step.shape[1]), lambda i, s: (i, 0)),
             whole(pattern.shape),
@@ -429,7 +470,7 @@
         compiler_params=params("arbitrary"),
         cost_estimate=cost(rows * width * Q * 2, 8),
         name="back_part",
-    )(core, scores, grad, step, pattern, skip)
+    )(core, top, low, grad, step, pattern, skip)
 
 
 def cross_kernel(
@@ -628,6 +669,7 @@
                 plans = [[part for part in plan if part[2]] for plan in plans]
                 self.crossing, *moving = cut(list(got), plans, width)
                 self.moving = moving or list(got)
+                self.crossing, self.moving = lax.optimization_barrier((self.crossing, self.moving))
         self.late = late
         return values
 
@@ -654,18 +696,15 @@
     )
 
 
-def pack_kernel(ring, across, place_ref, first_ref, second_ref, own_ref, far_ref, mine_ref, *sent_refs):
-    sums = (first_ref[...], second_ref[...])
-    wide = sums[0].shape[1]
+def pack_kernel(ring, across, place_ref, sum_ref, own_ref, far_ref, mine_ref, *sent_refs):
     other = own_ref[...] + far_ref[...].astype(F32)
-    width_a = 2 * wide // (ring * across)
+    width_a = sum_ref.shape[1] // (ring * across)
     width_b = other.shape[1] // (ring * across)
     for member in range(ring):
         blocks = []
         for x in range(across):
             chip = member * across + x
-            start = chip * width_a % wide
-            part = sums[chip * width_a // wide][:, start : start + width_a]
+            part = sum_ref[:, chip * width_a : (chip + 1) * width_a]
             blocks.append((part, other[:, chip * width_b : (chip + 1) * width_b]))
         for turn in range(across):
             target = (place_ref[1] + turn) % across
@@ -722,15 +761,15 @@
     )(*scalars, *arrays)
 
 
-def packed(sums_a, own_b, far_b):
+def packed(sum_a, own_b, far_b):
     ring, across = lax.axis_size("dp"), lax.axis_size("x")
     place = jnp.stack([lax.axis_index("dp"), lax.axis_index("x")]).astype(jnp.int32)
     count = ring * across
-    shape = (ring, own_b.shape[0], (2 * sums_a[0].shape[1] + own_b.shape[1]) // count)
+    shape = (ring, own_b.shape[0], (sum_a.shape[1] + own_b.shape[1]) // count)
     mine, *sent = small_call(
         functools.partial(pack_kernel, ring, across),
         [place],
-        [*sums_a, own_b, far_b],
+        [sum_a, own_b, far_b],
         [jax.ShapeDtypeStruct(shape, F32)] + [jax.ShapeDtypeStruct(shape, BF16)] * (across - 1),
         "pack_sums",
     )
@@ -776,12 +815,32 @@
     )
 
 
-def everywhere(value, distance):
-    value = value + far_in_dp(value, distance)
-    for axis in ("core", "x"):
-        turns = rotations(lax.axis_size(axis))[1:]
-        value = functools.reduce(jnp.add, [lax.ppermute(value, axis, turn) for turn in turns], value)
-    return value
+def finish_kernel(entries, total_ref, square_ref, first_ref, second_ref):
+    width = first_ref.shape[1]
+    for out, count, column, lanes in (
+        (first_ref, entries[0], 0, slice(0, width)),
+        (second_ref, entries[1], 1, slice(width, width + second_ref.shape[1])),
+    ):
+        mean = square_ref[0:1, column : column + 1] / count
+        out[...] = total_ref[:, lanes] / jnp.maximum(1.0, jnp.sqrt(mean + CLIP_EPSILON))
+
+
+def finished(total, squares, width_a):
+    rank, width = total.shape
+    devices = lax.axis_size(AXES)
+    widths = (width_a, width - width_a)
+    return small_call(
+        functools.partial(finish_kernel, tuple(float(rank * part * devices) for part in widths)),
+        [],
+        [total, squares],
+        [jax.ShapeDtypeStruct((rank, part), F32) for part in widths],
+        "finish",
+    )
+
+
+def over_axis(value, axis):
+    turns = rotations(lax.axis_size(axis))[1:]
+    return functools.reduce(jnp.add, [lax.ppermute(value, axis, turn) for turn in turns], value)
 
 
 def on_device(
@@ -857,11 +916,6 @@
     gain = norm_gain[None, :]
     pattern = spread_pattern(heads)
 
-    def inside(group, x_far, b, c, step, cum, cum_t):
-        return local_part(
-            group, groups, heads, which, state_input, x_far, b, c, step, cum, cum_t, skip, pattern
-        )
-
     def prepare():
         step, cum, cum_t = step_part(
             which, step_unbiased, raw_far, step_bias[None, :], decay_rate_log[None, :]
@@ -869,14 +923,15 @@
         cut = groups * width
         b = in_order(half(input_matrix, core), x_far[:, cut : cut + groups * N])
         c = in_order(half(readout_matrix, core), x_far[:, cut + groups * N :])
-        local = [inside(group, x_far, b, c, step, cum, cum_t) for group in range(groups)]
+        local = local_part(
+            groups, heads, which, state_input, x_far, b, c, step, cum, cum_t, skip, pattern
+        )
         return step, cum, cum_t, b, c, local
 
     step, cum, cum_t, b, c, local = gather.step(1, prepare)
 
     def second():
-        fresh = jnp.concatenate([part[3].astype(BF16) for part in local], axis=0)
-        incoming = carried(fresh, cum, forward)
+        ssd, state, fresh = local[2:]
         up_near = (
             ADAPTER_SCALE * dot(output_cotangent, adapter_up, ((1,), (1,))).astype(BF16)
         ).astype(BF16)
@@ -886,22 +941,18 @@
             for chip in offset
         ]
         near = jnp.concatenate([half(gate_values, 1 - core)] + parts, axis=1)
+        up_near, fresh = lax.optimization_barrier((up_near, fresh))
+        incoming = carried(fresh, cum, forward)
         up_twice = in_order(up_near, swapped(up_near))
         far = swapped(near)
-        normed = []
-        for group in range(groups):
-            scores, ssd, state, total = local[group]
-            normed.append(
-                norm_part(
-                    group, groups, heads, which, c, incoming, state, cum, pattern, ssd, gate_values,
-                    far, gain, adapter_down, up_twice,
-                )
-            )
-        product = functools.reduce(jnp.add, [part[2] for part in normed])
+        hat, slope, product, sum_a = norm_part(
+            groups, heads, which, c, incoming, state, cum, pattern, ssd, gate_values, far, gain, adapter_down,
+            up_twice,
+        )
         far_product = swapped(half(product, 1 - core, 0))
-        return up_twice, near, far, normed, half(product, core, 0), far_product
-
-    up_twice, cot_near, cot_far, normed, product, far_product = gather.step(2, second)
+        return up_twice, near, far, (hat, slope), sum_a, half(product, core, 0), far_product
+
+    up_twice, cot_near, cot_far, normed, sum_a, product, far_product = gather.step(2, second)
     cot_width = output_cotangent.shape[1]
 
     def during(index, beside):
@@ -911,8 +962,8 @@
 
     def third():
         own_b, sent_b = down_part(which, product, far_product, output_cotangent)
-        mine, sent = packed([part[3] for part in normed], own_b, swapped(sent_b))
-        return halved(mine, over_x(sent), distances[0])
+        mine, sent = packed(sum_a, own_b, swapped(sent_b))
+        return mine, over_x(sent)
 
     mine, sent = during(3, third)
 
@@ -933,7 +984,8 @@
 
     def fourth():
         held = list(range(len(stages) - 1))[:2]
-        return doubled(mine, sent, distances[:-2]), products(held, [None] * groups)
+        halves = halved(mine, sent, distances[0])
+        return doubled(*halves, distances[:-2]), products(held, [None] * groups)
 
     (mine, sent), earlier = during(4, fourth)
     width_a = 2 * width // (ring * across)
@@ -945,39 +997,46 @@
     (mine, sent), earlier = during(5, fifth)
     for index in range(6, gather.steps):
         gather.step(index, lambda: ())
-    total, squares = totals(mine, far_in_dp(sent, distances[-1]), width_a)
+    arrived = far_in_dp(sent, distances[-1])
 
     grads = [
         grad_part(
             group, groups, heads, which, cot_near, cot_far, cot_width, depth(len(stages) - 1), earlier[group],
-            up_twice, adapter_down, gain, *normed[group][:2], cum, pattern, c, staged(len(stages) - 1, group),
+            up_twice, adapter_down, gain, *normed, cum, pattern, c, staged(len(stages) - 1, group),
         )
         for group in range(groups)
     ]
+    arrived, grads = lax.optimization_barrier((arrived, grads))
     outgoing = [carried(part[2], cum, backward, group) for group, part in enumerate(grads)]
-    bases = [
-        back_part(group, groups, heads, which, local[group][0], grads[group][0], step, pattern, skip)
-        for group in range(groups)
-    ]
-    near, far = [], []
-    for group in range(groups):
-        own, others = cross_part(
-            group, heads, which, b, outgoing[group], grads[group][1], step, cum, pattern, bases[group]
-        )
-        far.append(swapped(others))
-        near.append(own)
-    entries = jnp.asarray([width_a, total.shape[1] - width_a], F32)
-    entries = entries * (total.shape[0] * ring * across * 2)
+    total, squares = totals(mine, arrived, width_a)
+
+    def back(group):
+        return back_part(
+            group, groups, heads, which, *local[:2], grads[group][0], step, pattern, skip
+        )
+
     count = ring * across
     homes = [
         (chip * 2 + number, number * count + chip) for chip in range(count) for number in range(2)
     ]
-    total, near[-1] = lax.optimization_barrier((total, near[-1]))
+    squares = squares + far_in_dp(squares, distances[0])
+    bases = [back(0)]
+    squares, bases, grads = lax.optimization_barrier((squares, bases, grads))
+    squares = over_axis(squares, "core")
+    bases.append(back(1))
+    squares, bases, total = lax.optimization_barrier((squares, bases, total))
+    squares = over_axis(squares, "x")
     total = lax.ppermute(total, AXES, homes)
-    squares = everywhere(squares, distances[0])[0, :2]
-    scale = 1.0 / jnp.maximum(1.0, jnp.sqrt(squares / entries + CLIP_EPSILON))
-    gradient_a = total[:, :width_a] * scale[0]
-    gradient_b = total[:, width_a:] * scale[1]
+    near, far = [], []
+    for group in range(groups):
+        if group == groups - 1:
+            squares, bases, total = lax.optimization_barrier((squares, bases, total))
+        own, others = cross_part(
+            group, heads, which, b, outgoing[group], grads[group][1], step, cum, pattern, bases[group]
+        )
+        far.append(swapped(others))
+        near.append(own)
+    gradient_a, gradient_b = finished(total, squares, width_a)
     input_gradient = in_order(
         jnp.concatenate(near, axis=1), jnp.concatenate(far, axis=1), axis=1
     )

time: 145 us -> 144 us (level)
  local copies, waits for them, and re-layouts: 9.97 us -> 16.4 us
  Pallas kernels: 48 us -> 42.2 us
  waiting for transfers between devices: 38.8 us -> 41.6 us
  other arithmetic: 6.89 us -> 4.23 us
    unnamed x118, local copies, waits for them, and re-layouts: 5.76 us -> 11.8 us
    pallas_call x6, Pallas kernels: 10.4 us -> 6.81 us  [product_part(): pl.pallas_call(functools.partial(product_kernel, first, tuple((piece[1:]...]
    ppermute x3, waiting for transfers between devices: 7.33 us -> 10.9 us  [carried(): arrived = lax.ppermute(sent, 'x', perm)]
    ppermute x4, waiting for transfers between devices: 9.44 us -> 6.76 us  [far_in_dp(): lax.ppermute(value, 'dp', [(i, i ^ distance) for i in range(lax.axis_size...]
    mul x2 -> x0, other arithmetic: 2.53 us -> none  [the longest x1 1.27 us: on_device(): gradient_b = total[:, width_a:] * scale[1]]
    ppermute x9, starting transfers between devices: 4.18 us -> 1.68 us  [swapped(): return lax.ppermute(value, 'core', swap)]
    ppermute x2, waiting for transfers between devices: 0.01 us -> 2.2 us  [over_axis(): lax.ppermute(value, axis, turn)]
    pallas_call x10 -> x11, Pallas kernels: 7.11 us -> 5.21 us  [small_call(): pl.pallas_call(kernel, grid_spec=spec, out_shape=outs, compiler_params=pa...]
  transfers between devices with their start and end apart: 35 -> 35, of which waited for: 10 -> 9; matrix products, arithmetic and copies ran while one was open for 6% -> 4% of each run, Pallas kernels for 32% -> 28%
where the time goes in v4:
time: 144 us; the launch traced here: 143 us
  Pallas kernels  42.2 us (29%)
  waiting for transfers between devices  41.6 us (29%)
  starting transfers between devices  36.2 us (25%)
  local copies, waits for them, and re-layouts  16.4 us (11%)
  other arithmetic  4.23 us (3%)
  between operations  1.77 us (1%)
    ppermute x1, waiting for transfers between devices, over_x(): lax.ppermute(value, 'x', turn)  13.5 us
    pallas_call x1, Pallas kernels, local_part(): pl.pallas_call(functools.partial(local_kernel, heads), grid_spec=spec, ou...  13.3 us
    unnamed x118, local copies, waits for them, and re-layouts  11.8 us
    ppermute x10, starting transfers between devices, step(): lax.ppermute(array, 'dp', perm)  11.6 us
    ppermute x3, waiting for transfers between devices, carried(): arrived = lax.ppermute(sent, 'x', perm)  10.9 us
    ppermute x5, starting transfers between devices, step(): lax.ppermute(self.crossing, 'x', turn)  7.7 us
    pallas_call x6, Pallas kernels, product_part(): pl.pallas_call(functools.partial(product_kernel, first, tuple((piece[1:]...  6.81 us
    ppermute x4, waiting for transfers between devices, far_in_dp(): lax.ppermute(value, 'dp', [(i, i ^ distance) for i in range(lax.axis_size...  6.76 us
  transfers between devices with their start and end apart: 35, of which 9 were waited for; matrix products, arithmetic and copies ran while one was open for 4% of the time, Pallas kernels for 28%

profile of v4, /device:TPU:0, one launch (start us, length us, event | category | flops | bytes accessed | tf_op | source)
XLA Modules:
  0.0 142.9 jit_solution(8135339767069466891)
XLA Ops:
  0.7 1.0 constant_dynamic-slice_fusion.5
  1.7 0.9 copy.22.near_ref
  2.7 0.5 collective-permute-start.4
  3.3 1.3 constant_dynamic-slice_fusion.4
  4.6 1.2 pad_maximum_fusion.1
  6.5 0.8 step_part.1
  7.8 2.6 %collective-permute-start.2 = (bf16[128,1024]{1,0:T(8,128)(2,1)S(1)}, bf16[128,1024]{1,0:T(8,128)(2,1)S(1)}, u32[]{:S(2)}, u32[]{:S(2)}) collective-permute-start(bf16[128,1024]{1,0:T(8,128)(2,1)S(1)} %slice.12.rest_0_), channel_id=1, source_target_pairs={{8,0},{16,8},{24,16},{28,24},{20,28},{12,20},{4,12},{0,4},{9,1},{1... | collective-permute-start | bytes 786440 | tf_op jit(solution)/shard_map/ppermute | solution.py:619
  10.5 1.9 %collective-permute-start.3 = (bf16[128,2048]{1,0:T(8,128)(2,1)S(1)}, bf16[128,2048]{1,0:T(8,128)(2,1)S(1)}, u32[]{:S(2)}, u32[]{:S(2)}) collective-permute-start(bf16[128,2048]{1,0:T(8,128)(2,1)S(1)} %pad_maximum_fusion.2.refs_0_), channel_id=1, source_target_pairs={{0,2},{2,0},{1,3},{3,1},{4,6},{6,4},{5,7},{7,5},{8,10},{10,8},{9,1... | collective-permute-start | bytes 1572872 | tf_op jit(solution)/shard_map/ppermute | solution.py:620
  13.8 1.1 broadcast_select_fusion.5
  14.9 13.3 %local_part.1 = (bf16[512,4096]{1,0:T(8,128)(2,1)}, bf16[512,2048]{1,0:T(8,128)(2,1)}, bf16[1024,1024]{1,0:T(8,128)(2,1)S(1)}, f32[512,1024]{1,0:T(8,128)S(1)}, bf16[256,1024]{1,0:T(8,128)(2,1)S(1)}) custom-call(s32[1]{0:T(128)} %bitcast.core_ref, bf16[256,4096]{1,0:T(8,128)(2,1)S(1)} %copy-done.31, bf16[256,2560]{1,0:T(8,128)(2,1)} %collective-permute-done.5.far_ref, ...), custom_call_target="tpu_custom_call" | custom-call | flops 17179869184 | tf_op jit(solution)/shard_map/local_part/pallas_call | solution.py:219
  28.3 2.2 %collective-permute-start.11 = (bf16[256,1024]{1,0:T(8,128)(2,1)S(1)}, bf16[256,1024]{1,0:T(8,128)(2,1)S(1)}, u32[]{:S(2)}, u32[]{:S(2)}) collective-permute-start(bf16[256,1024]{1,0:T(8,128)(2,1)S(1)} %get-tuple-element.149), channel_id=1, source_target_pairs={{0,2},{1,3},{4,6},{5,7},{8,10},{9,11},{12,14},{13,15},{16,18},{17,... | collective-permute-start | bytes 1572872 | tf_op jit(solution)/shard_map/ppermute | solution.py:905
  31.0 2.0 %collective-permute-start.6 = (bf16[384,1024]{1,0:T(8,128)(2,1)S(1)}, bf16[384,1024]{1,0:T(8,128)(2,1)S(1)}, u32[]{:S(2)}, u32[]{:S(2)}) collective-permute-start(bf16[384,1024]{1,0:T(8,128)(2,1)S(1)} %get-tuple-element.141), channel_id=1, source_target_pairs={{0,8},{8,16},{16,24},{24,28},{28,20},{20,12},{12,4},{4,0},{1,9},{9... | collective-permute-start | bytes 2359304 | tf_op jit(solution)/shard_map/ppermute | solution.py:619
  33.0 0.7 collective-permute-start.7
  33.8 8.9 %collective-permute-done.11.incoming_ref = bf16[256,1024]{1,0:T(8,128)(2,1)S(1)} collective-permute-done((bf16[256,1024]{1,0:T(8,128)(2,1)S(1)}, bf16[256,1024]{1,0:T(8,128)(2,1)S(1)}, u32[]{:S(2)}, u32[]{:S(2)}) %collective-permute-start.11) | collective-permute-done | bytes 524320 | tf_op jit(solution)/shard_map/ppermute | solution.py:905
  42.7 5.1 %norm_part.1 = (bf16[1024,1024]{1,0:T(8,128)(2,1)S(1)}, bf16[1024,1024]{1,0:T(8,128)(2,1)S(1)}, f32[512,64]{1,0:T(8,128)S(1)}, f32[64,2048]{1,0:T(8,128)S(1)}) custom-call(s32[1]{0:T(128)} %bitcast.core_ref, bf16[512,256]{1,0:T(8,128)(2,1)S(1)} %pad_maximum_fusion.4.c_ref, bf16[256,1024]{1,0:T(8,128)(2,1)S(1)} %collective-permute-done.11.incoming_ref, ...), custom_call_target="tpu_custom_call" | custom-call | flops 6442450944 | tf_op jit(solution)/shard_map/norm_part/pallas_call | solution.py:298
  47.9 1.4 copy-done.7
  49.3 4.2 %collective-permute-done.8.rest_3_.rest_5_ = bf16[256,1024]{1,0:T(8,128)(2,1)S(1)} collective-permute-done((bf16[256,1024]{1,0:T(8,128)(2,1)S(1)}, bf16[256,1024]{1,0:T(8,128)(2,1)S(1)}, u32[]{:S(2)}, u32[]{:S(2)}) %collective-permute-start.8) | collective-permute-done | bytes 524320 | tf_op jit(solution)/shard_map/ppermute | solution.py:620
  53.6 2.0 %collective-permute-start.13 = (bf16[384,1024]{1,0:T(8,128)(2,1)S(1)}, bf16[384,1024]{1,0:T(8,128)(2,1)S(1)}, u32[]{:S(2)}, u32[]{:S(2)}) collective-permute-start(bf16[384,1024]{1,0:T(8,128)(2,1)S(1)} %collective-permute-done.6.refs_0_.rest_1_), channel_id=1, source_target_pairs={{0,8},{8,16},{16,24},{24,28},{28,20},{20,12},{12,4},{4,0},{1,9},{9... | collective-permute-start | bytes 2359304 | tf_op jit(solution)/shard_map/ppermute | solution.py:619
  55.7 2.5 %collective-permute-start.15 = (bf16[256,1024]{1,0:T(8,128)(2,1)S(1)}, bf16[256,1024]{1,0:T(8,128)(2,1)S(1)}, u32[]{:S(2)}, u32[]{:S(2)}) collective-permute-start(bf16[256,1024]{1,0:T(8,128)(2,1)S(1)} %cut_rows.5), channel_id=1, source_target_pairs={{0,2},{2,0},{1,3},{3,1},{4,6},{6,4},{5,7},{7,5},{8,10},{10,8},{9,1... | collective-permute-start | bytes 1572872 | tf_op jit(solution)/shard_map/ppermute | solution.py:620
  58.7 1.3 collective-permute-done.16.far_ref
  59.9 1.0 pack_sums.1
  61.0 0.8 copy-done.44
  61.8 13.5 %collective-permute-done.17.refs_0_ = bf16[8,64,192]{2,1,0:T(8,128)(2,1)S(1)} collective-permute-done((bf16[8,64,192]{2,1,0:T(8,128)(2,1)S(1)}, bf16[8,64,192]{2,1,0:T(8,128)(2,1)S(1)}, u32[]{:S(2)}, u32[]{:S(2)}) %collective-permute-start.17) | collective-permute-done | bytes 196640 | tf_op jit(solution)/shard_map/ppermute | solution.py:791
  75.3 0.7 copy-done.40
  76.0 0.8 copy-done.22
  76.8 1.3 cut_rows.6
  78.1 1.0 copy-done.16
  79.1 0.8 copy-done.39
  79.9 1.7 %collective-permute-start.18 = (bf16[320,1024]{1,0:T(8,128)(2,1)}, bf16[320,1024]{1,0:T(8,128)(2,1)}, u32[]{:S(2)}, u32[]{:S(2)}) collective-permute-start(bf16[320,1024]{1,0:T(8,128)(2,1)} %get-tuple-element.171), channel_id=1, source_target_pairs={{0,8},{8,16},{16,24},{24,28},{28,20},{20,12},{12,4},{4,0},{1,9},{9... | collective-permute-start | bytes 1966088 | tf_op jit(solution)/shard_map/ppermute | solution.py:619
  81.9 1.0 slice.15.rest_1_
  82.9 1.8 %collective-permute-start.20 = (bf16[256,1024]{1,0:T(8,128)(2,1)}, bf16[256,1024]{1,0:T(8,128)(2,1)S(1)}, u32[]{:S(2)}, u32[]{:S(2)}) collective-permute-start(bf16[256,1024]{1,0:T(8,128)(2,1)} %copy-done.39), channel_id=1, source_target_pairs={{0,2},{2,0},{1,3},{3,1},{4,6},{6,4},{5,7},{7,5},{8,10},{10,8},{9,1... | collective-permute-start | bytes 1572872 | tf_op jit(solution)/shard_map/ppermute | solution.py:620
  84.7 1.6 %copy-done.3 = bf16[256,4096]{1,0:T(8,128)(2,1)S(1)} copy-done((bf16[256,4096]{1,0:T(8,128)(2,1)S(1)}, bf16[256,4096]{1,0:T(8,128)(2,1)}, u32[]{:S(2)}) %copy-start.3) | copy-done | bytes 2097176
  86.3 1.1 copy-done.13
  87.4 1.1 copy-done.15
  88.5 1.0 copy-done.30
  89.6 1.0 product_part.6.rest_0_
  90.8 1.0 product_part.8.rest_0_
  92.0 2.8 %collective-permute-start.21 = (bf16[4,64,192]{2,1,0:T(8,128)(2,1)S(1)}, bf16[4,64,192]{2,1,0:T(8,128)(2,1)S(1)}, u32[]{:S(2)}, u32[]{:S(2)}) collective-permute-start(bf16[4,64,192]{2,1,0:T(8,128)(2,1)S(1)} %get-tuple-element.177), channel_id=1, source_target_pairs={{0,16},{4,20},{8,24},{12,28},{16,0},{20,4},{24,8},{28,12},{1,17},{... | collective-permute-start | bytes 294920 | tf_op jit(solution)/shard_map/ppermute | solution.py:795
  94.8 0.9 product_part.7.rest_0_
  95.7 0.9 product_part.9.rest_0_
  96.6 6.8 %collective-permute-done.21.arrived_ref = bf16[4,64,192]{2,1,0:T(8,128)(2,1)S(1)} collective-permute-done((bf16[4,64,192]{2,1,0:T(8,128)(2,1)S(1)}, bf16[4,64,192]{2,1,0:T(8,128)(2,1)S(1)}, u32[]{:S(2)}, u32[]{:S(2)}) %collective-permute-start.21) | collective-permute-done | bytes 98336 | tf_op jit(solution)/shard_map/ppermute | solution.py:795
  103.5 1.3 cut_rows.7
  104.8 2.1 %collective-permute-start.22 = (bf16[128,1024]{1,0:T(8,128)(2,1)S(1)}, bf16[128,1024]{1,0:T(8,128)(2,1)S(1)}, u32[]{:S(2)}, u32[]{:S(2)}) collective-permute-start(bf16[128,1024]{1,0:T(8,128)(2,1)S(1)} %get-tuple-element.187), channel_id=1, source_target_pairs={{0,8},{8,16},{16,24},{24,28},{28,20},{20,12},{12,4},{4,0},{1,9},{9... | collective-permute-start | bytes 786440 | tf_op jit(solution)/shard_map/ppermute | solution.py:619
  106.9 1.5 %collective-permute-start.24 = (bf16[128,1024]{1,0:T(8,128)(2,1)S(1)}, bf16[128,1024]{1,0:T(8,128)(2,1)S(1)}, u32[]{:S(2)}, u32[]{:S(2)}) collective-permute-start(bf16[128,1024]{1,0:T(8,128)(2,1)S(1)} %get-tuple-element.189), channel_id=1, source_target_pairs={{0,2},{2,0},{1,3},{3,1},{4,6},{6,4},{5,7},{7,5},{8,10},{10,8},{9,1... | collective-permute-start | bytes 786440 | tf_op jit(solution)/shard_map/ppermute | solution.py:620
  108.4 2.2 %product_part.10.earlier_ref = f32[512,1024]{1,0:T(8,128)S(1)} custom-call(s32[1]{0:T(128)} %bitcast.core_ref, bf16[256,4096]{1,0:T(8,128)(2,1)S(1)} %dynamic-slice_dynamic-update-slice_fusion.1.near_ref, bf16[256,4096]{1,0:T(8,128)(2,1)S(1)} %copy-done.4, f32[512,1024]{1,0:T(8,128)S(1)} %product_part.7.rest_0_, ...), custom_call_target="tpu_custom_call", output_to_operand_aliasing={{}: (3, {})} | custom-call | flops 1073741824 | tf_op jit(solution)/shard_map/product_part/pallas_call | solution.py:343
  110.6 0.9 product_part.11.earlier_ref
  111.6 1.7 %collective-permute-done.23.rest_1_ = bf16[128,1024]{1,0:T(8,128)(2,1)S(1)} collective-permute-done((bf16[128,1024]{1,0:T(8,128)(2,1)S(1)}, bf16[128,1024]{1,0:T(8,128)(2,1)S(1)}, u32[]{:S(2)}, u32[]{:S(2)}) %collective-permute-start.23) | collective-permute-done | bytes 262176 | tf_op jit(solution)/shard_map/ppermute | solution.py:619
  113.3 1.4 collective-permute-start.26
  114.7 3.0 %grad_part.3 = (bf16[512,1024]{1,0:T(8,128)(2,1)S(1)}, f32[256,1024]{1,0:T(8,128)S(1)}, bf16[128,1024]{1,0:T(8,128)(2,1)S(1)}) custom-call(s32[1]{0:T(128)} %bitcast.core_ref, bf16[256,4096]{1,0:T(8,128)(2,1)S(1)} %dynamic-slice_dynamic-update-slice_fusion.1.near_ref, bf16[256,4096]{1,0:T(8,128)(2,1)S(1)} %copy-done.4, ...), custom_call_target="tpu_custom_call" | custom-call | flops 2147483648 | tf_op jit(solution)/shard_map/grad_part/pallas_call | solution.py:412
  117.8 1.7 %grad_part.2 = (bf16[512,1024]{1,0:T(8,128)(2,1)S(1)}, f32[256,1024]{1,0:T(8,128)S(1)}, bf16[128,1024]{1,0:T(8,128)(2,1)S(1)}) custom-call(s32[1]{0:T(128)} %bitcast.core_ref, bf16[256,4096]{1,0:T(8,128)(2,1)S(1)} %dynamic-slice_dynamic-update-slice_fusion.1.near_ref, bf16[256,4096]{1,0:T(8,128)(2,1)S(1)} %copy-done.4, ...), custom_call_target="tpu_custom_call" | custom-call | flops 2147483648 | tf_op jit(solution)/shard_map/grad_part/pallas_call | solution.py:412
  119.7 2.1 %collective-permute-start.28 = (f32[8,128]{1,0:T(8,128)S(1)}, f32[8,128]{1,0:T(8,128)S(1)}, u32[]{:S(2)}, u32[]{:S(2)}) collective-permute-start(f32[8,128]{1,0:T(8,128)S(1)} %get-tuple-element.215), channel_id=1, source_target_pairs={{0,16},{4,20},{8,24},{12,28},{16,0},{20,4},{24,8},{28,12},{1,17},{... | collective-permute-start | bytes 12296 | tf_op jit(solution)/shard_map/ppermute | solution.py:795
  121.8 1.3 collective-permute-start.27
  123.1 1.3 collective-permute-start.30
  124.4 1.8 %back_part.2.base_ref = f32[512,1024]{1,0:T(8,128)S(1)} custom-call(s32[1]{0:T(128)} %bitcast.core_ref, bf16[512,4096]{1,0:T(8,128)(2,1)S(1)} %copy-done.5, bf16[512,2048]{1,0:T(8,128)(2,1)S(1)} %copy-done.6, bf16[512,1024]{1,0:T(8,128)(2,1)S(1)} %get-tuple-element.218.grad_ref, f32[512,64]{1,0:T(8,128)S(1)} %get-tuple-element.219.step_ref, ...), custom_call_target="tpu_custom_call" | custom-call | flops 2147483648 | tf_op jit(solution)/shard_map/back_part/pallas_call | solution.py:466
  126.3 1.8 %back_part.3.base_ref = f32[512,1024]{1,0:T(8,128)S(1)} custom-call(s32[1]{0:T(128)} %bitcast.core_ref, bf16[512,4096]{1,0:T(8,128)(2,1)S(1)} %copy-done.5, bf16[512,2048]{1,0:T(8,128)(2,1)S(1)} %copy-done.6, bf16[512,1024]{1,0:T(8,128)(2,1)S(1)} %get-tuple-element.227.grad_ref, f32[512,64]{1,0:T(8,128)S(1)} %get-tuple-element.219.step_ref, ...), custom_call_target="tpu_custom_call" | custom-call | flops 2147483648 | tf_op jit(solution)/shard_map/back_part/pallas_call | solution.py:466
  128.2 2.1 %collective-permute-done.27.outgoing_ref = bf16[128,1024]{1,0:T(8,128)(2,1)S(1)} collective-permute-done((bf16[128,1024]{1,0:T(8,128)(2,1)S(1)}, bf16[128,1024]{1,0:T(8,128)(2,1)S(1)}, u32[]{:S(2)}, u32[]{:S(2)}) %collective-permute-start.27) | collective-permute-done | bytes 262176 | tf_op jit(solution)/shard_map/ppermute | solution.py:905
  130.2 1.3 cross_part.2
  131.6 0.7 collective-permute-start.32
  132.3 3.4 %collective-permute-start.31 = (f32[8,128]{1,0:T(8,128)S(1)}, f32[8,128]{1,0:T(8,128)S(1)}, u32[]{:S(2)}, u32[]{:S(2)}) collective-permute-start(f32[8,128]{1,0:T(8,128)S(1)} %add.339), channel_id=1, source_target_pairs={{0,2},{2,0},{1,3},{3,1},{4,6},{6,4},{5,7},{7,5},{8,10},{10,8},{9,1... | collective-permute-start | bytes 12296 | tf_op jit(solution)/shard_map/ppermute | solution.py:843
  135.7 2.2 %collective-permute-done.31 = f32[8,128]{1,0:T(8,128)S(1)} collective-permute-done((f32[8,128]{1,0:T(8,128)S(1)}, f32[8,128]{1,0:T(8,128)S(1)}, u32[]{:S(2)}, u32[]{:S(2)}) %collective-permute-start.31) | collective-permute-done | bytes 4128 | tf_op jit(solution)/shard_map/ppermute | solution.py:843
  137.9 1.3 cross_part.3
  139.2 0.7 finish.1
  140.1 1.0 collective-permute-done.34
  141.3 1.5 %pad_maximum_fusion = bf16[256,4096]{1,0:T(8,128)(2,1)} fusion(bf16[256,2048]{1,0:T(8,128)(2,1)S(1)} %get-tuple-element.244, bf16[256,2048]{1,0:T(8,128)(2,1)S(1)} %get-tuple-element.243), kind=kLoop, calls=%fused_computation | loop fusion | flops 4194304 | bytes 4194304 | tf_op jit(solution)/shard_map/concatenate | solution.py:864
  (177 shorter events, 5.5 us)
Async XLA Ops:
  0.6 12.7 %copy-start = (bf16[64,2048]{1,0:T(8,128)(2,1)S(1)}, bf16[64,2048]{1,0:T(8,128)(2,1)}, u32[]{:S(2)}) copy-start(bf16[64,2048]{1,0:T(8,128)(2,1)} %param.24) | copy-start | bytes 786436
  0.6 3.9 %copy-start.47 = (bf16[256,512]{1,0:T(8,128)(2,1)S(1)}, bf16[256,512]{1,0:T(8,128)(2,1)}, u32[]{:S(2)}) copy-start(bf16[256,512]{1,0:T(8,128)(2,1)} %param.17) | copy-start | bytes 786436
  0.7 3.9 %copy-start.48 = (bf16[256,512]{1,0:T(8,128)(2,1)S(1)}, bf16[256,512]{1,0:T(8,128)(2,1)}, u32[]{:S(2)}) copy-start(bf16[256,512]{1,0:T(8,128)(2,1)} %param.16) | copy-start | bytes 786436
  2.7 3.8 %collective-permute-start.4 = (f32[256,64]{1,0:T(8,128)S(1)}, f32[256,64]{1,0:T(8,128)S(1)}, u32[]{:S(2)}, u32[]{:S(2)}) collective-permute-start(f32[256,64]{1,0:T(8,128)S(1)} %copy.22.near_ref), channel_id=1, source_target_pairs={{0,1},{1,0},{2,3},{3,2},{4,5},{5,4},{6,7},{7,6},{8,9},{9,8},{10,11... | collective-permute-start | bytes 196616 | tf_op jit(solution)/shard_map/ppermute | solution.py:869
  3.2 4.2 %collective-permute-start = (bf16[64,2048]{1,0:T(8,128)(2,1)S(1)}, bf16[64,2048]{1,0:T(8,128)(2,1)S(1)}, u32[]{:S(2)}, u32[]{:S(2)}) collective-permute-start(bf16[64,2048]{1,0:T(8,128)(2,1)S(1)} %constant_dynamic-slice_fusion.5), channel_id=1, source_target_pairs={{0,1},{1,0},{2,3},{3,2},{4,5},{5,4},{6,7},{7,6},{8,9},{9,8},{10,11... | collective-permute-start | bytes 786440 | tf_op jit(solution)/shard_map/ppermute | solution.py:869
  4.6 1.9 %copy-start.42 = (f32[64]{0:T(128)S(1)}, f32[64]{0:T(128)}, u32[]{:S(2)}) copy-start(f32[64]{0:T(128)} %param.19) | copy-start | bytes 772
  4.6 1.9 %copy-start.43 = (f32[64]{0:T(128)S(1)}, f32[64]{0:T(128)}, u32[]{:S(2)}) copy-start(f32[64]{0:T(128)} %param.20) | copy-start | bytes 772
  5.8 8.0 %collective-permute-start.5 = (bf16[256,2560]{1,0:T(8,128)(2,1)}, bf16[256,2560]{1,0:T(8,128)(2,1)}, u32[]{:S(2)}, u32[]{:S(2)}) collective-permute-start(bf16[256,2560]{1,0:T(8,128)(2,1)} %pad_maximum_fusion.1), channel_id=1, source_target_pairs={{0,1},{1,0},{2,3},{3,2},{4,5},{5,4},{6,7},{7,6},{8,9},{9,8},{10,11... | collective-permute-start | bytes 3932168 | tf_op jit(solution)/shard_map/ppermute | solution.py:869
  7.3 5.1 %copy-start.32 = (bf16[256,4096]{1,0:T(8,128)(2,1)S(1)}, bf16[256,4096]{1,0:T(8,128)(2,1)}, u32[]{:S(2)}) copy-start(bf16[256,4096]{1,0:T(8,128)(2,1)} %near_ref.1) | copy-start | bytes 6291460
  7.7 4.9 %copy-start.26 = (bf16[256,2048]{1,0:T(8,128)(2,1)S(1)}, bf16[256,2048]{1,0:T(8,128)(2,1)}, u32[]{:S(2)}) copy-start(bf16[256,2048]{1,0:T(8,128)(2,1)} %cot_ref) | copy-start | bytes 3145732
  7.8 5.5 %copy-start.27 = (bf16[128,1024]{1,0:T(8,128)(2,1)}, bf16[128,1024]{1,0:T(8,128)(2,1)S(1)}, u32[]{:S(2)}) copy-start(bf16[128,1024]{1,0:T(8,128)(2,1)S(1)} %slice.12.rest_0_) | copy-start | bytes 786436
  7.8 20.4 %collective-permute-start.2 = (bf16[128,1024]{1,0:T(8,128)(2,1)S(1)}, bf16[128,1024]{1,0:T(8,128)(2,1)S(1)}, u32[]{:S(2)}, u32[]{:S(2)}) collective-permute-start(bf16[128,1024]{1,0:T(8,128)(2,1)S(1)} %slice.12.rest_0_), channel_id=1, source_target_pairs={{8,0},{16,8},{24,16},{28,24},{20,28},{12,20},{4,12},{0,4},{9,1},{1... | collective-permute-start | bytes 786440 | tf_op jit(solution)/shard_map/ppermute | solution.py:619
  10.4 17.8 %collective-permute-start.1 = (bf16[128,1024]{1,0:T(8,128)(2,1)S(1)}, bf16[128,1024]{1,0:T(8,128)(2,1)S(1)}, u32[]{:S(2)}, u32[]{:S(2)}) collective-permute-start(bf16[128,1024]{1,0:T(8,128)(2,1)S(1)} %slice.12.rest_0_), channel_id=1, source_target_pairs={{0,8},{8,16},{16,24},{24,28},{28,20},{20,12},{12,4},{4,0},{1,9},{9... | collective-permute-start | bytes 786440 | tf_op jit(solution)/shard_map/ppermute | solution.py:619
  10.5 17.7 %collective-permute-start.3 = (bf16[128,2048]{1,0:T(8,128)(2,1)S(1)}, bf16[128,2048]{1,0:T(8,128)(2,1)S(1)}, u32[]{:S(2)}, u32[]{:S(2)}) collective-permute-start(bf16[128,2048]{1,0:T(8,128)(2,1)S(1)} %pad_maximum_fusion.2.refs_0_), channel_id=1, source_target_pairs={{0,2},{2,0},{1,3},{3,1},{4,6},{6,4},{5,7},{7,5},{8,10},{10,8},{9,1... | collective-permute-start | bytes 1572872 | tf_op jit(solution)/shard_map/ppermute | solution.py:620
  13.0 1.9 %copy-start.11 = (bf16[48,1024]{1,0:T(8,128)(2,1)S(1)}, bf16[48,1024]{1,0:T(8,128)(2,1)}, u32[]{:S(2)}) copy-start(bf16[48,1024]{1,0:T(8,128)(2,1)} %constant.191.clone.pattern_ref) | copy-start | bytes 294916
  13.2 29.4 %collective-permute-start.10 = (bf16[256,4096]{1,0:T(8,128)(2,1)S(1)}, bf16[256,4096]{1,0:T(8,128)(2,1)S(1)}, u32[]{:S(2)}, u32[]{:S(2)}) collective-permute-start(bf16[256,4096]{1,0:T(8,128)(2,1)S(1)} %dynamic-slice_dynamic-update-slice_fusion.1.near_ref), channel_id=1, source_target_pairs={{0,1},{1,0},{2,3},{3,2},{4,5},{5,4},{6,7},{7,6},{8,9},{9,8},{10,11... | collective-permute-start | bytes 6291464 | tf_op jit(solution)/shard_map/ppermute | solution.py:869
  28.2 5.6 %copy-start.33 = (bf16[128,1024]{1,0:T(8,128)(2,1)}, bf16[128,1024]{1,0:T(8,128)(2,1)S(1)}, u32[]{:S(2)}) copy-start(bf16[128,1024]{1,0:T(8,128)(2,1)S(1)} %collective-permute-done.2.refs_3_.rest_4_) | copy-start | bytes 786436
  28.2 5.6 %copy-start.35 = (bf16[128,1024]{1,0:T(8,128)(2,1)}, bf16[128,1024]{1,0:T(8,128)(2,1)S(1)}, u32[]{:S(2)}) copy-start(bf16[128,1024]{1,0:T(8,128)(2,1)S(1)} %collective-permute-done.1.refs_2_.rest_2_) | copy-start | bytes 786436
  28.2 5.6 %copy-start.37 = (bf16[128,2048]{1,0:T(8,128)(2,1)}, bf16[128,2048]{1,0:T(8,128)(2,1)S(1)}, u32[]{:S(2)}) copy-start(bf16[128,2048]{1,0:T(8,128)(2,1)S(1)} %collective-permute-done.3.refs_1_) | copy-start | bytes 1572868
  28.2 14.4 %copy-start.24 = (bf16[64,4096]{1,0:T(8,128)(2,1)S(1)}, bf16[64,4096]{1,0:T(8,128)(2,1)}, u32[]{:S(2)}) copy-start(bf16[64,4096]{1,0:T(8,128)(2,1)} %down_ref.5) | copy-start | bytes 1572868
  28.3 14.4 %copy-start.38 = (f32[4096]{0:T(1024)S(1)}, f32[4096]{0:T(1024)}, u32[]{:S(2)}) copy-start(f32[4096]{0:T(1024)} %param.22) | copy-start | bytes 49156
  28.3 14.4 %collective-permute-start.11 = (bf16[256,1024]{1,0:T(8,128)(2,1)S(1)}, bf16[256,1024]{1,0:T(8,128)(2,1)S(1)}, u32[]{:S(2)}, u32[]{:S(2)}) collective-permute-start(bf16[256,1024]{1,0:T(8,128)(2,1)S(1)} %get-tuple-element.149), channel_id=1, source_target_pairs={{0,2},{1,3},{4,6},{5,7},{8,10},{9,11},{12,14},{13,15},{16,18},{17,... | collective-permute-start | bytes 1572872 | tf_op jit(solution)/shard_map/ppermute | solution.py:905
  30.5 2.6 %collective-permute-start.9 = (bf16[256,64]{1,0:T(8,128)(2,1)S(1)}, bf16[256,64]{1,0:T(8,128)(2,1)S(1)}, u32[]{:S(2)}, u32[]{:S(2)}) collective-permute-start(bf16[256,64]{1,0:T(8,128)(2,1)S(1)} %fusion), channel_id=1, source_target_pairs={{0,1},{1,0},{2,3},{3,2},{4,5},{5,4},{6,7},{7,6},{8,9},{9,8},{10,11... | collective-permute-start | bytes 98312 | tf_op jit(solution)/shard_map/ppermute | solution.py:869
  30.9 11.7 %copy-start.29 = (bf16[256,1024]{1,0:T(8,128)(2,1)}, bf16[256,1024]{1,0:T(8,128)(2,1)S(1)}, u32[]{:S(2)}) copy-start(bf16[256,1024]{1,0:T(8,128)(2,1)S(1)} %get-tuple-element.182.rest_0_) | copy-start | bytes 1572868
  31.0 22.6 %collective-permute-start.8 = (bf16[256,1024]{1,0:T(8,128)(2,1)S(1)}, bf16[256,1024]{1,0:T(8,128)(2,1)S(1)}, u32[]{:S(2)}, u32[]{:S(2)}) collective-permute-start(bf16[256,1024]{1,0:T(8,128)(2,1)S(1)} %get-tuple-element.143), channel_id=1, source_target_pairs={{0,2},{2,0},{1,3},{3,1},{4,6},{6,4},{5,7},{7,5},{8,10},{10,8},{9,1... | collective-permute-start | bytes 1572872 | tf_op jit(solution)/shard_map/ppermute | solution.py:620
  31.0 22.5 %collective-permute-start.6 = (bf16[384,1024]{1,0:T(8,128)(2,1)S(1)}, bf16[384,1024]{1,0:T(8,128)(2,1)S(1)}, u32[]{:S(2)}, u32[]{:S(2)}) collective-permute-start(bf16[384,1024]{1,0:T(8,128)(2,1)S(1)} %get-tuple-element.141), channel_id=1, source_target_pairs={{0,8},{8,16},{16,24},{24,28},{28,20},{20,12},{12,4},{4,0},{1,9},{9... | collective-permute-start | bytes 2359304 | tf_op jit(solution)/shard_map/ppermute | solution.py:619
  33.0 20.5 %collective-permute-start.7 = (bf16[384,1024]{1,0:T(8,128)(2,1)S(1)}, bf16[384,1024]{1,0:T(8,128)(2,1)S(1)}, u32[]{:S(2)}, u32[]{:S(2)}) collective-permute-start(bf16[384,1024]{1,0:T(8,128)(2,1)S(1)} %get-tuple-element.142), channel_id=1, source_target_pairs={{8,0},{16,8},{24,16},{28,24},{20,28},{12,20},{4,12},{0,4},{9,1},{1... | collective-permute-start | bytes 2359304 | tf_op jit(solution)/shard_map/ppermute | solution.py:619
  42.7 5.2 %copy-start.2 = (bf16[256,4096]{1,0:T(8,128)(2,1)}, bf16[256,4096]{1,0:T(8,128)(2,1)S(1)}, u32[]{:S(2)}) copy-start(bf16[256,4096]{1,0:T(8,128)(2,1)S(1)} %collective-permute-done.10.far_ref) | copy-start | bytes 6291460
  49.2 4.4 %copy-start.9 = (bf16[1024,1024]{1,0:T(8,128)(2,1)}, bf16[1024,1024]{1,0:T(8,128)(2,1)S(1)}, u32[]{:S(2)}) copy-start(bf16[1024,1024]{1,0:T(8,128)(2,1)S(1)} %get-tuple-element.201.slope_ref) | copy-start | bytes 6291460
  49.3 4.3 %collective-permute-start.12 = (f32[256,64]{1,0:T(8,128)S(1)}, f32[256,64]{1,0:T(8,128)S(1)}, u32[]{:S(2)}, u32[]{:S(2)}) collective-permute-start(f32[256,64]{1,0:T(8,128)S(1)} %get-tuple-element.253), channel_id=1, source_target_pairs={{0,1},{1,0},{2,3},{3,2},{4,5},{5,4},{6,7},{7,6},{8,9},{9,8},{10,11... | collective-permute-start | bytes 196616 | tf_op jit(solution)/shard_map/ppermute | solution.py:869
  53.5 5.0 %copy-start.20 = (bf16[256,1024]{1,0:T(8,128)(2,1)}, bf16[256,1024]{1,0:T(8,128)(2,1)S(1)}, u32[]{:S(2)}) copy-start(bf16[256,1024]{1,0:T(8,128)(2,1)S(1)} %collective-permute-done.8.rest_3_.rest_5_) | copy-start | bytes 1572868
  53.5 5.0 %copy-start.12 = (bf16[384,1024]{1,0:T(8,128)(2,1)}, bf16[384,1024]{1,0:T(8,128)(2,1)S(1)}, u32[]{:S(2)}) copy-start(bf16[384,1024]{1,0:T(8,128)(2,1)S(1)} %collective-permute-done.6.refs_0_.rest_1_) | copy-start | bytes 2359300
  53.5 5.0 %copy-start.14 = (bf16[384,1024]{1,0:T(8,128)(2,1)}, bf16[384,1024]{1,0:T(8,128)(2,1)S(1)}, u32[]{:S(2)}) copy-start(bf16[384,1024]{1,0:T(8,128)(2,1)S(1)} %collective-permute-done.7.refs_1_.rest_2_.rest_3_) | copy-start | bytes 2359300
  53.6 23.2 %collective-permute-start.13 = (bf16[384,1024]{1,0:T(8,128)(2,1)S(1)}, bf16[384,1024]{1,0:T(8,128)(2,1)S(1)}, u32[]{:S(2)}, u32[]{:S(2)}) collective-permute-start(bf16[384,1024]{1,0:T(8,128)(2,1)S(1)} %collective-permute-done.6.refs_0_.rest_1_), channel_id=1, source_target_pairs={{0,8},{8,16},{16,24},{24,28},{28,20},{20,12},{12,4},{4,0},{1,9},{9... | collective-permute-start | bytes 2359304 | tf_op jit(solution)/shard_map/ppermute | solution.py:619
  55.6 21.2 %collective-permute-start.14 = (bf16[384,1024]{1,0:T(8,128)(2,1)S(1)}, bf16[384,1024]{1,0:T(8,128)(2,1)S(1)}, u32[]{:S(2)}, u32[]{:S(2)}) collective-permute-start(bf16[384,1024]{1,0:T(8,128)(2,1)S(1)} %collective-permute-done.7.refs_1_.rest_2_.rest_3_), channel_id=1, source_target_pairs={{8,0},{16,8},{24,16},{28,24},{20,28},{12,20},{4,12},{0,4},{9,1},{1... | collective-permute-start | bytes 2359304 | tf_op jit(solution)/shard_map/ppermute | solution.py:619
  55.7 20.3 %collective-permute-start.15 = (bf16[256,1024]{1,0:T(8,128)(2,1)S(1)}, bf16[256,1024]{1,0:T(8,128)(2,1)S(1)}, u32[]{:S(2)}, u32[]{:S(2)}) collective-permute-start(bf16[256,1024]{1,0:T(8,128)(2,1)S(1)} %cut_rows.5), channel_id=1, source_target_pairs={{0,2},{2,0},{1,3},{3,1},{4,6},{6,4},{5,7},{7,5},{8,10},{10,8},{9,1... | collective-permute-start | bytes 1572872 | tf_op jit(solution)/shard_map/ppermute | solution.py:620
  58.5 1.4 collective-permute-start.16
  61.8 13.5 %collective-permute-start.17 = (bf16[8,64,192]{2,1,0:T(8,128)(2,1)S(1)}, bf16[8,64,192]{2,1,0:T(8,128)(2,1)S(1)}, u32[]{:S(2)}, u32[]{:S(2)}) collective-permute-start(bf16[8,64,192]{2,1,0:T(8,128)(2,1)S(1)} %get-tuple-element.168), channel_id=1, source_target_pairs={{0,2},{2,0},{1,3},{3,1},{4,6},{6,4},{5,7},{7,5},{8,10},{10,8},{9,1... | collective-permute-start | bytes 589832 | tf_op jit(solution)/shard_map/ppermute | solution.py:791
  79.9 23.5 %collective-permute-start.18 = (bf16[320,1024]{1,0:T(8,128)(2,1)}, bf16[320,1024]{1,0:T(8,128)(2,1)}, u32[]{:S(2)}, u32[]{:S(2)}) collective-permute-start(bf16[320,1024]{1,0:T(8,128)(2,1)} %get-tuple-element.171), channel_id=1, source_target_pairs={{0,8},{8,16},{16,24},{24,28},{28,20},{20,12},{12,4},{4,0},{1,9},{9... | collective-permute-start | bytes 1966088 | tf_op jit(solution)/shard_map/ppermute | solution.py:619
  81.6 21.8 %collective-permute-start.19 = (bf16[320,1024]{1,0:T(8,128)(2,1)}, bf16[320,1024]{1,0:T(8,128)(2,1)}, u32[]{:S(2)}, u32[]{:S(2)}) collective-permute-start(bf16[320,1024]{1,0:T(8,128)(2,1)} %get-tuple-element.172), channel_id=1, source_target_pairs={{8,0},{16,8},{24,16},{28,24},{20,28},{12,20},{4,12},{0,4},{9,1},{1... | collective-permute-start | bytes 1966088 | tf_op jit(solution)/shard_map/ppermute | solution.py:619
  82.9 20.5 %collective-permute-start.20 = (bf16[256,1024]{1,0:T(8,128)(2,1)}, bf16[256,1024]{1,0:T(8,128)(2,1)S(1)}, u32[]{:S(2)}, u32[]{:S(2)}) collective-permute-start(bf16[256,1024]{1,0:T(8,128)(2,1)} %copy-done.39), channel_id=1, source_target_pairs={{0,2},{2,0},{1,3},{3,1},{4,6},{6,4},{5,7},{7,5},{8,10},{10,8},{9,1... | collective-permute-start | bytes 1572872 | tf_op jit(solution)/shard_map/ppermute | solution.py:620
  91.8 3.0 %copy-start.4 = (bf16[256,4096]{1,0:T(8,128)(2,1)S(1)}, bf16[256,4096]{1,0:T(8,128)(2,1)}, u32[]{:S(2)}) copy-start(bf16[256,4096]{1,0:T(8,128)(2,1)} %copy-done.2) | copy-start | bytes 6291460
  91.8 3.0 %copy-start.17 = (bf16[384,1024]{1,0:T(8,128)(2,1)S(1)}, bf16[384,1024]{1,0:T(8,128)(2,1)}, u32[]{:S(2)}) copy-start(bf16[384,1024]{1,0:T(8,128)(2,1)} %copy-done.16) | copy-start | bytes 2359300
  91.8 3.0 %copy-start.19 = (bf16[384,1024]{1,0:T(8,128)(2,1)S(1)}, bf16[384,1024]{1,0:T(8,128)(2,1)}, u32[]{:S(2)}) copy-start(bf16[384,1024]{1,0:T(8,128)(2,1)} %copy-done.18) | copy-start | bytes 2359300
  92.0 3.7 %copy-start.23 = (bf16[256,1024]{1,0:T(8,128)(2,1)S(1)}, bf16[256,1024]{1,0:T(8,128)(2,1)}, u32[]{:S(2)}) copy-start(bf16[256,1024]{1,0:T(8,128)(2,1)} %copy-done.22) | copy-start | bytes 1572868
  92.0 11.3 %collective-permute-start.21 = (bf16[4,64,192]{2,1,0:T(8,128)(2,1)S(1)}, bf16[4,64,192]{2,1,0:T(8,128)(2,1)S(1)}, u32[]{:S(2)}, u32[]{:S(2)}) collective-permute-start(bf16[4,64,192]{2,1,0:T(8,128)(2,1)S(1)} %get-tuple-element.177), channel_id=1, source_target_pairs={{0,16},{4,20},{8,24},{12,28},{16,0},{20,4},{24,8},{28,12},{1,17},{... | collective-permute-start | bytes 294920 | tf_op jit(solution)/shard_map/ppermute | solution.py:795
  103.4 8.1 %collective-permute-start.25 = (bf16[4,64,192]{2,1,0:T(8,128)(2,1)S(1)}, bf16[4,64,192]{2,1,0:T(8,128)(2,1)S(1)}, u32[]{:S(2)}, u32[]{:S(2)}) collective-permute-start(bf16[4,64,192]{2,1,0:T(8,128)(2,1)S(1)} %get-tuple-element.191), channel_id=1, source_target_pairs={{0,8},{4,12},{8,0},{12,4},{16,24},{20,28},{24,16},{28,20},{1,9},{5... | collective-permute-start | bytes 294920 | tf_op jit(solution)/shard_map/ppermute | solution.py:795
  104.8 6.7 %collective-permute-start.22 = (bf16[128,1024]{1,0:T(8,128)(2,1)S(1)}, bf16[128,1024]{1,0:T(8,128)(2,1)S(1)}, u32[]{:S(2)}, u32[]{:S(2)}) collective-permute-start(bf16[128,1024]{1,0:T(8,128)(2,1)S(1)} %get-tuple-element.187), channel_id=1, source_target_pairs={{0,8},{8,16},{16,24},{24,28},{28,20},{20,12},{12,4},{4,0},{1,9},{9... | collective-permute-start | bytes 786440 | tf_op jit(solution)/shard_map/ppermute | solution.py:619
  106.9 6.4 %collective-permute-start.23 = (bf16[128,1024]{1,0:T(8,128)(2,1)S(1)}, bf16[128,1024]{1,0:T(8,128)(2,1)S(1)}, u32[]{:S(2)}, u32[]{:S(2)}) collective-permute-start(bf16[128,1024]{1,0:T(8,128)(2,1)S(1)} %get-tuple-element.188), channel_id=1, source_target_pairs={{8,0},{16,8},{24,16},{28,24},{20,28},{12,20},{4,12},{0,4},{9,1},{1... | collective-permute-start | bytes 786440 | tf_op jit(solution)/shard_map/ppermute | solution.py:619
  106.9 6.4 %collective-permute-start.24 = (bf16[128,1024]{1,0:T(8,128)(2,1)S(1)}, bf16[128,1024]{1,0:T(8,128)(2,1)S(1)}, u32[]{:S(2)}, u32[]{:S(2)}) collective-permute-start(bf16[128,1024]{1,0:T(8,128)(2,1)S(1)} %get-tuple-element.189), channel_id=1, source_target_pairs={{0,2},{2,0},{1,3},{3,1},{4,6},{6,4},{5,7},{7,5},{8,10},{10,8},{9,1... | collective-permute-start | bytes 786440 | tf_op jit(solution)/shard_map/ppermute | solution.py:620
  110.6 4.1 %copy-start.10 = (bf16[1024,1024]{1,0:T(8,128)(2,1)S(1)}, bf16[1024,1024]{1,0:T(8,128)(2,1)}, u32[]{:S(2)}) copy-start(bf16[1024,1024]{1,0:T(8,128)(2,1)} %copy-done.9) | copy-start | bytes 6291460
  111.5 3.2 %copy-start.8 = (bf16[1024,1024]{1,0:T(8,128)(2,1)S(1)}, bf16[1024,1024]{1,0:T(8,128)(2,1)}, u32[]{:S(2)}) copy-start(bf16[1024,1024]{1,0:T(8,128)(2,1)} %copy-done.7) | copy-start | bytes 6291460
  111.5 3.2 %copy-start.25 = (bf16[64,4096]{1,0:T(8,128)(2,1)S(1)}, bf16[64,4096]{1,0:T(8,128)(2,1)}, u32[]{:S(2)}) copy-start(bf16[64,4096]{1,0:T(8,128)(2,1)} %down_ref.5) | copy-start | bytes 1572868
  113.3 6.2 %collective-permute-start.26 = (bf16[4,64,192]{2,1,0:T(8,128)(2,1)S(1)}, bf16[4,64,192]{2,1,0:T(8,128)(2,1)S(1)}, u32[]{:S(2)}, u32[]{:S(2)}) collective-permute-start(bf16[4,64,192]{2,1,0:T(8,128)(2,1)S(1)} %get-tuple-element.197), channel_id=1, source_target_pairs={{0,4},{4,0},{8,12},{12,8},{16,20},{20,16},{24,28},{28,24},{1,5},{5... | collective-permute-start | bytes 294920 | tf_op jit(solution)/shard_map/ppermute | solution.py:795
  117.8 6.6 %copy-start.5 = (bf16[512,4096]{1,0:T(8,128)(2,1)S(1)}, bf16[512,4096]{1,0:T(8,128)(2,1)}, u32[]{:S(2)}) copy-start(bf16[512,4096]{1,0:T(8,128)(2,1)} %get-tuple-element.216.top_ref) | copy-start | bytes 12582916
  119.5 4.9 %copy-start.6 = (bf16[512,2048]{1,0:T(8,128)(2,1)S(1)}, bf16[512,2048]{1,0:T(8,128)(2,1)}, u32[]{:S(2)}) copy-start(bf16[512,2048]{1,0:T(8,128)(2,1)} %get-tuple-element.217.low_ref) | copy-start | bytes 6291460
  119.7 6.5 %collective-permute-start.28 = (f32[8,128]{1,0:T(8,128)S(1)}, f32[8,128]{1,0:T(8,128)S(1)}, u32[]{:S(2)}, u32[]{:S(2)}) collective-permute-start(f32[8,128]{1,0:T(8,128)S(1)} %get-tuple-element.215), channel_id=1, source_target_pairs={{0,16},{4,20},{8,24},{12,28},{16,0},{20,4},{24,8},{28,12},{1,17},{... | collective-permute-start | bytes 12296 | tf_op jit(solution)/shard_map/ppermute | solution.py:795
  121.8 8.5 %collective-permute-start.27 = (bf16[128,1024]{1,0:T(8,128)(2,1)S(1)}, bf16[128,1024]{1,0:T(8,128)(2,1)S(1)}, u32[]{:S(2)}, u32[]{:S(2)}) collective-permute-start(bf16[128,1024]{1,0:T(8,128)(2,1)S(1)} %get-tuple-element.212), channel_id=1, source_target_pairs={{2,0},{3,1},{6,4},{7,5},{10,8},{11,9},{14,12},{15,13},{18,16},{19,... | collective-permute-start | bytes 786440 | tf_op jit(solution)/shard_map/ppermute | solution.py:905
  123.1 14.8 %collective-permute-start.30 = (bf16[128,1024]{1,0:T(8,128)(2,1)S(1)}, bf16[128,1024]{1,0:T(8,128)(2,1)S(1)}, u32[]{:S(2)}, u32[]{:S(2)}) collective-permute-start(bf16[128,1024]{1,0:T(8,128)(2,1)S(1)} %get-tuple-element.223), channel_id=1, source_target_pairs={{2,0},{3,1},{6,4},{7,5},{10,8},{11,9},{14,12},{15,13},{18,16},{19,... | collective-permute-start | bytes 786440 | tf_op jit(solution)/shard_map/ppermute | solution.py:905
  126.2 1.9 %collective-permute-start.29 = (f32[8,128]{1,0:T(8,128)S(1)}, f32[8,128]{1,0:T(8,128)S(1)}, u32[]{:S(2)}, u32[]{:S(2)}) collective-permute-start(f32[8,128]{1,0:T(8,128)S(1)} %add.338), channel_id=1, source_target_pairs={{0,1},{1,0},{2,3},{3,2},{4,5},{5,4},{6,7},{7,6},{8,9},{9,8},{10,11... | collective-permute-start | bytes 12296 | tf_op jit(solution)/shard_map/ppermute | solution.py:843
  131.5 8.6 %collective-permute-start.33 = (bf16[256,1024]{1,0:T(8,128)(2,1)S(1)}, bf16[256,1024]{1,0:T(8,128)(2,1)S(1)}, u32[]{:S(2)}, u32[]{:S(2)}) collective-permute-start(bf16[256,1024]{1,0:T(8,128)(2,1)S(1)} %get-tuple-element.237), channel_id=1, source_target_pairs={{0,1},{1,0},{2,3},{3,2},{4,5},{5,4},{6,7},{7,6},{8,9},{9,8},{10,11... | collective-permute-start | bytes 1572872 | tf_op jit(solution)/shard_map/ppermute | solution.py:869
  131.6 6.3 %collective-permute-start.32 = (f32[64,192]{1,0:T(8,128)S(1)}, f32[64,192]{1,0:T(8,128)S(1)}, u32[]{:S(2)}, u32[]{:S(2)}) collective-permute-start(f32[64,192]{1,0:T(8,128)S(1)} %get-tuple-element.234), channel_id=1, source_target_pairs={{0,0},{1,16},{2,1},{3,17},{4,2},{5,18},{6,3},{7,19},{8,4},{9,20},{... | collective-permute-start | bytes 147464 | tf_op jit(solution)/shard_map/ppermute | solution.py:1029
  132.3 5.6 %collective-permute-start.31 = (f32[8,128]{1,0:T(8,128)S(1)}, f32[8,128]{1,0:T(8,128)S(1)}, u32[]{:S(2)}, u32[]{:S(2)}) collective-permute-start(f32[8,128]{1,0:T(8,128)S(1)} %add.339), channel_id=1, source_target_pairs={{0,2},{2,0},{1,3},{3,1},{4,6},{6,4},{5,7},{7,5},{8,10},{10,8},{9,1... | collective-permute-start | bytes 12296 | tf_op jit(solution)/shard_map/ppermute | solution.py:843
  139.2 2.0 %collective-permute-start.34 = (bf16[256,1024]{1,0:T(8,128)(2,1)S(1)}, bf16[256,1024]{1,0:T(8,128)(2,1)S(1)}, u32[]{:S(2)}, u32[]{:S(2)}) collective-permute-start(bf16[256,1024]{1,0:T(8,128)(2,1)S(1)} %get-tuple-element.238), channel_id=1, source_target_pairs={{0,1},{1,0},{2,3},{3,2},{4,5},{5,4},{6,7},{7,6},{8,9},{9,8},{10,11... | collective-permute-start | bytes 1572872 | tf_op jit(solution)/shard_map/ppermute | solution.py:869
  (21 other events, 24.6 us)

commit v5 on v4

--- a/solution.py
+++ b/solution.py
@@ -1023,10 +1023,10 @@
     bases = [back(0)]
     squares, bases, grads = lax.optimization_barrier((squares, bases, grads))
     squares = over_axis(squares, "core")
+    total = lax.ppermute(total, AXES, homes)
     bases.append(back(1))
     squares, bases, total = lax.optimization_barrier((squares, bases, total))
     squares = over_axis(squares, "x")
-    total = lax.ppermute(total, AXES, homes)
     near, far = [], []
     for group in range(groups):
         if group == groups - 1:

time: 144 us -> 146 us (1.014)
    ppermute x9, starting transfers between devices: 1.68 us -> 4.08 us  [swapped(): return lax.ppermute(value, 'core', swap)]
where the time goes in v5:
time: 146 us; the launch traced here: 145 us
  waiting for transfers between devices  42.4 us (29%)
  Pallas kernels  42.2 us (29%)
  starting transfers between devices  37.5 us (26%)
  local copies, waits for them, and re-layouts  16.4 us (11%)
  other arithmetic  4.23 us (3%)
  between operations  1.76 us (1%)
    ppermute x1, waiting for transfers between devices, over_x(): lax.ppermute(value, 'x', turn)  13.5 us
    pallas_call x1, Pallas kernels, local_part(): pl.pallas_call(functools.partial(local_kernel, heads), grid_spec=spec, ou...  13.3 us
    unnamed x118, local copies, waits for them, and re-layouts  11.8 us
    ppermute x10, starting transfers between devices, step(): lax.ppermute(array, 'dp', perm)  11.6 us
    ppermute x3, waiting for transfers between devices, carried(): arrived = lax.ppermute(sent, 'x', perm)  10.3 us
    ppermute x5, starting transfers between devices, step(): lax.ppermute(self.crossing, 'x', turn)  7.7 us
    pallas_call x6, Pallas kernels, product_part(): pl.pallas_call(functools.partial(product_kernel, first, tuple((piece[1:]...  6.81 us
    ppermute x4, waiting for transfers between devices, far_in_dp(): lax.ppermute(value, 'dp', [(i, i ^ distance) for i in range(lax.axis_size...  6.76 us
  transfers between devices with their start and end apart: 35, of which 9 were waited for; matrix products, arithmetic and copies ran while one was open for 4% of the time, Pallas kernels for 28%

profile of v5, /device:TPU:0, one launch (start us, length us, event | category | flops | bytes accessed | tf_op | source)
XLA Modules:
  0.0 144.9 jit_solution(17583994758298045064)
XLA Ops:
  0.7 1.0 constant_dynamic-slice_fusion.5
  1.7 0.9 copy.22.near_ref
  3.3 1.3 constant_dynamic-slice_fusion.4
  4.6 1.2 pad_maximum_fusion.1
  6.5 0.8 step_part.1
  7.8 2.6 %collective-permute-start.2 = (bf16[128,1024]{1,0:T(8,128)(2,1)S(1)}, bf16[128,1024]{1,0:T(8,128)(2,1)S(1)}, u32[]{:S(2)}, u32[]{:S(2)}) collective-permute-start(bf16[128,1024]{1,0:T(8,128)(2,1)S(1)} %slice.12.rest_0_), channel_id=1, source_target_pairs={{8,0},{16,8},{24,16},{28,24},{20,28},{12,20},{4,12},{0,4},{9,1},{1... | collective-permute-start | bytes 786440 | tf_op jit(solution)/shard_map/ppermute | solution.py:619
  10.5 1.9 %collective-permute-start.3 = (bf16[128,2048]{1,0:T(8,128)(2,1)S(1)}, bf16[128,2048]{1,0:T(8,128)(2,1)S(1)}, u32[]{:S(2)}, u32[]{:S(2)}) collective-permute-start(bf16[128,2048]{1,0:T(8,128)(2,1)S(1)} %pad_maximum_fusion.2.refs_0_), channel_id=1, source_target_pairs={{0,2},{2,0},{1,3},{3,1},{4,6},{6,4},{5,7},{7,5},{8,10},{10,8},{9,1... | collective-permute-start | bytes 1572872 | tf_op jit(solution)/shard_map/ppermute | solution.py:620
  13.8 1.1 broadcast_select_fusion.5
  14.9 13.3 %local_part.1 = (bf16[512,4096]{1,0:T(8,128)(2,1)}, bf16[512,2048]{1,0:T(8,128)(2,1)}, bf16[1024,1024]{1,0:T(8,128)(2,1)S(1)}, f32[512,1024]{1,0:T(8,128)S(1)}, bf16[256,1024]{1,0:T(8,128)(2,1)S(1)}) custom-call(s32[1]{0:T(128)} %bitcast.core_ref, bf16[256,4096]{1,0:T(8,128)(2,1)S(1)} %copy-done.31, bf16[256,2560]{1,0:T(8,128)(2,1)} %collective-permute-done.5.far_ref, ...), custom_call_target="tpu_custom_call" | custom-call | flops 17179869184 | tf_op jit(solution)/shard_map/local_part/pallas_call | solution.py:219
  28.3 2.2 %collective-permute-start.11 = (bf16[256,1024]{1,0:T(8,128)(2,1)S(1)}, bf16[256,1024]{1,0:T(8,128)(2,1)S(1)}, u32[]{:S(2)}, u32[]{:S(2)}) collective-permute-start(bf16[256,1024]{1,0:T(8,128)(2,1)S(1)} %get-tuple-element.149), channel_id=1, source_target_pairs={{0,2},{1,3},{4,6},{5,7},{8,10},{9,11},{12,14},{13,15},{16,18},{17,... | collective-permute-start | bytes 1572872 | tf_op jit(solution)/shard_map/ppermute | solution.py:905
  31.0 2.0 %collective-permute-start.6 = (bf16[384,1024]{1,0:T(8,128)(2,1)S(1)}, bf16[384,1024]{1,0:T(8,128)(2,1)S(1)}, u32[]{:S(2)}, u32[]{:S(2)}) collective-permute-start(bf16[384,1024]{1,0:T(8,128)(2,1)S(1)} %get-tuple-element.141), channel_id=1, source_target_pairs={{0,8},{8,16},{16,24},{24,28},{28,20},{20,12},{12,4},{4,0},{1,9},{9... | collective-permute-start | bytes 2359304 | tf_op jit(solution)/shard_map/ppermute | solution.py:619
  33.0 0.7 collective-permute-start.7
  33.8 8.9 %collective-permute-done.11.incoming_ref = bf16[256,1024]{1,0:T(8,128)(2,1)S(1)} collective-permute-done((bf16[256,1024]{1,0:T(8,128)(2,1)S(1)}, bf16[256,1024]{1,0:T(8,128)(2,1)S(1)}, u32[]{:S(2)}, u32[]{:S(2)}) %collective-permute-start.11) | collective-permute-done | bytes 524320 | tf_op jit(solution)/shard_map/ppermute | solution.py:905
  42.7 5.1 %norm_part.1 = (bf16[1024,1024]{1,0:T(8,128)(2,1)S(1)}, bf16[1024,1024]{1,0:T(8,128)(2,1)S(1)}, f32[512,64]{1,0:T(8,128)S(1)}, f32[64,2048]{1,0:T(8,128)S(1)}) custom-call(s32[1]{0:T(128)} %bitcast.core_ref, bf16[512,256]{1,0:T(8,128)(2,1)S(1)} %pad_maximum_fusion.4.c_ref, bf16[256,1024]{1,0:T(8,128)(2,1)S(1)} %collective-permute-done.11.incoming_ref, ...), custom_call_target="tpu_custom_call" | custom-call | flops 6442450944 | tf_op jit(solution)/shard_map/norm_part/pallas_call | solution.py:298
  47.9 1.4 copy-done.7
  49.3 4.2 %collective-permute-done.8.rest_3_.rest_5_ = bf16[256,1024]{1,0:T(8,128)(2,1)S(1)} collective-permute-done((bf16[256,1024]{1,0:T(8,128)(2,1)S(1)}, bf16[256,1024]{1,0:T(8,128)(2,1)S(1)}, u32[]{:S(2)}, u32[]{:S(2)}) %collective-permute-start.8) | collective-permute-done | bytes 524320 | tf_op jit(solution)/shard_map/ppermute | solution.py:620
  53.6 2.0 %collective-permute-start.13 = (bf16[384,1024]{1,0:T(8,128)(2,1)S(1)}, bf16[384,1024]{1,0:T(8,128)(2,1)S(1)}, u32[]{:S(2)}, u32[]{:S(2)}) collective-permute-start(bf16[384,1024]{1,0:T(8,128)(2,1)S(1)} %collective-permute-done.6.refs_0_.rest_1_), channel_id=1, source_target_pairs={{0,8},{8,16},{16,24},{24,28},{28,20},{20,12},{12,4},{4,0},{1,9},{9... | collective-permute-start | bytes 2359304 | tf_op jit(solution)/shard_map/ppermute | solution.py:619
  55.7 2.5 %collective-permute-start.15 = (bf16[256,1024]{1,0:T(8,128)(2,1)S(1)}, bf16[256,1024]{1,0:T(8,128)(2,1)S(1)}, u32[]{:S(2)}, u32[]{:S(2)}) collective-permute-start(bf16[256,1024]{1,0:T(8,128)(2,1)S(1)} %cut_rows.5), channel_id=1, source_target_pairs={{0,2},{2,0},{1,3},{3,1},{4,6},{6,4},{5,7},{7,5},{8,10},{10,8},{9,1... | collective-permute-start | bytes 1572872 | tf_op jit(solution)/shard_map/ppermute | solution.py:620
  58.7 1.3 collective-permute-done.16.far_ref
  59.9 1.0 pack_sums.1
  61.0 0.8 copy-done.44
  61.8 13.5 %collective-permute-done.17.refs_0_ = bf16[8,64,192]{2,1,0:T(8,128)(2,1)S(1)} collective-permute-done((bf16[8,64,192]{2,1,0:T(8,128)(2,1)S(1)}, bf16[8,64,192]{2,1,0:T(8,128)(2,1)S(1)}, u32[]{:S(2)}, u32[]{:S(2)}) %collective-permute-start.17) | collective-permute-done | bytes 196640 | tf_op jit(solution)/shard_map/ppermute | solution.py:791
  75.3 0.7 copy-done.40
  76.0 0.8 copy-done.22
  76.8 1.3 cut_rows.6
  78.1 1.0 copy-done.16
  79.1 0.8 copy-done.39
  79.9 1.7 %collective-permute-start.18 = (bf16[320,1024]{1,0:T(8,128)(2,1)}, bf16[320,1024]{1,0:T(8,128)(2,1)}, u32[]{:S(2)}, u32[]{:S(2)}) collective-permute-start(bf16[320,1024]{1,0:T(8,128)(2,1)} %get-tuple-element.171), channel_id=1, source_target_pairs={{0,8},{8,16},{16,24},{24,28},{28,20},{20,12},{12,4},{4,0},{1,9},{9... | collective-permute-start | bytes 1966088 | tf_op jit(solution)/shard_map/ppermute | solution.py:619
  81.9 1.0 slice.15.rest_1_
  82.9 1.8 %collective-permute-start.20 = (bf16[256,1024]{1,0:T(8,128)(2,1)}, bf16[256,1024]{1,0:T(8,128)(2,1)S(1)}, u32[]{:S(2)}, u32[]{:S(2)}) collective-permute-start(bf16[256,1024]{1,0:T(8,128)(2,1)} %copy-done.39), channel_id=1, source_target_pairs={{0,2},{2,0},{1,3},{3,1},{4,6},{6,4},{5,7},{7,5},{8,10},{10,8},{9,1... | collective-permute-start | bytes 1572872 | tf_op jit(solution)/shard_map/ppermute | solution.py:620
  84.7 1.6 %copy-done.3 = bf16[256,4096]{1,0:T(8,128)(2,1)S(1)} copy-done((bf16[256,4096]{1,0:T(8,128)(2,1)S(1)}, bf16[256,4096]{1,0:T(8,128)(2,1)}, u32[]{:S(2)}) %copy-start.3) | copy-done | bytes 2097176
  86.3 1.1 copy-done.13
  87.4 1.1 copy-done.15
  88.5 1.0 copy-done.30
  89.6 1.0 product_part.6.rest_0_
  90.8 1.0 product_part.8.rest_0_
  92.0 2.8 %collective-permute-start.21 = (bf16[4,64,192]{2,1,0:T(8,128)(2,1)S(1)}, bf16[4,64,192]{2,1,0:T(8,128)(2,1)S(1)}, u32[]{:S(2)}, u32[]{:S(2)}) collective-permute-start(bf16[4,64,192]{2,1,0:T(8,128)(2,1)S(1)} %get-tuple-element.177), channel_id=1, source_target_pairs={{0,16},{4,20},{8,24},{12,28},{16,0},{20,4},{24,8},{28,12},{1,17},{... | collective-permute-start | bytes 294920 | tf_op jit(solution)/shard_map/ppermute | solution.py:795
  94.8 0.9 product_part.7.rest_0_
  95.7 0.9 product_part.9.rest_0_
  96.6 6.8 %collective-permute-done.21.arrived_ref = bf16[4,64,192]{2,1,0:T(8,128)(2,1)S(1)} collective-permute-done((bf16[4,64,192]{2,1,0:T(8,128)(2,1)S(1)}, bf16[4,64,192]{2,1,0:T(8,128)(2,1)S(1)}, u32[]{:S(2)}, u32[]{:S(2)}) %collective-permute-start.21) | collective-permute-done | bytes 98336 | tf_op jit(solution)/shard_map/ppermute | solution.py:795
  103.5 1.3 cut_rows.7
  104.8 2.1 %collective-permute-start.22 = (bf16[128,1024]{1,0:T(8,128)(2,1)S(1)}, bf16[128,1024]{1,0:T(8,128)(2,1)S(1)}, u32[]{:S(2)}, u32[]{:S(2)}) collective-permute-start(bf16[128,1024]{1,0:T(8,128)(2,1)S(1)} %get-tuple-element.187), channel_id=1, source_target_pairs={{0,8},{8,16},{16,24},{24,28},{28,20},{20,12},{12,4},{4,0},{1,9},{9... | collective-permute-start | bytes 786440 | tf_op jit(solution)/shard_map/ppermute | solution.py:619
  106.9 1.5 %collective-permute-start.24 = (bf16[128,1024]{1,0:T(8,128)(2,1)S(1)}, bf16[128,1024]{1,0:T(8,128)(2,1)S(1)}, u32[]{:S(2)}, u32[]{:S(2)}) collective-permute-start(bf16[128,1024]{1,0:T(8,128)(2,1)S(1)} %get-tuple-element.189), channel_id=1, source_target_pairs={{0,2},{2,0},{1,3},{3,1},{4,6},{6,4},{5,7},{7,5},{8,10},{10,8},{9,1... | collective-permute-start | bytes 786440 | tf_op jit(solution)/shard_map/ppermute | solution.py:620
  108.4 2.2 %product_part.10.earlier_ref = f32[512,1024]{1,0:T(8,128)S(1)} custom-call(s32[1]{0:T(128)} %bitcast.core_ref, bf16[256,4096]{1,0:T(8,128)(2,1)S(1)} %dynamic-slice_dynamic-update-slice_fusion.1.near_ref, bf16[256,4096]{1,0:T(8,128)(2,1)S(1)} %copy-done.4, f32[512,1024]{1,0:T(8,128)S(1)} %product_part.7.rest_0_, ...), custom_call_target="tpu_custom_call", output_to_operand_aliasing={{}: (3, {})} | custom-call | flops 1073741824 | tf_op jit(solution)/shard_map/product_part/pallas_call | solution.py:343
  110.6 0.9 product_part.11.earlier_ref
  111.6 1.7 %collective-permute-done.23.rest_1_ = bf16[128,1024]{1,0:T(8,128)(2,1)S(1)} collective-permute-done((bf16[128,1024]{1,0:T(8,128)(2,1)S(1)}, bf16[128,1024]{1,0:T(8,128)(2,1)S(1)}, u32[]{:S(2)}, u32[]{:S(2)}) %collective-permute-start.23) | collective-permute-done | bytes 262176 | tf_op jit(solution)/shard_map/ppermute | solution.py:619
  113.3 1.4 collective-permute-start.26
  114.7 3.0 %grad_part.3 = (bf16[512,1024]{1,0:T(8,128)(2,1)S(1)}, f32[256,1024]{1,0:T(8,128)S(1)}, bf16[128,1024]{1,0:T(8,128)(2,1)S(1)}) custom-call(s32[1]{0:T(128)} %bitcast.core_ref, bf16[256,4096]{1,0:T(8,128)(2,1)S(1)} %dynamic-slice_dynamic-update-slice_fusion.1.near_ref, bf16[256,4096]{1,0:T(8,128)(2,1)S(1)} %copy-done.4, ...), custom_call_target="tpu_custom_call" | custom-call | flops 2147483648 | tf_op jit(solution)/shard_map/grad_part/pallas_call | solution.py:412
  117.8 1.7 %grad_part.2 = (bf16[512,1024]{1,0:T(8,128)(2,1)S(1)}, f32[256,1024]{1,0:T(8,128)S(1)}, bf16[128,1024]{1,0:T(8,128)(2,1)S(1)}) custom-call(s32[1]{0:T(128)} %bitcast.core_ref, bf16[256,4096]{1,0:T(8,128)(2,1)S(1)} %dynamic-slice_dynamic-update-slice_fusion.1.near_ref, bf16[256,4096]{1,0:T(8,128)(2,1)S(1)} %copy-done.4, ...), custom_call_target="tpu_custom_call" | custom-call | flops 2147483648 | tf_op jit(solution)/shard_map/grad_part/pallas_call | solution.py:412
  119.7 2.1 %collective-permute-start.28 = (f32[8,128]{1,0:T(8,128)S(1)}, f32[8,128]{1,0:T(8,128)S(1)}, u32[]{:S(2)}, u32[]{:S(2)}) collective-permute-start(f32[8,128]{1,0:T(8,128)S(1)} %get-tuple-element.215), channel_id=1, source_target_pairs={{0,16},{4,20},{8,24},{12,28},{16,0},{20,4},{24,8},{28,12},{1,17},{... | collective-permute-start | bytes 12296 | tf_op jit(solution)/shard_map/ppermute | solution.py:795
  121.8 0.7 collective-permute-start.30
  122.4 1.3 collective-permute-start.27
  123.7 1.3 collective-permute-start.31
  125.1 1.8 %back_part.2.base_ref = f32[512,1024]{1,0:T(8,128)S(1)} custom-call(s32[1]{0:T(128)} %bitcast.core_ref, bf16[512,4096]{1,0:T(8,128)(2,1)S(1)} %copy-done.5, bf16[512,2048]{1,0:T(8,128)(2,1)S(1)} %copy-done.6, bf16[512,1024]{1,0:T(8,128)(2,1)S(1)} %get-tuple-element.218.grad_ref, f32[512,64]{1,0:T(8,128)S(1)} %get-tuple-element.219.step_ref, ...), custom_call_target="tpu_custom_call" | custom-call | flops 2147483648 | tf_op jit(solution)/shard_map/back_part/pallas_call | solution.py:466
  126.9 2.3 %collective-permute-start.29 = (f32[8,128]{1,0:T(8,128)S(1)}, f32[8,128]{1,0:T(8,128)S(1)}, u32[]{:S(2)}, u32[]{:S(2)}) collective-permute-start(f32[8,128]{1,0:T(8,128)S(1)} %add.338), channel_id=1, source_target_pairs={{0,1},{1,0},{2,3},{3,2},{4,5},{5,4},{6,7},{7,6},{8,9},{9,8},{10,11... | collective-permute-start | bytes 12296 | tf_op jit(solution)/shard_map/ppermute | solution.py:843
  129.3 1.8 %back_part.3.base_ref = f32[512,1024]{1,0:T(8,128)S(1)} custom-call(s32[1]{0:T(128)} %bitcast.core_ref, bf16[512,4096]{1,0:T(8,128)(2,1)S(1)} %copy-done.5, bf16[512,2048]{1,0:T(8,128)(2,1)S(1)} %copy-done.6, bf16[512,1024]{1,0:T(8,128)(2,1)S(1)} %get-tuple-element.227.grad_ref, f32[512,64]{1,0:T(8,128)S(1)} %get-tuple-element.219.step_ref, ...), custom_call_target="tpu_custom_call" | custom-call | flops 2147483648 | tf_op jit(solution)/shard_map/back_part/pallas_call | solution.py:466
  131.1 1.4 collective-permute-done.27.outgoing_ref
  132.5 1.3 cross_part.2
  133.8 2.5 %collective-permute-start.33 = (bf16[256,1024]{1,0:T(8,128)(2,1)S(1)}, bf16[256,1024]{1,0:T(8,128)(2,1)S(1)}, u32[]{:S(2)}, u32[]{:S(2)}) collective-permute-start(bf16[256,1024]{1,0:T(8,128)(2,1)S(1)} %get-tuple-element.237), channel_id=1, source_target_pairs={{0,1},{1,0},{2,3},{3,2},{4,5},{5,4},{6,7},{7,6},{8,9},{9,8},{10,11... | collective-permute-start | bytes 1572872 | tf_op jit(solution)/shard_map/ppermute | solution.py:869
  136.3 3.6 %collective-permute-done.32 = f32[8,128]{1,0:T(8,128)S(1)} collective-permute-done((f32[8,128]{1,0:T(8,128)S(1)}, f32[8,128]{1,0:T(8,128)S(1)}, u32[]{:S(2)}, u32[]{:S(2)}) %collective-permute-start.32) | collective-permute-done | bytes 4128 | tf_op jit(solution)/shard_map/ppermute | solution.py:843
  139.9 1.3 cross_part.3
  141.2 0.7 finish.1
  142.1 1.0 collective-permute-done.34
  143.3 1.5 %pad_maximum_fusion = bf16[256,4096]{1,0:T(8,128)(2,1)} fusion(bf16[256,2048]{1,0:T(8,128)(2,1)S(1)} %get-tuple-element.244, bf16[256,2048]{1,0:T(8,128)(2,1)S(1)} %get-tuple-element.243), kind=kLoop, calls=%fused_computation | loop fusion | flops 4194304 | bytes 4194304 | tf_op jit(solution)/shard_map/concatenate | solution.py:864
  (177 shorter events, 5.9 us)
Async XLA Ops:
  0.6 12.7 %copy-start = (bf16[64,2048]{1,0:T(8,128)(2,1)S(1)}, bf16[64,2048]{1,0:T(8,128)(2,1)}, u32[]{:S(2)}) copy-start(bf16[64,2048]{1,0:T(8,128)(2,1)} %param.24) | copy-start | bytes 786436
  0.6 3.9 %copy-start.47 = (bf16[256,512]{1,0:T(8,128)(2,1)S(1)}, bf16[256,512]{1,0:T(8,128)(2,1)}, u32[]{:S(2)}) copy-start(bf16[256,512]{1,0:T(8,128)(2,1)} %param.17) | copy-start | bytes 786436
  0.7 3.9 %copy-start.48 = (bf16[256,512]{1,0:T(8,128)(2,1)S(1)}, bf16[256,512]{1,0:T(8,128)(2,1)}, u32[]{:S(2)}) copy-start(bf16[256,512]{1,0:T(8,128)(2,1)} %param.16) | copy-start | bytes 786436
  2.7 3.8 %collective-permute-start.4 = (f32[256,64]{1,0:T(8,128)S(1)}, f32[256,64]{1,0:T(8,128)S(1)}, u32[]{:S(2)}, u32[]{:S(2)}) collective-permute-start(f32[256,64]{1,0:T(8,128)S(1)} %copy.22.near_ref), channel_id=1, source_target_pairs={{0,1},{1,0},{2,3},{3,2},{4,5},{5,4},{6,7},{7,6},{8,9},{9,8},{10,11... | collective-permute-start | bytes 196616 | tf_op jit(solution)/shard_map/ppermute | solution.py:869
  3.2 4.2 %collective-permute-start = (bf16[64,2048]{1,0:T(8,128)(2,1)S(1)}, bf16[64,2048]{1,0:T(8,128)(2,1)S(1)}, u32[]{:S(2)}, u32[]{:S(2)}) collective-permute-start(bf16[64,2048]{1,0:T(8,128)(2,1)S(1)} %constant_dynamic-slice_fusion.5), channel_id=1, source_target_pairs={{0,1},{1,0},{2,3},{3,2},{4,5},{5,4},{6,7},{7,6},{8,9},{9,8},{10,11... | collective-permute-start | bytes 786440 | tf_op jit(solution)/shard_map/ppermute | solution.py:869
  4.6 1.9 %copy-start.42 = (f32[64]{0:T(128)S(1)}, f32[64]{0:T(128)}, u32[]{:S(2)}) copy-start(f32[64]{0:T(128)} %param.19) | copy-start | bytes 772
  4.6 1.9 %copy-start.43 = (f32[64]{0:T(128)S(1)}, f32[64]{0:T(128)}, u32[]{:S(2)}) copy-start(f32[64]{0:T(128)} %param.20) | copy-start | bytes 772
  5.8 8.0 %collective-permute-start.5 = (bf16[256,2560]{1,0:T(8,128)(2,1)}, bf16[256,2560]{1,0:T(8,128)(2,1)}, u32[]{:S(2)}, u32[]{:S(2)}) collective-permute-start(bf16[256,2560]{1,0:T(8,128)(2,1)} %pad_maximum_fusion.1), channel_id=1, source_target_pairs={{0,1},{1,0},{2,3},{3,2},{4,5},{5,4},{6,7},{7,6},{8,9},{9,8},{10,11... | collective-permute-start | bytes 3932168 | tf_op jit(solution)/shard_map/ppermute | solution.py:869
  7.3 5.1 %copy-start.32 = (bf16[256,4096]{1,0:T(8,128)(2,1)S(1)}, bf16[256,4096]{1,0:T(8,128)(2,1)}, u32[]{:S(2)}) copy-start(bf16[256,4096]{1,0:T(8,128)(2,1)} %near_ref.1) | copy-start | bytes 6291460
  7.7 4.9 %copy-start.26 = (bf16[256,2048]{1,0:T(8,128)(2,1)S(1)}, bf16[256,2048]{1,0:T(8,128)(2,1)}, u32[]{:S(2)}) copy-start(bf16[256,2048]{1,0:T(8,128)(2,1)} %cot_ref) | copy-start | bytes 3145732
  7.8 5.5 %copy-start.27 = (bf16[128,1024]{1,0:T(8,128)(2,1)}, bf16[128,1024]{1,0:T(8,128)(2,1)S(1)}, u32[]{:S(2)}) copy-start(bf16[128,1024]{1,0:T(8,128)(2,1)S(1)} %slice.12.rest_0_) | copy-start | bytes 786436
  7.8 20.4 %collective-permute-start.2 = (bf16[128,1024]{1,0:T(8,128)(2,1)S(1)}, bf16[128,1024]{1,0:T(8,128)(2,1)S(1)}, u32[]{:S(2)}, u32[]{:S(2)}) collective-permute-start(bf16[128,1024]{1,0:T(8,128)(2,1)S(1)} %slice.12.rest_0_), channel_id=1, source_target_pairs={{8,0},{16,8},{24,16},{28,24},{20,28},{12,20},{4,12},{0,4},{9,1},{1... | collective-permute-start | bytes 786440 | tf_op jit(solution)/shard_map/ppermute | solution.py:619
  10.4 17.8 %collective-permute-start.1 = (bf16[128,1024]{1,0:T(8,128)(2,1)S(1)}, bf16[128,1024]{1,0:T(8,128)(2,1)S(1)}, u32[]{:S(2)}, u32[]{:S(2)}) collective-permute-start(bf16[128,1024]{1,0:T(8,128)(2,1)S(1)} %slice.12.rest_0_), channel_id=1, source_target_pairs={{0,8},{8,16},{16,24},{24,28},{28,20},{20,12},{12,4},{4,0},{1,9},{9... | collective-permute-start | bytes 786440 | tf_op jit(solution)/shard_map/ppermute | solution.py:619
  10.5 17.7 %collective-permute-start.3 = (bf16[128,2048]{1,0:T(8,128)(2,1)S(1)}, bf16[128,2048]{1,0:T(8,128)(2,1)S(1)}, u32[]{:S(2)}, u32[]{:S(2)}) collective-permute-start(bf16[128,2048]{1,0:T(8,128)(2,1)S(1)} %pad_maximum_fusion.2.refs_0_), channel_id=1, source_target_pairs={{0,2},{2,0},{1,3},{3,1},{4,6},{6,4},{5,7},{7,5},{8,10},{10,8},{9,1... | collective-permute-start | bytes 1572872 | tf_op jit(solution)/shard_map/ppermute | solution.py:620
  13.0 1.9 %copy-start.11 = (bf16[48,1024]{1,0:T(8,128)(2,1)S(1)}, bf16[48,1024]{1,0:T(8,128)(2,1)}, u32[]{:S(2)}) copy-start(bf16[48,1024]{1,0:T(8,128)(2,1)} %constant.191.clone.pattern_ref) | copy-start | bytes 294916
  13.2 29.4 %collective-permute-start.10 = (bf16[256,4096]{1,0:T(8,128)(2,1)S(1)}, bf16[256,4096]{1,0:T(8,128)(2,1)S(1)}, u32[]{:S(2)}, u32[]{:S(2)}) collective-permute-start(bf16[256,4096]{1,0:T(8,128)(2,1)S(1)} %dynamic-slice_dynamic-update-slice_fusion.1.near_ref), channel_id=1, source_target_pairs={{0,1},{1,0},{2,3},{3,2},{4,5},{5,4},{6,7},{7,6},{8,9},{9,8},{10,11... | collective-permute-start | bytes 6291464 | tf_op jit(solution)/shard_map/ppermute | solution.py:869
  28.2 5.6 %copy-start.33 = (bf16[128,1024]{1,0:T(8,128)(2,1)}, bf16[128,1024]{1,0:T(8,128)(2,1)S(1)}, u32[]{:S(2)}) copy-start(bf16[128,1024]{1,0:T(8,128)(2,1)S(1)} %collective-permute-done.2.refs_3_.rest_4_) | copy-start | bytes 786436
  28.2 5.6 %copy-start.35 = (bf16[128,1024]{1,0:T(8,128)(2,1)}, bf16[128,1024]{1,0:T(8,128)(2,1)S(1)}, u32[]{:S(2)}) copy-start(bf16[128,1024]{1,0:T(8,128)(2,1)S(1)} %collective-permute-done.1.refs_2_.rest_2_) | copy-start | bytes 786436
  28.2 5.6 %copy-start.37 = (bf16[128,2048]{1,0:T(8,128)(2,1)}, bf16[128,2048]{1,0:T(8,128)(2,1)S(1)}, u32[]{:S(2)}) copy-start(bf16[128,2048]{1,0:T(8,128)(2,1)S(1)} %collective-permute-done.3.refs_1_) | copy-start | bytes 1572868
  28.2 14.4 %copy-start.24 = (bf16[64,4096]{1,0:T(8,128)(2,1)S(1)}, bf16[64,4096]{1,0:T(8,128)(2,1)}, u32[]{:S(2)}) copy-start(bf16[64,4096]{1,0:T(8,128)(2,1)} %down_ref.5) | copy-start | bytes 1572868
  28.3 14.4 %copy-start.38 = (f32[4096]{0:T(1024)S(1)}, f32[4096]{0:T(1024)}, u32[]{:S(2)}) copy-start(f32[4096]{0:T(1024)} %param.22) | copy-start | bytes 49156
  28.3 14.4 %collective-permute-start.11 = (bf16[256,1024]{1,0:T(8,128)(2,1)S(1)}, bf16[256,1024]{1,0:T(8,128)(2,1)S(1)}, u32[]{:S(2)}, u32[]{:S(2)}) collective-permute-start(bf16[256,1024]{1,0:T(8,128)(2,1)S(1)} %get-tuple-element.149), channel_id=1, source_target_pairs={{0,2},{1,3},{4,6},{5,7},{8,10},{9,11},{12,14},{13,15},{16,18},{17,... | collective-permute-start | bytes 1572872 | tf_op jit(solution)/shard_map/ppermute | solution.py:905
  30.5 2.6 %collective-permute-start.9 = (bf16[256,64]{1,0:T(8,128)(2,1)S(1)}, bf16[256,64]{1,0:T(8,128)(2,1)S(1)}, u32[]{:S(2)}, u32[]{:S(2)}) collective-permute-start(bf16[256,64]{1,0:T(8,128)(2,1)S(1)} %fusion), channel_id=1, source_target_pairs={{0,1},{1,0},{2,3},{3,2},{4,5},{5,4},{6,7},{7,6},{8,9},{9,8},{10,11... | collective-permute-start | bytes 98312 | tf_op jit(solution)/shard_map/ppermute | solution.py:869
  30.9 11.7 %copy-start.29 = (bf16[256,1024]{1,0:T(8,128)(2,1)}, bf16[256,1024]{1,0:T(8,128)(2,1)S(1)}, u32[]{:S(2)}) copy-start(bf16[256,1024]{1,0:T(8,128)(2,1)S(1)} %get-tuple-element.182.rest_0_) | copy-start | bytes 1572868
  31.0 22.6 %collective-permute-start.8 = (bf16[256,1024]{1,0:T(8,128)(2,1)S(1)}, bf16[256,1024]{1,0:T(8,128)(2,1)S(1)}, u32[]{:S(2)}, u32[]{:S(2)}) collective-permute-start(bf16[256,1024]{1,0:T(8,128)(2,1)S(1)} %get-tuple-element.143), channel_id=1, source_target_pairs={{0,2},{2,0},{1,3},{3,1},{4,6},{6,4},{5,7},{7,5},{8,10},{10,8},{9,1... | collective-permute-start | bytes 1572872 | tf_op jit(solution)/shard_map/ppermute | solution.py:620
  31.0 22.5 %collective-permute-start.6 = (bf16[384,1024]{1,0:T(8,128)(2,1)S(1)}, bf16[384,1024]{1,0:T(8,128)(2,1)S(1)}, u32[]{:S(2)}, u32[]{:S(2)}) collective-permute-start(bf16[384,1024]{1,0:T(8,128)(2,1)S(1)} %get-tuple-element.141), channel_id=1, source_target_pairs={{0,8},{8,16},{16,24},{24,28},{28,20},{20,12},{12,4},{4,0},{1,9},{9... | collective-permute-start | bytes 2359304 | tf_op jit(solution)/shard_map/ppermute | solution.py:619
  33.0 20.5 %collective-permute-start.7 = (bf16[384,1024]{1,0:T(8,128)(2,1)S(1)}, bf16[384,1024]{1,0:T(8,128)(2,1)S(1)}, u32[]{:S(2)}, u32[]{:S(2)}) collective-permute-start(bf16[384,1024]{1,0:T(8,128)(2,1)S(1)} %get-tuple-element.142), channel_id=1, source_target_pairs={{8,0},{16,8},{24,16},{28,24},{20,28},{12,20},{4,12},{0,4},{9,1},{1... | collective-permute-start | bytes 2359304 | tf_op jit(solution)/shard_map/ppermute | solution.py:619
  42.7 5.2 %copy-start.2 = (bf16[256,4096]{1,0:T(8,128)(2,1)}, bf16[256,4096]{1,0:T(8,128)(2,1)S(1)}, u32[]{:S(2)}) copy-start(bf16[256,4096]{1,0:T(8,128)(2,1)S(1)} %collective-permute-done.10.far_ref) | copy-start | bytes 6291460
  49.2 4.4 %copy-start.9 = (bf16[1024,1024]{1,0:T(8,128)(2,1)}, bf16[1024,1024]{1,0:T(8,128)(2,1)S(1)}, u32[]{:S(2)}) copy-start(bf16[1024,1024]{1,0:T(8,128)(2,1)S(1)} %get-tuple-element.201.slope_ref) | copy-start | bytes 6291460
  49.3 4.3 %collective-permute-start.12 = (f32[256,64]{1,0:T(8,128)S(1)}, f32[256,64]{1,0:T(8,128)S(1)}, u32[]{:S(2)}, u32[]{:S(2)}) collective-permute-start(f32[256,64]{1,0:T(8,128)S(1)} %get-tuple-element.253), channel_id=1, source_target_pairs={{0,1},{1,0},{2,3},{3,2},{4,5},{5,4},{6,7},{7,6},{8,9},{9,8},{10,11... | collective-permute-start | bytes 196616 | tf_op jit(solution)/shard_map/ppermute | solution.py:869
  53.5 5.0 %copy-start.20 = (bf16[256,1024]{1,0:T(8,128)(2,1)}, bf16[256,1024]{1,0:T(8,128)(2,1)S(1)}, u32[]{:S(2)}) copy-start(bf16[256,1024]{1,0:T(8,128)(2,1)S(1)} %collective-permute-done.8.rest_3_.rest_5_) | copy-start | bytes 1572868
  53.5 5.0 %copy-start.12 = (bf16[384,1024]{1,0:T(8,128)(2,1)}, bf16[384,1024]{1,0:T(8,128)(2,1)S(1)}, u32[]{:S(2)}) copy-start(bf16[384,1024]{1,0:T(8,128)(2,1)S(1)} %collective-permute-done.6.refs_0_.rest_1_) | copy-start | bytes 2359300
  53.5 5.0 %copy-start.14 = (bf16[384,1024]{1,0:T(8,128)(2,1)}, bf16[384,1024]{1,0:T(8,128)(2,1)S(1)}, u32[]{:S(2)}) copy-start(bf16[384,1024]{1,0:T(8,128)(2,1)S(1)} %collective-permute-done.7.refs_1_.rest_2_.rest_3_) | copy-start | bytes 2359300
  53.6 23.2 %collective-permute-start.13 = (bf16[384,1024]{1,0:T(8,128)(2,1)S(1)}, bf16[384,1024]{1,0:T(8,128)(2,1)S(1)}, u32[]{:S(2)}, u32[]{:S(2)}) collective-permute-start(bf16[384,1024]{1,0:T(8,128)(2,1)S(1)} %collective-permute-done.6.refs_0_.rest_1_), channel_id=1, source_target_pairs={{0,8},{8,16},{16,24},{24,28},{28,20},{20,12},{12,4},{4,0},{1,9},{9... | collective-permute-start | bytes 2359304 | tf_op jit(solution)/shard_map/ppermute | solution.py:619
  55.6 21.2 %collective-permute-start.14 = (bf16[384,1024]{1,0:T(8,128)(2,1)S(1)}, bf16[384,1024]{1,0:T(8,128)(2,1)S(1)}, u32[]{:S(2)}, u32[]{:S(2)}) collective-permute-start(bf16[384,1024]{1,0:T(8,128)(2,1)S(1)} %collective-permute-done.7.refs_1_.rest_2_.rest_3_), channel_id=1, source_target_pairs={{8,0},{16,8},{24,16},{28,24},{20,28},{12,20},{4,12},{0,4},{9,1},{1... | collective-permute-start | bytes 2359304 | tf_op jit(solution)/shard_map/ppermute | solution.py:619
  55.7 20.3 %collective-permute-start.15 = (bf16[256,1024]{1,0:T(8,128)(2,1)S(1)}, bf16[256,1024]{1,0:T(8,128)(2,1)S(1)}, u32[]{:S(2)}, u32[]{:S(2)}) collective-permute-start(bf16[256,1024]{1,0:T(8,128)(2,1)S(1)} %cut_rows.5), channel_id=1, source_target_pairs={{0,2},{2,0},{1,3},{3,1},{4,6},{6,4},{5,7},{7,5},{8,10},{10,8},{9,1... | collective-permute-start | bytes 1572872 | tf_op jit(solution)/shard_map/ppermute | solution.py:620
  58.5 1.4 collective-permute-start.16
  61.8 13.5 %collective-permute-start.17 = (bf16[8,64,192]{2,1,0:T(8,128)(2,1)S(1)}, bf16[8,64,192]{2,1,0:T(8,128)(2,1)S(1)}, u32[]{:S(2)}, u32[]{:S(2)}) collective-permute-start(bf16[8,64,192]{2,1,0:T(8,128)(2,1)S(1)} %get-tuple-element.168), channel_id=1, source_target_pairs={{0,2},{2,0},{1,3},{3,1},{4,6},{6,4},{5,7},{7,5},{8,10},{10,8},{9,1... | collective-permute-start | bytes 589832 | tf_op jit(solution)/shard_map/ppermute | solution.py:791
  79.9 23.5 %collective-permute-start.18 = (bf16[320,1024]{1,0:T(8,128)(2,1)}, bf16[320,1024]{1,0:T(8,128)(2,1)}, u32[]{:S(2)}, u32[]{:S(2)}) collective-permute-start(bf16[320,1024]{1,0:T(8,128)(2,1)} %get-tuple-element.171), channel_id=1, source_target_pairs={{0,8},{8,16},{16,24},{24,28},{28,20},{20,12},{12,4},{4,0},{1,9},{9... | collective-permute-start | bytes 1966088 | tf_op jit(solution)/shard_map/ppermute | solution.py:619
  81.6 21.8 %collective-permute-start.19 = (bf16[320,1024]{1,0:T(8,128)(2,1)}, bf16[320,1024]{1,0:T(8,128)(2,1)}, u32[]{:S(2)}, u32[]{:S(2)}) collective-permute-start(bf16[320,1024]{1,0:T(8,128)(2,1)} %get-tuple-element.172), channel_id=1, source_target_pairs={{8,0},{16,8},{24,16},{28,24},{20,28},{12,20},{4,12},{0,4},{9,1},{1... | collective-permute-start | bytes 1966088 | tf_op jit(solution)/shard_map/ppermute | solution.py:619
  82.9 20.5 %collective-permute-start.20 = (bf16[256,1024]{1,0:T(8,128)(2,1)}, bf16[256,1024]{1,0:T(8,128)(2,1)S(1)}, u32[]{:S(2)}, u32[]{:S(2)}) collective-permute-start(bf16[256,1024]{1,0:T(8,128)(2,1)} %copy-done.39), channel_id=1, source_target_pairs={{0,2},{2,0},{1,3},{3,1},{4,6},{6,4},{5,7},{7,5},{8,10},{10,8},{9,1... | collective-permute-start | bytes 1572872 | tf_op jit(solution)/shard_map/ppermute | solution.py:620
  91.8 3.0 %copy-start.4 = (bf16[256,4096]{1,0:T(8,128)(2,1)S(1)}, bf16[256,4096]{1,0:T(8,128)(2,1)}, u32[]{:S(2)}) copy-start(bf16[256,4096]{1,0:T(8,128)(2,1)} %copy-done.2) | copy-start | bytes 6291460
  91.8 3.0 %copy-start.17 = (bf16[384,1024]{1,0:T(8,128)(2,1)S(1)}, bf16[384,1024]{1,0:T(8,128)(2,1)}, u32[]{:S(2)}) copy-start(bf16[384,1024]{1,0:T(8,128)(2,1)} %copy-done.16) | copy-start | bytes 2359300
  91.8 3.0 %copy-start.19 = (bf16[384,1024]{1,0:T(8,128)(2,1)S(1)}, bf16[384,1024]{1,0:T(8,128)(2,1)}, u32[]{:S(2)}) copy-start(bf16[384,1024]{1,0:T(8,128)(2,1)} %copy-done.18) | copy-start | bytes 2359300
  92.0 3.7 %copy-start.23 = (bf16[256,1024]{1,0:T(8,128)(2,1)S(1)}, bf16[256,1024]{1,0:T(8,128)(2,1)}, u32[]{:S(2)}) copy-start(bf16[256,1024]{1,0:T(8,128)(2,1)} %copy-done.22) | copy-start | bytes 1572868
  92.0 11.3 %collective-permute-start.21 = (bf16[4,64,192]{2,1,0:T(8,128)(2,1)S(1)}, bf16[4,64,192]{2,1,0:T(8,128)(2,1)S(1)}, u32[]{:S(2)}, u32[]{:S(2)}) collective-permute-start(bf16[4,64,192]{2,1,0:T(8,128)(2,1)S(1)} %get-tuple-element.177), channel_id=1, source_target_pairs={{0,16},{4,20},{8,24},{12,28},{16,0},{20,4},{24,8},{28,12},{1,17},{... | collective-permute-start | bytes 294920 | tf_op jit(solution)/shard_map/ppermute | solution.py:795
  103.4 8.1 %collective-permute-start.25 = (bf16[4,64,192]{2,1,0:T(8,128)(2,1)S(1)}, bf16[4,64,192]{2,1,0:T(8,128)(2,1)S(1)}, u32[]{:S(2)}, u32[]{:S(2)}) collective-permute-start(bf16[4,64,192]{2,1,0:T(8,128)(2,1)S(1)} %get-tuple-element.191), channel_id=1, source_target_pairs={{0,8},{4,12},{8,0},{12,4},{16,24},{20,28},{24,16},{28,20},{1,9},{5... | collective-permute-start | bytes 294920 | tf_op jit(solution)/shard_map/ppermute | solution.py:795
  104.8 6.7 %collective-permute-start.22 = (bf16[128,1024]{1,0:T(8,128)(2,1)S(1)}, bf16[128,1024]{1,0:T(8,128)(2,1)S(1)}, u32[]{:S(2)}, u32[]{:S(2)}) collective-permute-start(bf16[128,1024]{1,0:T(8,128)(2,1)S(1)} %get-tuple-element.187), channel_id=1, source_target_pairs={{0,8},{8,16},{16,24},{24,28},{28,20},{20,12},{12,4},{4,0},{1,9},{9... | collective-permute-start | bytes 786440 | tf_op jit(solution)/shard_map/ppermute | solution.py:619
  106.9 6.4 %collective-permute-start.23 = (bf16[128,1024]{1,0:T(8,128)(2,1)S(1)}, bf16[128,1024]{1,0:T(8,128)(2,1)S(1)}, u32[]{:S(2)}, u32[]{:S(2)}) collective-permute-start(bf16[128,1024]{1,0:T(8,128)(2,1)S(1)} %get-tuple-element.188), channel_id=1, source_target_pairs={{8,0},{16,8},{24,16},{28,24},{20,28},{12,20},{4,12},{0,4},{9,1},{1... | collective-permute-start | bytes 786440 | tf_op jit(solution)/shard_map/ppermute | solution.py:619
  106.9 6.4 %collective-permute-start.24 = (bf16[128,1024]{1,0:T(8,128)(2,1)S(1)}, bf16[128,1024]{1,0:T(8,128)(2,1)S(1)}, u32[]{:S(2)}, u32[]{:S(2)}) collective-permute-start(bf16[128,1024]{1,0:T(8,128)(2,1)S(1)} %get-tuple-element.189), channel_id=1, source_target_pairs={{0,2},{2,0},{1,3},{3,1},{4,6},{6,4},{5,7},{7,5},{8,10},{10,8},{9,1... | collective-permute-start | bytes 786440 | tf_op jit(solution)/shard_map/ppermute | solution.py:620
  110.6 4.1 %copy-start.10 = (bf16[1024,1024]{1,0:T(8,128)(2,1)S(1)}, bf16[1024,1024]{1,0:T(8,128)(2,1)}, u32[]{:S(2)}) copy-start(bf16[1024,1024]{1,0:T(8,128)(2,1)} %copy-done.9) | copy-start | bytes 6291460
  111.5 3.2 %copy-start.8 = (bf16[1024,1024]{1,0:T(8,128)(2,1)S(1)}, bf16[1024,1024]{1,0:T(8,128)(2,1)}, u32[]{:S(2)}) copy-start(bf16[1024,1024]{1,0:T(8,128)(2,1)} %copy-done.7) | copy-start | bytes 6291460
  111.5 3.2 %copy-start.25 = (bf16[64,4096]{1,0:T(8,128)(2,1)S(1)}, bf16[64,4096]{1,0:T(8,128)(2,1)}, u32[]{:S(2)}) copy-start(bf16[64,4096]{1,0:T(8,128)(2,1)} %down_ref.5) | copy-start | bytes 1572868
  113.3 6.2 %collective-permute-start.26 = (bf16[4,64,192]{2,1,0:T(8,128)(2,1)S(1)}, bf16[4,64,192]{2,1,0:T(8,128)(2,1)S(1)}, u32[]{:S(2)}, u32[]{:S(2)}) collective-permute-start(bf16[4,64,192]{2,1,0:T(8,128)(2,1)S(1)} %get-tuple-element.197), channel_id=1, source_target_pairs={{0,4},{4,0},{8,12},{12,8},{16,20},{20,16},{24,28},{28,24},{1,5},{5... | collective-permute-start | bytes 294920 | tf_op jit(solution)/shard_map/ppermute | solution.py:795
  117.8 7.3 %copy-start.5 = (bf16[512,4096]{1,0:T(8,128)(2,1)S(1)}, bf16[512,4096]{1,0:T(8,128)(2,1)}, u32[]{:S(2)}) copy-start(bf16[512,4096]{1,0:T(8,128)(2,1)} %get-tuple-element.216.top_ref) | copy-start | bytes 12582916
  119.5 5.5 %copy-start.6 = (bf16[512,2048]{1,0:T(8,128)(2,1)S(1)}, bf16[512,2048]{1,0:T(8,128)(2,1)}, u32[]{:S(2)}) copy-start(bf16[512,2048]{1,0:T(8,128)(2,1)} %get-tuple-element.217.low_ref) | copy-start | bytes 6291460
  119.7 7.2 %collective-permute-start.28 = (f32[8,128]{1,0:T(8,128)S(1)}, f32[8,128]{1,0:T(8,128)S(1)}, u32[]{:S(2)}, u32[]{:S(2)}) collective-permute-start(f32[8,128]{1,0:T(8,128)S(1)} %get-tuple-element.215), channel_id=1, source_target_pairs={{0,16},{4,20},{8,24},{12,28},{16,0},{20,4},{24,8},{28,12},{1,17},{... | collective-permute-start | bytes 12296 | tf_op jit(solution)/shard_map/ppermute | solution.py:795
  121.8 9.3 %collective-permute-start.30 = (f32[64,192]{1,0:T(8,128)S(1)}, f32[64,192]{1,0:T(8,128)S(1)}, u32[]{:S(2)}, u32[]{:S(2)}) collective-permute-start(f32[64,192]{1,0:T(8,128)S(1)} %get-tuple-element.228), channel_id=1, source_target_pairs={{0,0},{1,16},{2,1},{3,17},{4,2},{5,18},{6,3},{7,19},{8,4},{9,20},{... | collective-permute-start | bytes 147464 | tf_op jit(solution)/shard_map/ppermute | solution.py:1026
  122.4 10.1 %collective-permute-start.27 = (bf16[128,1024]{1,0:T(8,128)(2,1)S(1)}, bf16[128,1024]{1,0:T(8,128)(2,1)S(1)}, u32[]{:S(2)}, u32[]{:S(2)}) collective-permute-start(bf16[128,1024]{1,0:T(8,128)(2,1)S(1)} %get-tuple-element.212), channel_id=1, source_target_pairs={{2,0},{3,1},{6,4},{7,5},{10,8},{11,9},{14,12},{15,13},{18,16},{19,... | collective-permute-start | bytes 786440 | tf_op jit(solution)/shard_map/ppermute | solution.py:905
  123.7 16.1 %collective-permute-start.31 = (bf16[128,1024]{1,0:T(8,128)(2,1)S(1)}, bf16[128,1024]{1,0:T(8,128)(2,1)S(1)}, u32[]{:S(2)}, u32[]{:S(2)}) collective-permute-start(bf16[128,1024]{1,0:T(8,128)(2,1)S(1)} %get-tuple-element.223), channel_id=1, source_target_pairs={{2,0},{3,1},{6,4},{7,5},{10,8},{11,9},{14,12},{15,13},{18,16},{19,... | collective-permute-start | bytes 786440 | tf_op jit(solution)/shard_map/ppermute | solution.py:905
  126.9 4.2 %collective-permute-start.29 = (f32[8,128]{1,0:T(8,128)S(1)}, f32[8,128]{1,0:T(8,128)S(1)}, u32[]{:S(2)}, u32[]{:S(2)}) collective-permute-start(f32[8,128]{1,0:T(8,128)S(1)} %add.338), channel_id=1, source_target_pairs={{0,1},{1,0},{2,3},{3,2},{4,5},{5,4},{6,7},{7,6},{8,9},{9,8},{10,11... | collective-permute-start | bytes 12296 | tf_op jit(solution)/shard_map/ppermute | solution.py:843
  133.8 8.3 %collective-permute-start.33 = (bf16[256,1024]{1,0:T(8,128)(2,1)S(1)}, bf16[256,1024]{1,0:T(8,128)(2,1)S(1)}, u32[]{:S(2)}, u32[]{:S(2)}) collective-permute-start(bf16[256,1024]{1,0:T(8,128)(2,1)S(1)} %get-tuple-element.237), channel_id=1, source_target_pairs={{0,1},{1,0},{2,3},{3,2},{4,5},{5,4},{6,7},{7,6},{8,9},{9,8},{10,11... | collective-permute-start | bytes 1572872 | tf_op jit(solution)/shard_map/ppermute | solution.py:869
  136.3 3.6 %collective-permute-start.32 = (f32[8,128]{1,0:T(8,128)S(1)}, f32[8,128]{1,0:T(8,128)S(1)}, u32[]{:S(2)}, u32[]{:S(2)}) collective-permute-start(f32[8,128]{1,0:T(8,128)S(1)} %add.339), channel_id=1, source_target_pairs={{0,2},{2,0},{1,3},{3,1},{4,6},{6,4},{5,7},{7,5},{8,10},{10,8},{9,1... | collective-permute-start | bytes 12296 | tf_op jit(solution)/shard_map/ppermute | solution.py:843
  141.1 2.0 %collective-permute-start.34 = (bf16[256,1024]{1,0:T(8,128)(2,1)S(1)}, bf16[256,1024]{1,0:T(8,128)(2,1)S(1)}, u32[]{:S(2)}, u32[]{:S(2)}) collective-permute-start(bf16[256,1024]{1,0:T(8,128)(2,1)S(1)} %get-tuple-element.238), channel_id=1, source_target_pairs={{0,1},{1,0},{2,3},{3,2},{4,5},{5,4},{6,7},{7,6},{8,9},{9,8},{10,11... | collective-permute-start | bytes 1572872 | tf_op jit(solution)/shard_map/ppermute | solution.py:869
  (21 other events, 24.6 us)
